TPU v7x, 32 devices: a whole 2x2x4 slice. The times are simulated.
32 devices in a mesh: seq: 8 (over y, x, core), head: 4 (over z).
Axes of the slice: x: 2, y: 2, z: 4, core: 2. Of those that a mesh axis runs over, the one named last changes fastest.
Arguments:
- queries: bfloat16 [2048, 16, 128], P('seq'), may hold values from -6 to 6
- keys: bfloat16 [2048, 2, 128], P(('seq', 'head')), may hold values from -6 to 6
- values: bfloat16 [2048, 2, 128], P(('seq', 'head')), may hold values from -6 to 6
- block_ids: int32 [8], P('seq'), may hold values from 0 to 7, each once
Outputs:
- attended: bfloat16 [2048, 16, 128], P('seq', 'head')
Inputs may be any that keep to these rules, and one draw needn't show every extreme that they name: `block_ids`: each block number appears exactly once.
All inputs are finite; a program needn't handle non-finite values.
Results may differ from a plain program's by a relative error of at most 0.014.
Values may be sent and summed in bfloat16 or wider, within the bound.
No kernel may reach another device: no remote copies, remote signals or barrier semaphores. Data moves between devices by JAX's collectives and lax.ppermute only.
A program may use at most 64 MiB of HBM per device.

v0:
```python
import math

import jax
import jax.numpy as jnp
from jax import lax
from jax.sharding import PartitionSpec as P


def update(
    state,
    query_part,
    key_rows,
    value_rows,
    key_place,
    query_place,
    score_form,
    value_form,
    score_scale,
):
    highest, total, accum = state
    scores = (
        jnp.einsum(score_form, query_part, key_rows, preferred_element_type=jnp.float32)
        * score_scale
    )
    visible = key_place[None, :] <= query_place[:, None]
    scores = jnp.where(visible, scores, -1e30)
    new_high = jnp.maximum(highest, jnp.max(scores, axis=-1))
    expo = jnp.where(visible, jnp.exp(scores - new_high[..., None]), 0.0)
    factor = jnp.exp(highest - new_high)
    total = total * factor + jnp.sum(expo, axis=-1)
    weights = expo.astype(jnp.bfloat16)
    accum = accum * factor[..., None] + jnp.einsum(
        value_form, weights, value_rows, preferred_element_type=jnp.float32
    )
    return (new_high, total, accum)


def shards(queries, keys, values, block_ids):
    rows_dev, all_heads, head_width = queries.shape
    kv_heads = keys.shape[1]
    group = all_heads // kv_heads
    score_scale = head_width ** (-0.5)
    head_index = lax.axis_index("head")
    heads_out = all_heads // lax.axis_size("head")
    all_ids = lax.all_gather(block_ids, "seq", axis=0, tiled=True)
    query_place = block_ids[0] * rows_dev + jnp.arange(rows_dev, dtype=jnp.int32)
    own_queries = lax.dynamic_slice_in_dim(queries, head_index * heads_out, heads_out, 1)
    query_heads = jnp.transpose(own_queries, (1, 0, 2))
    kv_head = head_index * heads_out // group
    start_state = (
        jnp.full((heads_out, rows_dev), -1e30, jnp.float32),
        jnp.zeros((heads_out, rows_dev), jnp.float32),
        jnp.zeros((heads_out, rows_dev, head_width), jnp.float32),
    )
    local_keys, local_values = (
        lax.all_gather(keys, "head", axis=0, tiled=True),
        lax.all_gather(values, "head", axis=0, tiled=True),
    )
    head_keys = lax.dynamic_index_in_dim(local_keys, kv_head, 1, keepdims=False)
    head_values = lax.dynamic_index_in_dim(local_values, kv_head, 1, keepdims=False)
    key_piece = lax.all_gather(head_keys, "seq", axis=0, tiled=True)
    value_piece = lax.all_gather(head_values, "seq", axis=0, tiled=True)
    row_index = jnp.arange(key_piece.shape[0], dtype=jnp.int32)
    key_place = jnp.take(all_ids, row_index // rows_dev) * rows_dev + row_index % rows_dev
    state = start_state
    piece_len = key_piece.shape[0]
    block_len = math.gcd(piece_len, 512)
    block_count = piece_len // block_len
    key_blocks = key_piece.reshape((block_count, block_len) + key_piece.shape[1:])
    value_blocks = value_piece.reshape((block_count, block_len) + value_piece.shape[1:])
    place_blocks = key_place.reshape(block_count, block_len)

    def advance(inner, items):
        key_rows, value_rows, block_place = items
        later = jnp.min(block_place) > jnp.max(query_place)
        inner = lax.cond(
            later,
            lambda held: held,
            lambda held: update(
                held,
                query_heads,
                key_rows,
                value_rows,
                block_place,
                query_place,
                "hqd,kd->hqk",
                "hqk,kd->hqd",
                score_scale,
            ),
            inner,
        )
        return (inner, None)

    state, unused = lax.scan(advance, state, (key_blocks, value_blocks, place_blocks))
    highest, total, accum = state
    result = accum / total[..., None]
    return jnp.transpose(result, (1, 0, 2)).astype(jnp.bfloat16)


def solution(mesh):
    return jax.shard_map(
        shards,
        mesh=mesh,
        in_specs=(
            P("seq", None, None),
            P(("seq", "head"), None, None),
            P(("seq", "head"), None, None),
            P("seq"),
        ),
        out_specs=P("seq", "head", None),
        check_vma=False,
    )
```

profile of v0, /device:TPU:0, one launch (start us, length us, event | category | flops | bytes accessed | tf_op | source)
XLA Modules:
  0.0 83.7 jit_solution(8455187294884223469)
XLA Ops:
  0.0 0.0 copy-start
  0.0 0.9 %copy.10 = bf16[64,2,128]{2,0,1:T(8,128)(2,1)S(1)} copy(bf16[64,2,128]{2,1,0:T(2,128)(2,1)} %param.9) | data formatting | bytes 65536 | tf_op args[1]
  0.9 15.0 %all_gather.16 = bf16[256,2,128]{2,0,1:T(8,128)(2,1)S(1)} all-gather(bf16[64,2,128]{2,0,1:T(8,128)(2,1)S(1)} %copy.10), channel_id=1, replica_groups=mesh['seq'=8,'head'=4] {'head'}, dimensions={0}, use_global_device_ids=true | all-gather | bytes 163840 | tf_op jit(solution)/shard_map/all_gather | solution.py:56
  15.9 9.9 %all-gather = bf16[2048,1,128]{2,0,1:T(8,128)(2,1)S(1)} all-gather(bf16[256,1,128]{2,0,1:T(8,128)(2,1)S(1)} %constant_dynamic-slice_fusion.3), channel_id=2, replica_groups=mesh['seq'=8,'head'=4] {'seq'}, dimensions={0}, use_global_device_ids=true | all-gather | bytes 589824 | tf_op jit(solution)/shard_map/all_gather | solution.py:61
  25.8 0.8 copy.12
  26.5 13.4 %all_gather.18 = bf16[256,2,128]{2,0,1:T(8,128)(2,1)S(1)} all-gather(bf16[64,2,128]{2,0,1:T(8,128)(2,1)S(1)} %copy.12), channel_id=1, replica_groups=mesh['seq'=8,'head'=4] {'head'}, dimensions={0}, use_global_device_ids=true | all-gather | bytes 163840 | tf_op jit(solution)/shard_map/all_gather | solution.py:57
  40.0 9.8 %all-gather.1 = bf16[2048,1,128]{2,0,1:T(8,128)(2,1)S(1)} all-gather(bf16[256,1,128]{2,0,1:T(8,128)(2,1)S(1)} %constant_dynamic-slice_fusion.1), channel_id=3, replica_groups=mesh['seq'=8,'head'=4] {'seq'}, dimensions={0}, use_global_device_ids=true | all-gather | bytes 589824 | tf_op jit(solution)/shard_map/all_gather | solution.py:62
  49.8 1.3 %dynamic-slice = u32[1]{0:T(128)} dynamic-slice(u32[32]{0:T(128)} %constant.143, u32[]{:T(128)S(6)} %add.85), dynamic_slice_sizes={1} | dynamic-slice | bytes 12
  51.8 0.8 dynamic-update-slice
  52.6 7.0 %all-reduce = s32[8]{0:T(128)S(1)} all-reduce(s32[8]{0:T(128)S(1)} %dynamic-update-slice), channel_id=1, replica_groups=mesh['seq'=8,'head'=4] {'seq'}, use_global_device_ids=true, to_apply=%add | all-reduce | flops 8 | bytes 64
  59.6 0.7 fusion.26
  60.3 4.3 %compare_select_fusion.1 = s32[2048,1]{0,1:T(1,128)S(1)} fusion(s32[]{:T(128)} %bitcast.8, s32[]{:T(128)} %bitcast.9, s32[]{:T(128)} %bitcast.10, s32[]{:T(128)} %bitcast.11, s32[]{:T(128)} %bitcast.12, s32[]{:T(128)} %bitcast.14, s32[]{:T(128)} %bitcast.13), kind=kLoop, calls=%fused_computation.32 | loop fusion | flops 47104 | bytes 8220 | tf_op jit(solution)/shard_map/jit(_take)/gather | solution.py:64
  64.6 0.1 compare_reduce_fusion
  64.6 0.7 broadcast_select_fusion
  65.4 0.0 copy-done
  65.4 0.1 constant_dynamic-slice_fusion.2
  65.6 0.6 add_reduce_fusion
  66.3 16.1 %while.16 = (s32[]{:T(128)}, f32[4,256]{1,0:T(4,128)S(1)}, f32[4,256]{1,0:T(4,128)S(1)}, f32[4,256,128]{2,1,0:T(8,128)S(1)}, s32[4,512]{1,0:T(4,128)S(1)}, /*ind...) while((s32[]{:T(128)}, f32[4,256]{1,0:T(4,128)S(1)}, ...), condition=%wide.region_7.8_spmd.clone, body=%wide.region_1.7_spmd.clone.sunk | while | flops 275647232 | bytes 8464655 | solution.py:94
  66.3 0.7 fusion.29
  68.2 2.1 %conditional.3 = (f32[4,256]{1,0:T(4,128)S(1)}, f32[4,256]{1,0:T(4,128)S(1)}, f32[4,256,128]{2,1,0:T(8,128)S(1)}) conditional(s32[]{:T(128)} %convert_element_type.24, (s32[1,512]{1,0:T(1,128)S(1)}, s32[]{:T(128)}, bf16[4,512,128]{2,1,0:T(8,128)(2,1)S(1)}, s32[]{:T(128)}, bf16[4,256,128]{2,1,0:T(8,128)(2,1)S(1)}, /*index=5*/f32[4,256]{1,0:T(4,128)S(1)}, ...), branch_computations={%region_3.5_spmd, %region_6.6_spmd} | conditional | flops 275646720 | bytes 8451108 | solution.py:76
  68.2 0.1 broadcast_compare_fusion
  68.4 0.5 fusion.2
  68.9 0.5 fusion.4
  69.4 0.9 %convolution_add_fusion = f32[4,256,128]{2,1,0:T(8,128)S(1)} fusion(f32[512,4,256]{2,0,1:T(8,128)S(1)} %get-tuple-element.234, f32[4,256]{1,0:T(4,128)S(1)} %max.4, pred[256,512]{0,1:T(8,128)(4,1)S(1)} %broadcast_compare_fusion, f32[4,256,128]{2,1,0:T(8,128)S(1)} %get-tuple-element.160, f32[4,256]{1,0:T(4,128)S(1)} %get-tuple-element.230, ...), kind=kOutput, calls=%fused_computation.6 | convolution fusion | flops 137101312 | bytes 3416068 | tf_op jit(solution)/shard_map/while/body/eval_jaxpr/cond/branch_0_fun/hqk,kd->hqd/dot_general | solution.py:32
  70.3 0.7 fusion.29
  72.2 2.1 %conditional.3 = (f32[4,256]{1,0:T(4,128)S(1)}, f32[4,256]{1,0:T(4,128)S(1)}, f32[4,256,128]{2,1,0:T(8,128)S(1)}) conditional(s32[]{:T(128)} %convert_element_type.24, (s32[1,512]{1,0:T(1,128)S(1)}, s32[]{:T(128)}, bf16[4,512,128]{2,1,0:T(8,128)(2,1)S(1)}, s32[]{:T(128)}, bf16[4,256,128]{2,1,0:T(8,128)(2,1)S(1)}, /*index=5*/f32[4,256]{1,0:T(4,128)S(1)}, ...), branch_computations={%region_3.5_spmd, %region_6.6_spmd} | conditional | flops 275646720 | bytes 8451108 | solution.py:76
  72.2 0.1 broadcast_compare_fusion
  72.4 0.5 fusion.2
  72.9 0.5 fusion.4
  73.4 0.9 %convolution_add_fusion = f32[4,256,128]{2,1,0:T(8,128)S(1)} fusion(f32[512,4,256]{2,0,1:T(8,128)S(1)} %get-tuple-element.234, f32[4,256]{1,0:T(4,128)S(1)} %max.4, pred[256,512]{0,1:T(8,128)(4,1)S(1)} %broadcast_compare_fusion, f32[4,256,128]{2,1,0:T(8,128)S(1)} %get-tuple-element.160, f32[4,256]{1,0:T(4,128)S(1)} %get-tuple-element.230, ...), kind=kOutput, calls=%fused_computation.6 | convolution fusion | flops 137101312 | bytes 3416068 | tf_op jit(solution)/shard_map/while/body/eval_jaxpr/cond/branch_0_fun/hqk,kd->hqd/dot_general | solution.py:32
  74.3 0.7 fusion.29
  76.2 2.1 %conditional.3 = (f32[4,256]{1,0:T(4,128)S(1)}, f32[4,256]{1,0:T(4,128)S(1)}, f32[4,256,128]{2,1,0:T(8,128)S(1)}) conditional(s32[]{:T(128)} %convert_element_type.24, (s32[1,512]{1,0:T(1,128)S(1)}, s32[]{:T(128)}, bf16[4,512,128]{2,1,0:T(8,128)(2,1)S(1)}, s32[]{:T(128)}, bf16[4,256,128]{2,1,0:T(8,128)(2,1)S(1)}, /*index=5*/f32[4,256]{1,0:T(4,128)S(1)}, ...), branch_computations={%region_3.5_spmd, %region_6.6_spmd} | conditional | flops 275646720 | bytes 8451108 | solution.py:76
  76.2 0.1 broadcast_compare_fusion
  76.4 0.5 fusion.2
  76.9 0.5 fusion.4
  77.4 0.9 %convolution_add_fusion = f32[4,256,128]{2,1,0:T(8,128)S(1)} fusion(f32[512,4,256]{2,0,1:T(8,128)S(1)} %get-tuple-element.234, f32[4,256]{1,0:T(4,128)S(1)} %max.4, pred[256,512]{0,1:T(8,128)(4,1)S(1)} %broadcast_compare_fusion, f32[4,256,128]{2,1,0:T(8,128)S(1)} %get-tuple-element.160, f32[4,256]{1,0:T(4,128)S(1)} %get-tuple-element.230, ...), kind=kOutput, calls=%fused_computation.6 | convolution fusion | flops 137101312 | bytes 3416068 | tf_op jit(solution)/shard_map/while/body/eval_jaxpr/cond/branch_0_fun/hqk,kd->hqd/dot_general | solution.py:32
  78.4 0.7 fusion.29
  80.2 2.1 %conditional.3 = (f32[4,256]{1,0:T(4,128)S(1)}, f32[4,256]{1,0:T(4,128)S(1)}, f32[4,256,128]{2,1,0:T(8,128)S(1)}) conditional(s32[]{:T(128)} %convert_element_type.24, (s32[1,512]{1,0:T(1,128)S(1)}, s32[]{:T(128)}, bf16[4,512,128]{2,1,0:T(8,128)(2,1)S(1)}, s32[]{:T(128)}, bf16[4,256,128]{2,1,0:T(8,128)(2,1)S(1)}, /*index=5*/f32[4,256]{1,0:T(4,128)S(1)}, ...), branch_computations={%region_3.5_spmd, %region_6.6_spmd} | conditional | flops 275646720 | bytes 8451108 | solution.py:76
  80.3 0.1 broadcast_compare_fusion
  80.4 0.5 fusion.2
  80.9 0.5 fusion.4
  81.5 0.9 %convolution_add_fusion = f32[4,256,128]{2,1,0:T(8,128)S(1)} fusion(f32[512,4,256]{2,0,1:T(8,128)S(1)} %get-tuple-element.234, f32[4,256]{1,0:T(4,128)S(1)} %max.4, pred[256,512]{0,1:T(8,128)(4,1)S(1)} %broadcast_compare_fusion, f32[4,256,128]{2,1,0:T(8,128)S(1)} %get-tuple-element.160, f32[4,256]{1,0:T(4,128)S(1)} %get-tuple-element.230, ...), kind=kOutput, calls=%fused_computation.6 | convolution fusion | flops 137101312 | bytes 3416068 | tf_op jit(solution)/shard_map/while/body/eval_jaxpr/cond/branch_0_fun/hqk,kd->hqd/dot_general | solution.py:32
  82.4 0.1 copy.13
  82.5 1.2 %fusion.21 = bf16[256,4,128]{2,1,0:T(4,128)(2,1)} fusion(f32[4,256]{0,1:T(8,128)S(1)} %copy.13, f32[4,256,128]{2,1,0:T(8,128)S(1)} %get-tuple-element.178), kind=kLoop, calls=%fused_computation.29 | loop fusion | flops 262144 | bytes 790528 | tf_op jit(solution)/shard_map/convert_element_type | solution.py:97
  (29 shorter events, 0.3 us)
Async XLA Ops:
  0.0 65.4 %copy-start = (bf16[256,16,128]{2,1,0:T(8,128)(2,1)S(1)}, bf16[256,16,128]{2,1,0:T(8,128)(2,1)}, u32[]{:S(2)}) copy-start(bf16[256,16,128]{2,1,0:T(8,128)(2,1)} %param.8) | copy-start | bytes 3145732
where the time goes:
time: 83.2 us; the launch traced here: 83.7 us
  blocking collectives  55.2 us (66%)
  other arithmetic  12.3 us (15%)
  matrix products  5.43 us (7%)
  loops' own time  5.14 us (6%)
  local copies, waits for them, and re-layouts  4.82 us (6%)
    all_gather x1, blocking collectives, shards(): lax.all_gather(keys, 'head', axis=0, tiled=True)  15 us
    all_gather x1, blocking collectives, shards(): lax.all_gather(values, 'head', axis=0, tiled=True)  13.4 us
    all_gather x1, blocking collectives, shards(): key_piece = lax.all_gather(head_keys, 'seq', axis=0, tiled=True)  9.85 us
    all_gather x1, blocking collectives, shards(): value_piece = lax.all_gather(head_values, 'seq', axis=0, tiled=True)  9.82 us
    unnamed x1, blocking collectives  7.03 us
    gather x3, other arithmetic, shards(): jnp.take(all_ids, row_index // rows_dev) * rows_dev + row_index % rows_dev  5.05 us
    another operation x1, loops' own time, shards(): lax.scan(advance, state, (key_blocks, value_blocks, place_blocks))  4.93 us
    unnamed x8, local copies, waits for them, and re-layouts  3.77 us

commit v1 on v0

v1 whole, which is shorter than its diff:
```python
import functools
import math

import jax
import jax.numpy as jnp
from jax import lax
from jax.experimental import pallas as pl
from jax.experimental.pallas import tpu as pltpu
from jax.sharding import PartitionSpec as P

MARK = 16
DIRECT_BYTES = 8 * 1024 * 1024


def attend(kv_heads, part, scale, own_ref, query_ref, rows_ref, out_ref, high_ref, total_ref, accum_ref):
    blocks, pieces = rows_ref.shape[:2]
    block_rows = pieces * part
    query_rows, head_width = query_ref.shape
    group = query_rows // block_rows
    own = own_ref[0]
    kv_head = own_ref[1]
    step = pl.program_id(0)

    @pl.when(step == 0)
    def _():
        high_ref[...] = jnp.full_like(high_ref, -1e30)
        total_ref[...] = jnp.zeros_like(total_ref)
        accum_ref[...] = jnp.zeros_like(accum_ref)

    def fold(block, diagonal):
        key_rows = jnp.concatenate(
            [rows_ref[block, piece, pl.ds(pl.multiple_of(kv_head * part, part), part), :] for piece in range(pieces)]
        )
        value_rows = jnp.concatenate(
            [
                rows_ref[block, piece, pl.ds(pl.multiple_of((kv_heads + kv_head) * part, part), part), :]
                for piece in range(pieces)
            ]
        )
        scores = lax.dot_general(
            key_rows, query_ref[...], (((1,), (1,)), ((), ())), preferred_element_type=jnp.float32
        )
        if diagonal:
            key_at = lax.broadcasted_iota(jnp.int32, scores.shape, 0)
            query_at = lax.broadcasted_iota(jnp.int32, scores.shape, 1) // group
            scores = jnp.where(key_at <= query_at, scores, -1e30)
        old_high = high_ref[...]
        new_high = jnp.maximum(old_high, jnp.max(scores, axis=0, keepdims=True))
        expo = jnp.exp((scores - new_high) * scale)
        factor = jnp.exp((old_high - new_high) * scale)
        high_ref[...] = new_high
        total_ref[...] = total_ref[...] * factor + jnp.sum(expo, axis=0, keepdims=True)
        accum_ref[...] = accum_ref[...] * factor + lax.dot_general(
            value_rows, expo.astype(jnp.bfloat16), (((0,), (0,)), ((), ())), preferred_element_type=jnp.float32
        )

    for block in range(blocks):
        mark = rows_ref[block, 0, pl.ds(2 * kv_heads * part, MARK), :]
        place = jnp.max(mark.astype(jnp.float32)).astype(jnp.int32)

        @pl.when(place < own)
        def _():
            fold(block, False)

        @pl.when(place == own)
        def _():
            fold(block, True)

    @pl.when(step == pl.num_programs(0) - 1)
    def _():
        result = accum_ref[...] / total_ref[...]
        out_ref[...] = result.T.astype(out_ref.dtype)


def shards(queries, keys, values, block_ids):
    rows_dev, all_heads, head_width = queries.shape
    part, kv_heads = keys.shape[:2]
    head_index = lax.axis_index("head")
    head_shards = lax.axis_size("head")
    seq_shards = lax.axis_size("seq")
    heads_out = all_heads // head_shards
    kv_head = head_index * heads_out // (all_heads // kv_heads)
    own_queries = lax.dynamic_slice_in_dim(queries, head_index * heads_out, heads_out, 1)
    own_queries = own_queries.reshape(rows_dev * heads_out, head_width)
    mark = jnp.broadcast_to(block_ids.astype(jnp.bfloat16)[:, None], (MARK, head_width))
    packed = jnp.concatenate(
        [
            jnp.transpose(keys, (1, 0, 2)).reshape(kv_heads * part, head_width),
            jnp.transpose(values, (1, 0, 2)).reshape(kv_heads * part, head_width),
            mark,
        ]
    )
    if seq_shards * head_shards * packed.size * 2 <= DIRECT_BYTES:
        rows = lax.all_gather(packed, ("seq", "head"), axis=0, tiled=False)
        rows = rows.reshape(seq_shards, head_shards, packed.shape[0], head_width)
    else:
        rows = lax.all_gather(packed, "head", axis=0, tiled=False)
        sets = rows[:, : 2 * kv_heads * part].reshape(head_shards, 2, kv_heads, part, head_width)
        sets = lax.dynamic_index_in_dim(sets, kv_head, 2, keepdims=False)
        sets = sets.reshape(head_shards, 2 * part, head_width)
        rows = jnp.concatenate([sets, rows[:, 2 * kv_heads * part :]], axis=1)
        rows = lax.all_gather(rows, "seq", axis=0, tiled=False)
        kv_heads, kv_head = 1, jnp.int32(0)
    own = jnp.stack([block_ids[0], kv_head.astype(jnp.int32)])
    unit = math.gcd(seq_shards, 8)
    query_rows = rows_dev * heads_out
    result = pl.pallas_call(
        functools.partial(attend, kv_heads, part, head_width ** (-0.5)),
        grid=(seq_shards // unit,),
        out_shape=jax.ShapeDtypeStruct((query_rows, head_width), jnp.bfloat16),
        in_specs=[
            pl.BlockSpec(memory_space=pltpu.SMEM),
            pl.BlockSpec((query_rows, head_width), lambda i: (0, 0)),
            pl.BlockSpec((unit,) + rows.shape[1:], lambda i: (i, 0, 0, 0)),
        ],
        out_specs=pl.BlockSpec((query_rows, head_width), lambda i: (0, 0)),
        scratch_shapes=[
            pltpu.VMEM((1, query_rows), jnp.float32),
            pltpu.VMEM((1, query_rows), jnp.float32),
            pltpu.VMEM((head_width, query_rows), jnp.float32),
        ],
        compiler_params=pltpu.CompilerParams(vmem_limit_bytes=32 * 1024 * 1024),
    )(own, own_queries, rows)
    return result.reshape(rows_dev, heads_out, head_width)


def solution(mesh):
    return jax.shard_map(
        shards,
        mesh=mesh,
        in_specs=(
            P("seq", None, None),
            P(("seq", "head"), None, None),
            P(("seq", "head"), None, None),
            P("seq"),
        ),
        out_specs=P("seq", "head", None),
        check_vma=False,
    )
```

time: 83.2 us -> 85.4 us (1.026); the launches traced: 83.7 us -> 84.5 us
  waiting for transfers between devices: 0 us -> 60.1 us
  blocking collectives: 55.2 us -> 0 us
  between operations: 0.74 us -> 14.2 us
  other arithmetic: 12.3 us -> 0.81 us
  Pallas kernels: 0 us -> 6.09 us
  matrix products: 5.43 us -> 0 us
  loops' own time: 5.14 us -> 0 us
  local copies, waits for them, and re-layouts: 4.82 us -> 3.31 us
    all_gather x0 -> x1, waiting for transfers between devices: none -> 60.1 us  [shards(): rows = lax.all_gather(packed, ('seq', 'head'), axis=0, tiled=False)]
    all_gather x4 -> x0, blocking collectives: 48.2 us -> none  [the longest x1 15 us: shards(): lax.all_gather(keys, 'head', axis=0, tiled=True)]
    unnamed x1 -> x0, blocking collectives: 7.03 us -> none
    pallas_call x0 -> x1, Pallas kernels: none -> 6.09 us  [shards(): pl.pallas_call(functools.partial(attend, kv_heads, part, head_width ** (-...]
    dot_general x8 -> x0, matrix products: 5.43 us -> none  [the longest x4 3.49 us: update(): jnp.einsum(value_form, weights, value_rows, preferred_element_type=jnp.fl...]
    another operation x5 -> x0, loops' own time: 5.14 us -> none  [the longest x1 4.93 us: shards(): lax.scan(advance, state, (key_blocks, value_blocks, place_blocks))]
    gather x3 -> x0, other arithmetic: 5.05 us -> none  [shards(): jnp.take(all_ids, row_index // rows_dev) * rows_dev + row_index % rows_dev]
    reduce_min x4 -> x0, other arithmetic: 2.67 us -> none  [advance(): later = jnp.min(block_place) > jnp.max(query_place)]
  transfers between devices with their start and end apart: 0 -> 1, of which waited for: 0 -> 1; matrix products, arithmetic and copies ran while one was open for 0% -> 0% of each run, Pallas kernels for 0% -> 0%
where the time goes in v1:
time: 85.4 us; the launch traced here: 84.5 us
  waiting for transfers between devices  60.1 us (70%)
  between operations  14.2 us (17%)
  Pallas kernels  6.09 us (7%)
  local copies, waits for them, and re-layouts  3.31 us (4%)
    all_gather x1, waiting for transfers between devices, shards(): rows = lax.all_gather(packed, ('seq', 'head'), axis=0, tiled=False)  60.1 us
    pallas_call x1, Pallas kernels, shards(): pl.pallas_call(functools.partial(attend, kv_heads, part, head_width ** (-...  6.09 us
    unnamed x6, local copies, waits for them, and re-layouts  3.16 us
  transfers between devices with their start and end apart: 1, of which 1 were waited for; matrix products, arithmetic and copies ran while one was open for 0% of the time, Pallas kernels for 0%

profile of v1, /device:TPU:0, one launch (start us, length us, event | category | flops | bytes accessed | tf_op | source)
XLA Modules:
  0.0 84.5 jit_solution(547033597282978892)
XLA Ops:
  6.5 0.0 copy-start
  6.5 0.0 all-gather.3.cloned.1.call-start
  7.3 0.8 copy.5
  8.1 0.8 copy.6
  8.8 0.7 maximum_maximum_fusion
  9.6 0.0 all-gather.3.cloned.1.call-update
  9.6 0.1 pad_add_fusion.own_ref
  9.7 0.0 copy-done
  9.7 0.1 constant_dynamic-slice_fusion
  9.8 60.1 %all-gather.3.cloned.1.call-done = bf16[8704,128]{1,0:T(8,128)(2,1)} async-done(((bf16[272,128]{1,0:T(8,128)(2,1)}), bf16[8704,128]{1,0:T(8,128)(2,1)}) %all-gather.3.cloned.1.call-update) | async-done | bytes 2228240 | tf_op jit(solution)/shard_map/all_gather | solution.py:94
  69.9 0.0 copy-start.1
  69.9 1.6 %copy-done.1 = bf16[8704,128]{1,0:T(8,128)(2,1)S(1)} copy-done((bf16[8704,128]{1,0:T(8,128)(2,1)S(1)}, bf16[8704,128]{1,0:T(8,128)(2,1)}, u32[]{:S(2)}) %copy-start.1) | copy-done | bytes 2228248
  71.5 6.1 %shard_map.46 = bf16[1024,128]{1,0:T(8,128)(2,1)} custom-call(s32[2]{0:T(128)S(1)} %pad_add_fusion.own_ref, bf16[1024,128]{1,0:T(8,128)(2,1)S(1)} %bitcast.12, bf16[8,4,272,128]{3,2,1,0:T(8,128)(2,1)S(1)} %bitcast.11), custom_call_target="tpu_custom_call" | custom-call | tf_op jit(solution)/shard_map/pallas_call | solution.py:107
  (2 shorter events, 0.0 us)
Async XLA Ops:
  6.5 3.2 %copy-start = (bf16[256,16,128]{2,1,0:T(8,128)(2,1)S(1)}, bf16[256,16,128]{2,1,0:T(8,128)(2,1)}, u32[]{:S(2)}) copy-start(bf16[256,16,128]{2,1,0:T(8,128)(2,1)} %param.4) | copy-start | bytes 3145732
  6.5 63.4 %all-gather.3.cloned.1.call-start = ((), (), s32[]{:S(2)}) async-start(), calls=%async_computation | async-start | bytes 2297856 | tf_op jit(solution)/shard_map/all_gather | solution.py:94
  69.9 1.6 %copy-start.1 = (bf16[8704,128]{1,0:T(8,128)(2,1)S(1)}, bf16[8704,128]{1,0:T(8,128)(2,1)}, u32[]{:S(2)}) copy-start(bf16[8704,128]{1,0:T(8,128)(2,1)} %all-gather.3.cloned.1.call-done) | copy-start | bytes 6684676
Sparse Core Ops, SparseCore 0:
  10.2 59.6 all-gather.2

commit v2 on v1

v2 whole, which is shorter than its diff:
```python
import functools
import math

import jax
import jax.numpy as jnp
from jax import lax
from jax.experimental import pallas as pl
from jax.experimental.pallas import tpu as pltpu
from jax.sharding import PartitionSpec as P

MARK = 16
PERMUTES = 8


def pack(heads_out, group, keys_ref, values_ref, *out_refs):
    kv_heads = keys_ref.shape[1]
    part = keys_ref.shape[0]
    shards = len(out_refs)
    here = lax.axis_index("head")
    key_rows = [keys_ref[:, head, :] for head in range(kv_heads)]
    value_rows = [values_ref[:, head, :] for head in range(kv_heads)]
    for shift, out_ref in enumerate(out_refs):
        kv_head = lax.rem(here + shift, shards) * heads_out // group
        chosen_key, chosen_value = key_rows[0], value_rows[0]
        for head in range(1, kv_heads):
            chosen_key = jnp.where(kv_head == head, key_rows[head], chosen_key)
            chosen_value = jnp.where(kv_head == head, value_rows[head], chosen_value)
        out_ref[:part, :] = chosen_key
        out_ref[part:, :] = chosen_value


def attend(pieces, part, scale, own_ref, query_ref, *refs):
    near_refs, far_refs = refs[:pieces], refs[pieces:-4]
    out_ref, high_ref, total_ref, accum_ref = refs[-4:]
    query_rows = query_ref.shape[0]
    group = query_rows // (pieces * part)
    own = own_ref[0]
    here = lax.axis_index("head")
    step = pl.program_id(0)

    def fold(key_parts, value_parts, diagonal):
        key_rows = jnp.concatenate(key_parts)
        value_rows = jnp.concatenate(value_parts)
        scores = lax.dot_general(
            key_rows, query_ref[...], (((1,), (1,)), ((), ())), preferred_element_type=jnp.float32
        )
        if diagonal:
            row = lax.broadcasted_iota(jnp.int32, scores.shape, 0)
            piece = lax.rem(here + pieces - row // part, pieces)
            key_at = piece * part + row % part
            query_at = lax.broadcasted_iota(jnp.int32, scores.shape, 1) // group
            scores = jnp.where(key_at <= query_at, scores, -1e30)
        high = jnp.max(scores, axis=0, keepdims=True)
        if not diagonal:
            old_high = high_ref[...]
            high = jnp.maximum(old_high, high)
            factor = jnp.exp((old_high - high) * scale)
        expo = jnp.exp((scores - high) * scale)
        total = jnp.sum(expo, axis=0, keepdims=True)
        product = lax.dot_general(
            value_rows, expo.astype(jnp.bfloat16), (((0,), (0,)), ((), ())), preferred_element_type=jnp.float32
        )
        if not diagonal:
            total = total_ref[...] * factor + total
            product = accum_ref[...] * factor + product
        high_ref[...] = high
        total_ref[...] = total
        accum_ref[...] = product

    @pl.when(step == 0)
    def _():
        fold([ref[:part, :] for ref in near_refs], [ref[part:, :] for ref in near_refs], True)

    for far_ref in far_refs:
        for block in range(far_ref.shape[0]):
            mark = far_ref[block, pl.ds(2 * pieces * part, MARK), :]
            place = jnp.max(mark.astype(jnp.float32)).astype(jnp.int32)

            @pl.when(place < own)
            def _():
                fold(
                    [far_ref[block, pl.ds(2 * piece * part, part), :] for piece in range(pieces)],
                    [far_ref[block, pl.ds((2 * piece + 1) * part, part), :] for piece in range(pieces)],
                    False,
                )

    @pl.when(step == pl.num_programs(0) - 1)
    def _():
        result = accum_ref[...] / total_ref[...]
        out_ref[...] = result.T.astype(out_ref.dtype)


def shards(queries, keys, values, block_ids):
    rows_dev, all_heads, head_width = queries.shape
    part, kv_heads = keys.shape[:2]
    head_index = lax.axis_index("head")
    pieces = lax.axis_size("head")
    blocks = lax.axis_size("seq")
    heads_out = all_heads // pieces
    own_queries = lax.dynamic_slice_in_dim(queries, head_index * heads_out, heads_out, 1)
    own_queries = own_queries.reshape(rows_dev * heads_out, head_width)
    mark = jnp.broadcast_to(block_ids.astype(jnp.bfloat16)[:, None], (MARK, head_width))
    whole = pl.BlockSpec(memory_space=pltpu.VMEM)
    packed = pl.pallas_call(
        functools.partial(pack, heads_out, all_heads // kv_heads),
        out_shape=[jax.ShapeDtypeStruct((2 * part, head_width), jnp.bfloat16)] * pieces,
        in_specs=[whole, whole],
        out_specs=[whole] * pieces,
    )(keys, values)
    near = [packed[0]] + [
        lax.ppermute(packed[shift], "head", [(i, (i + shift) % pieces) for i in range(pieces)])
        for shift in range(1, pieces)
    ]
    block = jnp.concatenate(near + [mark])
    if blocks <= PERMUTES:
        far = [
            lax.ppermute(block, "seq", [(i, (i + shift) % blocks) for i in range(blocks)])[None]
            for shift in range(1, blocks)
        ]
        unit = steps = 1
    else:
        far = [lax.all_gather(block, "seq", axis=0, tiled=False)]
        unit = math.gcd(blocks, 8)
        steps = blocks // unit
    query_rows = rows_dev * heads_out
    result = pl.pallas_call(
        functools.partial(attend, pieces, part, head_width ** (-0.5)),
        grid=(steps,),
        out_shape=jax.ShapeDtypeStruct((query_rows, head_width), jnp.bfloat16),
        in_specs=[pl.BlockSpec(memory_space=pltpu.SMEM), pl.BlockSpec((query_rows, head_width), lambda i: (0, 0))]
        + [pl.BlockSpec(near[0].shape, lambda i: (0, 0))] * pieces
        + [pl.BlockSpec((unit,) + block.shape, lambda i: (i, 0, 0))] * len(far),
        out_specs=pl.BlockSpec((query_rows, head_width), lambda i: (0, 0)),
        scratch_shapes=[
            pltpu.VMEM((1, query_rows), jnp.float32),
            pltpu.VMEM((1, query_rows), jnp.float32),
            pltpu.VMEM((head_width, query_rows), jnp.float32),
        ],
        compiler_params=pltpu.CompilerParams(vmem_limit_bytes=32 * 1024 * 1024),
    )(block_ids, own_queries, *near, *far)
    return result.reshape(rows_dev, heads_out, head_width)


def solution(mesh):
    return jax.shard_map(
        shards,
        mesh=mesh,
        in_specs=(
            P("seq", None, None),
            P(("seq", "head"), None, None),
            P(("seq", "head"), None, None),
            P("seq"),
        ),
        out_specs=P("seq", "head", None),
        check_vma=False,
    )
```

time: 85.4 us -> 34 us (0.40)
  the two profiles are of different devices: /device:TPU:0 before, /device:TPU:1 now
where the time goes in v2:
time: 34 us; the launch traced here: 33.8 us
  starting transfers between devices  15.6 us (46%)
  Pallas kernels  8.89 us (26%)
  waiting for transfers between devices  7.64 us (22%)
  local copies, waits for them, and re-layouts  0.95 us (3%)
  between operations  0.72 us (2%)
    ppermute x7, starting transfers between devices, shards(): lax.ppermute(block, 'seq', [(i, (i + shift) % blocks) for i in range(bloc...  10.1 us
    pallas_call x1, Pallas kernels, shards(): pl.pallas_call(functools.partial(attend, pieces, part, head_width ** (-0....  6.88 us
    ppermute x7, waiting for transfers between devices, shards(): lax.ppermute(block, 'seq', [(i, (i + shift) % blocks) for i in range(bloc...  6.6 us
    ppermute x3, starting transfers between devices, shards(): lax.ppermute(packed[shift], 'head', [(i, (i + shift) % pieces) for i in r...  5.5 us
    pallas_call x1, Pallas kernels, shards(): pl.pallas_call(functools.partial(pack, heads_out, all_heads // kv_heads),...  2.01 us
    ppermute x3, waiting for transfers between devices, shards(): lax.ppermute(packed[shift], 'head', [(i, (i + shift) % pieces) for i in r...  1.04 us
    unnamed x8, local copies, waits for them, and re-layouts  0.8 us
  transfers between devices with their start and end apart: 10, of which 3 were waited for; matrix products, arithmetic and copies ran while one was open for 3% of the time, Pallas kernels for 0%

profile of v2, /device:TPU:1, one launch (start us, length us, event | category | flops | bytes accessed | tf_op | source)
XLA Modules:
  0.0 33.8 jit_solution(15203954846270572435)
XLA Ops:
  0.0 0.0 copy-start
  0.0 2.0 %shard_map.46 = (bf16[128,128]{1,0:T(8,128)(2,1)}, bf16[128,128]{1,0:T(8,128)(2,1)}, bf16[128,128]{1,0:T(8,128)(2,1)}, bf16[128,128]{1,0:T(8,128)(2,1)}) custom-call(bf16[64,2,128]{2,1,0:T(2,128)(2,1)} %keys_ref.1, bf16[64,2,128]{2,1,0:T(2,128)(2,1)} %values_ref.1), custom_call_target="tpu_custom_call" | custom-call | tf_op jit(solution)/shard_map/pallas_call | solution.py:104
  2.0 2.1 %collective-permute-start = (bf16[128,128]{1,0:T(8,128)(2,1)}, bf16[128,128]{1,0:T(8,128)(2,1)S(1)}, u32[]{:S(2)}, u32[]{:S(2)}) collective-permute-start(bf16[128,128]{1,0:T(8,128)(2,1)} %get-tuple-element.10), channel_id=1, source_target_pairs={{0,1},{1,2},{2,3},{3,0},{4,5},{5,6},{6,7},{7,4},{8,9},{9,10},{10,1... | collective-permute-start | bytes 98312 | tf_op jit(solution)/shard_map/ppermute | solution.py:111
  4.1 2.3 %collective-permute-start.1 = (bf16[128,128]{1,0:T(8,128)(2,1)}, bf16[128,128]{1,0:T(8,128)(2,1)S(1)}, u32[]{:S(2)}, u32[]{:S(2)}) collective-permute-start(bf16[128,128]{1,0:T(8,128)(2,1)} %get-tuple-element.11), channel_id=1, source_target_pairs={{0,2},{1,3},{2,0},{3,1},{4,6},{5,7},{6,4},{7,5},{8,10},{9,11},{10,... | collective-permute-start | bytes 98312 | tf_op jit(solution)/shard_map/ppermute | solution.py:111
  6.5 1.1 %collective-permute-start.2 = (bf16[128,128]{1,0:T(8,128)(2,1)}, bf16[128,128]{1,0:T(8,128)(2,1)S(1)}, u32[]{:S(2)}, u32[]{:S(2)}) collective-permute-start(bf16[128,128]{1,0:T(8,128)(2,1)} %get-tuple-element.12), channel_id=1, source_target_pairs={{0,3},{1,0},{2,1},{3,2},{4,7},{5,4},{6,5},{7,6},{8,11},{9,8},{10,9... | collective-permute-start | bytes 98312 | tf_op jit(solution)/shard_map/ppermute | solution.py:111
  7.5 0.8 %constant_dynamic-update-slice_fusion.4 = bf16[528,128]{1,0:T(8,128)(2,1)S(1)} fusion(bf16[128,128]{1,0:T(8,128)(2,1)} %get-tuple-element.9.refs_0_), kind=kLoop, calls=%fused_computation.4 | loop fusion | bytes 65536
  8.9 0.0 collective-permute-done.refs_1_
  9.0 0.0 collective-permute-done.1.refs_2_
  9.0 1.0 %collective-permute-done.2.refs_3_ = bf16[128,128]{1,0:T(8,128)(2,1)S(1)} collective-permute-done((bf16[128,128]{1,0:T(8,128)(2,1)}, bf16[128,128]{1,0:T(8,128)(2,1)S(1)}, u32[]{:S(2)}, u32[]{:S(2)}) %collective-permute-start.2) | collective-permute-done | bytes 32800 | tf_op jit(solution)/shard_map/ppermute | solution.py:111
  10.0 1.8 %collective-permute-start.9 = (bf16[528,128]{1,0:T(8,128)(2,1)S(1)}, bf16[528,128]{1,0:T(8,128)(2,1)S(1)}, u32[]{:S(2)}, u32[]{:S(2)}) collective-permute-start(bf16[528,128]{1,0:T(8,128)(2,1)S(1)} %constant_dynamic-update-slice_fusion), channel_id=1, source_target_pairs={{0,28},{4,0},{8,4},{12,8},{16,12},{20,16},{24,20},{28,24},{1,29},{... | collective-permute-start | bytes 405512 | tf_op jit(solution)/shard_map/ppermute | solution.py:117
  11.9 2.2 %collective-permute-start.8 = (bf16[528,128]{1,0:T(8,128)(2,1)S(1)}, bf16[528,128]{1,0:T(8,128)(2,1)S(1)}, u32[]{:S(2)}, u32[]{:S(2)}) collective-permute-start(bf16[528,128]{1,0:T(8,128)(2,1)S(1)} %constant_dynamic-update-slice_fusion), channel_id=1, source_target_pairs={{0,24},{4,28},{8,0},{12,4},{16,8},{20,12},{24,16},{28,20},{1,25},{... | collective-permute-start | bytes 405512 | tf_op jit(solution)/shard_map/ppermute | solution.py:117
  14.0 0.5 %collective-permute-start.7 = (bf16[528,128]{1,0:T(8,128)(2,1)S(1)}, bf16[528,128]{1,0:T(8,128)(2,1)S(1)}, u32[]{:S(2)}, u32[]{:S(2)}) collective-permute-start(bf16[528,128]{1,0:T(8,128)(2,1)S(1)} %constant_dynamic-update-slice_fusion), channel_id=1, source_target_pairs={{0,20},{4,24},{8,28},{12,0},{16,4},{20,8},{24,12},{28,16},{1,21},{... | collective-permute-start | bytes 405512 | tf_op jit(solution)/shard_map/ppermute | solution.py:117
  14.5 0.9 %collective-permute-start.6 = (bf16[528,128]{1,0:T(8,128)(2,1)S(1)}, bf16[528,128]{1,0:T(8,128)(2,1)S(1)}, u32[]{:S(2)}, u32[]{:S(2)}) collective-permute-start(bf16[528,128]{1,0:T(8,128)(2,1)S(1)} %constant_dynamic-update-slice_fusion), channel_id=1, source_target_pairs={{0,16},{4,20},{8,24},{12,28},{16,0},{20,4},{24,8},{28,12},{1,17},{... | collective-permute-start | bytes 405512 | tf_op jit(solution)/shard_map/ppermute | solution.py:117
  15.5 0.9 %collective-permute-start.5 = (bf16[528,128]{1,0:T(8,128)(2,1)S(1)}, bf16[528,128]{1,0:T(8,128)(2,1)S(1)}, u32[]{:S(2)}, u32[]{:S(2)}) collective-permute-start(bf16[528,128]{1,0:T(8,128)(2,1)S(1)} %constant_dynamic-update-slice_fusion), channel_id=1, source_target_pairs={{0,12},{4,16},{8,20},{12,24},{16,28},{20,0},{24,4},{28,8},{1,13},{... | collective-permute-start | bytes 405512 | tf_op jit(solution)/shard_map/ppermute | solution.py:117
  16.3 0.7 %collective-permute-done.9 = bf16[528,128]{1,0:T(8,128)(2,1)S(1)} collective-permute-done((bf16[528,128]{1,0:T(8,128)(2,1)S(1)}, bf16[528,128]{1,0:T(8,128)(2,1)S(1)}, u32[]{:S(2)}, u32[]{:S(2)}) %collective-permute-start.9) | collective-permute-done | bytes 135200 | tf_op jit(solution)/shard_map/ppermute | solution.py:117
  17.1 0.4 %collective-permute-start.4 = (bf16[528,128]{1,0:T(8,128)(2,1)S(1)}, bf16[528,128]{1,0:T(8,128)(2,1)S(1)}, u32[]{:S(2)}, u32[]{:S(2)}) collective-permute-start(bf16[528,128]{1,0:T(8,128)(2,1)S(1)} %constant_dynamic-update-slice_fusion), channel_id=1, source_target_pairs={{0,8},{4,12},{8,16},{12,20},{16,24},{20,28},{24,0},{28,4},{1,9},{5... | collective-permute-start | bytes 405512 | tf_op jit(solution)/shard_map/ppermute | solution.py:117
  17.5 0.0 collective-permute-done.8
  17.5 3.5 %collective-permute-start.3 = (bf16[528,128]{1,0:T(8,128)(2,1)S(1)}, bf16[528,128]{1,0:T(8,128)(2,1)S(1)}, u32[]{:S(2)}, u32[]{:S(2)}) collective-permute-start(bf16[528,128]{1,0:T(8,128)(2,1)S(1)} %constant_dynamic-update-slice_fusion), channel_id=1, source_target_pairs={{0,4},{4,8},{8,12},{12,16},{16,20},{20,24},{24,28},{28,0},{1,5},{5... | collective-permute-start | bytes 405512 | tf_op jit(solution)/shard_map/ppermute | solution.py:117
  20.9 0.0 copy-done
  20.9 0.0 copy-start.1
  20.9 0.1 constant_dynamic-slice_fusion
  21.1 0.0 collective-permute-done.7
  21.1 0.0 collective-permute-done.6
  21.1 5.8 %collective-permute-done.5 = bf16[528,128]{1,0:T(8,128)(2,1)S(1)} collective-permute-done((bf16[528,128]{1,0:T(8,128)(2,1)S(1)}, bf16[528,128]{1,0:T(8,128)(2,1)S(1)}, u32[]{:S(2)}, u32[]{:S(2)}) %collective-permute-start.5) | collective-permute-done | bytes 135200 | tf_op jit(solution)/shard_map/ppermute | solution.py:117
  26.9 0.0 collective-permute-done.4
  26.9 0.0 collective-permute-done.3
  27.0 0.0 copy-done.1
  27.0 6.9 %shard_map.47 = bf16[1024,128]{1,0:T(8,128)(2,1)} custom-call(s32[1]{0:T(128)S(6)} %copy.9.own_ref, bf16[1024,128]{1,0:T(8,128)(2,1)S(1)} %bitcast.10, bf16[128,128]{1,0:T(8,128)(2,1)S(1)} %copy-done.1, bf16[128,128]{1,0:T(8,128)(2,1)S(1)} %collective-permute-done.refs_1_, bf16[128,128]{1,0:T(8,128)(2,1)S(1)} %collective-permute-done.1.refs_2_, ...), custom_call_target="tpu_custom_call" | custom-call | tf_op jit(solution)/shard_map/pallas_call | solution.py:126
  (4 shorter events, 0.0 us)
Async XLA Ops:
  0.0 20.9 %copy-start = (bf16[256,16,128]{2,1,0:T(8,128)(2,1)S(1)}, bf16[256,16,128]{2,1,0:T(8,128)(2,1)}, u32[]{:S(2)}) copy-start(bf16[256,16,128]{2,1,0:T(8,128)(2,1)} %param.4) | copy-start | bytes 3145732
  2.0 6.9 %collective-permute-start = (bf16[128,128]{1,0:T(8,128)(2,1)}, bf16[128,128]{1,0:T(8,128)(2,1)S(1)}, u32[]{:S(2)}, u32[]{:S(2)}) collective-permute-start(bf16[128,128]{1,0:T(8,128)(2,1)} %get-tuple-element.10), channel_id=1, source_target_pairs={{0,1},{1,2},{2,3},{3,0},{4,5},{5,6},{6,7},{7,4},{8,9},{9,10},{10,1... | collective-permute-start | bytes 98312 | tf_op jit(solution)/shard_map/ppermute | solution.py:111
  4.1 4.8 %collective-permute-start.1 = (bf16[128,128]{1,0:T(8,128)(2,1)}, bf16[128,128]{1,0:T(8,128)(2,1)S(1)}, u32[]{:S(2)}, u32[]{:S(2)}) collective-permute-start(bf16[128,128]{1,0:T(8,128)(2,1)} %get-tuple-element.11), channel_id=1, source_target_pairs={{0,2},{1,3},{2,0},{3,1},{4,6},{5,7},{6,4},{7,5},{8,10},{9,11},{10,... | collective-permute-start | bytes 98312 | tf_op jit(solution)/shard_map/ppermute | solution.py:111
  6.5 3.6 %collective-permute-start.2 = (bf16[128,128]{1,0:T(8,128)(2,1)}, bf16[128,128]{1,0:T(8,128)(2,1)S(1)}, u32[]{:S(2)}, u32[]{:S(2)}) collective-permute-start(bf16[128,128]{1,0:T(8,128)(2,1)} %get-tuple-element.12), channel_id=1, source_target_pairs={{0,3},{1,0},{2,1},{3,2},{4,7},{5,4},{6,5},{7,6},{8,11},{9,8},{10,9... | collective-permute-start | bytes 98312 | tf_op jit(solution)/shard_map/ppermute | solution.py:111
  10.0 7.0 %collective-permute-start.9 = (bf16[528,128]{1,0:T(8,128)(2,1)S(1)}, bf16[528,128]{1,0:T(8,128)(2,1)S(1)}, u32[]{:S(2)}, u32[]{:S(2)}) collective-permute-start(bf16[528,128]{1,0:T(8,128)(2,1)S(1)} %constant_dynamic-update-slice_fusion), channel_id=1, source_target_pairs={{0,28},{4,0},{8,4},{12,8},{16,12},{20,16},{24,20},{28,24},{1,29},{... | collective-permute-start | bytes 405512 | tf_op jit(solution)/shard_map/ppermute | solution.py:117
  11.9 5.6 %collective-permute-start.8 = (bf16[528,128]{1,0:T(8,128)(2,1)S(1)}, bf16[528,128]{1,0:T(8,128)(2,1)S(1)}, u32[]{:S(2)}, u32[]{:S(2)}) collective-permute-start(bf16[528,128]{1,0:T(8,128)(2,1)S(1)} %constant_dynamic-update-slice_fusion), channel_id=1, source_target_pairs={{0,24},{4,28},{8,0},{12,4},{16,8},{20,12},{24,16},{28,20},{1,25},{... | collective-permute-start | bytes 405512 | tf_op jit(solution)/shard_map/ppermute | solution.py:117
  14.0 7.0 %collective-permute-start.7 = (bf16[528,128]{1,0:T(8,128)(2,1)S(1)}, bf16[528,128]{1,0:T(8,128)(2,1)S(1)}, u32[]{:S(2)}, u32[]{:S(2)}) collective-permute-start(bf16[528,128]{1,0:T(8,128)(2,1)S(1)} %constant_dynamic-update-slice_fusion), channel_id=1, source_target_pairs={{0,20},{4,24},{8,28},{12,0},{16,4},{20,8},{24,12},{28,16},{1,21},{... | collective-permute-start | bytes 405512 | tf_op jit(solution)/shard_map/ppermute | solution.py:117
  14.5 6.6 %collective-permute-start.6 = (bf16[528,128]{1,0:T(8,128)(2,1)S(1)}, bf16[528,128]{1,0:T(8,128)(2,1)S(1)}, u32[]{:S(2)}, u32[]{:S(2)}) collective-permute-start(bf16[528,128]{1,0:T(8,128)(2,1)S(1)} %constant_dynamic-update-slice_fusion), channel_id=1, source_target_pairs={{0,16},{4,20},{8,24},{12,28},{16,0},{20,4},{24,8},{28,12},{1,17},{... | collective-permute-start | bytes 405512 | tf_op jit(solution)/shard_map/ppermute | solution.py:117
  15.5 11.5 %collective-permute-start.5 = (bf16[528,128]{1,0:T(8,128)(2,1)S(1)}, bf16[528,128]{1,0:T(8,128)(2,1)S(1)}, u32[]{:S(2)}, u32[]{:S(2)}) collective-permute-start(bf16[528,128]{1,0:T(8,128)(2,1)S(1)} %constant_dynamic-update-slice_fusion), channel_id=1, source_target_pairs={{0,12},{4,16},{8,20},{12,24},{16,28},{20,0},{24,4},{28,8},{1,13},{... | collective-permute-start | bytes 405512 | tf_op jit(solution)/shard_map/ppermute | solution.py:117
  17.1 9.9 %collective-permute-start.4 = (bf16[528,128]{1,0:T(8,128)(2,1)S(1)}, bf16[528,128]{1,0:T(8,128)(2,1)S(1)}, u32[]{:S(2)}, u32[]{:S(2)}) collective-permute-start(bf16[528,128]{1,0:T(8,128)(2,1)S(1)} %constant_dynamic-update-slice_fusion), channel_id=1, source_target_pairs={{0,8},{4,12},{8,16},{12,20},{16,24},{20,28},{24,0},{28,4},{1,9},{5... | collective-permute-start | bytes 405512 | tf_op jit(solution)/shard_map/ppermute | solution.py:117
  17.5 9.5 %collective-permute-start.3 = (bf16[528,128]{1,0:T(8,128)(2,1)S(1)}, bf16[528,128]{1,0:T(8,128)(2,1)S(1)}, u32[]{:S(2)}, u32[]{:S(2)}) collective-permute-start(bf16[528,128]{1,0:T(8,128)(2,1)S(1)} %constant_dynamic-update-slice_fusion), channel_id=1, source_target_pairs={{0,4},{4,8},{8,12},{12,16},{16,20},{20,24},{24,28},{28,0},{1,5},{5... | collective-permute-start | bytes 405512 | tf_op jit(solution)/shard_map/ppermute | solution.py:117
  20.9 6.0 %copy-start.1 = (bf16[128,128]{1,0:T(8,128)(2,1)S(1)}, bf16[128,128]{1,0:T(8,128)(2,1)}, u32[]{:S(2)}) copy-start(bf16[128,128]{1,0:T(8,128)(2,1)} %get-tuple-element.9.refs_0_) | copy-start | bytes 98308

commit v3 on v2

v3 whole, which is shorter than its diff:
```python
import functools
import math

import jax
import jax.numpy as jnp
from jax import lax
from jax.experimental import pallas as pl
from jax.experimental.pallas import tpu as pltpu
from jax.sharding import PartitionSpec as P

MARK = 16


def pack(copies, keys_ref, values_ref, *out_refs):
    part, kv_heads = keys_ref.shape[:2]
    kv_here = lax.axis_index("head") // copies
    key_rows = [keys_ref[:, head, :] for head in range(kv_heads)]
    value_rows = [values_ref[:, head, :] for head in range(kv_heads)]
    for shift, out_ref in enumerate(out_refs):
        kv_head = lax.rem(kv_here + shift, kv_heads)
        chosen_key, chosen_value = key_rows[0], value_rows[0]
        for head in range(1, kv_heads):
            chosen_key = jnp.where(kv_head == head, key_rows[head], chosen_key)
            chosen_value = jnp.where(kv_head == head, value_rows[head], chosen_value)
        out_ref[:part, :] = chosen_key
        out_ref[part:, :] = chosen_value


def attend(pieces, copies, part, scale, own_ref, query_ref, near_ref, *refs):
    far_refs = refs[:-4]
    out_ref, high_ref, total_ref, accum_ref = refs[-4:]
    query_rows = query_ref.shape[0]
    group = query_rows // (pieces * part)
    own = own_ref[0]
    here = lax.axis_index("head")
    step = pl.program_id(0)

    def fold(key_parts, value_parts, diagonal):
        key_rows = jnp.concatenate(key_parts)
        value_rows = jnp.concatenate(value_parts)
        scores = lax.dot_general(
            key_rows, query_ref[...], (((1,), (1,)), ((), ())), preferred_element_type=jnp.float32
        )
        if diagonal:
            row = lax.broadcasted_iota(jnp.int32, scores.shape, 0)
            slot = row // part
            kv_heads = pieces // copies
            kv_from = lax.rem(here // copies + kv_heads - slot % kv_heads, kv_heads)
            copy_from = lax.rem(here % copies + copies - slot // kv_heads, copies)
            piece = kv_from * copies + copy_from
            key_at = piece * part + row % part
            query_at = lax.broadcasted_iota(jnp.int32, scores.shape, 1) // group
            scores = jnp.where(key_at <= query_at, scores, -1e30)
        high = jnp.max(scores, axis=0, keepdims=True)
        if not diagonal:
            old_high = high_ref[...]
            high = jnp.maximum(old_high, high)
            factor = jnp.exp((old_high - high) * scale)
        expo = jnp.exp((scores - high) * scale)
        total = jnp.sum(expo, axis=0, keepdims=True)
        product = lax.dot_general(
            value_rows, expo.astype(jnp.bfloat16), (((0,), (0,)), ((), ())), preferred_element_type=jnp.float32
        )
        if not diagonal:
            total = total_ref[...] * factor + total
            product = accum_ref[...] * factor + product
        high_ref[...] = high
        total_ref[...] = total
        accum_ref[...] = product

    def fold_rows(rows_ref, diagonal):
        fold(
            [rows_ref[pl.ds(2 * piece * part, part), :] for piece in range(pieces)],
            [rows_ref[pl.ds((2 * piece + 1) * part, part), :] for piece in range(pieces)],
            diagonal,
        )

    @pl.when(step == 0)
    def _():
        fold_rows(near_ref, True)

    for far_ref in far_refs:
        for block in range(far_ref.shape[0]):
            rows_ref = far_ref.at[block]
            mark = rows_ref[pl.ds(2 * pieces * part, MARK), :]
            place = jnp.max(mark.astype(jnp.float32)).astype(jnp.int32)

            @pl.when(place < own)
            def _():
                fold_rows(rows_ref, False)

    @pl.when(step == pl.num_programs(0) - 1)
    def _():
        result = accum_ref[...] / total_ref[...]
        out_ref[...] = result.T.astype(out_ref.dtype)


def shards(queries, keys, values, block_ids):
    rows_dev, all_heads, head_width = queries.shape
    part, kv_heads = keys.shape[:2]
    head_index = lax.axis_index("head")
    pieces = lax.axis_size("head")
    blocks = lax.axis_size("seq")
    heads_out = all_heads // pieces
    own_queries = lax.dynamic_slice_in_dim(queries, head_index * heads_out, heads_out, 1)
    own_queries = own_queries.reshape(rows_dev * heads_out, head_width)
    mark = jnp.broadcast_to(block_ids.astype(jnp.bfloat16)[:, None], (MARK, head_width))
    whole = pl.BlockSpec(memory_space=pltpu.VMEM)
    copies = pieces // kv_heads
    packed = pl.pallas_call(
        functools.partial(pack, copies),
        out_shape=[jax.ShapeDtypeStruct((2 * part, head_width), jnp.bfloat16)] * kv_heads,
        in_specs=[whole, whole],
        out_specs=[whole] * kv_heads,
    )(keys, values)
    held = jnp.concatenate(
        [packed[0]]
        + [
            lax.ppermute(packed[shift], "head", [(i, (i + shift * copies) % pieces) for i in range(pieces)])
            for shift in range(1, kv_heads)
        ]
    )
    block = jnp.concatenate(
        [held]
        + [
            lax.ppermute(
                held, "head", [(i, i // copies * copies + (i + shift) % copies) for i in range(pieces)]
            )
            for shift in range(1, copies)
        ]
        + [mark]
    )[None]
    if blocks == 8:
        first = lax.ppermute(block, "seq", [(i, i ^ (4 if i & 1 else 2)) for i in range(blocks)])
        pair = jnp.concatenate([block, first])
        second = lax.ppermute(pair, "seq", [(i, i ^ (2 if i & 1 else 4)) for i in range(blocks)])
        third = lax.ppermute(jnp.concatenate([pair, second]), "seq", [(i, i ^ 1) for i in range(blocks)])
        far = [first, second, third]
        steps = 1
    else:
        far = [lax.all_gather(block, "seq", axis=0, tiled=True)]
        steps = blocks // math.gcd(blocks, 8)
    query_rows = rows_dev * heads_out
    result = pl.pallas_call(
        functools.partial(attend, pieces, copies, part, head_width ** (-0.5)),
        grid=(steps,),
        out_shape=jax.ShapeDtypeStruct((query_rows, head_width), jnp.bfloat16),
        in_specs=[pl.BlockSpec(memory_space=pltpu.SMEM), pl.BlockSpec((query_rows, head_width), lambda i: (0, 0))]
        + [pl.BlockSpec(block.shape[1:], lambda i: (0, 0))]
        + [pl.BlockSpec((rows.shape[0] // steps,) + rows.shape[1:], lambda i: (i, 0, 0)) for rows in far],
        out_specs=pl.BlockSpec((query_rows, head_width), lambda i: (0, 0)),
        scratch_shapes=[
            pltpu.VMEM((1, query_rows), jnp.float32),
            pltpu.VMEM((1, query_rows), jnp.float32),
            pltpu.VMEM((head_width, query_rows), jnp.float32),
        ],
        compiler_params=pltpu.CompilerParams(vmem_limit_bytes=32 * 1024 * 1024),
    )(block_ids, own_queries, block[0], *far)
    return result.reshape(rows_dev, heads_out, head_width)


def solution(mesh):
    return jax.shard_map(
        shards,
        mesh=mesh,
        in_specs=(
            P("seq", None, None),
            P(("seq", "head"), None, None),
            P(("seq", "head"), None, None),
            P("seq"),
        ),
        out_specs=P("seq", "head", None),
        check_vma=False,
    )
```

time: 34 us -> 35.3 us (1.038)
  waiting for transfers between devices: 7.64 us -> 11.4 us
  starting transfers between devices: 15.6 us -> 12.8 us
  other arithmetic: 0 us -> 1.19 us
  local copies, waits for them, and re-layouts: 0.95 us -> 0.16 us
    ppermute x10 -> x5, waiting for transfers between devices: 7.64 us -> 11.4 us  [the longest x1 5.04 us: shards(): lax.ppermute(pair, 'seq', [(i, i ^ (2 if i & 1 else 4)) for i in range(bl...]
    ppermute x10 -> x5, starting transfers between devices: 15.6 us -> 12.8 us  [the longest x1 5.48 us: shards(): lax.ppermute(jnp.concatenate([pair, second]), 'seq', [(i, i ^ 1) for i in...]
    concatenate x0 -> x4, other arithmetic: none -> 1.05 us  [the longest x1 0.83 us: shards(): jnp.concatenate([packed[0]] + [lax.ppermute(packed[shift], 'head', [(i, (...]
    unnamed x8 -> x4, local copies, waits for them, and re-layouts: 0.8 us -> 0.01 us
  transfers between devices with their start and end apart: 10 -> 5, of which waited for: 3 -> 5; matrix products, arithmetic and copies ran while one was open for 3% -> 1% of each run, Pallas kernels for 0% -> 0%
where the time goes in v3:
time: 35.3 us; the launch traced here: 34.8 us
  starting transfers between devices  12.8 us (36%)
  waiting for transfers between devices  11.4 us (32%)
  Pallas kernels  8.64 us (24%)
  other arithmetic  1.19 us (3%)
  between operations  0.7 us (2%)
    pallas_call x1, Pallas kernels, shards(): pl.pallas_call(functools.partial(attend, pieces, copies, part, head_width...  6.87 us
    ppermute x1, starting transfers between devices, shards(): lax.ppermute(jnp.concatenate([pair, second]), 'seq', [(i, i ^ 1) for i in...  5.48 us
    ppermute x1, waiting for transfers between devices, shards(): lax.ppermute(pair, 'seq', [(i, i ^ (2 if i & 1 else 4)) for i in range(bl...  5.04 us
    ppermute x1, starting transfers between devices, shards(): lax.ppermute(packed[shift], 'head', [(i, (i + shift * copies) % pieces) f...  3.14 us
    ppermute x1, waiting for transfers between devices, shards(): lax.ppermute(block, 'seq', [(i, i ^ (4 if i & 1 else 2)) for i in range(b...  2.57 us
    pallas_call x1, Pallas kernels, shards(): pl.pallas_call(functools.partial(pack, copies), out_shape=[jax.ShapeDtype...  1.77 us
    ppermute x1, waiting for transfers between devices, shards(): lax.ppermute(packed[shift], 'head', [(i, (i + shift * copies) % pieces) f...  1.51 us
    ppermute x1, starting transfers between devices, shards(): lax.ppermute(held, 'head', [(i, i // copies * copies + (i + shift) % copi...  1.45 us
  transfers between devices with their start and end apart: 5, of which 5 were waited for; matrix products, arithmetic and copies ran while one was open for 1% of the time, Pallas kernels for 0%

profile of v3, /device:TPU:1, one launch (start us, length us, event | category | flops | bytes accessed | tf_op | source)
XLA Modules:
  0.0 34.8 jit_solution(14828909626474242761)
XLA Ops:
  0.0 0.0 copy-start
  0.0 1.8 %shard_map.46 = (bf16[128,128]{1,0:T(8,128)(2,1)}, bf16[128,128]{1,0:T(8,128)(2,1)}) custom-call(bf16[64,2,128]{2,1,0:T(2,128)(2,1)} %keys_ref.1, bf16[64,2,128]{2,1,0:T(2,128)(2,1)} %values_ref.1), custom_call_target="tpu_custom_call" | custom-call | tf_op jit(solution)/shard_map/pallas_call | solution.py:110
  1.8 3.1 %collective-permute-start = (bf16[128,128]{1,0:T(8,128)(2,1)}, bf16[128,128]{1,0:T(8,128)(2,1)S(1)}, u32[]{:S(2)}, u32[]{:S(2)}) collective-permute-start(bf16[128,128]{1,0:T(8,128)(2,1)} %get-tuple-element.8), channel_id=1, source_target_pairs={{0,2},{1,3},{2,0},{3,1},{4,6},{5,7},{6,4},{7,5},{8,10},{9,11},{10,... | collective-permute-start | bytes 98312 | tf_op jit(solution)/shard_map/ppermute | solution.py:119
  4.9 1.5 %collective-permute-done = bf16[128,128]{1,0:T(8,128)(2,1)S(1)} collective-permute-done((bf16[128,128]{1,0:T(8,128)(2,1)}, bf16[128,128]{1,0:T(8,128)(2,1)S(1)}, u32[]{:S(2)}, u32[]{:S(2)}) %collective-permute-start) | collective-permute-done | bytes 32800 | tf_op jit(solution)/shard_map/ppermute | solution.py:119
  6.4 0.0 copy-start.1
  6.4 0.8 %pad_maximum_fusion.2 = bf16[256,128]{1,0:T(8,128)(2,1)S(1)} fusion(bf16[128,128]{1,0:T(8,128)(2,1)S(1)} %collective-permute-done, bf16[128,128]{1,0:T(8,128)(2,1)} %get-tuple-element.7), kind=kLoop, calls=%fused_computation.3 | loop fusion | flops 131072 | bytes 131072 | tf_op jit(solution)/shard_map/concatenate | solution.py:116
  7.3 1.5 %collective-permute-start.1 = (bf16[256,128]{1,0:T(8,128)(2,1)S(1)}, bf16[256,128]{1,0:T(8,128)(2,1)S(1)}, u32[]{:S(2)}, u32[]{:S(2)}) collective-permute-start(bf16[256,128]{1,0:T(8,128)(2,1)S(1)} %pad_maximum_fusion.2), channel_id=1, source_target_pairs={{0,1},{1,0},{2,3},{3,2},{4,5},{5,4},{6,7},{7,6},{8,9},{9,8},{10,11... | collective-permute-start | bytes 196616 | tf_op jit(solution)/shard_map/ppermute | solution.py:126
  9.4 1.0 %collective-permute-done.1 = bf16[256,128]{1,0:T(8,128)(2,1)S(1)} collective-permute-done((bf16[256,128]{1,0:T(8,128)(2,1)S(1)}, bf16[256,128]{1,0:T(8,128)(2,1)S(1)}, u32[]{:S(2)}, u32[]{:S(2)}) %collective-permute-start.1) | collective-permute-done | bytes 65568 | tf_op jit(solution)/shard_map/ppermute | solution.py:126
  10.4 0.0 copy-done.1
  10.4 0.1 fusion
  10.5 1.4 %collective-permute-start.2 = (bf16[1,528,128]{2,1,0:T(8,128)(2,1)S(1)}, bf16[1,528,128]{2,1,0:T(8,128)(2,1)S(1)}, u32[]{:S(2)}, u32[]{:S(2)}) collective-permute-start(bf16[1,528,128]{2,1,0:T(8,128)(2,1)S(1)} %fusion), channel_id=1, source_target_pairs={{0,8},{4,20},{8,0},{12,28},{16,24},{20,4},{24,16},{28,12},{1,9},{5... | collective-permute-start | bytes 405512 | tf_op jit(solution)/shard_map/ppermute | solution.py:134
  11.9 2.6 %collective-permute-done.2.refs_0_ = bf16[1,528,128]{2,1,0:T(8,128)(2,1)S(1)} collective-permute-done((bf16[1,528,128]{2,1,0:T(8,128)(2,1)S(1)}, bf16[1,528,128]{2,1,0:T(8,128)(2,1)S(1)}, u32[]{:S(2)}, u32[]{:S(2)}) %collective-permute-start.2) | collective-permute-done | bytes 135200 | tf_op jit(solution)/shard_map/ppermute | solution.py:134
  14.5 1.3 %collective-permute-start.3 = (bf16[2,528,128]{2,1,0:T(8,128)(2,1)S(1)}, bf16[2,528,128]{2,1,0:T(8,128)(2,1)S(1)}, u32[]{:S(2)}, u32[]{:S(2)}) collective-permute-start(bf16[2,528,128]{2,1,0:T(8,128)(2,1)S(1)} %pad_maximum_fusion.1), channel_id=1, source_target_pairs={{0,16},{4,12},{8,24},{12,4},{16,0},{20,28},{24,8},{28,20},{1,17},{... | collective-permute-start | bytes 811016 | tf_op jit(solution)/shard_map/ppermute | solution.py:136
  15.8 5.0 %collective-permute-done.3.refs_1_ = bf16[2,528,128]{2,1,0:T(8,128)(2,1)S(1)} collective-permute-done((bf16[2,528,128]{2,1,0:T(8,128)(2,1)S(1)}, bf16[2,528,128]{2,1,0:T(8,128)(2,1)S(1)}, u32[]{:S(2)}, u32[]{:S(2)}) %collective-permute-start.3) | collective-permute-done | bytes 270368 | tf_op jit(solution)/shard_map/ppermute | solution.py:136
  20.9 0.1 pad_maximum_fusion
  20.9 5.5 %collective-permute-start.4 = (bf16[4,528,128]{2,1,0:T(8,128)(2,1)S(1)}, bf16[4,528,128]{2,1,0:T(8,128)(2,1)S(1)}, u32[]{:S(2)}, u32[]{:S(2)}) collective-permute-start(bf16[4,528,128]{2,1,0:T(8,128)(2,1)S(1)} %pad_maximum_fusion), channel_id=1, source_target_pairs={{0,4},{4,0},{8,12},{12,8},{16,20},{20,16},{24,28},{28,24},{1,5},{5... | collective-permute-start | bytes 1622024 | tf_op jit(solution)/shard_map/ppermute | solution.py:137
  26.4 0.0 copy-done
  26.4 0.1 constant_dynamic-slice_fusion
  26.5 0.1 maximum_maximum_fusion.near_ref
  26.7 1.3 %collective-permute-done.4.refs_2_ = bf16[4,528,128]{2,1,0:T(8,128)(2,1)S(1)} collective-permute-done((bf16[4,528,128]{2,1,0:T(8,128)(2,1)S(1)}, bf16[4,528,128]{2,1,0:T(8,128)(2,1)S(1)}, u32[]{:S(2)}, u32[]{:S(2)}) %collective-permute-start.4) | collective-permute-done | bytes 540704 | tf_op jit(solution)/shard_map/ppermute | solution.py:137
  28.0 6.9 %shard_map.47 = bf16[1024,128]{1,0:T(8,128)(2,1)} custom-call(s32[1]{0:T(128)S(6)} %copy.5.own_ref, bf16[1024,128]{1,0:T(8,128)(2,1)S(1)} %bitcast.5, bf16[528,128]{1,0:T(8,128)(2,1)S(1)} %maximum_maximum_fusion.near_ref, bf16[1,528,128]{2,1,0:T(8,128)(2,1)S(1)} %collective-permute-done.2.refs_0_, bf16[2,528,128]{2,1,0:T(8,128)(2,1)S(1)} %collective-permute-done.3.refs_1_, ...), custom_call_target="tpu_custom_call" | custom-call | tf_op jit(solution)/shard_map/pallas_call | solution.py:144
  (3 shorter events, 0.0 us)
Async XLA Ops:
  0.0 26.4 %copy-start = (bf16[256,16,128]{2,1,0:T(8,128)(2,1)S(1)}, bf16[256,16,128]{2,1,0:T(8,128)(2,1)}, u32[]{:S(2)}) copy-start(bf16[256,16,128]{2,1,0:T(8,128)(2,1)} %param.4) | copy-start | bytes 3145732
  1.8 4.7 %collective-permute-start = (bf16[128,128]{1,0:T(8,128)(2,1)}, bf16[128,128]{1,0:T(8,128)(2,1)S(1)}, u32[]{:S(2)}, u32[]{:S(2)}) collective-permute-start(bf16[128,128]{1,0:T(8,128)(2,1)} %get-tuple-element.8), channel_id=1, source_target_pairs={{0,2},{1,3},{2,0},{3,1},{4,6},{5,7},{6,4},{7,5},{8,10},{9,11},{10,... | collective-permute-start | bytes 98312 | tf_op jit(solution)/shard_map/ppermute | solution.py:119
  6.4 4.0 %copy-start.1 = (bf16[128,128]{1,0:T(8,128)(2,1)S(1)}, bf16[128,128]{1,0:T(8,128)(2,1)}, u32[]{:S(2)}) copy-start(bf16[128,128]{1,0:T(8,128)(2,1)} %get-tuple-element.7) | copy-start | bytes 98308
  7.3 3.1 %collective-permute-start.1 = (bf16[256,128]{1,0:T(8,128)(2,1)S(1)}, bf16[256,128]{1,0:T(8,128)(2,1)S(1)}, u32[]{:S(2)}, u32[]{:S(2)}) collective-permute-start(bf16[256,128]{1,0:T(8,128)(2,1)S(1)} %pad_maximum_fusion.2), channel_id=1, source_target_pairs={{0,1},{1,0},{2,3},{3,2},{4,5},{5,4},{6,7},{7,6},{8,9},{9,8},{10,11... | collective-permute-start | bytes 196616 | tf_op jit(solution)/shard_map/ppermute | solution.py:126
  10.5 3.9 %collective-permute-start.2 = (bf16[1,528,128]{2,1,0:T(8,128)(2,1)S(1)}, bf16[1,528,128]{2,1,0:T(8,128)(2,1)S(1)}, u32[]{:S(2)}, u32[]{:S(2)}) collective-permute-start(bf16[1,528,128]{2,1,0:T(8,128)(2,1)S(1)} %fusion), channel_id=1, source_target_pairs={{0,8},{4,20},{8,0},{12,28},{16,24},{20,4},{24,16},{28,12},{1,9},{5... | collective-permute-start | bytes 405512 | tf_op jit(solution)/shard_map/ppermute | solution.py:134
  14.5 6.4 %collective-permute-start.3 = (bf16[2,528,128]{2,1,0:T(8,128)(2,1)S(1)}, bf16[2,528,128]{2,1,0:T(8,128)(2,1)S(1)}, u32[]{:S(2)}, u32[]{:S(2)}) collective-permute-start(bf16[2,528,128]{2,1,0:T(8,128)(2,1)S(1)} %pad_maximum_fusion.1), channel_id=1, source_target_pairs={{0,16},{4,12},{8,24},{12,4},{16,0},{20,28},{24,8},{28,20},{1,17},{... | collective-permute-start | bytes 811016 | tf_op jit(solution)/shard_map/ppermute | solution.py:136
  20.9 7.0 %collective-permute-start.4 = (bf16[4,528,128]{2,1,0:T(8,128)(2,1)S(1)}, bf16[4,528,128]{2,1,0:T(8,128)(2,1)S(1)}, u32[]{:S(2)}, u32[]{:S(2)}) collective-permute-start(bf16[4,528,128]{2,1,0:T(8,128)(2,1)S(1)} %pad_maximum_fusion), channel_id=1, source_target_pairs={{0,4},{4,0},{8,12},{12,8},{16,20},{20,16},{24,28},{28,24},{1,5},{5... | collective-permute-start | bytes 1622024 | tf_op jit(solution)/shard_map/ppermute | solution.py:137

commit v4 on v2

v4 whole, which is shorter than its diff:
```python
import functools
import math

import jax
import jax.numpy as jnp
from jax import lax
from jax.experimental import pallas as pl
from jax.experimental.pallas import tpu as pltpu
from jax.sharding import PartitionSpec as P

MARK = 16
LANES = 256
LOW = -1e30
HIGH = 1e30
MIB = 1024 * 1024


def pack(heads_out, group, part, pieces, keys_ref, values_ref, *out_refs):
    here = lax.axis_index("head")
    rows = keys_ref.shape[0]
    kv_heads = rows // part
    at = lax.broadcasted_iota(jnp.int32, (part, rows), 0)
    source = lax.broadcasted_iota(jnp.int32, (part, rows), 1)
    chosen = []
    for head in range(kv_heads):
        pick = jnp.where(source == at * kv_heads + head, 1.0, 0.0).astype(jnp.bfloat16)
        chosen.append(
            [
                jnp.dot(pick, ref[...], preferred_element_type=jnp.float32).astype(jnp.bfloat16)
                for ref in (keys_ref, values_ref)
            ]
        )
    for shift, out_ref in enumerate(out_refs):
        kv_head = lax.rem(here + shift, pieces) * heads_out // group
        for half in range(2):
            rows_out = chosen[0][half]
            for head in range(1, kv_heads):
                rows_out = jnp.where(kv_head == head, chosen[head][half], rows_out)
            out_ref[pl.ds(half * part, part), :] = rows_out


def attend(pieces, part, scale, first, last, counts, own_ref, query_ref, *refs):
    refs = list(refs)
    state = None if first else [refs.pop(0) for _ in range(3)]
    near_ref = refs.pop(0) if first else None
    far_refs = [refs.pop(0) for _ in counts]
    outs = refs
    query_rows, head_width = query_ref.shape
    block_rows = pieces * part
    group = query_rows // block_rows
    factor = scale * math.log2(math.e)
    here = lax.axis_index("head")
    own = own_ref[0].astype(jnp.float32)

    blocks = []
    if first:
        blocks.append((near_ref, None))
    for count, ref in zip(counts, far_refs):
        for block in range(count):
            rows_ref = ref.at[block]
            mark = rows_ref[pl.ds(2 * block_rows, MARK), :].astype(jnp.float32)[:1]
            seen = jnp.concatenate([mark] * (LANES // head_width), axis=1) < own
            blocks.append((rows_ref, seen))

    def side(rows_ref, offset):
        return jnp.concatenate(
            [rows_ref[pl.ds((2 * piece + offset) * part, part), :] for piece in range(pieces)]
        )

    keys = [side(rows_ref, 0) for rows_ref, _ in blocks]
    values = [side(rows_ref, 1).T for rows_ref, _ in blocks]

    for lane in range(0, query_rows, LANES):
        span = pl.ds(lane, LANES)
        query = query_ref[span, :]
        scores, tops = [], []
        for key_rows, (_, seen) in zip(keys, blocks):
            score = lax.dot_general(
                key_rows, query, (((1,), (1,)), ((), ())), preferred_element_type=jnp.float32
            )
            if seen is None:
                row = lax.broadcasted_iota(jnp.int32, score.shape, 0)
                piece = lax.rem(here + pieces - row // part, pieces)
                key_at = piece * part + row % part
                query_at = (lane + lax.broadcasted_iota(jnp.int32, score.shape, 1)) // group
                score = jnp.where(key_at <= query_at, score, LOW)
            top = jnp.max(score, axis=0, keepdims=True)
            scores.append(score)
            tops.append(top if seen is None else jnp.where(seen, top, LOW))
        high = functools.reduce(jnp.maximum, tops)
        if not first:
            old_high = state[0][:, span]
            high = jnp.maximum(old_high, high)
        total = accum = None
        for score, value_rows, (_, seen) in zip(scores, values, blocks):
            base = high if seen is None else jnp.where(seen, high, HIGH)
            expo = jnp.exp2((score - base) * factor)
            part_total = jnp.sum(expo, axis=0, keepdims=True)
            product = jnp.dot(value_rows, expo.astype(jnp.bfloat16), preferred_element_type=jnp.float32)
            total = part_total if total is None else total + part_total
            accum = product if accum is None else accum + product
        if not first:
            keep = jnp.exp2((old_high - high) * factor)
            total = total + state[1][:, span] * keep
            accum = accum + state[2][:, span] * keep
        if last:
            outs[0][span, :] = (accum / total).T.astype(outs[0].dtype)
        else:
            outs[0][:, span] = high
            outs[1][:, span] = total
            outs[2][:, span] = accum


def attend_call(pieces, part, own, query, state, near, far, last):
    query_rows, head_width = query.shape
    whole = pl.BlockSpec(memory_space=pltpu.VMEM)
    first = near is not None
    counts = [rows.shape[0] for rows in far]
    operands = ([near] if first else list(state)) + list(far)
    if last:
        shapes = jax.ShapeDtypeStruct((query_rows, head_width), jnp.bfloat16)
        out_specs = whole
    else:
        shapes = [
            jax.ShapeDtypeStruct((1, query_rows), jnp.float32),
            jax.ShapeDtypeStruct((1, query_rows), jnp.float32),
            jax.ShapeDtypeStruct((head_width, query_rows), jnp.float32),
        ]
        out_specs = [whole] * 3
    blocks = sum(counts) + first
    pairs = blocks * query_rows * pieces * part
    return pl.pallas_call(
        functools.partial(attend, pieces, part, head_width ** (-0.5), first, last, counts),
        out_shape=shapes,
        in_specs=[pl.BlockSpec(memory_space=pltpu.SMEM)] + [whole] * (1 + len(operands)),
        out_specs=out_specs,
        compiler_params=pltpu.CompilerParams(vmem_limit_bytes=24 * MIB),
        cost_estimate=pl.CostEstimate(
            flops=4 * pairs * head_width, bytes_accessed=2 * MIB, transcendentals=pairs
        ),
    )(own, query, *operands)


def shards(queries, keys, values, block_ids):
    rows_dev, all_heads, head_width = queries.shape
    part, kv_heads = keys.shape[:2]
    head_index = lax.axis_index("head")
    pieces = lax.axis_size("head")
    blocks = lax.axis_size("seq")
    heads_out = all_heads // pieces
    own_queries = lax.dynamic_slice_in_dim(queries, head_index * heads_out, heads_out, 1)
    own_queries = own_queries.reshape(rows_dev * heads_out, head_width)
    mark = jnp.broadcast_to(block_ids.astype(jnp.bfloat16)[:, None], (MARK, head_width))
    whole = pl.BlockSpec(memory_space=pltpu.VMEM)
    packed = pl.pallas_call(
        functools.partial(pack, heads_out, all_heads // kv_heads, part, pieces),
        out_shape=[jax.ShapeDtypeStruct((2 * part, head_width), jnp.bfloat16)] * pieces,
        in_specs=[whole, whole],
        out_specs=[whole] * pieces,
        compiler_params=pltpu.CompilerParams(vmem_limit_bytes=4 * MIB),
    )(keys.reshape(part * kv_heads, head_width), values.reshape(part * kv_heads, head_width))
    near = [packed[0]] + [
        lax.ppermute(packed[shift], "head", [(i, (i + shift) % pieces) for i in range(pieces)])
        for shift in range(1, pieces)
    ]
    block = jnp.concatenate(near + [mark])
    fold = functools.partial(attend_call, pieces, part, block_ids, own_queries)
    if blocks == 8:

        def swap(rows, flip):
            return lax.ppermute(rows, "seq", [(i, i ^ flip) for i in range(blocks)])

        sent = block[None]
        along_x, along_y, across = swap(sent, 2), swap(sent, 4), swap(sent, 6)
        other = swap(sent, 1)
        state = fold(None, block, [other], False)
        along_x, along_y, across, state = lax.optimization_barrier((along_x, along_y, across, state))
        others = [swap(rows, 1) for rows in (along_x, along_y, across)]
        state = fold(state, None, [along_x, along_y, across], False)
        result = fold(state, None, others, True)
    else:
        far = lax.all_gather(block, "seq", axis=0, tiled=False)
        unit = math.gcd(blocks, 8)
        far = far.reshape((blocks // unit, unit) + block.shape)
        state = fold(None, block, [], False)
        state, _ = lax.scan(lambda held, rows: (tuple(fold(held, None, [rows], False)), None), tuple(state), far[:-1])
        result = fold(state, None, [far[-1]], True)
    return result.reshape(rows_dev, heads_out, head_width)


def solution(mesh):
    return jax.shard_map(
        shards,
        mesh=mesh,
        in_specs=(
            P("seq", None, None),
            P(("seq", "head"), None, None),
            P(("seq", "head"), None, None),
            P("seq"),
        ),
        out_specs=P("seq", "head", None),
        check_vma=False,
    )
```

time: 34 us -> 26.9 us (0.79)
  the two profiles are of different devices: /device:TPU:1 before, /device:TPU:0 now
where the time goes in v4:
time: 26.9 us; the launch traced here: 26.7 us
  starting transfers between devices  11.1 us (41%)
  Pallas kernels  6.62 us (25%)
  waiting for transfers between devices  6.42 us (24%)
  local copies, waits for them, and re-layouts  1.79 us (7%)
  between operations  0.75 us (3%)
    ppermute x3, starting transfers between devices, shards(): lax.ppermute(packed[shift], 'head', [(i, (i + shift) % pieces) for i in r...  7.01 us
    pallas_call x3, Pallas kernels, attend_call(): pl.pallas_call(functools.partial(attend, pieces, part, head_width ** (-0....  6.44 us
    ppermute x7, waiting for transfers between devices, swap(): return lax.ppermute(rows, 'seq', [(i, i ^ flip) for i in range(blocks)])  4.55 us
    ppermute x7, starting transfers between devices, swap(): return lax.ppermute(rows, 'seq', [(i, i ^ flip) for i in range(blocks)])  4.13 us
    ppermute x3, waiting for transfers between devices, shards(): lax.ppermute(packed[shift], 'head', [(i, (i + shift) % pieces) for i in r...  1.87 us
    unnamed x10, local copies, waits for them, and re-layouts  1.64 us
  transfers between devices with their start and end apart: 10, of which 5 were waited for; matrix products, arithmetic and copies ran while one was open for 1% of the time, Pallas kernels for 14%

profile of v4, /device:TPU:0, one launch (start us, length us, event | category | flops | bytes accessed | tf_op | source)
XLA Modules:
  0.0 26.7 jit_solution(7628070114381862237)
XLA Ops:
  0.0 0.0 copy-start
  0.0 0.0 copy-start.1
  0.0 0.8 %copy-done.1 = bf16[64,2,128]{2,1,0:T(2,128)(2,1)S(1)} copy-done((bf16[64,2,128]{2,1,0:T(2,128)(2,1)S(1)}, bf16[64,2,128]{2,1,0:T(2,128)(2,1)}, u32[]{:S(2)}) %copy-start.1) | copy-done | bytes 32792
  0.9 0.0 copy-start.2
  0.9 0.8 %copy-done.2 = bf16[64,2,128]{2,1,0:T(2,128)(2,1)S(1)} copy-done((bf16[64,2,128]{2,1,0:T(2,128)(2,1)S(1)}, bf16[64,2,128]{2,1,0:T(2,128)(2,1)}, u32[]{:S(2)}) %copy-start.2) | copy-done | bytes 32792
  1.6 0.2 shard_map.46
  1.8 3.1 %collective-permute-start = (bf16[128,128]{1,0:T(8,128)(2,1)S(1)}, bf16[128,128]{1,0:T(8,128)(2,1)S(1)}, u32[]{:S(2)}, u32[]{:S(2)}) collective-permute-start(bf16[128,128]{1,0:T(8,128)(2,1)S(1)} %get-tuple-element.22), channel_id=1, source_target_pairs={{0,1},{1,2},{2,3},{3,0},{4,5},{5,6},{6,7},{7,4},{8,9},{9,10},{10,1... | collective-permute-start | bytes 98312 | tf_op jit(solution)/shard_map/ppermute | solution.py:163
  4.9 2.6 %collective-permute-start.1 = (bf16[128,128]{1,0:T(8,128)(2,1)S(1)}, bf16[128,128]{1,0:T(8,128)(2,1)S(1)}, u32[]{:S(2)}, u32[]{:S(2)}) collective-permute-start(bf16[128,128]{1,0:T(8,128)(2,1)S(1)} %get-tuple-element.23), channel_id=1, source_target_pairs={{0,2},{1,3},{2,0},{3,1},{4,6},{5,7},{6,4},{7,5},{8,10},{9,11},{10,... | collective-permute-start | bytes 98312 | tf_op jit(solution)/shard_map/ppermute | solution.py:163
  7.5 1.3 %collective-permute-start.2 = (bf16[128,128]{1,0:T(8,128)(2,1)S(1)}, bf16[128,128]{1,0:T(8,128)(2,1)S(1)}, u32[]{:S(2)}, u32[]{:S(2)}) collective-permute-start(bf16[128,128]{1,0:T(8,128)(2,1)S(1)} %get-tuple-element.24), channel_id=1, source_target_pairs={{0,3},{1,0},{2,1},{3,2},{4,7},{5,4},{6,5},{7,6},{8,11},{9,8},{10,9... | collective-permute-start | bytes 98312 | tf_op jit(solution)/shard_map/ppermute | solution.py:163
  9.5 0.0 collective-permute-done
  9.5 0.5 %collective-permute-done.1 = bf16[128,128]{1,0:T(8,128)(2,1)S(1)} collective-permute-done((bf16[128,128]{1,0:T(8,128)(2,1)S(1)}, bf16[128,128]{1,0:T(8,128)(2,1)S(1)}, u32[]{:S(2)}, u32[]{:S(2)}) %collective-permute-start.1) | collective-permute-done | bytes 32800 | tf_op jit(solution)/shard_map/ppermute | solution.py:163
  10.0 1.3 %collective-permute-done.2 = bf16[128,128]{1,0:T(8,128)(2,1)S(1)} collective-permute-done((bf16[128,128]{1,0:T(8,128)(2,1)S(1)}, bf16[128,128]{1,0:T(8,128)(2,1)S(1)}, u32[]{:S(2)}, u32[]{:S(2)}) %collective-permute-start.2) | collective-permute-done | bytes 32800 | tf_op jit(solution)/shard_map/ppermute | solution.py:163
  11.4 0.1 collective-permute-start.6
  11.5 2.5 %collective-permute-start.5 = (bf16[1,528,128]{2,1,0:T(8,128)(2,1)S(1)}, bf16[1,528,128]{2,1,0:T(8,128)(2,1)S(1)}, u32[]{:S(2)}, u32[]{:S(2)}) collective-permute-start(bf16[1,528,128]{2,1,0:T(8,128)(2,1)S(1)} %bitcast.12), channel_id=1, source_target_pairs={{0,24},{4,28},{8,16},{12,20},{16,8},{20,12},{24,0},{28,4},{1,25},{... | collective-permute-start | bytes 405512 | tf_op jit(solution)/shard_map/ppermute | solution.py:171
  14.0 0.5 %collective-permute-start.4 = (bf16[1,528,128]{2,1,0:T(8,128)(2,1)S(1)}, bf16[1,528,128]{2,1,0:T(8,128)(2,1)S(1)}, u32[]{:S(2)}, u32[]{:S(2)}) collective-permute-start(bf16[1,528,128]{2,1,0:T(8,128)(2,1)S(1)} %bitcast.13), channel_id=1, source_target_pairs={{0,16},{4,20},{8,24},{12,28},{16,0},{20,4},{24,8},{28,12},{1,17},{... | collective-permute-start | bytes 405512 | tf_op jit(solution)/shard_map/ppermute | solution.py:171
  14.5 0.5 %collective-permute-start.3 = (bf16[1,528,128]{2,1,0:T(8,128)(2,1)S(1)}, bf16[1,528,128]{2,1,0:T(8,128)(2,1)S(1)}, u32[]{:S(2)}, u32[]{:S(2)}) collective-permute-start(bf16[1,528,128]{2,1,0:T(8,128)(2,1)S(1)} %bitcast.14), channel_id=1, source_target_pairs={{0,8},{4,12},{8,0},{12,4},{16,24},{20,28},{24,16},{28,20},{1,9},{5... | collective-permute-start | bytes 405512 | tf_op jit(solution)/shard_map/ppermute | solution.py:171
  15.0 0.0 copy-done
  15.0 0.1 constant_dynamic-slice_fusion
  15.2 0.0 collective-permute-done.6.refs_1_
  15.2 1.6 %shard_map.47 = (f32[1,1024]{1,0:T(1,128)S(1)}, f32[1,1024]{1,0:T(1,128)S(1)}, f32[128,1024]{1,0:T(8,128)S(1)}) custom-call(s32[1]{0:T(128)S(6)} %copy.9.own_ref, bf16[1024,128]{1,0:T(8,128)(2,1)S(1)} %bitcast.6, bf16[528,128]{1,0:T(8,128)(2,1)S(1)} %constant_dynamic-update-slice_fusion.refs_0_, bf16[1,528,128]{2,1,0:T(8,128)(2,1)S(1)} %collective-permute-done.6.refs_1_), custom_call_target="tpu_custom_call" | custom-call | flops 268435456 | bytes 2097152 | tf_op jit(solution)/shard_map/pallas_call | solution.py:132
  16.8 1.9 %collective-permute-done.5.refs_5_ = bf16[1,528,128]{2,1,0:T(8,128)(2,1)S(1)} collective-permute-done((bf16[1,528,128]{2,1,0:T(8,128)(2,1)S(1)}, bf16[1,528,128]{2,1,0:T(8,128)(2,1)S(1)}, u32[]{:S(2)}, u32[]{:S(2)}) %collective-permute-start.5) | collective-permute-done | bytes 135200 | tf_op jit(solution)/shard_map/ppermute | solution.py:171
  18.7 2.5 %collective-permute-done.4.refs_4_ = bf16[1,528,128]{2,1,0:T(8,128)(2,1)S(1)} collective-permute-done((bf16[1,528,128]{2,1,0:T(8,128)(2,1)S(1)}, bf16[1,528,128]{2,1,0:T(8,128)(2,1)S(1)}, u32[]{:S(2)}, u32[]{:S(2)}) %collective-permute-start.4) | collective-permute-done | bytes 135200 | tf_op jit(solution)/shard_map/ppermute | solution.py:171
  21.3 0.1 collective-permute-done.3.refs_3_
  21.4 0.0 collective-permute-start.7
  21.4 0.5 %collective-permute-start.8 = (bf16[1,528,128]{2,1,0:T(8,128)(2,1)S(1)}, bf16[1,528,128]{2,1,0:T(8,128)(2,1)S(1)}, u32[]{:S(2)}, u32[]{:S(2)}) collective-permute-start(bf16[1,528,128]{2,1,0:T(8,128)(2,1)S(1)} %collective-permute-done.4.refs_4_), channel_id=1, source_target_pairs={{0,4},{4,0},{8,12},{12,8},{16,20},{20,16},{24,28},{28,24},{1,5},{5... | collective-permute-start | bytes 405512 | tf_op jit(solution)/shard_map/ppermute | solution.py:171
  21.9 0.0 collective-permute-start.9
  21.9 2.0 %shard_map.48 = (f32[1,1024]{1,0:T(1,128)S(1)}, f32[1,1024]{1,0:T(1,128)S(1)}, f32[128,1024]{1,0:T(8,128)S(1)}) custom-call(s32[1]{0:T(128)S(6)} %copy.9.own_ref, bf16[1024,128]{1,0:T(8,128)(2,1)S(1)} %bitcast.7, f32[1,1024]{1,0:T(1,128)S(1)} %get-tuple-element.28.refs_0_, f32[1,1024]{1,0:T(1,128)S(1)} %get-tuple-element.29.refs_1_, ...), custom_call_target="tpu_custom_call" | custom-call | flops 402653184 | bytes 2097152 | tf_op jit(solution)/shard_map/pallas_call | solution.py:132
  23.9 0.0 collective-permute-done.7.refs_3_
  23.9 0.0 collective-permute-done.8.refs_4_
  24.0 0.0 collective-permute-done.9.refs_5_
  24.0 2.8 %shard_map.49 = bf16[1024,128]{1,0:T(8,128)(2,1)} custom-call(s32[1]{0:T(128)S(6)} %copy.9.own_ref, bf16[1024,128]{1,0:T(8,128)(2,1)S(1)} %bitcast.8, f32[1,1024]{1,0:T(1,128)S(1)} %get-tuple-element.34.refs_0_, f32[1,1024]{1,0:T(1,128)S(1)} %get-tuple-element.35.refs_1_, f32[128,1024]{1,0:T(8,128)S(1)} %get-tuple-element.36.refs_2_, ...), custom_call_target="tpu_custom_call" | custom-call | flops 402653184 | bytes 2097152 | tf_op jit(solution)/shard_map/pallas_call | solution.py:132
  (5 shorter events, 0.0 us)
Async XLA Ops:
  0.0 15.0 %copy-start = (bf16[256,16,128]{2,1,0:T(8,128)(2,1)S(1)}, bf16[256,16,128]{2,1,0:T(8,128)(2,1)}, u32[]{:S(2)}) copy-start(bf16[256,16,128]{2,1,0:T(8,128)(2,1)} %param.4) | copy-start | bytes 3145732
  0.0 0.8 %copy-start.1 = (bf16[64,2,128]{2,1,0:T(2,128)(2,1)S(1)}, bf16[64,2,128]{2,1,0:T(2,128)(2,1)}, u32[]{:S(2)}) copy-start(bf16[64,2,128]{2,1,0:T(2,128)(2,1)} %param.5) | copy-start | bytes 98308
  0.9 0.8 %copy-start.2 = (bf16[64,2,128]{2,1,0:T(2,128)(2,1)S(1)}, bf16[64,2,128]{2,1,0:T(2,128)(2,1)}, u32[]{:S(2)}) copy-start(bf16[64,2,128]{2,1,0:T(2,128)(2,1)} %param.6) | copy-start | bytes 98308
  1.8 7.7 %collective-permute-start = (bf16[128,128]{1,0:T(8,128)(2,1)S(1)}, bf16[128,128]{1,0:T(8,128)(2,1)S(1)}, u32[]{:S(2)}, u32[]{:S(2)}) collective-permute-start(bf16[128,128]{1,0:T(8,128)(2,1)S(1)} %get-tuple-element.22), channel_id=1, source_target_pairs={{0,1},{1,2},{2,3},{3,0},{4,5},{5,6},{6,7},{7,4},{8,9},{9,10},{10,1... | collective-permute-start | bytes 98312 | tf_op jit(solution)/shard_map/ppermute | solution.py:163
  4.9 5.2 %collective-permute-start.1 = (bf16[128,128]{1,0:T(8,128)(2,1)S(1)}, bf16[128,128]{1,0:T(8,128)(2,1)S(1)}, u32[]{:S(2)}, u32[]{:S(2)}) collective-permute-start(bf16[128,128]{1,0:T(8,128)(2,1)S(1)} %get-tuple-element.23), channel_id=1, source_target_pairs={{0,2},{1,3},{2,0},{3,1},{4,6},{5,7},{6,4},{7,5},{8,10},{9,11},{10,... | collective-permute-start | bytes 98312 | tf_op jit(solution)/shard_map/ppermute | solution.py:163
  7.5 3.9 %collective-permute-start.2 = (bf16[128,128]{1,0:T(8,128)(2,1)S(1)}, bf16[128,128]{1,0:T(8,128)(2,1)S(1)}, u32[]{:S(2)}, u32[]{:S(2)}) collective-permute-start(bf16[128,128]{1,0:T(8,128)(2,1)S(1)} %get-tuple-element.24), channel_id=1, source_target_pairs={{0,3},{1,0},{2,1},{3,2},{4,7},{5,4},{6,5},{7,6},{8,11},{9,8},{10,9... | collective-permute-start | bytes 98312 | tf_op jit(solution)/shard_map/ppermute | solution.py:163
  11.4 3.8 %collective-permute-start.6 = (bf16[1,528,128]{2,1,0:T(8,128)(2,1)S(1)}, bf16[1,528,128]{2,1,0:T(8,128)(2,1)S(1)}, u32[]{:S(2)}, u32[]{:S(2)}) collective-permute-start(bf16[1,528,128]{2,1,0:T(8,128)(2,1)S(1)} %bitcast.11), channel_id=1, source_target_pairs={{0,4},{4,0},{8,12},{12,8},{16,20},{20,16},{24,28},{28,24},{1,5},{5... | collective-permute-start | bytes 405512 | tf_op jit(solution)/shard_map/ppermute | solution.py:171
  11.5 7.3 %collective-permute-start.5 = (bf16[1,528,128]{2,1,0:T(8,128)(2,1)S(1)}, bf16[1,528,128]{2,1,0:T(8,128)(2,1)S(1)}, u32[]{:S(2)}, u32[]{:S(2)}) collective-permute-start(bf16[1,528,128]{2,1,0:T(8,128)(2,1)S(1)} %bitcast.12), channel_id=1, source_target_pairs={{0,24},{4,28},{8,16},{12,20},{16,8},{20,12},{24,0},{28,4},{1,25},{... | collective-permute-start | bytes 405512 | tf_op jit(solution)/shard_map/ppermute | solution.py:171
  14.0 7.3 %collective-permute-start.4 = (bf16[1,528,128]{2,1,0:T(8,128)(2,1)S(1)}, bf16[1,528,128]{2,1,0:T(8,128)(2,1)S(1)}, u32[]{:S(2)}, u32[]{:S(2)}) collective-permute-start(bf16[1,528,128]{2,1,0:T(8,128)(2,1)S(1)} %bitcast.13), channel_id=1, source_target_pairs={{0,16},{4,20},{8,24},{12,28},{16,0},{20,4},{24,8},{28,12},{1,17},{... | collective-permute-start | bytes 405512 | tf_op jit(solution)/shard_map/ppermute | solution.py:171
  14.5 6.9 %collective-permute-start.3 = (bf16[1,528,128]{2,1,0:T(8,128)(2,1)S(1)}, bf16[1,528,128]{2,1,0:T(8,128)(2,1)S(1)}, u32[]{:S(2)}, u32[]{:S(2)}) collective-permute-start(bf16[1,528,128]{2,1,0:T(8,128)(2,1)S(1)} %bitcast.14), channel_id=1, source_target_pairs={{0,8},{4,12},{8,0},{12,4},{16,24},{20,28},{24,16},{28,20},{1,9},{5... | collective-permute-start | bytes 405512 | tf_op jit(solution)/shard_map/ppermute | solution.py:171
  21.4 2.6 %collective-permute-start.7 = (bf16[1,528,128]{2,1,0:T(8,128)(2,1)S(1)}, bf16[1,528,128]{2,1,0:T(8,128)(2,1)S(1)}, u32[]{:S(2)}, u32[]{:S(2)}) collective-permute-start(bf16[1,528,128]{2,1,0:T(8,128)(2,1)S(1)} %collective-permute-done.3.refs_3_), channel_id=1, source_target_pairs={{0,4},{4,0},{8,12},{12,8},{16,20},{20,16},{24,28},{28,24},{1,5},{5... | collective-permute-start | bytes 405512 | tf_op jit(solution)/shard_map/ppermute | solution.py:171
  21.4 2.6 %collective-permute-start.8 = (bf16[1,528,128]{2,1,0:T(8,128)(2,1)S(1)}, bf16[1,528,128]{2,1,0:T(8,128)(2,1)S(1)}, u32[]{:S(2)}, u32[]{:S(2)}) collective-permute-start(bf16[1,528,128]{2,1,0:T(8,128)(2,1)S(1)} %collective-permute-done.4.refs_4_), channel_id=1, source_target_pairs={{0,4},{4,0},{8,12},{12,8},{16,20},{20,16},{24,28},{28,24},{1,5},{5... | collective-permute-start | bytes 405512 | tf_op jit(solution)/shard_map/ppermute | solution.py:171
  21.9 2.1 %collective-permute-start.9 = (bf16[1,528,128]{2,1,0:T(8,128)(2,1)S(1)}, bf16[1,528,128]{2,1,0:T(8,128)(2,1)S(1)}, u32[]{:S(2)}, u32[]{:S(2)}) collective-permute-start(bf16[1,528,128]{2,1,0:T(8,128)(2,1)S(1)} %collective-permute-done.5.refs_5_), channel_id=1, source_target_pairs={{0,4},{4,0},{8,12},{12,8},{16,20},{20,16},{24,28},{28,24},{1,5},{5... | collective-permute-start | bytes 405512 | tf_op jit(solution)/shard_map/ppermute | solution.py:171

commit v5 on v4

--- a/solution.py
+++ b/solution.py
@@ -15,8 +15,7 @@
 MIB = 1024 * 1024
 
 
-def pack(heads_out, group, part, pieces, keys_ref, values_ref, *out_refs):
-    here = lax.axis_index("head")
+def pack(heads_out, group, part, pieces, keys_ref, values_ref, out_ref):
     rows = keys_ref.shape[0]
     kv_heads = rows // part
     at = lax.broadcasted_iota(jnp.int32, (part, rows), 0)
@@ -30,13 +29,9 @@
                 for ref in (keys_ref, values_ref)
             ]
         )
-    for shift, out_ref in enumerate(out_refs):
-        kv_head = lax.rem(here + shift, pieces) * heads_out // group
+    for target in range(pieces):
         for half in range(2):
-            rows_out = chosen[0][half]
-            for head in range(1, kv_heads):
-                rows_out = jnp.where(kv_head == head, chosen[head][half], rows_out)
-            out_ref[pl.ds(half * part, part), :] = rows_out
+            out_ref[target, pl.ds(half * part, part), :] = chosen[target * heads_out // group][half]
 
 
 def attend(pieces, part, scale, first, last, counts, own_ref, query_ref, *refs):
@@ -49,7 +44,6 @@
     block_rows = pieces * part
     group = query_rows // block_rows
     factor = scale * math.log2(math.e)
-    here = lax.axis_index("head")
     own = own_ref[0].astype(jnp.float32)
 
     blocks = []
@@ -80,10 +74,8 @@
             )
             if seen is None:
                 row = lax.broadcasted_iota(jnp.int32, score.shape, 0)
-                piece = lax.rem(here + pieces - row // part, pieces)
-                key_at = piece * part + row % part
                 query_at = (lane + lax.broadcasted_iota(jnp.int32, score.shape, 1)) // group
-                score = jnp.where(key_at <= query_at, score, LOW)
+                score = jnp.where(row <= query_at, score, LOW)
             top = jnp.max(score, axis=0, keepdims=True)
             scores.append(score)
             tops.append(top if seen is None else jnp.where(seen, top, LOW))
@@ -154,30 +146,31 @@
     whole = pl.BlockSpec(memory_space=pltpu.VMEM)
     packed = pl.pallas_call(
         functools.partial(pack, heads_out, all_heads // kv_heads, part, pieces),
-        out_shape=[jax.ShapeDtypeStruct((2 * part, head_width), jnp.bfloat16)] * pieces,
+        out_shape=jax.ShapeDtypeStruct((pieces, 2 * part, head_width), jnp.bfloat16),
         in_specs=[whole, whole],
-        out_specs=[whole] * pieces,
+        out_specs=whole,
         compiler_params=pltpu.CompilerParams(vmem_limit_bytes=4 * MIB),
     )(keys.reshape(part * kv_heads, head_width), values.reshape(part * kv_heads, head_width))
-    near = [packed[0]] + [
-        lax.ppermute(packed[shift], "head", [(i, (i + shift) % pieces) for i in range(pieces)])
-        for shift in range(1, pieces)
-    ]
-    block = jnp.concatenate(near + [mark])
+    near = lax.all_to_all(packed, "head", 0, 0, tiled=False).reshape(pieces * 2 * part, head_width)
+    block = jnp.concatenate([near, mark])
     fold = functools.partial(attend_call, pieces, part, block_ids, own_queries)
     if blocks == 8:
 
         def swap(rows, flip):
             return lax.ppermute(rows, "seq", [(i, i ^ flip) for i in range(blocks)])
 
-        sent = block[None]
-        along_x, along_y, across = swap(sent, 2), swap(sent, 4), swap(sent, 6)
-        other = swap(sent, 1)
-        state = fold(None, block, [other], False)
-        along_x, along_y, across, state = lax.optimization_barrier((along_x, along_y, across, state))
-        others = [swap(rows, 1) for rows in (along_x, along_y, across)]
-        state = fold(state, None, [along_x, along_y, across], False)
-        result = fold(state, None, others, True)
+        plane = lax.all_to_all(
+            jnp.broadcast_to(block[None], (4,) + block.shape),
+            "seq",
+            0,
+            0,
+            axis_index_groups=[[i for i in range(blocks) if i % 2 == core] for core in range(2)],
+        )
+        state = fold(None, block, [], False)
+        plane, state = lax.optimization_barrier((plane, state))
+        others = swap(plane, 1)
+        state = fold(state, None, [plane], False)
+        result = fold(state, None, [others], True)
     else:
         far = lax.all_gather(block, "seq", axis=0, tiled=False)
         unit = math.gcd(blocks, 8)

time: 26.9 us -> 32 us (1.19)
  waiting for transfers between devices: 6.42 us -> 10.8 us
  starting transfers between devices: 11.1 us -> 10 us
  Pallas kernels: 6.62 us -> 7.51 us
  local copies, waits for them, and re-layouts: 1.79 us -> 2.63 us
    all_to_all x0 -> x2, waiting for transfers between devices: none -> 10.8 us  [the longest x1 5.42 us: shards(): lax.all_to_all(packed, 'head', 0, 0, tiled=False)]
    all_to_all x0 -> x2, starting transfers between devices: none -> 10 us  [the longest x1 6.32 us: shards(): lax.all_to_all(packed, 'head', 0, 0, tiled=False)]
    ppermute x3 -> x0, starting transfers between devices: 7.01 us -> none  [shards(): lax.ppermute(packed[shift], 'head', [(i, (i + shift) % pieces) for i in r...]
    ppermute x7 -> x1, waiting for transfers between devices: 4.55 us -> 0.01 us  [swap(): return lax.ppermute(rows, 'seq', [(i, i ^ flip) for i in range(blocks)])]
    ppermute x7 -> x1, starting transfers between devices: 4.13 us -> 0.01 us  [swap(): return lax.ppermute(rows, 'seq', [(i, i ^ flip) for i in range(blocks)])]
    ppermute x3 -> x0, waiting for transfers between devices: 1.87 us -> none  [shards(): lax.ppermute(packed[shift], 'head', [(i, (i + shift) % pieces) for i in r...]
    broadcast_in_dim x0 -> x1, local copies, waits for them, and re-layouts: none -> 0.87 us  [shards(): jnp.broadcast_to(block[None], (4,) + block.shape)]
    pallas_call x1, Pallas kernels: 0.18 us -> 0.82 us  [shards(): pl.pallas_call(functools.partial(pack, heads_out, all_heads // kv_heads,...]
  transfers between devices with their start and end apart: 10 -> 3, of which waited for: 5 -> 2; matrix products, arithmetic and copies ran while one was open for 1% -> 0% of each run, Pallas kernels for 14% -> 11%
where the time goes in v5:
time: 32 us; the launch traced here: 31.6 us
  waiting for transfers between devices  10.8 us (34%)
  starting transfers between devices  10 us (31%)
  Pallas kernels  7.51 us (23%)
  local copies, waits for them, and re-layouts  2.63 us (8%)
  between operations  0.69 us (2%)
    pallas_call x3, Pallas kernels, attend_call(): pl.pallas_call(functools.partial(attend, pieces, part, head_width ** (-0....  6.68 us
    all_to_all x1, starting transfers between devices, shards(): lax.all_to_all(packed, 'head', 0, 0, tiled=False)  6.32 us
    all_to_all x1, waiting for transfers between devices, shards(): lax.all_to_all(packed, 'head', 0, 0, tiled=False)  5.42 us
    all_to_all x1, waiting for transfers between devices, shards(): lax.all_to_all(jnp.broadcast_to(block[None], (4,) + block.shape), 'seq',...  5.36 us
    all_to_all x1, starting transfers between devices, shards(): lax.all_to_all(jnp.broadcast_to(block[None], (4,) + block.shape), 'seq',...  3.72 us
    unnamed x6, local copies, waits for them, and re-layouts  1.61 us
    broadcast_in_dim x1, local copies, waits for them, and re-layouts, shards(): jnp.broadcast_to(block[None], (4,) + block.shape)  0.87 us
    pallas_call x1, Pallas kernels, shards(): pl.pallas_call(functools.partial(pack, heads_out, all_heads // kv_heads,...  0.82 us
  transfers between devices with their start and end apart: 3, of which 2 were waited for; matrix products, arithmetic and copies ran while one was open for 0% of the time, Pallas kernels for 11%

profile of v5, /device:TPU:0, one launch (start us, length us, event | category | flops | bytes accessed | tf_op | source)
XLA Modules:
  0.0 31.6 jit_solution(3165570033038222059)
XLA Ops:
  0.0 0.0 copy-start
  0.0 0.0 copy-start.1
  0.0 0.8 %copy-done.1 = bf16[64,2,128]{2,1,0:T(2,128)(2,1)S(1)} copy-done((bf16[64,2,128]{2,1,0:T(2,128)(2,1)S(1)}, bf16[64,2,128]{2,1,0:T(2,128)(2,1)}, u32[]{:S(2)}) %copy-start.1) | copy-done | bytes 32792
  0.9 0.0 copy-start.2
  0.9 0.8 %copy-done.2 = bf16[64,2,128]{2,1,0:T(2,128)(2,1)S(1)} copy-done((bf16[64,2,128]{2,1,0:T(2,128)(2,1)S(1)}, bf16[64,2,128]{2,1,0:T(2,128)(2,1)}, u32[]{:S(2)}) %copy-start.2) | copy-done | bytes 32792
  1.6 0.8 %shard_map.46 = bf16[4,128,128]{2,1,0:T(8,128)(2,1)} custom-call(bf16[128,128]{1,0:T(8,128)(2,1)S(1)} %bitcast.9, bf16[128,128]{1,0:T(8,128)(2,1)S(1)} %bitcast.10), custom_call_target="tpu_custom_call" | custom-call | tf_op jit(solution)/shard_map/pallas_call | solution.py:147
  2.4 6.3 %all-to-all-start = ((bf16[4,128,128]{2,1,0:T(8,128)(2,1)}), bf16[4,128,128]{2,1,0:T(8,128)(2,1)S(1)}, u32[]{:S(2)}, u32[]{:S(2)}) async-start(bf16[4,128,128]{2,1,0:T(8,128)(2,1)} %shard_map.46), calls=%async_computation | async-start | bytes 262144 | tf_op jit(solution)/shard_map/all_to_all | solution.py:154
  9.4 5.4 %all-to-all-done = bf16[4,128,128]{2,1,0:T(8,128)(2,1)S(1)} async-done(((bf16[4,128,128]{2,1,0:T(8,128)(2,1)}), bf16[4,128,128]{2,1,0:T(8,128)(2,1)S(1)}, u32[]{:S(2)}, u32[]{:S(2)}) %all-to-all-start) | async-done | bytes 131104 | tf_op jit(solution)/shard_map/all_to_all | solution.py:154
  14.8 0.9 %broadcast_in_dim.5 = bf16[4,528,128]{2,1,0:T(8,128)(2,1)} broadcast(bf16[528,128]{1,0:T(8,128)(2,1)S(1)} %concatenate.3.refs_0_), dimensions={1,2} | broadcast | bytes 675840 | tf_op jit(solution)/shard_map/broadcast_in_dim | solution.py:163
  15.7 3.7 %all-to-all-start.1 = ((bf16[4,528,128]{2,1,0:T(8,128)(2,1)}), bf16[4,528,128]{2,1,0:T(8,128)(2,1)S(1)}, u32[]{:S(2)}, u32[]{:S(2)}) async-start(bf16[4,528,128]{2,1,0:T(8,128)(2,1)} %broadcast_in_dim.5), calls=%async_computation.1 | async-start | bytes 1081344 | tf_op jit(solution)/shard_map/all_to_all | solution.py:162
  19.4 0.0 copy-done
  19.4 0.1 constant_dynamic-slice_fusion
  19.6 1.2 %shard_map.47 = (f32[1,1024]{1,0:T(1,128)S(1)}, f32[1,1024]{1,0:T(1,128)S(1)}, f32[128,1024]{1,0:T(8,128)S(1)}) custom-call(s32[1]{0:T(128)S(6)} %copy.5.own_ref, bf16[1024,128]{1,0:T(8,128)(2,1)S(1)} %bitcast.6, bf16[528,128]{1,0:T(8,128)(2,1)S(1)} %concatenate.3.refs_0_), custom_call_target="tpu_custom_call" | custom-call | flops 134217728 | bytes 2097152 | tf_op jit(solution)/shard_map/pallas_call | solution.py:124
  20.8 5.4 %all-to-all-done.1.refs_3_ = bf16[4,528,128]{2,1,0:T(8,128)(2,1)S(1)} async-done(((bf16[4,528,128]{2,1,0:T(8,128)(2,1)}), bf16[4,528,128]{2,1,0:T(8,128)(2,1)S(1)}, u32[]{:S(2)}, u32[]{:S(2)}) %all-to-all-start.1) | async-done | bytes 540704 | tf_op jit(solution)/shard_map/all_to_all | solution.py:162
  26.1 0.0 collective-permute-start
  26.1 2.4 %shard_map.48 = (f32[1,1024]{1,0:T(1,128)S(1)}, f32[1,1024]{1,0:T(1,128)S(1)}, f32[128,1024]{1,0:T(8,128)S(1)}) custom-call(s32[1]{0:T(128)S(6)} %copy.5.own_ref, bf16[1024,128]{1,0:T(8,128)(2,1)S(1)} %bitcast.7, f32[1,1024]{1,0:T(1,128)S(1)} %get-tuple-element.18.refs_0_, f32[1,1024]{1,0:T(1,128)S(1)} %get-tuple-element.19.refs_1_, ...), custom_call_target="tpu_custom_call" | custom-call | flops 536870912 | bytes 2097152 | tf_op jit(solution)/shard_map/pallas_call | solution.py:124
  28.5 0.0 collective-permute-done.refs_3_
  28.5 3.1 %shard_map.49 = bf16[1024,128]{1,0:T(8,128)(2,1)} custom-call(s32[1]{0:T(128)S(6)} %copy.5.own_ref, bf16[1024,128]{1,0:T(8,128)(2,1)S(1)} %bitcast.8, f32[1,1024]{1,0:T(1,128)S(1)} %get-tuple-element.22.refs_0_, f32[1,1024]{1,0:T(1,128)S(1)} %get-tuple-element.23.refs_1_, f32[128,1024]{1,0:T(8,128)S(1)} %get-tuple-element.24.refs_2_, ...), custom_call_target="tpu_custom_call" | custom-call | flops 536870912 | bytes 2097152 | tf_op jit(solution)/shard_map/pallas_call | solution.py:124
  (1 shorter events, 0.0 us)
Async XLA Ops:
  0.0 19.4 %copy-start = (bf16[256,16,128]{2,1,0:T(8,128)(2,1)S(1)}, bf16[256,16,128]{2,1,0:T(8,128)(2,1)}, u32[]{:S(2)}) copy-start(bf16[256,16,128]{2,1,0:T(8,128)(2,1)} %param.4) | copy-start | bytes 3145732
  0.0 0.8 %copy-start.1 = (bf16[64,2,128]{2,1,0:T(2,128)(2,1)S(1)}, bf16[64,2,128]{2,1,0:T(2,128)(2,1)}, u32[]{:S(2)}) copy-start(bf16[64,2,128]{2,1,0:T(2,128)(2,1)} %param.5) | copy-start | bytes 98308
  0.9 0.8 %copy-start.2 = (bf16[64,2,128]{2,1,0:T(2,128)(2,1)S(1)}, bf16[64,2,128]{2,1,0:T(2,128)(2,1)}, u32[]{:S(2)}) copy-start(bf16[64,2,128]{2,1,0:T(2,128)(2,1)} %param.6) | copy-start | bytes 98308
  2.4 12.4 %all-to-all-start = ((bf16[4,128,128]{2,1,0:T(8,128)(2,1)}), bf16[4,128,128]{2,1,0:T(8,128)(2,1)S(1)}, u32[]{:S(2)}, u32[]{:S(2)}) async-start(bf16[4,128,128]{2,1,0:T(8,128)(2,1)} %shard_map.46), calls=%async_computation | async-start | bytes 262144 | tf_op jit(solution)/shard_map/all_to_all | solution.py:154
  15.7 10.4 %all-to-all-start.1 = ((bf16[4,528,128]{2,1,0:T(8,128)(2,1)}), bf16[4,528,128]{2,1,0:T(8,128)(2,1)S(1)}, u32[]{:S(2)}, u32[]{:S(2)}) async-start(bf16[4,528,128]{2,1,0:T(8,128)(2,1)} %broadcast_in_dim.5), calls=%async_computation.1 | async-start | bytes 1081344 | tf_op jit(solution)/shard_map/all_to_all | solution.py:162
  26.1 2.4 %collective-permute-start = (bf16[4,528,128]{2,1,0:T(8,128)(2,1)S(1)}, bf16[4,528,128]{2,1,0:T(8,128)(2,1)S(1)}, u32[]{:S(2)}, u32[]{:S(2)}) collective-permute-start(bf16[4,528,128]{2,1,0:T(8,128)(2,1)S(1)} %all-to-all-done.1.refs_3_), channel_id=1, source_target_pairs={{0,4},{4,0},{8,12},{12,8},{16,20},{20,16},{24,28},{28,24},{1,5},{5... | collective-permute-start | bytes 1622024 | tf_op jit(solution)/shard_map/ppermute | solution.py:160

commit v6 on v4

v6 whole, which is shorter than its diff:
```python
import functools
import math

import jax
import jax.numpy as jnp
from jax import lax
from jax.experimental import pallas as pl
from jax.experimental.pallas import tpu as pltpu
from jax.sharding import PartitionSpec as P

MARK = 16
SUBLANES = 8
LANES = 256
LOW = -1e30
HIGH = 1e30
MIB = 1024 * 1024


def pack(heads_out, group, part, pieces, keys_hbm, values_hbm, *refs):
    out_refs = refs[:pieces]
    keys_ref, values_ref, sems = refs[pieces:]
    copies = [
        pltpu.make_async_copy(source, target, sems.at[i])
        for i, (source, target) in enumerate([(keys_hbm, keys_ref), (values_hbm, values_ref)])
    ]
    for copy in copies:
        copy.start()
    here = lax.axis_index("head")
    rows = keys_ref.shape[0]
    kv_heads = rows // part
    at = lax.broadcasted_iota(jnp.int32, (part, rows), 0)
    source = lax.broadcasted_iota(jnp.int32, (part, rows), 1)
    picks = [
        jnp.where(source == at * kv_heads + head, 1.0, 0.0).astype(jnp.bfloat16) for head in range(kv_heads)
    ]
    for half, ref in enumerate((keys_ref, values_ref)):
        copies[half].wait()
        chosen = [
            jnp.dot(pick, ref[...], preferred_element_type=jnp.float32).astype(jnp.bfloat16) for pick in picks
        ]
        for shift, out_ref in enumerate(out_refs):
            kv_head = lax.rem(here + shift, pieces) * heads_out // group
            rows_out = chosen[0]
            for head in range(1, kv_heads):
                rows_out = jnp.where(kv_head == head, chosen[head], rows_out)
            out_ref[pl.ds(half * part, part), :] = rows_out


def scale_queries(scale, query_ref, out_ref):
    head_width = query_ref.shape[1]
    scaled = query_ref[...].astype(jnp.float32) * (scale * math.log2(math.e))
    coarse = scaled.astype(jnp.bfloat16)
    out_ref[:head_width, :] = coarse.T
    out_ref[head_width:, :] = (scaled - coarse.astype(jnp.float32)).astype(jnp.bfloat16).T


def attend(pieces, part, first, last, counts, own_ref, query_ref, *refs):
    refs = list(refs)
    state = None if first else [refs.pop(0) for _ in range(2)]
    near_ref = refs.pop(0) if first else None
    far_refs = [refs.pop(0) for _ in counts]
    outs = refs
    head_width = query_ref.shape[0] // 2
    query_rows = query_ref.shape[1]
    block_rows = pieces * part
    group = query_rows // block_rows
    here = lax.axis_index("head")
    own = own_ref[0].astype(jnp.float32)

    blocks = []
    if first:
        blocks.append((near_ref, None))
    for count, ref in zip(counts, far_refs):
        for block in range(count):
            rows_ref = ref.at[block]
            mark = rows_ref[pl.ds(2 * block_rows, MARK), :].astype(jnp.float32)[:SUBLANES]
            seen = jnp.concatenate([mark] * (LANES // head_width), axis=1) < own
            blocks.append((rows_ref, seen))

    def side(offset):
        return jnp.concatenate(
            [
                rows_ref[pl.ds((2 * piece + offset) * part, part), :]
                for rows_ref, _ in blocks
                for piece in range(pieces)
            ]
        )

    keys = side(0)
    keys = jnp.concatenate([keys, keys], axis=1)
    values = jnp.concatenate(
        [side(1).T, jnp.ones((MARK, len(blocks) * block_rows), jnp.bfloat16)]
    )
    spans = [pl.ds(lane, LANES) for lane in range(0, query_rows, LANES)]
    if not first:
        old = [(state[0][:, span], state[1][:, span]) for span in spans]

    results = []
    for at, span in enumerate(spans):
        scores = jnp.dot(keys, query_ref[:, span], preferred_element_type=jnp.float32)
        scores = [scores[i * block_rows : (i + 1) * block_rows] for i in range(len(blocks))]
        tops = []
        for i, (_, seen) in enumerate(blocks):
            if seen is None:
                row = lax.broadcasted_iota(jnp.int32, scores[i].shape, 0)
                piece = lax.rem(here + pieces - row // part, pieces)
                key_at = piece * part + row % part
                query_at = (at * LANES + lax.broadcasted_iota(jnp.int32, scores[i].shape, 1)) // group
                scores[i] = jnp.where(key_at <= query_at, scores[i], LOW)
            top = jnp.max(scores[i].reshape(-1, SUBLANES, LANES), axis=0)
            tops.append(top if seen is None else jnp.where(seen, top, LOW))
        high = jnp.max(functools.reduce(jnp.maximum, tops), axis=0, keepdims=True)
        if not first:
            high = jnp.maximum(old[at][0], high)
        weights = []
        for score, (_, seen) in zip(scores, blocks):
            base = high if seen is None else jnp.where(seen[:1], high, HIGH)
            weights.append(jnp.exp2(score - base).astype(jnp.bfloat16))
        accum = jnp.dot(values, jnp.concatenate(weights), preferred_element_type=jnp.float32)[
            : head_width + SUBLANES
        ]
        if not first:
            accum = accum + old[at][1] * jnp.exp2(old[at][0] - high)
        results.append((high, accum))

    for (high, accum), span in zip(results, spans):
        if last:
            inverse = 1.0 / accum[head_width : head_width + 1]
            outs[0][span, :] = (accum[:head_width] * inverse).T.astype(outs[0].dtype)
        else:
            outs[0][:, span] = high
            outs[1][:, span] = accum


def attend_call(pieces, part, own, query, state, near, far, last):
    head_width, query_rows = query.shape[0] // 2, query.shape[1]
    whole = pl.BlockSpec(memory_space=pltpu.VMEM)
    first = near is not None
    counts = [rows.shape[0] for rows in far]
    operands = ([near] if first else list(state)) + list(far)
    if last:
        shapes = jax.ShapeDtypeStruct((query_rows, head_width), jnp.bfloat16)
        out_specs = whole
    else:
        shapes = [
            jax.ShapeDtypeStruct((1, query_rows), jnp.float32),
            jax.ShapeDtypeStruct((head_width + SUBLANES, query_rows), jnp.float32),
        ]
        out_specs = [whole] * 2
    pairs = (sum(counts) + first) * query_rows * pieces * part
    return pl.pallas_call(
        functools.partial(attend, pieces, part, first, last, counts),
        out_shape=shapes,
        in_specs=[pl.BlockSpec(memory_space=pltpu.SMEM)] + [whole] * (1 + len(operands)),
        out_specs=out_specs,
        compiler_params=pltpu.CompilerParams(vmem_limit_bytes=24 * MIB),
        cost_estimate=pl.CostEstimate(
            flops=6 * pairs * head_width, bytes_accessed=2 * MIB, transcendentals=pairs
        ),
    )(own, query, *operands)


def shards(queries, keys, values, block_ids):
    rows_dev, all_heads, head_width = queries.shape
    part, kv_heads = keys.shape[:2]
    head_index = lax.axis_index("head")
    pieces = lax.axis_size("head")
    blocks = lax.axis_size("seq")
    heads_out = all_heads // pieces
    own_queries = lax.dynamic_slice_in_dim(queries, head_index * heads_out, heads_out, 1)
    own_queries = own_queries.reshape(rows_dev * heads_out, head_width)
    whole = pl.BlockSpec(memory_space=pltpu.VMEM)
    scaled = pl.pallas_call(
        functools.partial(scale_queries, head_width ** (-0.5)),
        out_shape=jax.ShapeDtypeStruct((2 * head_width, rows_dev * heads_out), jnp.bfloat16),
        in_specs=[whole],
        out_specs=whole,
        compiler_params=pltpu.CompilerParams(vmem_limit_bytes=8 * MIB),
    )(own_queries)
    mark = jnp.broadcast_to(block_ids.astype(jnp.bfloat16)[:, None], (MARK, head_width))
    packed = pl.pallas_call(
        functools.partial(pack, heads_out, all_heads // kv_heads, part, pieces),
        out_shape=[jax.ShapeDtypeStruct((2 * part, head_width), jnp.bfloat16)] * pieces,
        in_specs=[pl.BlockSpec(memory_space=pltpu.HBM)] * 2,
        out_specs=[whole] * pieces,
        scratch_shapes=[pltpu.VMEM((part * kv_heads, head_width), jnp.bfloat16)] * 2
        + [pltpu.SemaphoreType.DMA((2,))],
        compiler_params=pltpu.CompilerParams(vmem_limit_bytes=4 * MIB),
    )(keys.reshape(part * kv_heads, head_width), values.reshape(part * kv_heads, head_width))
    near = [packed[0]] + [
        lax.ppermute(packed[shift], "head", [(i, (i + shift) % pieces) for i in range(pieces)])
        for shift in range(1, pieces)
    ]
    block = jnp.concatenate(near + [mark])
    fold = functools.partial(attend_call, pieces, part, block_ids, scaled)
    if blocks == 8:

        def swap(rows, flip):
            return lax.ppermute(rows, "seq", [(i, i ^ flip) for i in range(blocks)])

        sent = block[None]
        along_x, along_y, across = swap(sent, 2), swap(sent, 4), swap(sent, 6)
        other = swap(sent, 1)
        state = fold(None, block, [other], False)
        along_x, along_y, across, state = lax.optimization_barrier((along_x, along_y, across, state))
        others = [swap(rows, 1) for rows in (along_x, along_y, across)]
        state = fold(state, None, [along_x, along_y, across], False)
        result = fold(state, None, others, True)
    else:
        far = lax.all_gather(block, "seq", axis=0, tiled=False)
        unit = math.gcd(blocks, 8)
        far = far.reshape((blocks // unit, unit) + block.shape)
        state = fold(None, block, [], False)
        state, _ = lax.scan(lambda held, rows: (tuple(fold(held, None, [rows], False)), None), tuple(state), far[:-1])
        result = fold(state, None, [far[-1]], True)
    return result.reshape(rows_dev, heads_out, head_width)


def solution(mesh):
    return jax.shard_map(
        shards,
        mesh=mesh,
        in_specs=(
            P("seq", None, None),
            P(("seq", "head"), None, None),
            P(("seq", "head"), None, None),
            P("seq"),
        ),
        out_specs=P("seq", "head", None),
        check_vma=False,
    )
```

time: 26.9 us -> 27.6 us (1.026)
  Pallas kernels: 6.62 us -> 7.7 us
  waiting for transfers between devices: 6.42 us -> 6.03 us
    pallas_call x3 -> x4, Pallas kernels: 6.44 us -> 7.34 us  [the longest x3 7.14 us: attend_call(): pl.pallas_call(functools.partial(attend, pieces, part, first, last, count...]
    ppermute x7, waiting for transfers between devices: 4.55 us -> 4.16 us  [swap(): return lax.ppermute(rows, 'seq', [(i, i ^ flip) for i in range(blocks)])]
  transfers between devices with their start and end apart: 10 -> 10, of which waited for: 5 -> 5; matrix products, arithmetic and copies ran while one was open for 1% -> 1% of each run, Pallas kernels for 14% -> 16%
where the time goes in v6:
time: 27.6 us; the launch traced here: 27.4 us
  starting transfers between devices  11.1 us (40%)
  Pallas kernels  7.7 us (28%)
  waiting for transfers between devices  6.03 us (22%)
  local copies, waits for them, and re-layouts  1.79 us (6%)
  between operations  0.76 us (3%)
    pallas_call x3, Pallas kernels, attend_call(): pl.pallas_call(functools.partial(attend, pieces, part, first, last, count...  7.14 us
    ppermute x3, starting transfers between devices, shards(): lax.ppermute(packed[shift], 'head', [(i, (i + shift) % pieces) for i in r...  7.01 us
    ppermute x7, waiting for transfers between devices, swap(): return lax.ppermute(rows, 'seq', [(i, i ^ flip) for i in range(blocks)])  4.16 us
    ppermute x7, starting transfers between devices, swap(): return lax.ppermute(rows, 'seq', [(i, i ^ flip) for i in range(blocks)])  4.13 us
    ppermute x3, waiting for transfers between devices, shards(): lax.ppermute(packed[shift], 'head', [(i, (i + shift) % pieces) for i in r...  1.87 us
    unnamed x10, local copies, waits for them, and re-layouts  1.64 us
  transfers between devices with their start and end apart: 10, of which 5 were waited for; matrix products, arithmetic and copies ran while one was open for 1% of the time, Pallas kernels for 16%

profile of v6, /device:TPU:0, one launch (start us, length us, event | category | flops | bytes accessed | tf_op | source)
XLA Modules:
  0.0 27.4 jit_solution(9316437376355147599)
XLA Ops:
  0.0 0.0 copy-start
  0.0 0.0 copy-start.1
  0.0 0.8 %copy-done.1 = bf16[64,2,128]{2,1,0:T(2,128)(2,1)S(1)} copy-done((bf16[64,2,128]{2,1,0:T(2,128)(2,1)S(1)}, bf16[64,2,128]{2,1,0:T(2,128)(2,1)}, u32[]{:S(2)}) %copy-start.1) | copy-done | bytes 32792
  0.9 0.0 copy-start.2
  0.9 0.8 %copy-done.2 = bf16[64,2,128]{2,1,0:T(2,128)(2,1)S(1)} copy-done((bf16[64,2,128]{2,1,0:T(2,128)(2,1)S(1)}, bf16[64,2,128]{2,1,0:T(2,128)(2,1)}, u32[]{:S(2)}) %copy-start.2) | copy-done | bytes 32792
  1.6 0.4 %shard_map.47 = (bf16[128,128]{1,0:T(8,128)(2,1)S(1)}, bf16[128,128]{1,0:T(8,128)(2,1)S(1)}, bf16[128,128]{1,0:T(8,128)(2,1)S(1)}, bf16[128,128]{1,0:T(8,128)(2,1)S(1)}) custom-call(bf16[128,128]{1,0:T(8,128)(2,1)S(1)} %bitcast.7, bf16[128,128]{1,0:T(8,128)(2,1)S(1)} %bitcast.8), custom_call_target="tpu_custom_call" | custom-call | tf_op jit(solution)/shard_map/pallas_call | solution.py:181
  2.0 3.1 %collective-permute-start = (bf16[128,128]{1,0:T(8,128)(2,1)S(1)}, bf16[128,128]{1,0:T(8,128)(2,1)S(1)}, u32[]{:S(2)}, u32[]{:S(2)}) collective-permute-start(bf16[128,128]{1,0:T(8,128)(2,1)S(1)} %get-tuple-element.19), channel_id=1, source_target_pairs={{0,1},{1,2},{2,3},{3,0},{4,5},{5,6},{6,7},{7,4},{8,9},{9,10},{10,1... | collective-permute-start | bytes 98312 | tf_op jit(solution)/shard_map/ppermute | solution.py:191
  5.1 2.6 %collective-permute-start.1 = (bf16[128,128]{1,0:T(8,128)(2,1)S(1)}, bf16[128,128]{1,0:T(8,128)(2,1)S(1)}, u32[]{:S(2)}, u32[]{:S(2)}) collective-permute-start(bf16[128,128]{1,0:T(8,128)(2,1)S(1)} %get-tuple-element.20), channel_id=1, source_target_pairs={{0,2},{1,3},{2,0},{3,1},{4,6},{5,7},{6,4},{7,5},{8,10},{9,11},{10,... | collective-permute-start | bytes 98312 | tf_op jit(solution)/shard_map/ppermute | solution.py:191
  7.6 1.3 %collective-permute-start.2 = (bf16[128,128]{1,0:T(8,128)(2,1)S(1)}, bf16[128,128]{1,0:T(8,128)(2,1)S(1)}, u32[]{:S(2)}, u32[]{:S(2)}) collective-permute-start(bf16[128,128]{1,0:T(8,128)(2,1)S(1)} %get-tuple-element.21), channel_id=1, source_target_pairs={{0,3},{1,0},{2,1},{3,2},{4,7},{5,4},{6,5},{7,6},{8,11},{9,8},{10,9... | collective-permute-start | bytes 98312 | tf_op jit(solution)/shard_map/ppermute | solution.py:191
  9.7 0.0 collective-permute-done
  9.7 0.5 %collective-permute-done.1 = bf16[128,128]{1,0:T(8,128)(2,1)S(1)} collective-permute-done((bf16[128,128]{1,0:T(8,128)(2,1)S(1)}, bf16[128,128]{1,0:T(8,128)(2,1)S(1)}, u32[]{:S(2)}, u32[]{:S(2)}) %collective-permute-start.1) | collective-permute-done | bytes 32800 | tf_op jit(solution)/shard_map/ppermute | solution.py:191
  10.2 1.3 %collective-permute-done.2 = bf16[128,128]{1,0:T(8,128)(2,1)S(1)} collective-permute-done((bf16[128,128]{1,0:T(8,128)(2,1)S(1)}, bf16[128,128]{1,0:T(8,128)(2,1)S(1)}, u32[]{:S(2)}, u32[]{:S(2)}) %collective-permute-start.2) | collective-permute-done | bytes 32800 | tf_op jit(solution)/shard_map/ppermute | solution.py:191
  11.6 0.1 collective-permute-start.6
  11.7 2.5 %collective-permute-start.5 = (bf16[1,528,128]{2,1,0:T(8,128)(2,1)S(1)}, bf16[1,528,128]{2,1,0:T(8,128)(2,1)S(1)}, u32[]{:S(2)}, u32[]{:S(2)}) collective-permute-start(bf16[1,528,128]{2,1,0:T(8,128)(2,1)S(1)} %bitcast.10), channel_id=1, source_target_pairs={{0,24},{4,28},{8,16},{12,20},{16,8},{20,12},{24,0},{28,4},{1,25},{... | collective-permute-start | bytes 405512 | tf_op jit(solution)/shard_map/ppermute | solution.py:199
  14.2 0.5 %collective-permute-start.4 = (bf16[1,528,128]{2,1,0:T(8,128)(2,1)S(1)}, bf16[1,528,128]{2,1,0:T(8,128)(2,1)S(1)}, u32[]{:S(2)}, u32[]{:S(2)}) collective-permute-start(bf16[1,528,128]{2,1,0:T(8,128)(2,1)S(1)} %bitcast.11), channel_id=1, source_target_pairs={{0,16},{4,20},{8,24},{12,28},{16,0},{20,4},{24,8},{28,12},{1,17},{... | collective-permute-start | bytes 405512 | tf_op jit(solution)/shard_map/ppermute | solution.py:199
  14.7 0.5 %collective-permute-start.3 = (bf16[1,528,128]{2,1,0:T(8,128)(2,1)S(1)}, bf16[1,528,128]{2,1,0:T(8,128)(2,1)S(1)}, u32[]{:S(2)}, u32[]{:S(2)}) collective-permute-start(bf16[1,528,128]{2,1,0:T(8,128)(2,1)S(1)} %bitcast.12), channel_id=1, source_target_pairs={{0,8},{4,12},{8,0},{12,4},{16,24},{20,28},{24,16},{28,20},{1,9},{5... | collective-permute-start | bytes 405512 | tf_op jit(solution)/shard_map/ppermute | solution.py:199
  15.2 0.0 copy-done
  15.2 0.1 constant_dynamic-slice_fusion
  15.4 0.2 shard_map.46.query_ref
  15.6 0.0 collective-permute-done.6.refs_1_
  15.6 1.8 %shard_map.48 = (f32[1,1024]{1,0:T(1,128)S(1)}, f32[136,1024]{1,0:T(8,128)S(1)}) custom-call(s32[1]{0:T(128)S(6)} %copy.9.own_ref, bf16[256,1024]{1,0:T(8,128)(2,1)S(1)} %shard_map.46.query_ref, bf16[528,128]{1,0:T(8,128)(2,1)S(1)} %constant_dynamic-update-slice_fusion.refs_0_, bf16[1,528,128]{2,1,0:T(8,128)(2,1)S(1)} %collective-permute-done.6.refs_1_), custom_call_target="tpu_custom_call" | custom-call | flops 402653184 | bytes 2097152 | tf_op jit(solution)/shard_map/pallas_call | solution.py:151
  17.4 1.5 %collective-permute-done.5.refs_4_ = bf16[1,528,128]{2,1,0:T(8,128)(2,1)S(1)} collective-permute-done((bf16[1,528,128]{2,1,0:T(8,128)(2,1)S(1)}, bf16[1,528,128]{2,1,0:T(8,128)(2,1)S(1)}, u32[]{:S(2)}, u32[]{:S(2)}) %collective-permute-start.5) | collective-permute-done | bytes 135200 | tf_op jit(solution)/shard_map/ppermute | solution.py:199
  18.9 2.5 %collective-permute-done.4.refs_3_ = bf16[1,528,128]{2,1,0:T(8,128)(2,1)S(1)} collective-permute-done((bf16[1,528,128]{2,1,0:T(8,128)(2,1)S(1)}, bf16[1,528,128]{2,1,0:T(8,128)(2,1)S(1)}, u32[]{:S(2)}, u32[]{:S(2)}) %collective-permute-start.4) | collective-permute-done | bytes 135200 | tf_op jit(solution)/shard_map/ppermute | solution.py:199
  21.5 0.1 collective-permute-done.3.refs_2_
  21.6 0.0 collective-permute-start.7
  21.6 0.5 %collective-permute-start.8 = (bf16[1,528,128]{2,1,0:T(8,128)(2,1)S(1)}, bf16[1,528,128]{2,1,0:T(8,128)(2,1)S(1)}, u32[]{:S(2)}, u32[]{:S(2)}) collective-permute-start(bf16[1,528,128]{2,1,0:T(8,128)(2,1)S(1)} %collective-permute-done.4.refs_3_), channel_id=1, source_target_pairs={{0,4},{4,0},{8,12},{12,8},{16,20},{20,16},{24,28},{28,24},{1,5},{5... | collective-permute-start | bytes 405512 | tf_op jit(solution)/shard_map/ppermute | solution.py:199
  22.1 0.0 collective-permute-start.9
  22.1 2.2 %shard_map.49 = (f32[1,1024]{1,0:T(1,128)S(1)}, f32[136,1024]{1,0:T(8,128)S(1)}) custom-call(s32[1]{0:T(128)S(6)} %copy.9.own_ref, bf16[256,1024]{1,0:T(8,128)(2,1)S(1)} %shard_map.46.query_ref, f32[1,1024]{1,0:T(1,128)S(1)} %get-tuple-element.24.refs_0_, f32[136,1024]{1,0:T(8,128)S(1)} %get-tuple-element.25.refs_1_, ...), custom_call_target="tpu_custom_call" | custom-call | flops 603979776 | bytes 2097152 | tf_op jit(solution)/shard_map/pallas_call | solution.py:151
  24.3 0.0 collective-permute-done.7.refs_2_
  24.3 0.0 collective-permute-done.8.refs_3_
  24.3 0.0 collective-permute-done.9.refs_4_
  24.4 3.1 %shard_map.50 = bf16[1024,128]{1,0:T(8,128)(2,1)} custom-call(s32[1]{0:T(128)S(6)} %copy.9.own_ref, bf16[256,1024]{1,0:T(8,128)(2,1)S(1)} %shard_map.46.query_ref, f32[1,1024]{1,0:T(1,128)S(1)} %get-tuple-element.29.refs_0_, f32[136,1024]{1,0:T(8,128)S(1)} %get-tuple-element.30.refs_1_, bf16[1,528,128]{2,1,0:T(8,128)(2,1)S(1)} %collective-permute-done.7.refs_2_, ...), custom_call_target="tpu_custom_call" | custom-call | flops 603979776 | bytes 2097152 | tf_op jit(solution)/shard_map/pallas_call | solution.py:151
  (5 shorter events, 0.0 us)
Async XLA Ops:
  0.0 15.2 %copy-start = (bf16[256,16,128]{2,1,0:T(8,128)(2,1)S(1)}, bf16[256,16,128]{2,1,0:T(8,128)(2,1)}, u32[]{:S(2)}) copy-start(bf16[256,16,128]{2,1,0:T(8,128)(2,1)} %param.4) | copy-start | bytes 3145732
  0.0 0.8 %copy-start.1 = (bf16[64,2,128]{2,1,0:T(2,128)(2,1)S(1)}, bf16[64,2,128]{2,1,0:T(2,128)(2,1)}, u32[]{:S(2)}) copy-start(bf16[64,2,128]{2,1,0:T(2,128)(2,1)} %param.5) | copy-start | bytes 98308
  0.9 0.8 %copy-start.2 = (bf16[64,2,128]{2,1,0:T(2,128)(2,1)S(1)}, bf16[64,2,128]{2,1,0:T(2,128)(2,1)}, u32[]{:S(2)}) copy-start(bf16[64,2,128]{2,1,0:T(2,128)(2,1)} %param.6) | copy-start | bytes 98308
  2.0 7.7 %collective-permute-start = (bf16[128,128]{1,0:T(8,128)(2,1)S(1)}, bf16[128,128]{1,0:T(8,128)(2,1)S(1)}, u32[]{:S(2)}, u32[]{:S(2)}) collective-permute-start(bf16[128,128]{1,0:T(8,128)(2,1)S(1)} %get-tuple-element.19), channel_id=1, source_target_pairs={{0,1},{1,2},{2,3},{3,0},{4,5},{5,6},{6,7},{7,4},{8,9},{9,10},{10,1... | collective-permute-start | bytes 98312 | tf_op jit(solution)/shard_map/ppermute | solution.py:191
  5.1 5.2 %collective-permute-start.1 = (bf16[128,128]{1,0:T(8,128)(2,1)S(1)}, bf16[128,128]{1,0:T(8,128)(2,1)S(1)}, u32[]{:S(2)}, u32[]{:S(2)}) collective-permute-start(bf16[128,128]{1,0:T(8,128)(2,1)S(1)} %get-tuple-element.20), channel_id=1, source_target_pairs={{0,2},{1,3},{2,0},{3,1},{4,6},{5,7},{6,4},{7,5},{8,10},{9,11},{10,... | collective-permute-start | bytes 98312 | tf_op jit(solution)/shard_map/ppermute | solution.py:191
  7.6 3.9 %collective-permute-start.2 = (bf16[128,128]{1,0:T(8,128)(2,1)S(1)}, bf16[128,128]{1,0:T(8,128)(2,1)S(1)}, u32[]{:S(2)}, u32[]{:S(2)}) collective-permute-start(bf16[128,128]{1,0:T(8,128)(2,1)S(1)} %get-tuple-element.21), channel_id=1, source_target_pairs={{0,3},{1,0},{2,1},{3,2},{4,7},{5,4},{6,5},{7,6},{8,11},{9,8},{10,9... | collective-permute-start | bytes 98312 | tf_op jit(solution)/shard_map/ppermute | solution.py:191
  11.6 4.0 %collective-permute-start.6 = (bf16[1,528,128]{2,1,0:T(8,128)(2,1)S(1)}, bf16[1,528,128]{2,1,0:T(8,128)(2,1)S(1)}, u32[]{:S(2)}, u32[]{:S(2)}) collective-permute-start(bf16[1,528,128]{2,1,0:T(8,128)(2,1)S(1)} %bitcast.9), channel_id=1, source_target_pairs={{0,4},{4,0},{8,12},{12,8},{16,20},{20,16},{24,28},{28,24},{1,5},{5... | collective-permute-start | bytes 405512 | tf_op jit(solution)/shard_map/ppermute | solution.py:199
  11.7 7.3 %collective-permute-start.5 = (bf16[1,528,128]{2,1,0:T(8,128)(2,1)S(1)}, bf16[1,528,128]{2,1,0:T(8,128)(2,1)S(1)}, u32[]{:S(2)}, u32[]{:S(2)}) collective-permute-start(bf16[1,528,128]{2,1,0:T(8,128)(2,1)S(1)} %bitcast.10), channel_id=1, source_target_pairs={{0,24},{4,28},{8,16},{12,20},{16,8},{20,12},{24,0},{28,4},{1,25},{... | collective-permute-start | bytes 405512 | tf_op jit(solution)/shard_map/ppermute | solution.py:199
  14.2 7.3 %collective-permute-start.4 = (bf16[1,528,128]{2,1,0:T(8,128)(2,1)S(1)}, bf16[1,528,128]{2,1,0:T(8,128)(2,1)S(1)}, u32[]{:S(2)}, u32[]{:S(2)}) collective-permute-start(bf16[1,528,128]{2,1,0:T(8,128)(2,1)S(1)} %bitcast.11), channel_id=1, source_target_pairs={{0,16},{4,20},{8,24},{12,28},{16,0},{20,4},{24,8},{28,12},{1,17},{... | collective-permute-start | bytes 405512 | tf_op jit(solution)/shard_map/ppermute | solution.py:199
  14.7 6.9 %collective-permute-start.3 = (bf16[1,528,128]{2,1,0:T(8,128)(2,1)S(1)}, bf16[1,528,128]{2,1,0:T(8,128)(2,1)S(1)}, u32[]{:S(2)}, u32[]{:S(2)}) collective-permute-start(bf16[1,528,128]{2,1,0:T(8,128)(2,1)S(1)} %bitcast.12), channel_id=1, source_target_pairs={{0,8},{4,12},{8,0},{12,4},{16,24},{20,28},{24,16},{28,20},{1,9},{5... | collective-permute-start | bytes 405512 | tf_op jit(solution)/shard_map/ppermute | solution.py:199
  21.6 2.8 %collective-permute-start.7 = (bf16[1,528,128]{2,1,0:T(8,128)(2,1)S(1)}, bf16[1,528,128]{2,1,0:T(8,128)(2,1)S(1)}, u32[]{:S(2)}, u32[]{:S(2)}) collective-permute-start(bf16[1,528,128]{2,1,0:T(8,128)(2,1)S(1)} %collective-permute-done.3.refs_2_), channel_id=1, source_target_pairs={{0,4},{4,0},{8,12},{12,8},{16,20},{20,16},{24,28},{28,24},{1,5},{5... | collective-permute-start | bytes 405512 | tf_op jit(solution)/shard_map/ppermute | solution.py:199
  21.6 2.8 %collective-permute-start.8 = (bf16[1,528,128]{2,1,0:T(8,128)(2,1)S(1)}, bf16[1,528,128]{2,1,0:T(8,128)(2,1)S(1)}, u32[]{:S(2)}, u32[]{:S(2)}) collective-permute-start(bf16[1,528,128]{2,1,0:T(8,128)(2,1)S(1)} %collective-permute-done.4.refs_3_), channel_id=1, source_target_pairs={{0,4},{4,0},{8,12},{12,8},{16,20},{20,16},{24,28},{28,24},{1,5},{5... | collective-permute-start | bytes 405512 | tf_op jit(solution)/shard_map/ppermute | solution.py:199
  22.1 2.3 %collective-permute-start.9 = (bf16[1,528,128]{2,1,0:T(8,128)(2,1)S(1)}, bf16[1,528,128]{2,1,0:T(8,128)(2,1)S(1)}, u32[]{:S(2)}, u32[]{:S(2)}) collective-permute-start(bf16[1,528,128]{2,1,0:T(8,128)(2,1)S(1)} %collective-permute-done.5.refs_4_), channel_id=1, source_target_pairs={{0,4},{4,0},{8,12},{12,8},{16,20},{20,16},{24,28},{28,24},{1,5},{5... | collective-permute-start | bytes 405512 | tf_op jit(solution)/shard_map/ppermute | solution.py:199

commit v7 on v6

--- a/solution.py
+++ b/solution.py
@@ -10,34 +10,23 @@
 
 MARK = 16
 SUBLANES = 8
-LANES = 256
 LOW = -1e30
 HIGH = 1e30
 MIB = 1024 * 1024
 
 
-def pack(heads_out, group, part, pieces, keys_hbm, values_hbm, *refs):
-    out_refs = refs[:pieces]
-    keys_ref, values_ref, sems = refs[pieces:]
-    copies = [
-        pltpu.make_async_copy(source, target, sems.at[i])
-        for i, (source, target) in enumerate([(keys_hbm, keys_ref), (values_hbm, values_ref)])
-    ]
-    for copy in copies:
-        copy.start()
+def pack(heads_out, group, part, pieces, rows_ref, *out_refs):
     here = lax.axis_index("head")
-    rows = keys_ref.shape[0]
+    rows = rows_ref.shape[0] // 2
     kv_heads = rows // part
     at = lax.broadcasted_iota(jnp.int32, (part, rows), 0)
     source = lax.broadcasted_iota(jnp.int32, (part, rows), 1)
     picks = [
         jnp.where(source == at * kv_heads + head, 1.0, 0.0).astype(jnp.bfloat16) for head in range(kv_heads)
     ]
-    for half, ref in enumerate((keys_ref, values_ref)):
-        copies[half].wait()
-        chosen = [
-            jnp.dot(pick, ref[...], preferred_element_type=jnp.float32).astype(jnp.bfloat16) for pick in picks
-        ]
+    for half in range(2):
+        both = rows_ref[pl.ds(half * rows, rows), :]
+        chosen = [jnp.dot(pick, both, preferred_element_type=jnp.float32).astype(jnp.bfloat16) for pick in picks]
         for shift, out_ref in enumerate(out_refs):
             kv_head = lax.rem(here + shift, pieces) * heads_out // group
             rows_out = chosen[0]
@@ -56,7 +45,7 @@
 
 def attend(pieces, part, first, last, counts, own_ref, query_ref, *refs):
     refs = list(refs)
-    state = None if first else [refs.pop(0) for _ in range(2)]
+    state = None if first else [refs.pop(0) for _ in range(3)]
     near_ref = refs.pop(0) if first else None
     far_refs = [refs.pop(0) for _ in counts]
     outs = refs
@@ -74,7 +63,7 @@
         for block in range(count):
             rows_ref = ref.at[block]
             mark = rows_ref[pl.ds(2 * block_rows, MARK), :].astype(jnp.float32)[:SUBLANES]
-            seen = jnp.concatenate([mark] * (LANES // head_width), axis=1) < own
+            seen = jnp.concatenate([mark] * (query_rows // head_width), axis=1) < own
             blocks.append((rows_ref, seen))
 
     def side(offset):
@@ -88,48 +77,41 @@
 
     keys = side(0)
     keys = jnp.concatenate([keys, keys], axis=1)
-    values = jnp.concatenate(
-        [side(1).T, jnp.ones((MARK, len(blocks) * block_rows), jnp.bfloat16)]
-    )
-    spans = [pl.ds(lane, LANES) for lane in range(0, query_rows, LANES)]
+    values = side(1).T
+    scores = jnp.dot(keys, query_ref[...], preferred_element_type=jnp.float32)
+    scores = [scores[i * block_rows : (i + 1) * block_rows] for i in range(len(blocks))]
+    tops = []
+    for i, (_, seen) in enumerate(blocks):
+        if seen is None:
+            row = lax.broadcasted_iota(jnp.int32, scores[i].shape, 0)
+            piece = lax.rem(here + pieces - row // part, pieces)
+            key_at = piece * part + row % part
+            query_at = lax.broadcasted_iota(jnp.int32, scores[i].shape, 1) // group
+            scores[i] = jnp.where(key_at <= query_at, scores[i], LOW)
+        top = jnp.max(scores[i].reshape(-1, SUBLANES, query_rows), axis=0)
+        tops.append(top if seen is None else jnp.where(seen, top, LOW))
+    high = jnp.max(functools.reduce(jnp.maximum, tops), axis=0, keepdims=True)
     if not first:
-        old = [(state[0][:, span], state[1][:, span]) for span in spans]
-
-    results = []
-    for at, span in enumerate(spans):
-        scores = jnp.dot(keys, query_ref[:, span], preferred_element_type=jnp.float32)
-        scores = [scores[i * block_rows : (i + 1) * block_rows] for i in range(len(blocks))]
-        tops = []
-        for i, (_, seen) in enumerate(blocks):
-            if seen is None:
-                row = lax.broadcasted_iota(jnp.int32, scores[i].shape, 0)
-                piece = lax.rem(here + pieces - row // part, pieces)
-                key_at = piece * part + row % part
-                query_at = (at * LANES + lax.broadcasted_iota(jnp.int32, scores[i].shape, 1)) // group
-                scores[i] = jnp.where(key_at <= query_at, scores[i], LOW)
-            top = jnp.max(scores[i].reshape(-1, SUBLANES, LANES), axis=0)
-            tops.append(top if seen is None else jnp.where(seen, top, LOW))
-        high = jnp.max(functools.reduce(jnp.maximum, tops), axis=0, keepdims=True)
-        if not first:
-            high = jnp.maximum(old[at][0], high)
-        weights = []
-        for score, (_, seen) in zip(scores, blocks):
-            base = high if seen is None else jnp.where(seen[:1], high, HIGH)
-            weights.append(jnp.exp2(score - base).astype(jnp.bfloat16))
-        accum = jnp.dot(values, jnp.concatenate(weights), preferred_element_type=jnp.float32)[
-            : head_width + SUBLANES
-        ]
-        if not first:
-            accum = accum + old[at][1] * jnp.exp2(old[at][0] - high)
-        results.append((high, accum))
-
-    for (high, accum), span in zip(results, spans):
-        if last:
-            inverse = 1.0 / accum[head_width : head_width + 1]
-            outs[0][span, :] = (accum[:head_width] * inverse).T.astype(outs[0].dtype)
-        else:
-            outs[0][:, span] = high
-            outs[1][:, span] = accum
+        old_high = state[0][...]
+        high = jnp.maximum(old_high, high)
+    weights, sums = [], []
+    for score, (_, seen) in zip(scores, blocks):
+        base = high if seen is None else jnp.where(seen[:1], high, HIGH)
+        expo = jnp.exp2(score - base)
+        sums.append(jnp.sum(expo.reshape(-1, SUBLANES, query_rows), axis=0))
+        weights.append(expo.astype(jnp.bfloat16))
+    total = jnp.sum(functools.reduce(jnp.add, sums), axis=0, keepdims=True)
+    accum = jnp.dot(values, jnp.concatenate(weights), preferred_element_type=jnp.float32)
+    if not first:
+        keep = jnp.exp2(old_high - high)
+        total = total + state[1][...] * keep
+        accum = accum + state[2][...] * keep
+    if last:
+        outs[0][...] = (accum * (1.0 / total)).astype(outs[0].dtype).T
+    else:
+        outs[0][...] = high
+        outs[1][...] = total
+        outs[2][...] = accum
 
 
 def attend_call(pieces, part, own, query, state, near, far, last):
@@ -144,9 +126,10 @@
     else:
         shapes = [
             jax.ShapeDtypeStruct((1, query_rows), jnp.float32),
-            jax.ShapeDtypeStruct((head_width + SUBLANES, query_rows), jnp.float32),
+            jax.ShapeDtypeStruct((1, query_rows), jnp.float32),
+            jax.ShapeDtypeStruct((head_width, query_rows), jnp.float32),
         ]
-        out_specs = [whole] * 2
+        out_specs = [whole] * 3
     pairs = (sum(counts) + first) * query_rows * pieces * part
     return pl.pallas_call(
         functools.partial(attend, pieces, part, first, last, counts),
@@ -181,12 +164,10 @@
     packed = pl.pallas_call(
         functools.partial(pack, heads_out, all_heads // kv_heads, part, pieces),
         out_shape=[jax.ShapeDtypeStruct((2 * part, head_width), jnp.bfloat16)] * pieces,
-        in_specs=[pl.BlockSpec(memory_space=pltpu.HBM)] * 2,
+        in_specs=[whole],
         out_specs=[whole] * pieces,
-        scratch_shapes=[pltpu.VMEM((part * kv_heads, head_width), jnp.bfloat16)] * 2
-        + [pltpu.SemaphoreType.DMA((2,))],
         compiler_params=pltpu.CompilerParams(vmem_limit_bytes=4 * MIB),
-    )(keys.reshape(part * kv_heads, head_width), values.reshape(part * kv_heads, head_width))
+    )(jnp.concatenate([keys, values]).reshape(2 * part * kv_heads, head_width))
     near = [packed[0]] + [
         lax.ppermute(packed[shift], "head", [(i, (i + shift) % pieces) for i in range(pieces)])
         for shift in range(1, pieces)

time: 27.6 us -> 24.9 us (0.902)
  Pallas kernels: 7.7 us -> 4.81 us
  local copies, waits for them, and re-layouts: 1.79 us -> 0.19 us
  other arithmetic: 0 us -> 0.95 us
  waiting for transfers between devices: 6.03 us -> 6.89 us
    pallas_call x3, Pallas kernels: 7.14 us -> 4.45 us  [attend_call(): pl.pallas_call(functools.partial(attend, pieces, part, first, last, count...]
    unnamed x10 -> x6, local copies, waits for them, and re-layouts: 1.64 us -> 0.04 us
    concatenate x0 -> x1, other arithmetic: none -> 0.95 us  [shards(): jnp.concatenate([keys, values]).reshape(2 * part * kv_heads, head_width)]
    ppermute x7, waiting for transfers between devices: 4.16 us -> 5.02 us  [swap(): return lax.ppermute(rows, 'seq', [(i, i ^ flip) for i in range(blocks)])]
  transfers between devices with their start and end apart: 10 -> 10, of which waited for: 5 -> 5; matrix products, arithmetic and copies ran while one was open for 1% -> 1% of each run, Pallas kernels for 16% -> 10%
where the time goes in v7:
time: 24.9 us; the launch traced here: 24.7 us
  starting transfers between devices  11.1 us (45%)
  waiting for transfers between devices  6.89 us (28%)
  Pallas kernels  4.81 us (19%)
  other arithmetic  0.95 us (4%)
  between operations  0.75 us (3%)
    ppermute x3, starting transfers between devices, shards(): lax.ppermute(packed[shift], 'head', [(i, (i + shift) % pieces) for i in r...  7.01 us
    ppermute x7, waiting for transfers between devices, swap(): return lax.ppermute(rows, 'seq', [(i, i ^ flip) for i in range(blocks)])  5.02 us
    pallas_call x3, Pallas kernels, attend_call(): pl.pallas_call(functools.partial(attend, pieces, part, first, last, count...  4.45 us
    ppermute x7, starting transfers between devices, swap(): return lax.ppermute(rows, 'seq', [(i, i ^ flip) for i in range(blocks)])  4.13 us
    ppermute x3, waiting for transfers between devices, shards(): lax.ppermute(packed[shift], 'head', [(i, (i + shift) % pieces) for i in r...  1.87 us
    concatenate x1, other arithmetic, shards(): jnp.concatenate([keys, values]).reshape(2 * part * kv_heads, head_width)  0.95 us
  transfers between devices with their start and end apart: 10, of which 5 were waited for; matrix products, arithmetic and copies ran while one was open for 1% of the time, Pallas kernels for 10%

profile of v7, /device:TPU:0, one launch (start us, length us, event | category | flops | bytes accessed | tf_op | source)
XLA Modules:
  0.0 24.7 jit_solution(4744668970163097700)
XLA Ops:
  0.0 0.0 copy-start
  0.0 1.0 %pad_maximum_fusion = bf16[128,2,128]{2,1,0:T(2,128)(2,1)S(1)} fusion(bf16[64,2,128]{2,1,0:T(2,128)(2,1)} %param.6, bf16[64,2,128]{2,1,0:T(2,128)(2,1)} %param.5), kind=kLoop, calls=%fused_computation | loop fusion | flops 32768 | bytes 131072 | tf_op jit(solution)/shard_map/concatenate | solution.py:170
  1.0 0.2 shard_map.47
  1.1 3.1 %collective-permute-start = (bf16[128,128]{1,0:T(8,128)(2,1)S(1)}, bf16[128,128]{1,0:T(8,128)(2,1)S(1)}, u32[]{:S(2)}, u32[]{:S(2)}) collective-permute-start(bf16[128,128]{1,0:T(8,128)(2,1)S(1)} %get-tuple-element.22), channel_id=1, source_target_pairs={{0,1},{1,2},{2,3},{3,0},{4,5},{5,6},{6,7},{7,4},{8,9},{9,10},{10,1... | collective-permute-start | bytes 98312 | tf_op jit(solution)/shard_map/ppermute | solution.py:172
  4.2 2.6 %collective-permute-start.1 = (bf16[128,128]{1,0:T(8,128)(2,1)S(1)}, bf16[128,128]{1,0:T(8,128)(2,1)S(1)}, u32[]{:S(2)}, u32[]{:S(2)}) collective-permute-start(bf16[128,128]{1,0:T(8,128)(2,1)S(1)} %get-tuple-element.23), channel_id=1, source_target_pairs={{0,2},{1,3},{2,0},{3,1},{4,6},{5,7},{6,4},{7,5},{8,10},{9,11},{10,... | collective-permute-start | bytes 98312 | tf_op jit(solution)/shard_map/ppermute | solution.py:172
  6.8 1.3 %collective-permute-start.2 = (bf16[128,128]{1,0:T(8,128)(2,1)S(1)}, bf16[128,128]{1,0:T(8,128)(2,1)S(1)}, u32[]{:S(2)}, u32[]{:S(2)}) collective-permute-start(bf16[128,128]{1,0:T(8,128)(2,1)S(1)} %get-tuple-element.24), channel_id=1, source_target_pairs={{0,3},{1,0},{2,1},{3,2},{4,7},{5,4},{6,5},{7,6},{8,11},{9,8},{10,9... | collective-permute-start | bytes 98312 | tf_op jit(solution)/shard_map/ppermute | solution.py:172
  8.8 0.0 collective-permute-done
  8.8 0.5 %collective-permute-done.1 = bf16[128,128]{1,0:T(8,128)(2,1)S(1)} collective-permute-done((bf16[128,128]{1,0:T(8,128)(2,1)S(1)}, bf16[128,128]{1,0:T(8,128)(2,1)S(1)}, u32[]{:S(2)}, u32[]{:S(2)}) %collective-permute-start.1) | collective-permute-done | bytes 32800 | tf_op jit(solution)/shard_map/ppermute | solution.py:172
  9.4 1.3 %collective-permute-done.2 = bf16[128,128]{1,0:T(8,128)(2,1)S(1)} collective-permute-done((bf16[128,128]{1,0:T(8,128)(2,1)S(1)}, bf16[128,128]{1,0:T(8,128)(2,1)S(1)}, u32[]{:S(2)}, u32[]{:S(2)}) %collective-permute-start.2) | collective-permute-done | bytes 32800 | tf_op jit(solution)/shard_map/ppermute | solution.py:172
  10.7 0.1 collective-permute-start.6
  10.8 2.5 %collective-permute-start.5 = (bf16[1,528,128]{2,1,0:T(8,128)(2,1)S(1)}, bf16[1,528,128]{2,1,0:T(8,128)(2,1)S(1)}, u32[]{:S(2)}, u32[]{:S(2)}) collective-permute-start(bf16[1,528,128]{2,1,0:T(8,128)(2,1)S(1)} %bitcast.8), channel_id=1, source_target_pairs={{0,24},{4,28},{8,16},{12,20},{16,8},{20,12},{24,0},{28,4},{1,25},{... | collective-permute-start | bytes 405512 | tf_op jit(solution)/shard_map/ppermute | solution.py:180
  13.3 0.5 %collective-permute-start.4 = (bf16[1,528,128]{2,1,0:T(8,128)(2,1)S(1)}, bf16[1,528,128]{2,1,0:T(8,128)(2,1)S(1)}, u32[]{:S(2)}, u32[]{:S(2)}) collective-permute-start(bf16[1,528,128]{2,1,0:T(8,128)(2,1)S(1)} %bitcast.9), channel_id=1, source_target_pairs={{0,16},{4,20},{8,24},{12,28},{16,0},{20,4},{24,8},{28,12},{1,17},{... | collective-permute-start | bytes 405512 | tf_op jit(solution)/shard_map/ppermute | solution.py:180
  13.8 0.5 %collective-permute-start.3 = (bf16[1,528,128]{2,1,0:T(8,128)(2,1)S(1)}, bf16[1,528,128]{2,1,0:T(8,128)(2,1)S(1)}, u32[]{:S(2)}, u32[]{:S(2)}) collective-permute-start(bf16[1,528,128]{2,1,0:T(8,128)(2,1)S(1)} %bitcast.10), channel_id=1, source_target_pairs={{0,8},{4,12},{8,0},{12,4},{16,24},{20,28},{24,16},{28,20},{1,9},{5... | collective-permute-start | bytes 405512 | tf_op jit(solution)/shard_map/ppermute | solution.py:180
  14.4 0.0 copy-done
  14.4 0.1 constant_dynamic-slice_fusion
  14.5 0.2 shard_map.46.query_ref
  14.7 0.0 collective-permute-done.6.refs_1_
  14.7 1.0 %shard_map.48 = (f32[1,1024]{1,0:T(1,128)S(1)}, f32[1,1024]{1,0:T(1,128)S(1)}, f32[128,1024]{1,0:T(8,128)S(1)}) custom-call(s32[1]{0:T(128)S(6)} %copy.9.own_ref, bf16[256,1024]{1,0:T(8,128)(2,1)S(1)} %shard_map.46.query_ref, bf16[528,128]{1,0:T(8,128)(2,1)S(1)} %constant_dynamic-update-slice_fusion.refs_0_, ...), custom_call_target="tpu_custom_call" | custom-call | flops 402653184 | bytes 2097152 | tf_op jit(solution)/shard_map/pallas_call | solution.py:134
  15.7 2.4 %collective-permute-done.5.refs_5_ = bf16[1,528,128]{2,1,0:T(8,128)(2,1)S(1)} collective-permute-done((bf16[1,528,128]{2,1,0:T(8,128)(2,1)S(1)}, bf16[1,528,128]{2,1,0:T(8,128)(2,1)S(1)}, u32[]{:S(2)}, u32[]{:S(2)}) %collective-permute-start.5) | collective-permute-done | bytes 135200 | tf_op jit(solution)/shard_map/ppermute | solution.py:180
  18.1 2.5 %collective-permute-done.4.refs_4_ = bf16[1,528,128]{2,1,0:T(8,128)(2,1)S(1)} collective-permute-done((bf16[1,528,128]{2,1,0:T(8,128)(2,1)S(1)}, bf16[1,528,128]{2,1,0:T(8,128)(2,1)S(1)}, u32[]{:S(2)}, u32[]{:S(2)}) %collective-permute-start.4) | collective-permute-done | bytes 135200 | tf_op jit(solution)/shard_map/ppermute | solution.py:180
  20.6 0.1 collective-permute-done.3.refs_3_
  20.7 0.0 collective-permute-start.7
  20.7 0.5 %collective-permute-start.8 = (bf16[1,528,128]{2,1,0:T(8,128)(2,1)S(1)}, bf16[1,528,128]{2,1,0:T(8,128)(2,1)S(1)}, u32[]{:S(2)}, u32[]{:S(2)}) collective-permute-start(bf16[1,528,128]{2,1,0:T(8,128)(2,1)S(1)} %collective-permute-done.4.refs_4_), channel_id=1, source_target_pairs={{0,4},{4,0},{8,12},{12,8},{16,20},{20,16},{24,28},{28,24},{1,5},{5... | collective-permute-start | bytes 405512 | tf_op jit(solution)/shard_map/ppermute | solution.py:180
  21.2 0.0 collective-permute-start.9
  21.2 1.4 %shard_map.49 = (f32[1,1024]{1,0:T(1,128)S(1)}, f32[1,1024]{1,0:T(1,128)S(1)}, f32[128,1024]{1,0:T(8,128)S(1)}) custom-call(s32[1]{0:T(128)S(6)} %copy.9.own_ref, bf16[256,1024]{1,0:T(8,128)(2,1)S(1)} %shard_map.46.query_ref, f32[1,1024]{1,0:T(1,128)S(1)} %get-tuple-element.28.refs_0_, f32[1,1024]{1,0:T(1,128)S(1)} %get-tuple-element.29.refs_1_, ...), custom_call_target="tpu_custom_call" | custom-call | flops 603979776 | bytes 2097152 | tf_op jit(solution)/shard_map/pallas_call | solution.py:134
  22.6 0.0 collective-permute-done.7.refs_3_
  22.6 0.0 collective-permute-done.8.refs_4_
  22.6 0.0 collective-permute-done.9.refs_5_
  22.6 2.1 %shard_map.50 = bf16[1024,128]{1,0:T(8,128)(2,1)} custom-call(s32[1]{0:T(128)S(6)} %copy.9.own_ref, bf16[256,1024]{1,0:T(8,128)(2,1)S(1)} %shard_map.46.query_ref, f32[1,1024]{1,0:T(1,128)S(1)} %get-tuple-element.34.refs_0_, f32[1,1024]{1,0:T(1,128)S(1)} %get-tuple-element.35.refs_1_, f32[128,1024]{1,0:T(8,128)S(1)} %get-tuple-element.36.refs_2_, ...), custom_call_target="tpu_custom_call" | custom-call | flops 603979776 | bytes 2097152 | tf_op jit(solution)/shard_map/pallas_call | solution.py:134
  (5 shorter events, 0.0 us)
Async XLA Ops:
  0.0 14.4 %copy-start = (bf16[256,16,128]{2,1,0:T(8,128)(2,1)S(1)}, bf16[256,16,128]{2,1,0:T(8,128)(2,1)}, u32[]{:S(2)}) copy-start(bf16[256,16,128]{2,1,0:T(8,128)(2,1)} %param.4) | copy-start | bytes 3145732
  1.1 7.7 %collective-permute-start = (bf16[128,128]{1,0:T(8,128)(2,1)S(1)}, bf16[128,128]{1,0:T(8,128)(2,1)S(1)}, u32[]{:S(2)}, u32[]{:S(2)}) collective-permute-start(bf16[128,128]{1,0:T(8,128)(2,1)S(1)} %get-tuple-element.22), channel_id=1, source_target_pairs={{0,1},{1,2},{2,3},{3,0},{4,5},{5,6},{6,7},{7,4},{8,9},{9,10},{10,1... | collective-permute-start | bytes 98312 | tf_op jit(solution)/shard_map/ppermute | solution.py:172
  4.2 5.2 %collective-permute-start.1 = (bf16[128,128]{1,0:T(8,128)(2,1)S(1)}, bf16[128,128]{1,0:T(8,128)(2,1)S(1)}, u32[]{:S(2)}, u32[]{:S(2)}) collective-permute-start(bf16[128,128]{1,0:T(8,128)(2,1)S(1)} %get-tuple-element.23), channel_id=1, source_target_pairs={{0,2},{1,3},{2,0},{3,1},{4,6},{5,7},{6,4},{7,5},{8,10},{9,11},{10,... | collective-permute-start | bytes 98312 | tf_op jit(solution)/shard_map/ppermute | solution.py:172
  6.8 3.9 %collective-permute-start.2 = (bf16[128,128]{1,0:T(8,128)(2,1)S(1)}, bf16[128,128]{1,0:T(8,128)(2,1)S(1)}, u32[]{:S(2)}, u32[]{:S(2)}) collective-permute-start(bf16[128,128]{1,0:T(8,128)(2,1)S(1)} %get-tuple-element.24), channel_id=1, source_target_pairs={{0,3},{1,0},{2,1},{3,2},{4,7},{5,4},{6,5},{7,6},{8,11},{9,8},{10,9... | collective-permute-start | bytes 98312 | tf_op jit(solution)/shard_map/ppermute | solution.py:172
  10.7 4.0 %collective-permute-start.6 = (bf16[1,528,128]{2,1,0:T(8,128)(2,1)S(1)}, bf16[1,528,128]{2,1,0:T(8,128)(2,1)S(1)}, u32[]{:S(2)}, u32[]{:S(2)}) collective-permute-start(bf16[1,528,128]{2,1,0:T(8,128)(2,1)S(1)} %bitcast.7), channel_id=1, source_target_pairs={{0,4},{4,0},{8,12},{12,8},{16,20},{20,16},{24,28},{28,24},{1,5},{5... | collective-permute-start | bytes 405512 | tf_op jit(solution)/shard_map/ppermute | solution.py:180
  10.8 7.3 %collective-permute-start.5 = (bf16[1,528,128]{2,1,0:T(8,128)(2,1)S(1)}, bf16[1,528,128]{2,1,0:T(8,128)(2,1)S(1)}, u32[]{:S(2)}, u32[]{:S(2)}) collective-permute-start(bf16[1,528,128]{2,1,0:T(8,128)(2,1)S(1)} %bitcast.8), channel_id=1, source_target_pairs={{0,24},{4,28},{8,16},{12,20},{16,8},{20,12},{24,0},{28,4},{1,25},{... | collective-permute-start | bytes 405512 | tf_op jit(solution)/shard_map/ppermute | solution.py:180
  13.3 7.3 %collective-permute-start.4 = (bf16[1,528,128]{2,1,0:T(8,128)(2,1)S(1)}, bf16[1,528,128]{2,1,0:T(8,128)(2,1)S(1)}, u32[]{:S(2)}, u32[]{:S(2)}) collective-permute-start(bf16[1,528,128]{2,1,0:T(8,128)(2,1)S(1)} %bitcast.9), channel_id=1, source_target_pairs={{0,16},{4,20},{8,24},{12,28},{16,0},{20,4},{24,8},{28,12},{1,17},{... | collective-permute-start | bytes 405512 | tf_op jit(solution)/shard_map/ppermute | solution.py:180
  13.8 6.9 %collective-permute-start.3 = (bf16[1,528,128]{2,1,0:T(8,128)(2,1)S(1)}, bf16[1,528,128]{2,1,0:T(8,128)(2,1)S(1)}, u32[]{:S(2)}, u32[]{:S(2)}) collective-permute-start(bf16[1,528,128]{2,1,0:T(8,128)(2,1)S(1)} %bitcast.10), channel_id=1, source_target_pairs={{0,8},{4,12},{8,0},{12,4},{16,24},{20,28},{24,16},{28,20},{1,9},{5... | collective-permute-start | bytes 405512 | tf_op jit(solution)/shard_map/ppermute | solution.py:180
  20.7 1.9 %collective-permute-start.7 = (bf16[1,528,128]{2,1,0:T(8,128)(2,1)S(1)}, bf16[1,528,128]{2,1,0:T(8,128)(2,1)S(1)}, u32[]{:S(2)}, u32[]{:S(2)}) collective-permute-start(bf16[1,528,128]{2,1,0:T(8,128)(2,1)S(1)} %collective-permute-done.3.refs_3_), channel_id=1, source_target_pairs={{0,4},{4,0},{8,12},{12,8},{16,20},{20,16},{24,28},{28,24},{1,5},{5... | collective-permute-start | bytes 405512 | tf_op jit(solution)/shard_map/ppermute | solution.py:180
  20.7 1.9 %collective-permute-start.8 = (bf16[1,528,128]{2,1,0:T(8,128)(2,1)S(1)}, bf16[1,528,128]{2,1,0:T(8,128)(2,1)S(1)}, u32[]{:S(2)}, u32[]{:S(2)}) collective-permute-start(bf16[1,528,128]{2,1,0:T(8,128)(2,1)S(1)} %collective-permute-done.4.refs_4_), channel_id=1, source_target_pairs={{0,4},{4,0},{8,12},{12,8},{16,20},{20,16},{24,28},{28,24},{1,5},{5... | collective-permute-start | bytes 405512 | tf_op jit(solution)/shard_map/ppermute | solution.py:180
  21.2 1.4 %collective-permute-start.9 = (bf16[1,528,128]{2,1,0:T(8,128)(2,1)S(1)}, bf16[1,528,128]{2,1,0:T(8,128)(2,1)S(1)}, u32[]{:S(2)}, u32[]{:S(2)}) collective-permute-start(bf16[1,528,128]{2,1,0:T(8,128)(2,1)S(1)} %collective-permute-done.5.refs_5_), channel_id=1, source_target_pairs={{0,4},{4,0},{8,12},{12,8},{16,20},{20,16},{24,28},{28,24},{1,5},{5... | collective-permute-start | bytes 405512 | tf_op jit(solution)/shard_map/ppermute | solution.py:180

commit v8 on v7

--- a/solution.py
+++ b/solution.py
@@ -9,10 +9,17 @@
 from jax.sharding import PartitionSpec as P
 
 MARK = 16
+COST = 0
 SUBLANES = 8
 LOW = -1e30
 HIGH = 1e30
 MIB = 1024 * 1024
+
+
+def partner(here, shift, count):
+    if count & (count - 1):
+        return (here + shift) % count, (here + count - shift) % count
+    return here ^ shift, here ^ shift
 
 
 def pack(heads_out, group, part, pieces, rows_ref, *out_refs):
@@ -28,7 +35,7 @@
         both = rows_ref[pl.ds(half * rows, rows), :]
         chosen = [jnp.dot(pick, both, preferred_element_type=jnp.float32).astype(jnp.bfloat16) for pick in picks]
         for shift, out_ref in enumerate(out_refs):
-            kv_head = lax.rem(here + shift, pieces) * heads_out // group
+            kv_head = partner(here, shift, pieces)[0] * heads_out // group
             rows_out = chosen[0]
             for head in range(1, kv_heads):
                 rows_out = jnp.where(kv_head == head, chosen[head], rows_out)
@@ -84,7 +91,7 @@
     for i, (_, seen) in enumerate(blocks):
         if seen is None:
             row = lax.broadcasted_iota(jnp.int32, scores[i].shape, 0)
-            piece = lax.rem(here + pieces - row // part, pieces)
+            piece = partner(here, row // part, pieces)[1]
             key_at = piece * part + row % part
             query_at = lax.broadcasted_iota(jnp.int32, scores[i].shape, 1) // group
             scores[i] = jnp.where(key_at <= query_at, scores[i], LOW)
@@ -130,16 +137,14 @@
             jax.ShapeDtypeStruct((head_width, query_rows), jnp.float32),
         ]
         out_specs = [whole] * 3
-    pairs = (sum(counts) + first) * query_rows * pieces * part
+    pairs = (sum(counts) + first)
     return pl.pallas_call(
         functools.partial(attend, pieces, part, first, last, counts),
         out_shape=shapes,
         in_specs=[pl.BlockSpec(memory_space=pltpu.SMEM)] + [whole] * (1 + len(operands)),
         out_specs=out_specs,
         compiler_params=pltpu.CompilerParams(vmem_limit_bytes=24 * MIB),
-        cost_estimate=pl.CostEstimate(
-            flops=6 * pairs * head_width, bytes_accessed=2 * MIB, transcendentals=pairs
-        ),
+        cost_estimate=pl.CostEstimate(flops=COST * pairs, bytes_accessed=COST * pairs, transcendentals=0),
     )(own, query, *operands)
 
 
@@ -169,7 +174,7 @@
         compiler_params=pltpu.CompilerParams(vmem_limit_bytes=4 * MIB),
     )(jnp.concatenate([keys, values]).reshape(2 * part * kv_heads, head_width))
     near = [packed[0]] + [
-        lax.ppermute(packed[shift], "head", [(i, (i + shift) % pieces) for i in range(pieces)])
+        lax.ppermute(packed[shift], "head", [(i, partner(i, shift, pieces)[0]) for i in range(pieces)])
         for shift in range(1, pieces)
     ]
     block = jnp.concatenate(near + [mark])
@@ -180,13 +185,16 @@
             return lax.ppermute(rows, "seq", [(i, i ^ flip) for i in range(blocks)])
 
         sent = block[None]
-        along_x, along_y, across = swap(sent, 2), swap(sent, 4), swap(sent, 6)
+        across, along_y, along_x = swap(sent, 6), swap(sent, 4), swap(sent, 2)
         other = swap(sent, 1)
         state = fold(None, block, [other], False)
-        along_x, along_y, across, state = lax.optimization_barrier((along_x, along_y, across, state))
-        others = [swap(rows, 1) for rows in (along_x, along_y, across)]
-        state = fold(state, None, [along_x, along_y, across], False)
-        result = fold(state, None, others, True)
+        along_x, along_y, state = lax.optimization_barrier((along_x, along_y, state))
+        others = [swap(rows, 1) for rows in (along_x, along_y)]
+        state = fold(state, None, [along_x, along_y], False)
+        across, state = lax.optimization_barrier((across, state))
+        other_across = swap(across, 1)
+        state = fold(state, None, [across] + others, False)
+        result = fold(state, None, [other_across], True)
     else:
         far = lax.all_gather(block, "seq", axis=0, tiled=False)
         unit = math.gcd(blocks, 8)

time: 24.9 us -> 27.4 us (1.10)
  waiting for transfers between devices: 6.89 us -> 10.3 us
  starting transfers between devices: 11.1 us -> 9.88 us
  Pallas kernels: 4.81 us -> 5.22 us
    ppermute x3, waiting for transfers between devices: 1.87 us -> 5.01 us  [shards(): lax.ppermute(packed[shift], 'head', [(i, partner(i, shift, pieces)[0]) fo...]
    ppermute x3, starting transfers between devices: 7.01 us -> 5.68 us  [shards(): lax.ppermute(packed[shift], 'head', [(i, partner(i, shift, pieces)[0]) fo...]
    pallas_call x3 -> x4, Pallas kernels: 4.45 us -> 4.85 us  [attend_call(): pl.pallas_call(functools.partial(attend, pieces, part, first, last, count...]
  transfers between devices with their start and end apart: 10 -> 10, of which waited for: 5 -> 4; matrix products, arithmetic and copies ran while one was open for 1% -> 1% of each run, Pallas kernels for 10% -> 13%
where the time goes in v8:
time: 27.4 us; the launch traced here: 27.3 us
  waiting for transfers between devices  10.3 us (38%)
  starting transfers between devices  9.88 us (36%)
  Pallas kernels  5.22 us (19%)
  other arithmetic  0.95 us (3%)
  between operations  0.77 us (3%)
    ppermute x3, starting transfers between devices, shards(): lax.ppermute(packed[shift], 'head', [(i, partner(i, shift, pieces)[0]) fo...  5.68 us
    ppermute x7, waiting for transfers between devices, swap(): return lax.ppermute(rows, 'seq', [(i, i ^ flip) for i in range(blocks)])  5.24 us
    ppermute x3, waiting for transfers between devices, shards(): lax.ppermute(packed[shift], 'head', [(i, partner(i, shift, pieces)[0]) fo...  5.01 us
    pallas_call x4, Pallas kernels, attend_call(): pl.pallas_call(functools.partial(attend, pieces, part, first, last, count...  4.85 us
    ppermute x7, starting transfers between devices, swap(): return lax.ppermute(rows, 'seq', [(i, i ^ flip) for i in range(blocks)])  4.2 us
    concatenate x1, other arithmetic, shards(): jnp.concatenate([keys, values]).reshape(2 * part * kv_heads, head_width)  0.95 us
  transfers between devices with their start and end apart: 10, of which 4 were waited for; matrix products, arithmetic and copies ran while one was open for 1% of the time, Pallas kernels for 13%

profile of v8, /device:TPU:0, one launch (start us, length us, event | category | flops | bytes accessed | tf_op | source)
XLA Modules:
  0.0 27.3 jit_solution(6149072221112564062)
XLA Ops:
  0.0 0.0 copy-start
  0.0 1.0 %pad_maximum_fusion = bf16[128,2,128]{2,1,0:T(2,128)(2,1)S(1)} fusion(bf16[64,2,128]{2,1,0:T(2,128)(2,1)} %param.6, bf16[64,2,128]{2,1,0:T(2,128)(2,1)} %param.5), kind=kLoop, calls=%fused_computation | loop fusion | flops 32768 | bytes 131072 | tf_op jit(solution)/shard_map/concatenate | solution.py:175
  1.0 0.2 shard_map.47
  1.1 3.1 %collective-permute-start = (bf16[128,128]{1,0:T(8,128)(2,1)S(1)}, bf16[128,128]{1,0:T(8,128)(2,1)S(1)}, u32[]{:S(2)}, u32[]{:S(2)}) collective-permute-start(bf16[128,128]{1,0:T(8,128)(2,1)S(1)} %get-tuple-element.28), channel_id=1, source_target_pairs={{0,1},{1,0},{2,3},{3,2},{4,5},{5,4},{6,7},{7,6},{8,9},{9,8},{10,11... | collective-permute-start | bytes 98312 | tf_op jit(solution)/shard_map/ppermute | solution.py:177
  4.2 2.6 %collective-permute-start.1 = (bf16[128,128]{1,0:T(8,128)(2,1)S(1)}, bf16[128,128]{1,0:T(8,128)(2,1)S(1)}, u32[]{:S(2)}, u32[]{:S(2)}) collective-permute-start(bf16[128,128]{1,0:T(8,128)(2,1)S(1)} %get-tuple-element.29), channel_id=1, source_target_pairs={{0,2},{1,3},{2,0},{3,1},{4,6},{5,7},{6,4},{7,5},{8,10},{9,11},{10,... | collective-permute-start | bytes 98312 | tf_op jit(solution)/shard_map/ppermute | solution.py:177
  6.8 0.0 collective-permute-start.2
  7.5 0.0 collective-permute-done
  7.5 2.1 %collective-permute-done.1 = bf16[128,128]{1,0:T(8,128)(2,1)S(1)} collective-permute-done((bf16[128,128]{1,0:T(8,128)(2,1)S(1)}, bf16[128,128]{1,0:T(8,128)(2,1)S(1)}, u32[]{:S(2)}, u32[]{:S(2)}) %collective-permute-start.1) | collective-permute-done | bytes 32800 | tf_op jit(solution)/shard_map/ppermute | solution.py:177
  9.6 2.9 %collective-permute-done.2 = bf16[128,128]{1,0:T(8,128)(2,1)S(1)} collective-permute-done((bf16[128,128]{1,0:T(8,128)(2,1)S(1)}, bf16[128,128]{1,0:T(8,128)(2,1)S(1)}, u32[]{:S(2)}, u32[]{:S(2)}) %collective-permute-start.2) | collective-permute-done | bytes 32800 | tf_op jit(solution)/shard_map/ppermute | solution.py:177
  12.5 0.1 collective-permute-start.6
  12.6 1.6 %collective-permute-start.4 = (bf16[1,528,128]{2,1,0:T(8,128)(2,1)S(1)}, bf16[1,528,128]{2,1,0:T(8,128)(2,1)S(1)}, u32[]{:S(2)}, u32[]{:S(2)}) collective-permute-start(bf16[1,528,128]{2,1,0:T(8,128)(2,1)S(1)} %bitcast.8), channel_id=1, source_target_pairs={{0,8},{4,12},{8,0},{12,4},{16,24},{20,28},{24,16},{28,20},{1,9},{5... | collective-permute-start | bytes 405512 | tf_op jit(solution)/shard_map/ppermute | solution.py:185
  14.2 1.5 %collective-permute-start.5 = (bf16[1,528,128]{2,1,0:T(8,128)(2,1)S(1)}, bf16[1,528,128]{2,1,0:T(8,128)(2,1)S(1)}, u32[]{:S(2)}, u32[]{:S(2)}) collective-permute-start(bf16[1,528,128]{2,1,0:T(8,128)(2,1)S(1)} %bitcast.9), channel_id=1, source_target_pairs={{0,16},{4,20},{8,24},{12,28},{16,0},{20,4},{24,8},{28,12},{1,17},{... | collective-permute-start | bytes 405512 | tf_op jit(solution)/shard_map/ppermute | solution.py:185
  15.7 0.5 %collective-permute-start.3 = (bf16[1,528,128]{2,1,0:T(8,128)(2,1)S(1)}, bf16[1,528,128]{2,1,0:T(8,128)(2,1)S(1)}, u32[]{:S(2)}, u32[]{:S(2)}) collective-permute-start(bf16[1,528,128]{2,1,0:T(8,128)(2,1)S(1)} %bitcast.10), channel_id=1, source_target_pairs={{0,24},{4,28},{8,16},{12,20},{16,8},{20,12},{24,0},{28,4},{1,25},{... | collective-permute-start | bytes 405512 | tf_op jit(solution)/shard_map/ppermute | solution.py:185
  16.2 0.0 copy-done
  16.2 0.1 constant_dynamic-slice_fusion
  16.3 0.2 shard_map.46.query_ref
  16.5 0.0 collective-permute-done.6.refs_1_
  16.5 1.0 %shard_map.48 = (f32[1,1024]{1,0:T(1,128)S(1)}, f32[1,1024]{1,0:T(1,128)S(1)}, f32[128,1024]{1,0:T(8,128)S(1)}) custom-call(s32[1]{0:T(128)S(6)} %copy.9.own_ref, bf16[256,1024]{1,0:T(8,128)(2,1)S(1)} %shard_map.46.query_ref, bf16[528,128]{1,0:T(8,128)(2,1)S(1)} %constant_dynamic-update-slice_fusion.refs_0_, ...), custom_call_target="tpu_custom_call" | custom-call | tf_op jit(solution)/shard_map/pallas_call | solution.py:141
  17.5 1.6 %collective-permute-done.4.refs_3_ = bf16[1,528,128]{2,1,0:T(8,128)(2,1)S(1)} collective-permute-done((bf16[1,528,128]{2,1,0:T(8,128)(2,1)S(1)}, bf16[1,528,128]{2,1,0:T(8,128)(2,1)S(1)}, u32[]{:S(2)}, u32[]{:S(2)}) %collective-permute-start.4) | collective-permute-done | bytes 135200 | tf_op jit(solution)/shard_map/ppermute | solution.py:185
  19.1 3.7 %collective-permute-done.5.refs_4_ = bf16[1,528,128]{2,1,0:T(8,128)(2,1)S(1)} collective-permute-done((bf16[1,528,128]{2,1,0:T(8,128)(2,1)S(1)}, bf16[1,528,128]{2,1,0:T(8,128)(2,1)S(1)}, u32[]{:S(2)}, u32[]{:S(2)}) %collective-permute-start.5) | collective-permute-done | bytes 135200 | tf_op jit(solution)/shard_map/ppermute | solution.py:185
  22.7 0.0 collective-permute-start.7
  22.7 0.5 %collective-permute-start.8 = (bf16[1,528,128]{2,1,0:T(8,128)(2,1)S(1)}, bf16[1,528,128]{2,1,0:T(8,128)(2,1)S(1)}, u32[]{:S(2)}, u32[]{:S(2)}) collective-permute-start(bf16[1,528,128]{2,1,0:T(8,128)(2,1)S(1)} %collective-permute-done.5.refs_4_), channel_id=1, source_target_pairs={{0,4},{4,0},{8,12},{12,8},{16,20},{20,16},{24,28},{28,24},{1,5},{5... | collective-permute-start | bytes 405512 | tf_op jit(solution)/shard_map/ppermute | solution.py:185
  23.2 1.0 %shard_map.49 = (f32[1,1024]{1,0:T(1,128)S(1)}, f32[1,1024]{1,0:T(1,128)S(1)}, f32[128,1024]{1,0:T(8,128)S(1)}) custom-call(s32[1]{0:T(128)S(6)} %copy.9.own_ref, bf16[256,1024]{1,0:T(8,128)(2,1)S(1)} %shard_map.46.query_ref, f32[1,1024]{1,0:T(1,128)S(1)} %get-tuple-element.34.refs_0_, f32[1,1024]{1,0:T(1,128)S(1)} %get-tuple-element.35.refs_1_, ...), custom_call_target="tpu_custom_call" | custom-call | tf_op jit(solution)/shard_map/pallas_call | solution.py:141
  24.3 0.0 collective-permute-done.3.refs_3_
  24.3 0.1 collective-permute-start.9
  24.4 0.0 collective-permute-done.7.refs_4_
  24.4 0.0 collective-permute-done.8.refs_5_
  24.4 1.4 %shard_map.50 = (f32[1,1024]{1,0:T(1,128)S(1)}, f32[1,1024]{1,0:T(1,128)S(1)}, f32[128,1024]{1,0:T(8,128)S(1)}) custom-call(s32[1]{0:T(128)S(6)} %copy.9.own_ref, bf16[256,1024]{1,0:T(8,128)(2,1)S(1)} %shard_map.46.query_ref, f32[1,1024]{1,0:T(1,128)S(1)} %get-tuple-element.42.refs_0_, f32[1,1024]{1,0:T(1,128)S(1)} %get-tuple-element.43.refs_1_, ...), custom_call_target="tpu_custom_call" | custom-call | tf_op jit(solution)/shard_map/pallas_call | solution.py:141
  25.8 0.0 collective-permute-done.9.refs_3_
  25.8 1.5 %shard_map.51 = bf16[1024,128]{1,0:T(8,128)(2,1)} custom-call(s32[1]{0:T(128)S(6)} %copy.9.own_ref, bf16[256,1024]{1,0:T(8,128)(2,1)S(1)} %shard_map.46.query_ref, f32[1,1024]{1,0:T(1,128)S(1)} %get-tuple-element.46.refs_0_, f32[1,1024]{1,0:T(1,128)S(1)} %get-tuple-element.47.refs_1_, f32[128,1024]{1,0:T(8,128)S(1)} %get-tuple-element.48.refs_2_, ...), custom_call_target="tpu_custom_call" | custom-call | tf_op jit(solution)/shard_map/pallas_call | solution.py:141
  (5 shorter events, 0.0 us)
Async XLA Ops:
  0.0 16.2 %copy-start = (bf16[256,16,128]{2,1,0:T(8,128)(2,1)S(1)}, bf16[256,16,128]{2,1,0:T(8,128)(2,1)}, u32[]{:S(2)}) copy-start(bf16[256,16,128]{2,1,0:T(8,128)(2,1)} %param.4) | copy-start | bytes 3145732
  1.1 6.3 %collective-permute-start = (bf16[128,128]{1,0:T(8,128)(2,1)S(1)}, bf16[128,128]{1,0:T(8,128)(2,1)S(1)}, u32[]{:S(2)}, u32[]{:S(2)}) collective-permute-start(bf16[128,128]{1,0:T(8,128)(2,1)S(1)} %get-tuple-element.28), channel_id=1, source_target_pairs={{0,1},{1,0},{2,3},{3,2},{4,5},{5,4},{6,7},{7,6},{8,9},{9,8},{10,11... | collective-permute-start | bytes 98312 | tf_op jit(solution)/shard_map/ppermute | solution.py:177
  4.2 5.4 %collective-permute-start.1 = (bf16[128,128]{1,0:T(8,128)(2,1)S(1)}, bf16[128,128]{1,0:T(8,128)(2,1)S(1)}, u32[]{:S(2)}, u32[]{:S(2)}) collective-permute-start(bf16[128,128]{1,0:T(8,128)(2,1)S(1)} %get-tuple-element.29), channel_id=1, source_target_pairs={{0,2},{1,3},{2,0},{3,1},{4,6},{5,7},{6,4},{7,5},{8,10},{9,11},{10,... | collective-permute-start | bytes 98312 | tf_op jit(solution)/shard_map/ppermute | solution.py:177
  6.8 5.7 %collective-permute-start.2 = (bf16[128,128]{1,0:T(8,128)(2,1)S(1)}, bf16[128,128]{1,0:T(8,128)(2,1)S(1)}, u32[]{:S(2)}, u32[]{:S(2)}) collective-permute-start(bf16[128,128]{1,0:T(8,128)(2,1)S(1)} %get-tuple-element.30), channel_id=1, source_target_pairs={{0,3},{1,2},{2,1},{3,0},{4,7},{5,6},{6,5},{7,4},{8,11},{9,10},{10,... | collective-permute-start | bytes 98312 | tf_op jit(solution)/shard_map/ppermute | solution.py:177
  12.5 4.0 %collective-permute-start.6 = (bf16[1,528,128]{2,1,0:T(8,128)(2,1)S(1)}, bf16[1,528,128]{2,1,0:T(8,128)(2,1)S(1)}, u32[]{:S(2)}, u32[]{:S(2)}) collective-permute-start(bf16[1,528,128]{2,1,0:T(8,128)(2,1)S(1)} %bitcast.7), channel_id=1, source_target_pairs={{0,4},{4,0},{8,12},{12,8},{16,20},{20,16},{24,28},{28,24},{1,5},{5... | collective-permute-start | bytes 405512 | tf_op jit(solution)/shard_map/ppermute | solution.py:185
  12.6 6.5 %collective-permute-start.4 = (bf16[1,528,128]{2,1,0:T(8,128)(2,1)S(1)}, bf16[1,528,128]{2,1,0:T(8,128)(2,1)S(1)}, u32[]{:S(2)}, u32[]{:S(2)}) collective-permute-start(bf16[1,528,128]{2,1,0:T(8,128)(2,1)S(1)} %bitcast.8), channel_id=1, source_target_pairs={{0,8},{4,12},{8,0},{12,4},{16,24},{20,28},{24,16},{28,20},{1,9},{5... | collective-permute-start | bytes 405512 | tf_op jit(solution)/shard_map/ppermute | solution.py:185
  14.2 8.6 %collective-permute-start.5 = (bf16[1,528,128]{2,1,0:T(8,128)(2,1)S(1)}, bf16[1,528,128]{2,1,0:T(8,128)(2,1)S(1)}, u32[]{:S(2)}, u32[]{:S(2)}) collective-permute-start(bf16[1,528,128]{2,1,0:T(8,128)(2,1)S(1)} %bitcast.9), channel_id=1, source_target_pairs={{0,16},{4,20},{8,24},{12,28},{16,0},{20,4},{24,8},{28,12},{1,17},{... | collective-permute-start | bytes 405512 | tf_op jit(solution)/shard_map/ppermute | solution.py:185
  15.7 8.6 %collective-permute-start.3 = (bf16[1,528,128]{2,1,0:T(8,128)(2,1)S(1)}, bf16[1,528,128]{2,1,0:T(8,128)(2,1)S(1)}, u32[]{:S(2)}, u32[]{:S(2)}) collective-permute-start(bf16[1,528,128]{2,1,0:T(8,128)(2,1)S(1)} %bitcast.10), channel_id=1, source_target_pairs={{0,24},{4,28},{8,16},{12,20},{16,8},{20,12},{24,0},{28,4},{1,25},{... | collective-permute-start | bytes 405512 | tf_op jit(solution)/shard_map/ppermute | solution.py:185
  22.7 1.7 %collective-permute-start.7 = (bf16[1,528,128]{2,1,0:T(8,128)(2,1)S(1)}, bf16[1,528,128]{2,1,0:T(8,128)(2,1)S(1)}, u32[]{:S(2)}, u32[]{:S(2)}) collective-permute-start(bf16[1,528,128]{2,1,0:T(8,128)(2,1)S(1)} %collective-permute-done.4.refs_3_), channel_id=1, source_target_pairs={{0,4},{4,0},{8,12},{12,8},{16,20},{20,16},{24,28},{28,24},{1,5},{5... | collective-permute-start | bytes 405512 | tf_op jit(solution)/shard_map/ppermute | solution.py:185
  22.7 1.7 %collective-permute-start.8 = (bf16[1,528,128]{2,1,0:T(8,128)(2,1)S(1)}, bf16[1,528,128]{2,1,0:T(8,128)(2,1)S(1)}, u32[]{:S(2)}, u32[]{:S(2)}) collective-permute-start(bf16[1,528,128]{2,1,0:T(8,128)(2,1)S(1)} %collective-permute-done.5.refs_4_), channel_id=1, source_target_pairs={{0,4},{4,0},{8,12},{12,8},{16,20},{20,16},{24,28},{28,24},{1,5},{5... | collective-permute-start | bytes 405512 | tf_op jit(solution)/shard_map/ppermute | solution.py:185
  24.3 1.5 %collective-permute-start.9 = (bf16[1,528,128]{2,1,0:T(8,128)(2,1)S(1)}, bf16[1,528,128]{2,1,0:T(8,128)(2,1)S(1)}, u32[]{:S(2)}, u32[]{:S(2)}) collective-permute-start(bf16[1,528,128]{2,1,0:T(8,128)(2,1)S(1)} %collective-permute-done.3.refs_3_), channel_id=1, source_target_pairs={{0,4},{4,0},{8,12},{12,8},{16,20},{20,16},{24,28},{28,24},{1,5},{5... | collective-permute-start | bytes 405512 | tf_op jit(solution)/shard_map/ppermute | solution.py:185

commit v9 on v8

v9 whole, which is shorter than its diff:
```python
import functools
import math

import jax
import jax.numpy as jnp
from jax import lax
from jax.experimental import pallas as pl
from jax.experimental.pallas import tpu as pltpu
from jax.sharding import PartitionSpec as P

MARK = 16
SUBLANES = 8
LOW = -1e30
HIGH = 1e30
MIB = 1024 * 1024


def partner(here, shift, count):
    if count & (count - 1):
        return (here + shift) % count, (here + count - shift) % count
    return here ^ shift, here ^ shift


def pack(copies, part, own_ref, rows_ref, *out_refs):
    kv_here = lax.axis_index("head") // copies
    rows = rows_ref.shape[0] // 2
    kv_heads = rows // part
    at = lax.broadcasted_iota(jnp.int32, (part, rows), 0)
    source = lax.broadcasted_iota(jnp.int32, (part, rows), 1)
    for shift, out_ref in enumerate(out_refs):
        kv_head = lax.rem(kv_here + shift, kv_heads)
        pick = jnp.where(source == at * kv_heads + kv_head, 1.0, 0.0).astype(jnp.bfloat16)
        for half in range(2):
            both = rows_ref[pl.ds(half * rows, rows), :]
            out_ref[pl.ds(half * part, part), :] = jnp.dot(
                pick, both, preferred_element_type=jnp.float32
            ).astype(jnp.bfloat16)
    mark_shape = (MARK, rows_ref.shape[1])
    place = jnp.full(mark_shape, own_ref[0], jnp.int32)
    out_refs[0][pl.ds(2 * part, MARK), :] = place.astype(jnp.float32).astype(jnp.bfloat16)


def scale_queries(scale, query_ref, out_ref):
    head_width = query_ref.shape[1]
    scaled = query_ref[...].astype(jnp.float32) * (scale * math.log2(math.e))
    coarse = scaled.astype(jnp.bfloat16)
    out_ref[:head_width, :] = coarse.T
    out_ref[head_width:, :] = (scaled - coarse.astype(jnp.float32)).astype(jnp.bfloat16).T


def attend(pieces, part, first, last, items, own_ref, query_ref, *refs):
    refs = list(refs)
    state = None if first else [refs.pop(0) for _ in range(3)]
    outs = [refs.pop() for _ in range(1 if last else 3)][::-1]
    head_width = query_ref.shape[0] // 2
    query_rows = query_ref.shape[1]
    group = query_rows // (pieces * part)
    here = lax.axis_index("head")
    own = own_ref[0].astype(jnp.float32)

    blocks = []
    for data, slot, offsets, shifts, mark in items:
        rows_ref = refs[data].at[slot]
        if shifts is None:
            mark_data, mark_slot, mark_at = mark
            place = refs[mark_data][mark_slot, pl.ds(mark_at, MARK), :].astype(jnp.float32)[:SUBLANES]
            seen = jnp.concatenate([place] * (query_rows // head_width), axis=1) < own
        else:
            seen = None
        blocks.append((rows_ref, offsets, shifts, seen))

    def side(half):
        return jnp.concatenate(
            [
                rows_ref[pl.ds(offset + half * part, part), :]
                for rows_ref, offsets, _, _ in blocks
                for offset in offsets
            ]
        )

    keys = side(0)
    keys = jnp.concatenate([keys, keys], axis=1)
    values = side(1).T
    scores = jnp.dot(keys, query_ref[...], preferred_element_type=jnp.float32)
    cuts, tops, at = [], [], 0
    for _, offsets, shifts, seen in blocks:
        score = scores[at : at + len(offsets) * part]
        at += len(offsets) * part
        if seen is None:
            parts = []
            for i, shift in enumerate(shifts):
                cut = score[i * part : (i + 1) * part]
                key_at = partner(here, shift, pieces)[1] * part + lax.broadcasted_iota(jnp.int32, cut.shape, 0)
                query_at = lax.broadcasted_iota(jnp.int32, cut.shape, 1) // group
                parts.append(jnp.where(key_at <= query_at, cut, LOW))
            score = jnp.concatenate(parts)
        top = jnp.max(score.reshape(-1, SUBLANES, query_rows), axis=0)
        cuts.append(score)
        tops.append(top if seen is None else jnp.where(seen, top, LOW))
    high = jnp.max(functools.reduce(jnp.maximum, tops), axis=0, keepdims=True)
    if not first:
        old_high = state[0][...]
        high = jnp.maximum(old_high, high)
    weights, sums = [], []
    for score, (_, _, _, seen) in zip(cuts, blocks):
        base = high if seen is None else jnp.where(seen[:1], high, HIGH)
        expo = jnp.exp2(score - base)
        sums.append(jnp.sum(expo.reshape(-1, SUBLANES, query_rows), axis=0))
        weights.append(expo.astype(jnp.bfloat16))
    total = jnp.sum(functools.reduce(jnp.add, sums), axis=0, keepdims=True)
    accum = jnp.dot(values, jnp.concatenate(weights), preferred_element_type=jnp.float32)
    if not first:
        keep = jnp.exp2(old_high - high)
        total = total + state[1][...] * keep
        accum = accum + state[2][...] * keep
    if last:
        outs[0][...] = (accum * (1.0 / total)).astype(outs[0].dtype).T
    else:
        outs[0][...] = high
        outs[1][...] = total
        outs[2][...] = accum


def attend_call(pieces, part, own, query, state, datas, items, last):
    head_width, query_rows = query.shape[0] // 2, query.shape[1]
    whole = pl.BlockSpec(memory_space=pltpu.VMEM)
    first = state is None
    operands = ([] if first else list(state)) + list(datas)
    if last:
        shapes = jax.ShapeDtypeStruct((query_rows, head_width), jnp.bfloat16)
        out_specs = whole
    else:
        shapes = [
            jax.ShapeDtypeStruct((1, query_rows), jnp.float32),
            jax.ShapeDtypeStruct((1, query_rows), jnp.float32),
            jax.ShapeDtypeStruct((head_width, query_rows), jnp.float32),
        ]
        out_specs = [whole] * 3
    return pl.pallas_call(
        functools.partial(attend, pieces, part, first, last, items),
        out_shape=shapes,
        in_specs=[pl.BlockSpec(memory_space=pltpu.SMEM)] + [whole] * (1 + len(operands)),
        out_specs=out_specs,
        compiler_params=pltpu.CompilerParams(vmem_limit_bytes=24 * MIB),
        cost_estimate=pl.CostEstimate(flops=0, bytes_accessed=0, transcendentals=0),
    )(own, query, *operands)


def shards(queries, keys, values, block_ids):
    rows_dev, all_heads, head_width = queries.shape
    part, kv_heads = keys.shape[:2]
    head_index = lax.axis_index("head")
    pieces = lax.axis_size("head")
    blocks = lax.axis_size("seq")
    heads_out = all_heads // pieces
    own_queries = lax.dynamic_slice_in_dim(queries, head_index * heads_out, heads_out, 1)
    own_queries = own_queries.reshape(rows_dev * heads_out, head_width)
    whole = pl.BlockSpec(memory_space=pltpu.VMEM)
    scaled = pl.pallas_call(
        functools.partial(scale_queries, head_width ** (-0.5)),
        out_shape=jax.ShapeDtypeStruct((2 * head_width, rows_dev * heads_out), jnp.bfloat16),
        in_specs=[whole],
        out_specs=whole,
        compiler_params=pltpu.CompilerParams(vmem_limit_bytes=8 * MIB),
    )(own_queries)
    copies = pieces // kv_heads
    own, *others = pl.pallas_call(
        functools.partial(pack, copies, part),
        out_shape=[
            jax.ShapeDtypeStruct((2 * part + (0 if shift else MARK), head_width), jnp.bfloat16)
            for shift in range(kv_heads)
        ],
        in_specs=[pl.BlockSpec(memory_space=pltpu.SMEM), whole],
        out_specs=[whole] * kv_heads,
        compiler_params=pltpu.CompilerParams(vmem_limit_bytes=4 * MIB),
    )(block_ids, jnp.concatenate([keys, values]).reshape(2 * part * kv_heads, head_width))
    fold = functools.partial(attend_call, pieces, part, block_ids, scaled)

    def along_z(rows, shift):
        return lax.ppermute(rows, "head", [(i, partner(i, shift, pieces)[0]) for i in range(pieces)])

    def along_seq(rows, flip, odd_flip=None):
        flips = (flip, flip if odd_flip is None else odd_flip)
        return lax.ppermute(rows, "seq", [(i, i ^ flips[i & 1]) for i in range(blocks)])

    if blocks == 8 and pieces == 4 and kv_heads == 2:
        far_z = along_z(others[0], 3)
        near = along_seq(own, 2, 4)
        next_z = along_z(others[0], 2)
        pair = jnp.stack([own, near])
        mine = jnp.concatenate([pair, along_seq(pair, 4, 2)])
        rest = jnp.concatenate([next_z, far_z])[None]
        rests = [along_seq(rest, 2, 4), along_seq(rest, 4, 2), along_seq(rest, 6)]
        twin = along_z(mine, 1)
        mine_other, rest_other = along_seq(mine, 1), along_seq(rest, 1)

        def small(data, mark, slots):
            return [(data, slot, (0,), None, (mark, slot, 2 * part)) for slot in slots]

        def large(data, mark, slot):
            return (data, 0, (0, 2 * part), None, (mark, slot, 2 * part))

        state = fold(
            None,
            [mine, rest],
            [(0, 0, (0,), (0,), None), (1, 0, (0, 2 * part), (2, 3), None)] + small(0, 0, range(1, 4)),
            False,
        )
        state = fold(state, [mine_other, rest_other], small(0, 0, range(4)) + [large(1, 0, 0)], False)
        *rests, twin, state = lax.optimization_barrier((*rests, twin, state))
        rests_other = [along_seq(rows, 1) for rows in rests]
        twin_other = along_seq(twin, 1)
        state = fold(
            state,
            [mine, twin] + rests,
            [(1, 0, (0,), (1,), None)]
            + small(1, 0, range(1, 4))
            + [large(2 + i, 0, 1 + i) for i in range(3)],
            False,
        )
        result = fold(
            state,
            [mine_other, twin_other] + rests_other,
            small(1, 0, range(4)) + [large(2 + i, 0, 1 + i) for i in range(3)],
            True,
        )
    else:
        payloads = jnp.stack([own[: 2 * part]] + others)
        kv_here = head_index // copies
        near = []
        for shift in range(pieces):
            kv_there = partner(head_index, shift, pieces)[0] // copies
            rows = lax.dynamic_index_in_dim(payloads, (kv_there - kv_here) % kv_heads, 0, keepdims=False)
            near.append(along_z(rows, shift) if shift else rows)
        block = jnp.concatenate(near + [own[2 * part :]])
        offsets = tuple(2 * part * i for i in range(pieces))
        far = lax.all_gather(block, "seq", axis=0, tiled=False)
        unit = math.gcd(blocks, 8)
        far = far.reshape((blocks // unit, unit) + block.shape)
        items = [(0, i, offsets, None, (0, i, 2 * part * pieces)) for i in range(unit)]
        state = fold(None, [block[None]], [(0, 0, offsets, tuple(range(pieces)), None)], False)
        state, _ = lax.scan(
            lambda held, rows: (tuple(fold(held, [rows], items, False)), None), tuple(state), far[:-1]
        )
        result = fold(state, [far[-1]], items, True)
    return result.reshape(rows_dev, heads_out, head_width)


def solution(mesh):
    return jax.shard_map(
        shards,
        mesh=mesh,
        in_specs=(
            P("seq", None, None),
            P(("seq", "head"), None, None),
            P(("seq", "head"), None, None),
            P("seq"),
        ),
        out_specs=P("seq", "head", None),
        check_vma=False,
    )
```

time: 27.4 us -> 25.8 us (0.942)
  waiting for transfers between devices: 10.3 us -> 5.3 us
  starting transfers between devices: 9.88 us -> 13.6 us
  Pallas kernels: 5.22 us -> 4.94 us
    ppermute x10 -> x14, waiting for transfers between devices: 10.3 us -> 5.3 us  [the longest x3 2.76 us: along_z(): lax.ppermute(rows, 'head', [(i, partner(i, shift, pieces)[0]) for i in ra...]
    ppermute x10 -> x14, starting transfers between devices: 9.88 us -> 13.6 us  [the longest x11 9.62 us: along_seq(): lax.ppermute(rows, 'seq', [(i, i ^ flips[i & 1]) for i in range(blocks)])]
    pallas_call x5, Pallas kernels: 5.02 us -> 4.75 us  [the longest x4 4.6 us: attend_call(): pl.pallas_call(functools.partial(attend, pieces, part, first, last, items...]
  transfers between devices with their start and end apart: 10 -> 14, of which waited for: 4 -> 3; matrix products, arithmetic and copies ran while one was open for 1% -> 1% of each run, Pallas kernels for 13% -> 11%
where the time goes in v9:
time: 25.8 us; the launch traced here: 25.7 us
  starting transfers between devices  13.6 us (53%)
  waiting for transfers between devices  5.3 us (21%)
  Pallas kernels  4.94 us (19%)
  other arithmetic  0.9 us (3%)
  between operations  0.85 us (3%)
    ppermute x11, starting transfers between devices, along_seq(): lax.ppermute(rows, 'seq', [(i, i ^ flips[i & 1]) for i in range(blocks)])  9.62 us
    pallas_call x4, Pallas kernels, attend_call(): pl.pallas_call(functools.partial(attend, pieces, part, first, last, items...  4.6 us
    ppermute x3, starting transfers between devices, along_z(): lax.ppermute(rows, 'head', [(i, partner(i, shift, pieces)[0]) for i in ra...  3.94 us
    ppermute x3, waiting for transfers between devices, along_z(): lax.ppermute(rows, 'head', [(i, partner(i, shift, pieces)[0]) for i in ra...  2.76 us
    ppermute x11, waiting for transfers between devices, along_seq(): lax.ppermute(rows, 'seq', [(i, i ^ flips[i & 1]) for i in range(blocks)])  2.54 us
    concatenate x1, other arithmetic, shards(): jnp.concatenate([keys, values]).reshape(2 * part * kv_heads, head_width)  0.87 us
  transfers between devices with their start and end apart: 14, of which 3 were waited for; matrix products, arithmetic and copies ran while one was open for 1% of the time, Pallas kernels for 11%

profile of v9, /device:TPU:0, one launch (start us, length us, event | category | flops | bytes accessed | tf_op | source)
XLA Modules:
  0.0 25.7 jit_solution(13030915548314456808)
XLA Ops:
  0.0 0.0 copy-start
  0.7 0.9 %pad_maximum_fusion.2 = bf16[128,2,128]{2,1,0:T(2,128)(2,1)S(1)} fusion(bf16[64,2,128]{2,1,0:T(2,128)(2,1)} %param.6, bf16[64,2,128]{2,1,0:T(2,128)(2,1)} %param.5), kind=kLoop, calls=%fused_computation.2 | loop fusion | flops 32768 | bytes 131072 | tf_op jit(solution)/shard_map/concatenate | solution.py:176
  1.6 0.1 shard_map.47
  1.8 3.0 %collective-permute-start.5 = (bf16[144,128]{1,0:T(8,128)(2,1)S(1)}, bf16[144,128]{1,0:T(8,128)(2,1)S(1)}, u32[]{:S(2)}, u32[]{:S(2)}) collective-permute-start(bf16[144,128]{1,0:T(8,128)(2,1)S(1)} %get-tuple-element.24), channel_id=1, source_target_pairs={{0,8},{4,20},{8,0},{12,28},{16,24},{20,4},{24,16},{28,12},{1,9},{5... | collective-permute-start | bytes 110600 | tf_op jit(solution)/shard_map/ppermute | solution.py:184
  4.8 2.6 %collective-permute-start = (bf16[128,128]{1,0:T(8,128)(2,1)S(1)}, bf16[128,128]{1,0:T(8,128)(2,1)S(1)}, u32[]{:S(2)}, u32[]{:S(2)}) collective-permute-start(bf16[128,128]{1,0:T(8,128)(2,1)S(1)} %get-tuple-element.23), channel_id=1, source_target_pairs={{0,2},{1,3},{2,0},{3,1},{4,6},{5,7},{6,4},{7,5},{8,10},{9,11},{10,... | collective-permute-start | bytes 98312 | tf_op jit(solution)/shard_map/ppermute | solution.py:180
  7.4 1.3 %collective-permute-start.1 = (bf16[128,128]{1,0:T(8,128)(2,1)S(1)}, bf16[128,128]{1,0:T(8,128)(2,1)S(1)}, u32[]{:S(2)}, u32[]{:S(2)}) collective-permute-start(bf16[128,128]{1,0:T(8,128)(2,1)S(1)} %get-tuple-element.23), channel_id=1, source_target_pairs={{0,3},{1,2},{2,1},{3,0},{4,7},{5,6},{6,5},{7,4},{8,11},{9,10},{10,... | collective-permute-start | bytes 98312 | tf_op jit(solution)/shard_map/ppermute | solution.py:180
  8.7 0.0 collective-permute-done.5
  8.7 1.6 %collective-permute-start.6 = (bf16[2,144,128]{2,1,0:T(8,128)(2,1)S(1)}, bf16[2,144,128]{2,1,0:T(8,128)(2,1)S(1)}, u32[]{:S(2)}, u32[]{:S(2)}) collective-permute-start(bf16[2,144,128]{2,1,0:T(8,128)(2,1)S(1)} %pad_maximum_fusion.1), channel_id=1, source_target_pairs={{0,16},{4,12},{8,24},{12,4},{16,0},{20,28},{24,8},{28,20},{1,17},{... | collective-permute-start | bytes 221192 | tf_op jit(solution)/shard_map/ppermute | solution.py:184
  10.3 0.0 collective-permute-done
  10.3 2.8 %collective-permute-done.1 = bf16[128,128]{1,0:T(8,128)(2,1)S(1)} collective-permute-done((bf16[128,128]{1,0:T(8,128)(2,1)S(1)}, bf16[128,128]{1,0:T(8,128)(2,1)S(1)}, u32[]{:S(2)}, u32[]{:S(2)}) %collective-permute-start.1) | collective-permute-done | bytes 32800 | tf_op jit(solution)/shard_map/ppermute | solution.py:180
  13.1 0.0 collective-permute-start.9
  13.1 0.1 collective-permute-done.6
  13.2 0.5 %collective-permute-start.8 = (bf16[4,144,128]{2,1,0:T(8,128)(2,1)S(1)}, bf16[4,144,128]{2,1,0:T(8,128)(2,1)S(1)}, u32[]{:S(2)}, u32[]{:S(2)}) collective-permute-start(bf16[4,144,128]{2,1,0:T(8,128)(2,1)S(1)} %pad_maximum_fusion.refs_0_.refs_3_), channel_id=1, source_target_pairs={{0,4},{4,0},{8,12},{12,8},{16,20},{20,16},{24,28},{28,24},{1,5},{5... | collective-permute-start | bytes 442376 | tf_op jit(solution)/shard_map/ppermute | solution.py:184
  13.7 0.0 collective-permute-start.7
  13.7 1.2 %collective-permute-start.2 = (bf16[1,256,128]{2,1,0:T(8,128)(2,1)S(1)}, bf16[1,256,128]{2,1,0:T(8,128)(2,1)S(1)}, u32[]{:S(2)}, u32[]{:S(2)}) collective-permute-start(bf16[1,256,128]{2,1,0:T(8,128)(2,1)S(1)} %maximum_bitcast_fusion.refs_1_), channel_id=1, source_target_pairs={{0,8},{4,20},{8,0},{12,28},{16,24},{20,4},{24,16},{28,12},{1,9},{5... | collective-permute-start | bytes 196616 | tf_op jit(solution)/shard_map/ppermute | solution.py:184
  14.9 1.6 %collective-permute-start.3 = (bf16[1,256,128]{2,1,0:T(8,128)(2,1)S(1)}, bf16[1,256,128]{2,1,0:T(8,128)(2,1)S(1)}, u32[]{:S(2)}, u32[]{:S(2)}) collective-permute-start(bf16[1,256,128]{2,1,0:T(8,128)(2,1)S(1)} %maximum_bitcast_fusion.refs_1_), channel_id=1, source_target_pairs={{0,16},{4,12},{8,24},{12,4},{16,0},{20,28},{24,8},{28,20},{1,17},{... | collective-permute-start | bytes 196616 | tf_op jit(solution)/shard_map/ppermute | solution.py:184
  16.5 0.0 collective-permute-done.9.refs_4_
  16.5 0.7 %collective-permute-start.4 = (bf16[1,256,128]{2,1,0:T(8,128)(2,1)S(1)}, bf16[1,256,128]{2,1,0:T(8,128)(2,1)S(1)}, u32[]{:S(2)}, u32[]{:S(2)}) collective-permute-start(bf16[1,256,128]{2,1,0:T(8,128)(2,1)S(1)} %maximum_bitcast_fusion.refs_1_), channel_id=1, source_target_pairs={{0,24},{4,28},{8,16},{12,20},{16,8},{20,12},{24,0},{28,4},{1,25},{... | collective-permute-start | bytes 196616 | tf_op jit(solution)/shard_map/ppermute | solution.py:184
  17.2 0.0 copy-done
  17.2 0.1 constant_dynamic-slice_fusion
  17.3 0.2 shard_map.46.query_ref
  17.5 0.8 %shard_map.48 = (f32[1,1024]{1,0:T(1,128)S(1)}, f32[1,1024]{1,0:T(1,128)S(1)}, f32[128,1024]{1,0:T(8,128)S(1)}) custom-call(s32[1]{0:T(128)S(6)} %copy.5.own_ref, bf16[256,1024]{1,0:T(8,128)(2,1)S(1)} %shard_map.46.query_ref, bf16[4,144,128]{2,1,0:T(8,128)(2,1)S(1)} %pad_maximum_fusion.refs_0_.refs_3_, bf16[1,256,128]{2,1,0:T(8,128)(2,1)S(1)} %maximum_bitcast_fusion.refs_1_), custom_call_target="tpu_custom_call" | custom-call | tf_op jit(solution)/shard_map/pallas_call | solution.py:139
  18.3 0.0 collective-permute-done.8.refs_3_
  18.3 0.8 %shard_map.49 = (f32[1,1024]{1,0:T(1,128)S(1)}, f32[1,1024]{1,0:T(1,128)S(1)}, f32[128,1024]{1,0:T(8,128)S(1)}) custom-call(s32[1]{0:T(128)S(6)} %copy.5.own_ref, bf16[256,1024]{1,0:T(8,128)(2,1)S(1)} %shard_map.46.query_ref, f32[1,1024]{1,0:T(1,128)S(1)} %get-tuple-element.25.refs_0_, f32[1,1024]{1,0:T(1,128)S(1)} %get-tuple-element.26.refs_1_, ...), custom_call_target="tpu_custom_call" | custom-call | tf_op jit(solution)/shard_map/pallas_call | solution.py:139
  19.1 0.0 collective-permute-done.2.refs_5_
  19.2 0.0 collective-permute-done.3.refs_6_
  19.2 2.5 %collective-permute-done.4.refs_7_ = bf16[1,256,128]{2,1,0:T(8,128)(2,1)S(1)} collective-permute-done((bf16[1,256,128]{2,1,0:T(8,128)(2,1)S(1)}, bf16[1,256,128]{2,1,0:T(8,128)(2,1)S(1)}, u32[]{:S(2)}, u32[]{:S(2)}) %collective-permute-start.4) | collective-permute-done | bytes 65568 | tf_op jit(solution)/shard_map/ppermute | solution.py:184
  21.6 0.0 collective-permute-done.7.refs_4_
  21.6 0.0 collective-permute-start.10
  21.6 0.5 %collective-permute-start.11 = (bf16[1,256,128]{2,1,0:T(8,128)(2,1)S(1)}, bf16[1,256,128]{2,1,0:T(8,128)(2,1)S(1)}, u32[]{:S(2)}, u32[]{:S(2)}) collective-permute-start(bf16[1,256,128]{2,1,0:T(8,128)(2,1)S(1)} %collective-permute-done.2.refs_5_), channel_id=1, source_target_pairs={{0,4},{4,0},{8,12},{12,8},{16,20},{20,16},{24,28},{28,24},{1,5},{5... | collective-permute-start | bytes 196616 | tf_op jit(solution)/shard_map/ppermute | solution.py:184
  22.1 0.0 collective-permute-start.12
  22.1 0.5 %collective-permute-start.13 = (bf16[1,256,128]{2,1,0:T(8,128)(2,1)S(1)}, bf16[1,256,128]{2,1,0:T(8,128)(2,1)S(1)}, u32[]{:S(2)}, u32[]{:S(2)}) collective-permute-start(bf16[1,256,128]{2,1,0:T(8,128)(2,1)S(1)} %collective-permute-done.4.refs_7_), channel_id=1, source_target_pairs={{0,4},{4,0},{8,12},{12,8},{16,20},{20,16},{24,28},{28,24},{1,5},{5... | collective-permute-start | bytes 196616 | tf_op jit(solution)/shard_map/ppermute | solution.py:184
  22.6 1.1 %shard_map.50 = (f32[1,1024]{1,0:T(1,128)S(1)}, f32[1,1024]{1,0:T(1,128)S(1)}, f32[128,1024]{1,0:T(8,128)S(1)}) custom-call(s32[1]{0:T(128)S(6)} %copy.5.own_ref, bf16[256,1024]{1,0:T(8,128)(2,1)S(1)} %shard_map.46.query_ref, f32[1,1024]{1,0:T(1,128)S(1)} %get-tuple-element.31.refs_0_, f32[1,1024]{1,0:T(1,128)S(1)} %get-tuple-element.32.refs_1_, ...), custom_call_target="tpu_custom_call" | custom-call | tf_op jit(solution)/shard_map/pallas_call | solution.py:139
  23.8 0.0 collective-permute-done.11.refs_5_
  23.8 0.0 collective-permute-done.12.refs_6_
  23.8 0.0 collective-permute-done.13.refs_7_
  23.8 0.0 collective-permute-done.10.refs_4_
  23.8 1.9 %shard_map.51 = bf16[1024,128]{1,0:T(8,128)(2,1)} custom-call(s32[1]{0:T(128)S(6)} %copy.5.own_ref, bf16[256,1024]{1,0:T(8,128)(2,1)S(1)} %shard_map.46.query_ref, f32[1,1024]{1,0:T(1,128)S(1)} %get-tuple-element.38.refs_0_, f32[1,1024]{1,0:T(1,128)S(1)} %get-tuple-element.39.refs_1_, f32[128,1024]{1,0:T(8,128)S(1)} %get-tuple-element.40.refs_2_, ...), custom_call_target="tpu_custom_call" | custom-call | tf_op jit(solution)/shard_map/pallas_call | solution.py:139
  (3 shorter events, 0.0 us)
Async XLA Ops:
  0.0 17.2 %copy-start = (bf16[256,16,128]{2,1,0:T(8,128)(2,1)S(1)}, bf16[256,16,128]{2,1,0:T(8,128)(2,1)}, u32[]{:S(2)}) copy-start(bf16[256,16,128]{2,1,0:T(8,128)(2,1)} %param.4) | copy-start | bytes 3145732
  1.8 6.9 %collective-permute-start.5 = (bf16[144,128]{1,0:T(8,128)(2,1)S(1)}, bf16[144,128]{1,0:T(8,128)(2,1)S(1)}, u32[]{:S(2)}, u32[]{:S(2)}) collective-permute-start(bf16[144,128]{1,0:T(8,128)(2,1)S(1)} %get-tuple-element.24), channel_id=1, source_target_pairs={{0,8},{4,20},{8,0},{12,28},{16,24},{20,4},{24,16},{28,12},{1,9},{5... | collective-permute-start | bytes 110600 | tf_op jit(solution)/shard_map/ppermute | solution.py:184
  4.8 5.5 %collective-permute-start = (bf16[128,128]{1,0:T(8,128)(2,1)S(1)}, bf16[128,128]{1,0:T(8,128)(2,1)S(1)}, u32[]{:S(2)}, u32[]{:S(2)}) collective-permute-start(bf16[128,128]{1,0:T(8,128)(2,1)S(1)} %get-tuple-element.23), channel_id=1, source_target_pairs={{0,2},{1,3},{2,0},{3,1},{4,6},{5,7},{6,4},{7,5},{8,10},{9,11},{10,... | collective-permute-start | bytes 98312 | tf_op jit(solution)/shard_map/ppermute | solution.py:180
  7.4 5.7 %collective-permute-start.1 = (bf16[128,128]{1,0:T(8,128)(2,1)S(1)}, bf16[128,128]{1,0:T(8,128)(2,1)S(1)}, u32[]{:S(2)}, u32[]{:S(2)}) collective-permute-start(bf16[128,128]{1,0:T(8,128)(2,1)S(1)} %get-tuple-element.23), channel_id=1, source_target_pairs={{0,3},{1,2},{2,1},{3,0},{4,7},{5,6},{6,5},{7,4},{8,11},{9,10},{10,... | collective-permute-start | bytes 98312 | tf_op jit(solution)/shard_map/ppermute | solution.py:180
  8.7 4.4 %collective-permute-start.6 = (bf16[2,144,128]{2,1,0:T(8,128)(2,1)S(1)}, bf16[2,144,128]{2,1,0:T(8,128)(2,1)S(1)}, u32[]{:S(2)}, u32[]{:S(2)}) collective-permute-start(bf16[2,144,128]{2,1,0:T(8,128)(2,1)S(1)} %pad_maximum_fusion.1), channel_id=1, source_target_pairs={{0,16},{4,12},{8,24},{12,4},{16,0},{20,28},{24,8},{28,20},{1,17},{... | collective-permute-start | bytes 221192 | tf_op jit(solution)/shard_map/ppermute | solution.py:184
  13.1 3.4 %collective-permute-start.9 = (bf16[1,256,128]{2,1,0:T(8,128)(2,1)S(1)}, bf16[1,256,128]{2,1,0:T(8,128)(2,1)S(1)}, u32[]{:S(2)}, u32[]{:S(2)}) collective-permute-start(bf16[1,256,128]{2,1,0:T(8,128)(2,1)S(1)} %maximum_bitcast_fusion.refs_1_), channel_id=1, source_target_pairs={{0,4},{4,0},{8,12},{12,8},{16,20},{20,16},{24,28},{28,24},{1,5},{5... | collective-permute-start | bytes 196616 | tf_op jit(solution)/shard_map/ppermute | solution.py:184
  13.2 5.2 %collective-permute-start.8 = (bf16[4,144,128]{2,1,0:T(8,128)(2,1)S(1)}, bf16[4,144,128]{2,1,0:T(8,128)(2,1)S(1)}, u32[]{:S(2)}, u32[]{:S(2)}) collective-permute-start(bf16[4,144,128]{2,1,0:T(8,128)(2,1)S(1)} %pad_maximum_fusion.refs_0_.refs_3_), channel_id=1, source_target_pairs={{0,4},{4,0},{8,12},{12,8},{16,20},{20,16},{24,28},{28,24},{1,5},{5... | collective-permute-start | bytes 442376 | tf_op jit(solution)/shard_map/ppermute | solution.py:184
  13.7 7.9 %collective-permute-start.7 = (bf16[4,144,128]{2,1,0:T(8,128)(2,1)S(1)}, bf16[4,144,128]{2,1,0:T(8,128)(2,1)S(1)}, u32[]{:S(2)}, u32[]{:S(2)}) collective-permute-start(bf16[4,144,128]{2,1,0:T(8,128)(2,1)S(1)} %pad_maximum_fusion.refs_0_.refs_3_), channel_id=1, source_target_pairs={{0,1},{1,0},{2,3},{3,2},{4,5},{5,4},{6,7},{7,6},{8,9},{9,8},{10,11... | collective-permute-start | bytes 442376 | tf_op jit(solution)/shard_map/ppermute | solution.py:180
  13.7 5.5 %collective-permute-start.2 = (bf16[1,256,128]{2,1,0:T(8,128)(2,1)S(1)}, bf16[1,256,128]{2,1,0:T(8,128)(2,1)S(1)}, u32[]{:S(2)}, u32[]{:S(2)}) collective-permute-start(bf16[1,256,128]{2,1,0:T(8,128)(2,1)S(1)} %maximum_bitcast_fusion.refs_1_), channel_id=1, source_target_pairs={{0,8},{4,20},{8,0},{12,28},{16,24},{20,4},{24,16},{28,12},{1,9},{5... | collective-permute-start | bytes 196616 | tf_op jit(solution)/shard_map/ppermute | solution.py:184
  14.9 4.3 %collective-permute-start.3 = (bf16[1,256,128]{2,1,0:T(8,128)(2,1)S(1)}, bf16[1,256,128]{2,1,0:T(8,128)(2,1)S(1)}, u32[]{:S(2)}, u32[]{:S(2)}) collective-permute-start(bf16[1,256,128]{2,1,0:T(8,128)(2,1)S(1)} %maximum_bitcast_fusion.refs_1_), channel_id=1, source_target_pairs={{0,16},{4,12},{8,24},{12,4},{16,0},{20,28},{24,8},{28,20},{1,17},{... | collective-permute-start | bytes 196616 | tf_op jit(solution)/shard_map/ppermute | solution.py:184
  16.5 5.2 %collective-permute-start.4 = (bf16[1,256,128]{2,1,0:T(8,128)(2,1)S(1)}, bf16[1,256,128]{2,1,0:T(8,128)(2,1)S(1)}, u32[]{:S(2)}, u32[]{:S(2)}) collective-permute-start(bf16[1,256,128]{2,1,0:T(8,128)(2,1)S(1)} %maximum_bitcast_fusion.refs_1_), channel_id=1, source_target_pairs={{0,24},{4,28},{8,16},{12,20},{16,8},{20,12},{24,0},{28,4},{1,25},{... | collective-permute-start | bytes 196616 | tf_op jit(solution)/shard_map/ppermute | solution.py:184
  21.6 2.2 %collective-permute-start.10 = (bf16[4,144,128]{2,1,0:T(8,128)(2,1)S(1)}, bf16[4,144,128]{2,1,0:T(8,128)(2,1)S(1)}, u32[]{:S(2)}, u32[]{:S(2)}) collective-permute-start(bf16[4,144,128]{2,1,0:T(8,128)(2,1)S(1)} %collective-permute-done.7.refs_4_), channel_id=1, source_target_pairs={{0,4},{4,0},{8,12},{12,8},{16,20},{20,16},{24,28},{28,24},{1,5},{5... | collective-permute-start | bytes 442376 | tf_op jit(solution)/shard_map/ppermute | solution.py:184
  21.6 2.2 %collective-permute-start.11 = (bf16[1,256,128]{2,1,0:T(8,128)(2,1)S(1)}, bf16[1,256,128]{2,1,0:T(8,128)(2,1)S(1)}, u32[]{:S(2)}, u32[]{:S(2)}) collective-permute-start(bf16[1,256,128]{2,1,0:T(8,128)(2,1)S(1)} %collective-permute-done.2.refs_5_), channel_id=1, source_target_pairs={{0,4},{4,0},{8,12},{12,8},{16,20},{20,16},{24,28},{28,24},{1,5},{5... | collective-permute-start | bytes 196616 | tf_op jit(solution)/shard_map/ppermute | solution.py:184
  22.1 1.7 %collective-permute-start.12 = (bf16[1,256,128]{2,1,0:T(8,128)(2,1)S(1)}, bf16[1,256,128]{2,1,0:T(8,128)(2,1)S(1)}, u32[]{:S(2)}, u32[]{:S(2)}) collective-permute-start(bf16[1,256,128]{2,1,0:T(8,128)(2,1)S(1)} %collective-permute-done.3.refs_6_), channel_id=1, source_target_pairs={{0,4},{4,0},{8,12},{12,8},{16,20},{20,16},{24,28},{28,24},{1,5},{5... | collective-permute-start | bytes 196616 | tf_op jit(solution)/shard_map/ppermute | solution.py:184
  22.1 1.7 %collective-permute-start.13 = (bf16[1,256,128]{2,1,0:T(8,128)(2,1)S(1)}, bf16[1,256,128]{2,1,0:T(8,128)(2,1)S(1)}, u32[]{:S(2)}, u32[]{:S(2)}) collective-permute-start(bf16[1,256,128]{2,1,0:T(8,128)(2,1)S(1)} %collective-permute-done.4.refs_7_), channel_id=1, source_target_pairs={{0,4},{4,0},{8,12},{12,8},{16,20},{20,16},{24,28},{28,24},{1,5},{5... | collective-permute-start | bytes 196616 | tf_op jit(solution)/shard_map/ppermute | solution.py:184

commit v10 on v9

--- a/solution.py
+++ b/solution.py
@@ -15,29 +15,26 @@
 MIB = 1024 * 1024
 
 
-def partner(here, shift, count):
-    if count & (count - 1):
-        return (here + shift) % count, (here + count - shift) % count
-    return here ^ shift, here ^ shift
-
-
-def pack(copies, part, own_ref, rows_ref, *out_refs):
-    kv_here = lax.axis_index("head") // copies
+def pack(copies, pieces, part, own_ref, rows_ref, *out_refs):
+    here = lax.axis_index("head")
     rows = rows_ref.shape[0] // 2
     kv_heads = rows // part
     at = lax.broadcasted_iota(jnp.int32, (part, rows), 0)
     source = lax.broadcasted_iota(jnp.int32, (part, rows), 1)
-    for shift, out_ref in enumerate(out_refs):
-        kv_head = lax.rem(kv_here + shift, kv_heads)
-        pick = jnp.where(source == at * kv_heads + kv_head, 1.0, 0.0).astype(jnp.bfloat16)
-        for half in range(2):
-            both = rows_ref[pl.ds(half * rows, rows), :]
-            out_ref[pl.ds(half * part, part), :] = jnp.dot(
-                pick, both, preferred_element_type=jnp.float32
-            ).astype(jnp.bfloat16)
-    mark_shape = (MARK, rows_ref.shape[1])
-    place = jnp.full(mark_shape, own_ref[0], jnp.int32)
-    out_refs[0][pl.ds(2 * part, MARK), :] = place.astype(jnp.float32).astype(jnp.bfloat16)
+    picks = [
+        jnp.where(source == at * kv_heads + head, 1.0, 0.0).astype(jnp.bfloat16) for head in range(kv_heads)
+    ]
+    for half in range(2):
+        both = rows_ref[pl.ds(half * rows, rows), :]
+        chosen = [jnp.dot(pick, both, preferred_element_type=jnp.float32).astype(jnp.bfloat16) for pick in picks]
+        for shift, out_ref in enumerate(out_refs):
+            kv_head = lax.rem(here + shift, pieces) // copies
+            rows_out = chosen[0]
+            for head in range(1, kv_heads):
+                rows_out = jnp.where(kv_head == head, chosen[head], rows_out)
+            out_ref[pl.ds(half * part, part), :] = rows_out
+    place = jnp.broadcast_to(own_ref[...].astype(jnp.float32), (MARK, rows_ref.shape[1]))
+    out_refs[0][pl.ds(2 * part, MARK), :] = place.astype(jnp.bfloat16)
 
 
 def scale_queries(scale, query_ref, out_ref):
@@ -90,7 +87,7 @@
             parts = []
             for i, shift in enumerate(shifts):
                 cut = score[i * part : (i + 1) * part]
-                key_at = partner(here, shift, pieces)[1] * part + lax.broadcasted_iota(jnp.int32, cut.shape, 0)
+                key_at = lax.rem(here + pieces - shift, pieces) * part + lax.broadcasted_iota(jnp.int32, cut.shape, 0)
                 query_at = lax.broadcasted_iota(jnp.int32, cut.shape, 1) // group
                 parts.append(jnp.where(key_at <= query_at, cut, LOW))
             score = jnp.concatenate(parts)
@@ -121,7 +118,7 @@
         outs[2][...] = accum
 
 
-def attend_call(pieces, part, own, query, state, datas, items, last):
+def attend_call(pieces, part, own, query, state, datas, items, last, cost=0):
     head_width, query_rows = query.shape[0] // 2, query.shape[1]
     whole = pl.BlockSpec(memory_space=pltpu.VMEM)
     first = state is None
@@ -142,7 +139,7 @@
         in_specs=[pl.BlockSpec(memory_space=pltpu.SMEM)] + [whole] * (1 + len(operands)),
         out_specs=out_specs,
         compiler_params=pltpu.CompilerParams(vmem_limit_bytes=24 * MIB),
-        cost_estimate=pl.CostEstimate(flops=0, bytes_accessed=0, transcendentals=0),
+        cost_estimate=pl.CostEstimate(flops=cost, bytes_accessed=0, transcendentals=0),
     )(own, query, *operands)
 
 
@@ -163,82 +160,59 @@
         out_specs=whole,
         compiler_params=pltpu.CompilerParams(vmem_limit_bytes=8 * MIB),
     )(own_queries)
-    copies = pieces // kv_heads
-    own, *others = pl.pallas_call(
-        functools.partial(pack, copies, part),
+    own, *payloads = pl.pallas_call(
+        functools.partial(pack, pieces // kv_heads, pieces, part),
         out_shape=[
             jax.ShapeDtypeStruct((2 * part + (0 if shift else MARK), head_width), jnp.bfloat16)
-            for shift in range(kv_heads)
+            for shift in range(pieces)
         ],
-        in_specs=[pl.BlockSpec(memory_space=pltpu.SMEM), whole],
-        out_specs=[whole] * kv_heads,
+        in_specs=[whole, whole],
+        out_specs=[whole] * pieces,
         compiler_params=pltpu.CompilerParams(vmem_limit_bytes=4 * MIB),
-    )(block_ids, jnp.concatenate([keys, values]).reshape(2 * part * kv_heads, head_width))
+    )(block_ids.reshape(1, 1), jnp.concatenate([keys, values]).reshape(2 * part * kv_heads, head_width))
+    near = [
+        lax.ppermute(rows, "head", [(i, (i + shift + 1) % pieces) for i in range(pieces)])
+        for shift, rows in enumerate(payloads)
+    ]
+    rest = jnp.concatenate(near)
     fold = functools.partial(attend_call, pieces, part, block_ids, scaled)
-
-    def along_z(rows, shift):
-        return lax.ppermute(rows, "head", [(i, partner(i, shift, pieces)[0]) for i in range(pieces)])
-
-    def along_seq(rows, flip, odd_flip=None):
-        flips = (flip, flip if odd_flip is None else odd_flip)
-        return lax.ppermute(rows, "seq", [(i, i ^ flips[i & 1]) for i in range(blocks)])
-
-    if blocks == 8 and pieces == 4 and kv_heads == 2:
-        far_z = along_z(others[0], 3)
-        near = along_seq(own, 2, 4)
-        next_z = along_z(others[0], 2)
-        pair = jnp.stack([own, near])
-        mine = jnp.concatenate([pair, along_seq(pair, 4, 2)])
-        rest = jnp.concatenate([next_z, far_z])[None]
-        rests = [along_seq(rest, 2, 4), along_seq(rest, 4, 2), along_seq(rest, 6)]
-        twin = along_z(mine, 1)
-        mine_other, rest_other = along_seq(mine, 1), along_seq(rest, 1)
-
-        def small(data, mark, slots):
-            return [(data, slot, (0,), None, (mark, slot, 2 * part)) for slot in slots]
+    shifts = tuple(range(pieces))
+    offsets = tuple(2 * part * i for i in range(pieces))
+
+    def swap(rows, flip):
+        return lax.ppermute(rows, "seq", [(i, i ^ flip) for i in range(blocks)])
+
+    if blocks == 8:
+        rest = rest[None]
+        mine = jnp.stack([own] + [swap(own, flip) for flip in (2, 4, 6)])
+        rests = [swap(rest, flip) for flip in (2, 4, 6)]
+
+        def small(data, slots):
+            return [(data, slot, (0,), None, (data, slot, 2 * part)) for slot in slots]
 
         def large(data, mark, slot):
-            return (data, 0, (0, 2 * part), None, (mark, slot, 2 * part))
+            return (data, 0, offsets[:-1], None, (mark, slot, 2 * part))
 
         state = fold(
             None,
             [mine, rest],
-            [(0, 0, (0,), (0,), None), (1, 0, (0, 2 * part), (2, 3), None)] + small(0, 0, range(1, 4)),
+            [(0, 0, (0,), shifts[:1], None), (1, 0, offsets[:-1], shifts[1:], None)] + small(0, range(1, 4)),
             False,
+            1000000000,
         )
-        state = fold(state, [mine_other, rest_other], small(0, 0, range(4)) + [large(1, 0, 0)], False)
-        *rests, twin, state = lax.optimization_barrier((*rests, twin, state))
-        rests_other = [along_seq(rows, 1) for rows in rests]
-        twin_other = along_seq(twin, 1)
-        state = fold(
-            state,
-            [mine, twin] + rests,
-            [(1, 0, (0,), (1,), None)]
-            + small(1, 0, range(1, 4))
-            + [large(2 + i, 0, 1 + i) for i in range(3)],
-            False,
-        )
-        result = fold(
-            state,
-            [mine_other, twin_other] + rests_other,
-            small(1, 0, range(4)) + [large(2 + i, 0, 1 + i) for i in range(3)],
-            True,
-        )
+        mine_other, rest_other = swap(mine, 1), swap(rest, 1)
+        state = fold(state, [mine_other, rest_other], small(0, range(4)) + [large(1, 0, 0)], False)
+        *rests, state = lax.optimization_barrier((*rests, state))
+        rests_other = [swap(rows, 1) for rows in rests]
+        state = fold(state, [mine] + rests, [large(i, 0, i) for i in range(1, 4)], False)
+        result = fold(state, [mine_other] + rests_other, [large(i, 0, i) for i in range(1, 4)], True)
     else:
-        payloads = jnp.stack([own[: 2 * part]] + others)
-        kv_here = head_index // copies
-        near = []
-        for shift in range(pieces):
-            kv_there = partner(head_index, shift, pieces)[0] // copies
-            rows = lax.dynamic_index_in_dim(payloads, (kv_there - kv_here) % kv_heads, 0, keepdims=False)
-            near.append(along_z(rows, shift) if shift else rows)
-        block = jnp.concatenate(near + [own[2 * part :]])
-        offsets = tuple(2 * part * i for i in range(pieces))
+        block = jnp.concatenate([own[: 2 * part], rest, own[2 * part :]])
         far = lax.all_gather(block, "seq", axis=0, tiled=False)
         unit = math.gcd(blocks, 8)
         far = far.reshape((blocks // unit, unit) + block.shape)
         items = [(0, i, offsets, None, (0, i, 2 * part * pieces)) for i in range(unit)]
-        state = fold(None, [block[None]], [(0, 0, offsets, tuple(range(pieces)), None)], False)
+        state = fold(None, [block[None]], [(0, 0, offsets, shifts, None)], False)
         state, _ = lax.scan(
             lambda held, rows: (tuple(fold(held, [rows], items, False)), None), tuple(state), far[:-1]
         )

time: 25.8 us -> 24.8 us (0.961)
  waiting for transfers between devices: 5.3 us -> 2.97 us
  starting transfers between devices: 13.6 us -> 14.7 us
    ppermute x14, waiting for transfers between devices: 5.3 us -> 2.97 us  [the longest x11 2.97 us: swap(): return lax.ppermute(rows, 'seq', [(i, i ^ flip) for i in range(blocks)])]
    ppermute x14, starting transfers between devices: 13.6 us -> 14.7 us  [the longest x11 7.7 us: swap(): return lax.ppermute(rows, 'seq', [(i, i ^ flip) for i in range(blocks)])]
  transfers between devices with their start and end apart: 14 -> 14, of which waited for: 3 -> 5; matrix products, arithmetic and copies ran while one was open for 1% -> 1% of each run, Pallas kernels for 11% -> 12%
where the time goes in v10:
time: 24.8 us; the launch traced here: 24.7 us
  starting transfers between devices  14.7 us (59%)
  Pallas kernels  5.08 us (20%)
  waiting for transfers between devices  2.97 us (12%)
  other arithmetic  0.89 us (4%)
  between operations  0.86 us (3%)
    ppermute x11, starting transfers between devices, swap(): return lax.ppermute(rows, 'seq', [(i, i ^ flip) for i in range(blocks)])  7.7 us
    ppermute x3, starting transfers between devices, shards(): lax.ppermute(rows, 'head', [(i, (i + shift + 1) % pieces) for i in range(...  7.01 us
    pallas_call x4, Pallas kernels, attend_call(): pl.pallas_call(functools.partial(attend, pieces, part, first, last, items...  4.71 us
    ppermute x11, waiting for transfers between devices, swap(): return lax.ppermute(rows, 'seq', [(i, i ^ flip) for i in range(blocks)])  2.97 us
    concatenate x1, other arithmetic, shards(): jnp.concatenate([keys, values]).reshape(2 * part * kv_heads, head_width)  0.87 us
  transfers between devices with their start and end apart: 14, of which 5 were waited for; matrix products, arithmetic and copies ran while one was open for 1% of the time, Pallas kernels for 12%

profile of v10, /device:TPU:0, one launch (start us, length us, event | category | flops | bytes accessed | tf_op | source)
XLA Modules:
  0.0 24.7 jit_solution(3583964130654065389)
XLA Ops:
  0.0 0.0 copy-start
  0.7 0.9 %pad_maximum_fusion.1 = bf16[128,2,128]{2,1,0:T(2,128)(2,1)S(1)} fusion(bf16[64,2,128]{2,1,0:T(2,128)(2,1)} %param.6, bf16[64,2,128]{2,1,0:T(2,128)(2,1)} %param.5), kind=kLoop, calls=%fused_computation.2 | loop fusion | flops 32768 | bytes 131072 | tf_op jit(solution)/shard_map/concatenate | solution.py:172
  1.6 0.2 shard_map.47
  1.8 3.1 %collective-permute-start = (bf16[128,128]{1,0:T(8,128)(2,1)S(1)}, bf16[128,128]{1,0:T(8,128)(2,1)S(1)}, u32[]{:S(2)}, u32[]{:S(2)}) collective-permute-start(bf16[128,128]{1,0:T(8,128)(2,1)S(1)} %get-tuple-element.24), channel_id=1, source_target_pairs={{0,1},{1,2},{2,3},{3,0},{4,5},{5,6},{6,7},{7,4},{8,9},{9,10},{10,1... | collective-permute-start | bytes 98312 | tf_op jit(solution)/shard_map/ppermute | solution.py:174
  4.9 2.6 %collective-permute-start.1 = (bf16[128,128]{1,0:T(8,128)(2,1)S(1)}, bf16[128,128]{1,0:T(8,128)(2,1)S(1)}, u32[]{:S(2)}, u32[]{:S(2)}) collective-permute-start(bf16[128,128]{1,0:T(8,128)(2,1)S(1)} %get-tuple-element.25), channel_id=1, source_target_pairs={{0,2},{1,3},{2,0},{3,1},{4,6},{5,7},{6,4},{7,5},{8,10},{9,11},{10,... | collective-permute-start | bytes 98312 | tf_op jit(solution)/shard_map/ppermute | solution.py:174
  7.5 1.3 %collective-permute-start.2 = (bf16[128,128]{1,0:T(8,128)(2,1)S(1)}, bf16[128,128]{1,0:T(8,128)(2,1)S(1)}, u32[]{:S(2)}, u32[]{:S(2)}) collective-permute-start(bf16[128,128]{1,0:T(8,128)(2,1)S(1)} %get-tuple-element.26), channel_id=1, source_target_pairs={{0,3},{1,0},{2,1},{3,2},{4,7},{5,4},{6,5},{7,6},{8,11},{9,8},{10,9... | collective-permute-start | bytes 98312 | tf_op jit(solution)/shard_map/ppermute | solution.py:174
  8.8 1.5 %collective-permute-start.6 = (bf16[144,128]{1,0:T(8,128)(2,1)S(1)}, bf16[144,128]{1,0:T(8,128)(2,1)S(1)}, u32[]{:S(2)}, u32[]{:S(2)}) collective-permute-start(bf16[144,128]{1,0:T(8,128)(2,1)S(1)} %get-tuple-element.27), channel_id=1, source_target_pairs={{0,8},{4,12},{8,0},{12,4},{16,24},{20,28},{24,16},{28,20},{1,9},{5... | collective-permute-start | bytes 110600 | tf_op jit(solution)/shard_map/ppermute | solution.py:183
  10.3 1.5 %collective-permute-start.7 = (bf16[144,128]{1,0:T(8,128)(2,1)S(1)}, bf16[144,128]{1,0:T(8,128)(2,1)S(1)}, u32[]{:S(2)}, u32[]{:S(2)}) collective-permute-start(bf16[144,128]{1,0:T(8,128)(2,1)S(1)} %get-tuple-element.27), channel_id=1, source_target_pairs={{0,16},{4,20},{8,24},{12,28},{16,0},{20,4},{24,8},{28,12},{1,17},{... | collective-permute-start | bytes 110600 | tf_op jit(solution)/shard_map/ppermute | solution.py:183
  11.8 0.0 collective-permute-done
  11.8 0.5 %collective-permute-start.8 = (bf16[144,128]{1,0:T(8,128)(2,1)S(1)}, bf16[144,128]{1,0:T(8,128)(2,1)S(1)}, u32[]{:S(2)}, u32[]{:S(2)}) collective-permute-start(bf16[144,128]{1,0:T(8,128)(2,1)S(1)} %get-tuple-element.27), channel_id=1, source_target_pairs={{0,24},{4,28},{8,16},{12,20},{16,8},{20,12},{24,0},{28,4},{1,25},{... | collective-permute-start | bytes 110600 | tf_op jit(solution)/shard_map/ppermute | solution.py:183
  12.3 0.0 collective-permute-done.1
  12.3 0.0 collective-permute-done.2
  12.3 0.1 collective-permute-start.10
  12.4 1.6 %collective-permute-start.3 = (bf16[1,384,128]{2,1,0:T(8,128)(2,1)S(1)}, bf16[1,384,128]{2,1,0:T(8,128)(2,1)S(1)}, u32[]{:S(2)}, u32[]{:S(2)}) collective-permute-start(bf16[1,384,128]{2,1,0:T(8,128)(2,1)S(1)} %maximum_bitcast_fusion.refs_1_), channel_id=1, source_target_pairs={{0,8},{4,12},{8,0},{12,4},{16,24},{20,28},{24,16},{28,20},{1,9},{5... | collective-permute-start | bytes 294920 | tf_op jit(solution)/shard_map/ppermute | solution.py:183
  14.0 0.0 collective-permute-done.6
  14.0 1.5 %collective-permute-start.4 = (bf16[1,384,128]{2,1,0:T(8,128)(2,1)S(1)}, bf16[1,384,128]{2,1,0:T(8,128)(2,1)S(1)}, u32[]{:S(2)}, u32[]{:S(2)}) collective-permute-start(bf16[1,384,128]{2,1,0:T(8,128)(2,1)S(1)} %maximum_bitcast_fusion.refs_1_), channel_id=1, source_target_pairs={{0,16},{4,20},{8,24},{12,28},{16,0},{20,4},{24,8},{28,12},{1,17},{... | collective-permute-start | bytes 294920 | tf_op jit(solution)/shard_map/ppermute | solution.py:183
  15.5 0.0 collective-permute-done.7
  15.5 0.5 %collective-permute-start.5 = (bf16[1,384,128]{2,1,0:T(8,128)(2,1)S(1)}, bf16[1,384,128]{2,1,0:T(8,128)(2,1)S(1)}, u32[]{:S(2)}, u32[]{:S(2)}) collective-permute-start(bf16[1,384,128]{2,1,0:T(8,128)(2,1)S(1)} %maximum_bitcast_fusion.refs_1_), channel_id=1, source_target_pairs={{0,24},{4,28},{8,16},{12,20},{16,8},{20,12},{24,0},{28,4},{1,25},{... | collective-permute-start | bytes 294920 | tf_op jit(solution)/shard_map/ppermute | solution.py:183
  16.0 0.9 %collective-permute-done.8 = bf16[144,128]{1,0:T(8,128)(2,1)S(1)} collective-permute-done((bf16[144,128]{1,0:T(8,128)(2,1)S(1)}, bf16[144,128]{1,0:T(8,128)(2,1)S(1)}, u32[]{:S(2)}, u32[]{:S(2)}) %collective-permute-start.8) | collective-permute-done | bytes 36896 | tf_op jit(solution)/shard_map/ppermute | solution.py:183
  16.9 0.1 collective-permute-start.9
  17.0 0.0 copy-done
  17.0 0.1 constant_dynamic-slice_fusion
  17.2 0.2 shard_map.46.query_ref
  17.4 0.9 %shard_map.48 = (f32[1,1024]{1,0:T(1,128)S(1)}, f32[1,1024]{1,0:T(1,128)S(1)}, f32[128,1024]{1,0:T(8,128)S(1)}) custom-call(s32[1]{0:T(128)} %copy.5.own_ref, bf16[256,1024]{1,0:T(8,128)(2,1)S(1)} %shard_map.46.query_ref, bf16[4,144,128]{2,1,0:T(8,128)(2,1)S(1)} %pad_maximum_fusion.refs_0_.refs_3_, bf16[1,384,128]{2,1,0:T(8,128)(2,1)S(1)} %maximum_bitcast_fusion.refs_1_), custom_call_target="tpu_custom_call" | custom-call | flops 1000000000 | tf_op jit(solution)/shard_map/pallas_call | solution.py:136
  18.3 0.0 collective-permute-done.10.refs_4_
  18.3 0.1 collective-permute-done.9.refs_3_
  18.4 0.9 %shard_map.49 = (f32[1,1024]{1,0:T(1,128)S(1)}, f32[1,1024]{1,0:T(1,128)S(1)}, f32[128,1024]{1,0:T(8,128)S(1)}) custom-call(s32[1]{0:T(128)} %copy.5.own_ref, bf16[256,1024]{1,0:T(8,128)(2,1)S(1)} %shard_map.46.query_ref, f32[1,1024]{1,0:T(1,128)S(1)} %get-tuple-element.28.refs_0_, f32[1,1024]{1,0:T(1,128)S(1)} %get-tuple-element.29.refs_1_, ...), custom_call_target="tpu_custom_call" | custom-call | tf_op jit(solution)/shard_map/pallas_call | solution.py:136
  19.3 0.0 collective-permute-done.3.refs_4_
  19.3 0.7 %collective-permute-done.4.refs_5_ = bf16[1,384,128]{2,1,0:T(8,128)(2,1)S(1)} collective-permute-done((bf16[1,384,128]{2,1,0:T(8,128)(2,1)S(1)}, bf16[1,384,128]{2,1,0:T(8,128)(2,1)S(1)}, u32[]{:S(2)}, u32[]{:S(2)}) %collective-permute-start.4) | collective-permute-done | bytes 98336 | tf_op jit(solution)/shard_map/ppermute | solution.py:183
  20.0 1.1 %collective-permute-done.5.refs_6_ = bf16[1,384,128]{2,1,0:T(8,128)(2,1)S(1)} collective-permute-done((bf16[1,384,128]{2,1,0:T(8,128)(2,1)S(1)}, bf16[1,384,128]{2,1,0:T(8,128)(2,1)S(1)}, u32[]{:S(2)}, u32[]{:S(2)}) %collective-permute-start.5) | collective-permute-done | bytes 98336 | tf_op jit(solution)/shard_map/ppermute | solution.py:183
  21.0 0.0 collective-permute-start.11
  21.0 0.5 %collective-permute-start.12 = (bf16[1,384,128]{2,1,0:T(8,128)(2,1)S(1)}, bf16[1,384,128]{2,1,0:T(8,128)(2,1)S(1)}, u32[]{:S(2)}, u32[]{:S(2)}) collective-permute-start(bf16[1,384,128]{2,1,0:T(8,128)(2,1)S(1)} %collective-permute-done.4.refs_5_), channel_id=1, source_target_pairs={{0,4},{4,0},{8,12},{12,8},{16,20},{20,16},{24,28},{28,24},{1,5},{5... | collective-permute-start | bytes 294920 | tf_op jit(solution)/shard_map/ppermute | solution.py:183
  21.5 0.0 collective-permute-start.13
  21.5 1.1 %shard_map.50 = (f32[1,1024]{1,0:T(1,128)S(1)}, f32[1,1024]{1,0:T(1,128)S(1)}, f32[128,1024]{1,0:T(8,128)S(1)}) custom-call(s32[1]{0:T(128)} %copy.5.own_ref, bf16[256,1024]{1,0:T(8,128)(2,1)S(1)} %shard_map.46.query_ref, f32[1,1024]{1,0:T(1,128)S(1)} %get-tuple-element.34.refs_0_, f32[1,1024]{1,0:T(1,128)S(1)} %get-tuple-element.35.refs_1_, ...), custom_call_target="tpu_custom_call" | custom-call | tf_op jit(solution)/shard_map/pallas_call | solution.py:136
  22.6 0.0 collective-permute-done.11.refs_4_
  22.6 0.0 collective-permute-done.12.refs_5_
  22.6 0.2 collective-permute-done.13.refs_6_
  22.8 1.8 %shard_map.51 = bf16[1024,128]{1,0:T(8,128)(2,1)} custom-call(s32[1]{0:T(128)} %copy.5.own_ref, bf16[256,1024]{1,0:T(8,128)(2,1)S(1)} %shard_map.46.query_ref, f32[1,1024]{1,0:T(1,128)S(1)} %get-tuple-element.40.refs_0_, f32[1,1024]{1,0:T(1,128)S(1)} %get-tuple-element.41.refs_1_, f32[128,1024]{1,0:T(8,128)S(1)} %get-tuple-element.42.refs_2_, ...), custom_call_target="tpu_custom_call" | custom-call | tf_op jit(solution)/shard_map/pallas_call | solution.py:136
  (2 shorter events, 0.0 us)
Async XLA Ops:
  0.0 17.0 %copy-start = (bf16[256,16,128]{2,1,0:T(8,128)(2,1)S(1)}, bf16[256,16,128]{2,1,0:T(8,128)(2,1)}, u32[]{:S(2)}) copy-start(bf16[256,16,128]{2,1,0:T(8,128)(2,1)} %param.4) | copy-start | bytes 3145732
  1.8 10.0 %collective-permute-start = (bf16[128,128]{1,0:T(8,128)(2,1)S(1)}, bf16[128,128]{1,0:T(8,128)(2,1)S(1)}, u32[]{:S(2)}, u32[]{:S(2)}) collective-permute-start(bf16[128,128]{1,0:T(8,128)(2,1)S(1)} %get-tuple-element.24), channel_id=1, source_target_pairs={{0,1},{1,2},{2,3},{3,0},{4,5},{5,6},{6,7},{7,4},{8,9},{9,10},{10,1... | collective-permute-start | bytes 98312 | tf_op jit(solution)/shard_map/ppermute | solution.py:174
  4.9 7.4 %collective-permute-start.1 = (bf16[128,128]{1,0:T(8,128)(2,1)S(1)}, bf16[128,128]{1,0:T(8,128)(2,1)S(1)}, u32[]{:S(2)}, u32[]{:S(2)}) collective-permute-start(bf16[128,128]{1,0:T(8,128)(2,1)S(1)} %get-tuple-element.25), channel_id=1, source_target_pairs={{0,2},{1,3},{2,0},{3,1},{4,6},{5,7},{6,4},{7,5},{8,10},{9,11},{10,... | collective-permute-start | bytes 98312 | tf_op jit(solution)/shard_map/ppermute | solution.py:174
  7.5 4.8 %collective-permute-start.2 = (bf16[128,128]{1,0:T(8,128)(2,1)S(1)}, bf16[128,128]{1,0:T(8,128)(2,1)S(1)}, u32[]{:S(2)}, u32[]{:S(2)}) collective-permute-start(bf16[128,128]{1,0:T(8,128)(2,1)S(1)} %get-tuple-element.26), channel_id=1, source_target_pairs={{0,3},{1,0},{2,1},{3,2},{4,7},{5,4},{6,5},{7,6},{8,11},{9,8},{10,9... | collective-permute-start | bytes 98312 | tf_op jit(solution)/shard_map/ppermute | solution.py:174
  8.8 5.2 %collective-permute-start.6 = (bf16[144,128]{1,0:T(8,128)(2,1)S(1)}, bf16[144,128]{1,0:T(8,128)(2,1)S(1)}, u32[]{:S(2)}, u32[]{:S(2)}) collective-permute-start(bf16[144,128]{1,0:T(8,128)(2,1)S(1)} %get-tuple-element.27), channel_id=1, source_target_pairs={{0,8},{4,12},{8,0},{12,4},{16,24},{20,28},{24,16},{28,20},{1,9},{5... | collective-permute-start | bytes 110600 | tf_op jit(solution)/shard_map/ppermute | solution.py:183
  10.3 5.2 %collective-permute-start.7 = (bf16[144,128]{1,0:T(8,128)(2,1)S(1)}, bf16[144,128]{1,0:T(8,128)(2,1)S(1)}, u32[]{:S(2)}, u32[]{:S(2)}) collective-permute-start(bf16[144,128]{1,0:T(8,128)(2,1)S(1)} %get-tuple-element.27), channel_id=1, source_target_pairs={{0,16},{4,20},{8,24},{12,28},{16,0},{20,4},{24,8},{28,12},{1,17},{... | collective-permute-start | bytes 110600 | tf_op jit(solution)/shard_map/ppermute | solution.py:183
  11.8 5.1 %collective-permute-start.8 = (bf16[144,128]{1,0:T(8,128)(2,1)S(1)}, bf16[144,128]{1,0:T(8,128)(2,1)S(1)}, u32[]{:S(2)}, u32[]{:S(2)}) collective-permute-start(bf16[144,128]{1,0:T(8,128)(2,1)S(1)} %get-tuple-element.27), channel_id=1, source_target_pairs={{0,24},{4,28},{8,16},{12,20},{16,8},{20,12},{24,0},{28,4},{1,25},{... | collective-permute-start | bytes 110600 | tf_op jit(solution)/shard_map/ppermute | solution.py:183
  12.3 5.9 %collective-permute-start.10 = (bf16[1,384,128]{2,1,0:T(8,128)(2,1)S(1)}, bf16[1,384,128]{2,1,0:T(8,128)(2,1)S(1)}, u32[]{:S(2)}, u32[]{:S(2)}) collective-permute-start(bf16[1,384,128]{2,1,0:T(8,128)(2,1)S(1)} %maximum_bitcast_fusion.refs_1_), channel_id=1, source_target_pairs={{0,4},{4,0},{8,12},{12,8},{16,20},{20,16},{24,28},{28,24},{1,5},{5... | collective-permute-start | bytes 294920 | tf_op jit(solution)/shard_map/ppermute | solution.py:183
  12.4 6.9 %collective-permute-start.3 = (bf16[1,384,128]{2,1,0:T(8,128)(2,1)S(1)}, bf16[1,384,128]{2,1,0:T(8,128)(2,1)S(1)}, u32[]{:S(2)}, u32[]{:S(2)}) collective-permute-start(bf16[1,384,128]{2,1,0:T(8,128)(2,1)S(1)} %maximum_bitcast_fusion.refs_1_), channel_id=1, source_target_pairs={{0,8},{4,12},{8,0},{12,4},{16,24},{20,28},{24,16},{28,20},{1,9},{5... | collective-permute-start | bytes 294920 | tf_op jit(solution)/shard_map/ppermute | solution.py:183
  14.0 6.0 %collective-permute-start.4 = (bf16[1,384,128]{2,1,0:T(8,128)(2,1)S(1)}, bf16[1,384,128]{2,1,0:T(8,128)(2,1)S(1)}, u32[]{:S(2)}, u32[]{:S(2)}) collective-permute-start(bf16[1,384,128]{2,1,0:T(8,128)(2,1)S(1)} %maximum_bitcast_fusion.refs_1_), channel_id=1, source_target_pairs={{0,16},{4,20},{8,24},{12,28},{16,0},{20,4},{24,8},{28,12},{1,17},{... | collective-permute-start | bytes 294920 | tf_op jit(solution)/shard_map/ppermute | solution.py:183
  15.5 5.5 %collective-permute-start.5 = (bf16[1,384,128]{2,1,0:T(8,128)(2,1)S(1)}, bf16[1,384,128]{2,1,0:T(8,128)(2,1)S(1)}, u32[]{:S(2)}, u32[]{:S(2)}) collective-permute-start(bf16[1,384,128]{2,1,0:T(8,128)(2,1)S(1)} %maximum_bitcast_fusion.refs_1_), channel_id=1, source_target_pairs={{0,24},{4,28},{8,16},{12,20},{16,8},{20,12},{24,0},{28,4},{1,25},{... | collective-permute-start | bytes 294920 | tf_op jit(solution)/shard_map/ppermute | solution.py:183
  16.9 1.4 %collective-permute-start.9 = (bf16[4,144,128]{2,1,0:T(8,128)(2,1)S(1)}, bf16[4,144,128]{2,1,0:T(8,128)(2,1)S(1)}, u32[]{:S(2)}, u32[]{:S(2)}) collective-permute-start(bf16[4,144,128]{2,1,0:T(8,128)(2,1)S(1)} %pad_maximum_fusion.refs_0_.refs_3_), channel_id=1, source_target_pairs={{0,4},{4,0},{8,12},{12,8},{16,20},{20,16},{24,28},{28,24},{1,5},{5... | collective-permute-start | bytes 442376 | tf_op jit(solution)/shard_map/ppermute | solution.py:183
  21.0 1.6 %collective-permute-start.11 = (bf16[1,384,128]{2,1,0:T(8,128)(2,1)S(1)}, bf16[1,384,128]{2,1,0:T(8,128)(2,1)S(1)}, u32[]{:S(2)}, u32[]{:S(2)}) collective-permute-start(bf16[1,384,128]{2,1,0:T(8,128)(2,1)S(1)} %collective-permute-done.3.refs_4_), channel_id=1, source_target_pairs={{0,4},{4,0},{8,12},{12,8},{16,20},{20,16},{24,28},{28,24},{1,5},{5... | collective-permute-start | bytes 294920 | tf_op jit(solution)/shard_map/ppermute | solution.py:183
  21.0 1.6 %collective-permute-start.12 = (bf16[1,384,128]{2,1,0:T(8,128)(2,1)S(1)}, bf16[1,384,128]{2,1,0:T(8,128)(2,1)S(1)}, u32[]{:S(2)}, u32[]{:S(2)}) collective-permute-start(bf16[1,384,128]{2,1,0:T(8,128)(2,1)S(1)} %collective-permute-done.4.refs_5_), channel_id=1, source_target_pairs={{0,4},{4,0},{8,12},{12,8},{16,20},{20,16},{24,28},{28,24},{1,5},{5... | collective-permute-start | bytes 294920 | tf_op jit(solution)/shard_map/ppermute | solution.py:183
  21.5 1.3 %collective-permute-start.13 = (bf16[1,384,128]{2,1,0:T(8,128)(2,1)S(1)}, bf16[1,384,128]{2,1,0:T(8,128)(2,1)S(1)}, u32[]{:S(2)}, u32[]{:S(2)}) collective-permute-start(bf16[1,384,128]{2,1,0:T(8,128)(2,1)S(1)} %collective-permute-done.5.refs_6_), channel_id=1, source_target_pairs={{0,4},{4,0},{8,12},{12,8},{16,20},{20,16},{24,28},{28,24},{1,5},{5... | collective-permute-start | bytes 294920 | tf_op jit(solution)/shard_map/ppermute | solution.py:183

commit v11 on v10

--- a/solution.py
+++ b/solution.py
@@ -15,7 +15,13 @@
 MIB = 1024 * 1024
 
 
-def pack(copies, pieces, part, own_ref, rows_ref, *out_refs):
+def partner(here, shift, count):
+    if count & (count - 1):
+        return (here + shift) % count, (here + count - shift) % count
+    return here ^ shift, here ^ shift
+
+
+def pack(copies, pieces, part, rows_ref, *out_refs):
     here = lax.axis_index("head")
     rows = rows_ref.shape[0] // 2
     kv_heads = rows // part
@@ -28,13 +34,11 @@
         both = rows_ref[pl.ds(half * rows, rows), :]
         chosen = [jnp.dot(pick, both, preferred_element_type=jnp.float32).astype(jnp.bfloat16) for pick in picks]
         for shift, out_ref in enumerate(out_refs):
-            kv_head = lax.rem(here + shift, pieces) // copies
+            kv_head = partner(here, shift, pieces)[0] // copies
             rows_out = chosen[0]
             for head in range(1, kv_heads):
                 rows_out = jnp.where(kv_head == head, chosen[head], rows_out)
             out_ref[pl.ds(half * part, part), :] = rows_out
-    place = jnp.broadcast_to(own_ref[...].astype(jnp.float32), (MARK, rows_ref.shape[1]))
-    out_refs[0][pl.ds(2 * part, MARK), :] = place.astype(jnp.bfloat16)
 
 
 def scale_queries(scale, query_ref, out_ref):
@@ -87,7 +91,7 @@
             parts = []
             for i, shift in enumerate(shifts):
                 cut = score[i * part : (i + 1) * part]
-                key_at = lax.rem(here + pieces - shift, pieces) * part + lax.broadcasted_iota(jnp.int32, cut.shape, 0)
+                key_at = partner(here, shift, pieces)[1] * part + lax.broadcasted_iota(jnp.int32, cut.shape, 0)
                 query_at = lax.broadcasted_iota(jnp.int32, cut.shape, 1) // group
                 parts.append(jnp.where(key_at <= query_at, cut, LOW))
             score = jnp.concatenate(parts)
@@ -160,63 +164,73 @@
         out_specs=whole,
         compiler_params=pltpu.CompilerParams(vmem_limit_bytes=8 * MIB),
     )(own_queries)
-    own, *payloads = pl.pallas_call(
+    payloads = pl.pallas_call(
         functools.partial(pack, pieces // kv_heads, pieces, part),
-        out_shape=[
-            jax.ShapeDtypeStruct((2 * part + (0 if shift else MARK), head_width), jnp.bfloat16)
-            for shift in range(pieces)
-        ],
-        in_specs=[whole, whole],
+        out_shape=[jax.ShapeDtypeStruct((2 * part, head_width), jnp.bfloat16)] * pieces,
+        in_specs=[whole],
         out_specs=[whole] * pieces,
         compiler_params=pltpu.CompilerParams(vmem_limit_bytes=4 * MIB),
-    )(block_ids.reshape(1, 1), jnp.concatenate([keys, values]).reshape(2 * part * kv_heads, head_width))
-    near = [
-        lax.ppermute(rows, "head", [(i, (i + shift + 1) % pieces) for i in range(pieces)])
-        for shift, rows in enumerate(payloads)
-    ]
-    rest = jnp.concatenate(near)
+    )(jnp.concatenate([keys, values]).reshape(2 * part * kv_heads, head_width))
+    mark = jnp.broadcast_to(block_ids.astype(jnp.bfloat16)[:, None], (MARK, head_width))
+    near = [payloads[0]] + [
+        lax.ppermute(payloads[shift], "head", [(i, partner(i, shift, pieces)[0]) for i in range(pieces)])
+        for shift in range(pieces - 1, 0, -1)
+    ][::-1]
     fold = functools.partial(attend_call, pieces, part, block_ids, scaled)
-    shifts = tuple(range(pieces))
-    offsets = tuple(2 * part * i for i in range(pieces))
-
-    def swap(rows, flip):
-        return lax.ppermute(rows, "seq", [(i, i ^ flip) for i in range(blocks)])
-
-    if blocks == 8:
-        rest = rest[None]
-        mine = jnp.stack([own] + [swap(own, flip) for flip in (2, 4, 6)])
-        rests = [swap(rest, flip) for flip in (2, 4, 6)]
+    step = 2 * part
+
+    def hop(rows, flip, odd_flip=None):
+        flips = (flip, flip if odd_flip is None else odd_flip)
+        return lax.ppermute(rows, "seq", [(i, i ^ flips[i & 1]) for i in range(blocks)])
+
+    if blocks == 8 and pieces == 4:
+        early = jnp.concatenate([near[0], mark])[None]
+        early_pair = jnp.concatenate([early, hop(early, 2, 4)])
+        early_far = hop(early_pair, 4, 2)
+        late = jnp.concatenate(near[1:])[None]
+        late_next = hop(late, 2, 4)
+        early_all = jnp.concatenate([early_pair, early_far])
+        late_far = hop(jnp.concatenate([late, late_next]), 4, 2)
 
         def small(data, slots):
-            return [(data, slot, (0,), None, (data, slot, 2 * part)) for slot in slots]
-
-        def large(data, mark, slot):
-            return (data, 0, offsets[:-1], None, (mark, slot, 2 * part))
+            return [(data, slot, (0,), None, (data, slot, step)) for slot in slots]
+
+        def large(data, mark_data, slots, base=0):
+            return [
+                (data, slot - base, (0, step, 2 * step), None, (mark_data, slot, step)) for slot in slots
+            ]
 
         state = fold(
             None,
-            [mine, rest],
-            [(0, 0, (0,), shifts[:1], None), (1, 0, offsets[:-1], shifts[1:], None)] + small(0, range(1, 4)),
+            [early_all, late],
+            [(0, 0, (0,), (0,), None), (1, 0, (0, step, 2 * step), (1, 2, 3), None)] + small(0, range(1, 4)),
             False,
-            1000000000,
-        )
-        mine_other, rest_other = swap(mine, 1), swap(rest, 1)
-        state = fold(state, [mine_other, rest_other], small(0, range(4)) + [large(1, 0, 0)], False)
-        *rests, state = lax.optimization_barrier((*rests, state))
-        rests_other = [swap(rows, 1) for rows in rests]
-        state = fold(state, [mine] + rests, [large(i, 0, i) for i in range(1, 4)], False)
-        result = fold(state, [mine_other] + rests_other, [large(i, 0, i) for i in range(1, 4)], True)
+        )
+        early_other, late_other = hop(early_all, 1), hop(late, 1)
+        state = fold(state, [early_other, late_other], small(0, range(4)) + large(1, 0, [0]), False)
+        late_next_other = hop(late_next, 1)
+        state = fold(
+            state,
+            [early_all, early_other, late_next, late_next_other],
+            large(2, 0, [1], 1) + large(3, 1, [1], 1),
+            False,
+        )
+        late_far, state = lax.optimization_barrier((late_far, state))
+        late_far_other = hop(late_far, 1)
+        state = fold(state, [early_all, late_far], large(1, 0, [2, 3], 2), False)
+        result = fold(state, [early_other, late_far_other], large(1, 0, [2, 3], 2), True)
     else:
-        block = jnp.concatenate([own[: 2 * part], rest, own[2 * part :]])
+        block = jnp.concatenate(near + [mark])
+        offsets = tuple(step * i for i in range(pieces))
         far = lax.all_gather(block, "seq", axis=0, tiled=False)
         unit = math.gcd(blocks, 8)
         far = far.reshape((blocks // unit, unit) + block.shape)
-        items = [(0, i, offsets, None, (0, i, 2 * part * pieces)) for i in range(unit)]
-        state = fold(None, [block[None]], [(0, 0, offsets, shifts, None)], False)
+        each = [(0, i, offsets, None, (0, i, step * pieces)) for i in range(unit)]
+        state = fold(None, [block[None]], [(0, 0, offsets, tuple(range(pieces)), None)], False)
         state, _ = lax.scan(
-            lambda held, rows: (tuple(fold(held, [rows], items, False)), None), tuple(state), far[:-1]
-        )
-        result = fold(state, [far[-1]], items, True)
+            lambda held, rows: (tuple(fold(held, [rows], each, False)), None), tuple(state), far[:-1]
+        )
+        result = fold(state, [far[-1]], each, True)
     return result.reshape(rows_dev, heads_out, head_width)
 
 

time: 24.8 us -> 26.4 us (1.065)
  waiting for transfers between devices: 2.97 us -> 6.02 us
  starting transfers between devices: 14.7 us -> 12.9 us
  Pallas kernels: 5.08 us -> 5.42 us
    ppermute x14 -> x11, waiting for transfers between devices: 2.97 us -> 6.02 us  [the longest x3 3.26 us: shards(): lax.ppermute(payloads[shift], 'head', [(i, partner(i, shift, pieces)[0])...]
    ppermute x14 -> x11, starting transfers between devices: 14.7 us -> 12.9 us  [the longest x8 7.23 us: hop(): lax.ppermute(rows, 'seq', [(i, i ^ flips[i & 1]) for i in range(blocks)])]
    pallas_call x4 -> x5, Pallas kernels: 4.71 us -> 5.06 us  [attend_call(): pl.pallas_call(functools.partial(attend, pieces, part, first, last, items...]
  transfers between devices with their start and end apart: 14 -> 11, of which waited for: 5 -> 5; matrix products, arithmetic and copies ran while one was open for 1% -> 1% of each run, Pallas kernels for 12% -> 14%
where the time goes in v11:
time: 26.4 us; the launch traced here: 26.3 us
  starting transfers between devices  12.9 us (49%)
  waiting for transfers between devices  6.02 us (23%)
  Pallas kernels  5.42 us (21%)
  other arithmetic  1.01 us (4%)
  between operations  0.77 us (3%)
    ppermute x8, starting transfers between devices, hop(): lax.ppermute(rows, 'seq', [(i, i ^ flips[i & 1]) for i in range(blocks)])  7.23 us
    ppermute x3, starting transfers between devices, shards(): lax.ppermute(payloads[shift], 'head', [(i, partner(i, shift, pieces)[0])...  5.68 us
    pallas_call x5, Pallas kernels, attend_call(): pl.pallas_call(functools.partial(attend, pieces, part, first, last, items...  5.06 us
    ppermute x3, waiting for transfers between devices, shards(): lax.ppermute(payloads[shift], 'head', [(i, partner(i, shift, pieces)[0])...  3.26 us
    ppermute x8, waiting for transfers between devices, hop(): lax.ppermute(rows, 'seq', [(i, i ^ flips[i & 1]) for i in range(blocks)])  2.76 us
    concatenate x1, other arithmetic, shards(): jnp.concatenate([keys, values]).reshape(2 * part * kv_heads, head_width)  0.95 us
  transfers between devices with their start and end apart: 11, of which 5 were waited for; matrix products, arithmetic and copies ran while one was open for 1% of the time, Pallas kernels for 14%

profile of v11, /device:TPU:0, one launch (start us, length us, event | category | flops | bytes accessed | tf_op | source)
XLA Modules:
  0.0 26.3 jit_solution(4723845557104154502)
XLA Ops:
  0.0 0.0 copy-start
  0.0 1.0 %pad_maximum_fusion.3 = bf16[128,2,128]{2,1,0:T(2,128)(2,1)S(1)} fusion(bf16[64,2,128]{2,1,0:T(2,128)(2,1)} %param.6, bf16[64,2,128]{2,1,0:T(2,128)(2,1)} %param.5), kind=kLoop, calls=%fused_computation.4 | loop fusion | flops 32768 | bytes 131072 | tf_op jit(solution)/shard_map/concatenate | solution.py:173
  1.0 0.2 shard_map.47
  1.1 3.1 %collective-permute-start = (bf16[128,128]{1,0:T(8,128)(2,1)S(1)}, bf16[128,128]{1,0:T(8,128)(2,1)S(1)}, u32[]{:S(2)}, u32[]{:S(2)}) collective-permute-start(bf16[128,128]{1,0:T(8,128)(2,1)S(1)} %get-tuple-element.25), channel_id=1, source_target_pairs={{0,1},{1,0},{2,3},{3,2},{4,5},{5,4},{6,7},{7,6},{8,9},{9,8},{10,11... | collective-permute-start | bytes 98312 | tf_op jit(solution)/shard_map/ppermute | solution.py:176
  4.2 2.6 %collective-permute-start.1 = (bf16[128,128]{1,0:T(8,128)(2,1)S(1)}, bf16[128,128]{1,0:T(8,128)(2,1)S(1)}, u32[]{:S(2)}, u32[]{:S(2)}) collective-permute-start(bf16[128,128]{1,0:T(8,128)(2,1)S(1)} %get-tuple-element.26), channel_id=1, source_target_pairs={{0,2},{1,3},{2,0},{3,1},{4,6},{5,7},{6,4},{7,5},{8,10},{9,11},{10,... | collective-permute-start | bytes 98312 | tf_op jit(solution)/shard_map/ppermute | solution.py:176
  6.8 0.0 collective-permute-start.2
  7.5 1.8 %collective-permute-start.5 = (bf16[1,144,128]{2,1,0:T(8,128)(2,1)S(1)}, bf16[1,144,128]{2,1,0:T(8,128)(2,1)S(1)}, u32[]{:S(2)}, u32[]{:S(2)}) collective-permute-start(bf16[1,144,128]{2,1,0:T(8,128)(2,1)S(1)} %pad_bitcast_fusion), channel_id=1, source_target_pairs={{0,8},{4,20},{8,0},{12,28},{16,24},{20,4},{24,16},{28,12},{1,9},{5... | collective-permute-start | bytes 110600 | tf_op jit(solution)/shard_map/ppermute | solution.py:184
  9.3 0.0 collective-permute-done
  9.3 0.4 %collective-permute-done.1 = bf16[128,128]{1,0:T(8,128)(2,1)S(1)} collective-permute-done((bf16[128,128]{1,0:T(8,128)(2,1)S(1)}, bf16[128,128]{1,0:T(8,128)(2,1)S(1)}, u32[]{:S(2)}, u32[]{:S(2)}) %collective-permute-start.1) | collective-permute-done | bytes 32800 | tf_op jit(solution)/shard_map/ppermute | solution.py:176
  9.6 2.9 %collective-permute-done.2 = bf16[128,128]{1,0:T(8,128)(2,1)S(1)} collective-permute-done((bf16[128,128]{1,0:T(8,128)(2,1)S(1)}, bf16[128,128]{1,0:T(8,128)(2,1)S(1)}, u32[]{:S(2)}, u32[]{:S(2)}) %collective-permute-start.2) | collective-permute-done | bytes 32800 | tf_op jit(solution)/shard_map/ppermute | solution.py:176
  12.5 1.6 %collective-permute-start.3 = (bf16[1,384,128]{2,1,0:T(8,128)(2,1)S(1)}, bf16[1,384,128]{2,1,0:T(8,128)(2,1)S(1)}, u32[]{:S(2)}, u32[]{:S(2)}) collective-permute-start(bf16[1,384,128]{2,1,0:T(8,128)(2,1)S(1)} %maximum_bitcast_fusion.refs_1_), channel_id=1, source_target_pairs={{0,8},{4,20},{8,0},{12,28},{16,24},{20,4},{24,16},{28,12},{1,9},{5... | collective-permute-start | bytes 294920 | tf_op jit(solution)/shard_map/ppermute | solution.py:184
  14.1 0.0 collective-permute-done.5
  14.1 1.6 %collective-permute-start.6 = (bf16[2,144,128]{2,1,0:T(8,128)(2,1)S(1)}, bf16[2,144,128]{2,1,0:T(8,128)(2,1)S(1)}, u32[]{:S(2)}, u32[]{:S(2)}) collective-permute-start(bf16[2,144,128]{2,1,0:T(8,128)(2,1)S(1)} %pad_maximum_fusion.2), channel_id=1, source_target_pairs={{0,16},{4,12},{8,24},{12,4},{16,0},{20,28},{24,8},{28,20},{1,17},{... | collective-permute-start | bytes 221192 | tf_op jit(solution)/shard_map/ppermute | solution.py:184
  15.7 1.8 %collective-permute-done.3.refs_5_ = bf16[1,384,128]{2,1,0:T(8,128)(2,1)S(1)} collective-permute-done((bf16[1,384,128]{2,1,0:T(8,128)(2,1)S(1)}, bf16[1,384,128]{2,1,0:T(8,128)(2,1)S(1)}, u32[]{:S(2)}, u32[]{:S(2)}) %collective-permute-start.3) | collective-permute-done | bytes 98336 | tf_op jit(solution)/shard_map/ppermute | solution.py:184
  17.5 1.6 %collective-permute-start.4 = (bf16[2,384,128]{2,1,0:T(8,128)(2,1)S(1)}, bf16[2,384,128]{2,1,0:T(8,128)(2,1)S(1)}, u32[]{:S(2)}, u32[]{:S(2)}) collective-permute-start(bf16[2,384,128]{2,1,0:T(8,128)(2,1)S(1)} %pad_maximum_fusion), channel_id=1, source_target_pairs={{0,16},{4,12},{8,24},{12,4},{16,0},{20,28},{24,8},{28,20},{1,17},{... | collective-permute-start | bytes 589832 | tf_op jit(solution)/shard_map/ppermute | solution.py:184
  19.1 0.0 collective-permute-done.6
  19.1 0.1 collective-permute-start.7
  19.2 0.5 %collective-permute-start.8 = (bf16[1,384,128]{2,1,0:T(8,128)(2,1)S(1)}, bf16[1,384,128]{2,1,0:T(8,128)(2,1)S(1)}, u32[]{:S(2)}, u32[]{:S(2)}) collective-permute-start(bf16[1,384,128]{2,1,0:T(8,128)(2,1)S(1)} %maximum_bitcast_fusion.refs_1_), channel_id=1, source_target_pairs={{0,4},{4,0},{8,12},{12,8},{16,20},{20,16},{24,28},{28,24},{1,5},{5... | collective-permute-start | bytes 294920 | tf_op jit(solution)/shard_map/ppermute | solution.py:184
  19.7 0.1 collective-permute-start.9
  19.8 0.0 copy-done
  19.8 0.1 constant_dynamic-slice_fusion
  19.9 0.2 shard_map.46.query_ref
  20.1 0.9 %shard_map.48 = (f32[1,1024]{1,0:T(1,128)S(1)}, f32[1,1024]{1,0:T(1,128)S(1)}, f32[128,1024]{1,0:T(8,128)S(1)}) custom-call(s32[1]{0:T(128)S(6)} %copy.5.own_ref, bf16[256,1024]{1,0:T(8,128)(2,1)S(1)} %shard_map.46.query_ref, bf16[4,144,128]{2,1,0:T(8,128)(2,1)S(1)} %pad_maximum_fusion.1.refs_0_.refs_3_, bf16[1,384,128]{2,1,0:T(8,128)(2,1)S(1)} %maximum_bitcast_fusion.refs_1_), custom_call_target="tpu_custom_call" | custom-call | tf_op jit(solution)/shard_map/pallas_call | solution.py:140
  21.0 0.0 collective-permute-done.8.refs_4_
  21.0 0.0 collective-permute-done.7.refs_3_.refs_4_
  21.0 0.9 %shard_map.49 = (f32[1,1024]{1,0:T(1,128)S(1)}, f32[1,1024]{1,0:T(1,128)S(1)}, f32[128,1024]{1,0:T(8,128)S(1)}) custom-call(s32[1]{0:T(128)S(6)} %copy.5.own_ref, bf16[256,1024]{1,0:T(8,128)(2,1)S(1)} %shard_map.46.query_ref, f32[1,1024]{1,0:T(1,128)S(1)} %get-tuple-element.29.refs_0_, f32[1,1024]{1,0:T(1,128)S(1)} %get-tuple-element.30.refs_1_, ...), custom_call_target="tpu_custom_call" | custom-call | tf_op jit(solution)/shard_map/pallas_call | solution.py:140
  22.0 0.0 collective-permute-done.9.refs_6_
  22.0 0.8 %shard_map.50 = (f32[1,1024]{1,0:T(1,128)S(1)}, f32[1,1024]{1,0:T(1,128)S(1)}, f32[128,1024]{1,0:T(8,128)S(1)}) custom-call(s32[1]{0:T(128)S(6)} %copy.5.own_ref, bf16[256,1024]{1,0:T(8,128)(2,1)S(1)} %shard_map.46.query_ref, f32[1,1024]{1,0:T(1,128)S(1)} %get-tuple-element.32.refs_0_, f32[1,1024]{1,0:T(1,128)S(1)} %get-tuple-element.33.refs_1_, ...), custom_call_target="tpu_custom_call" | custom-call | tf_op jit(solution)/shard_map/pallas_call | solution.py:140
  22.8 0.4 %collective-permute-done.4.refs_4_ = bf16[2,384,128]{2,1,0:T(8,128)(2,1)S(1)} collective-permute-done((bf16[2,384,128]{2,1,0:T(8,128)(2,1)S(1)}, bf16[2,384,128]{2,1,0:T(8,128)(2,1)S(1)}, u32[]{:S(2)}, u32[]{:S(2)}) %collective-permute-start.4) | collective-permute-done | bytes 196640 | tf_op jit(solution)/shard_map/ppermute | solution.py:184
  23.2 0.1 collective-permute-start.10
  23.3 0.8 %shard_map.51 = (f32[1,1024]{1,0:T(1,128)S(1)}, f32[1,1024]{1,0:T(1,128)S(1)}, f32[128,1024]{1,0:T(8,128)S(1)}) custom-call(s32[1]{0:T(128)S(6)} %copy.5.own_ref, bf16[256,1024]{1,0:T(8,128)(2,1)S(1)} %shard_map.46.query_ref, f32[1,1024]{1,0:T(1,128)S(1)} %get-tuple-element.38.refs_0_, f32[1,1024]{1,0:T(1,128)S(1)} %get-tuple-element.39.refs_1_, ...), custom_call_target="tpu_custom_call" | custom-call | tf_op jit(solution)/shard_map/pallas_call | solution.py:140
  24.1 0.5 %collective-permute-done.10.refs_4_ = bf16[2,384,128]{2,1,0:T(8,128)(2,1)S(1)} collective-permute-done((bf16[2,384,128]{2,1,0:T(8,128)(2,1)S(1)}, bf16[2,384,128]{2,1,0:T(8,128)(2,1)S(1)}, u32[]{:S(2)}, u32[]{:S(2)}) %collective-permute-start.10) | collective-permute-done | bytes 196640 | tf_op jit(solution)/shard_map/ppermute | solution.py:184
  24.7 1.6 %shard_map.52 = bf16[1024,128]{1,0:T(8,128)(2,1)} custom-call(s32[1]{0:T(128)S(6)} %copy.5.own_ref, bf16[256,1024]{1,0:T(8,128)(2,1)S(1)} %shard_map.46.query_ref, f32[1,1024]{1,0:T(1,128)S(1)} %get-tuple-element.42.refs_0_, f32[1,1024]{1,0:T(1,128)S(1)} %get-tuple-element.43.refs_1_, f32[128,1024]{1,0:T(8,128)S(1)} %get-tuple-element.44.refs_2_, ...), custom_call_target="tpu_custom_call" | custom-call | tf_op jit(solution)/shard_map/pallas_call | solution.py:140
  (5 shorter events, 0.1 us)
Async XLA Ops:
  0.0 19.8 %copy-start = (bf16[256,16,128]{2,1,0:T(8,128)(2,1)S(1)}, bf16[256,16,128]{2,1,0:T(8,128)(2,1)}, u32[]{:S(2)}) copy-start(bf16[256,16,128]{2,1,0:T(8,128)(2,1)} %param.4) | copy-start | bytes 3145732
  1.1 8.1 %collective-permute-start = (bf16[128,128]{1,0:T(8,128)(2,1)S(1)}, bf16[128,128]{1,0:T(8,128)(2,1)S(1)}, u32[]{:S(2)}, u32[]{:S(2)}) collective-permute-start(bf16[128,128]{1,0:T(8,128)(2,1)S(1)} %get-tuple-element.25), channel_id=1, source_target_pairs={{0,1},{1,0},{2,3},{3,2},{4,5},{5,4},{6,7},{7,6},{8,9},{9,8},{10,11... | collective-permute-start | bytes 98312 | tf_op jit(solution)/shard_map/ppermute | solution.py:176
  4.2 5.4 %collective-permute-start.1 = (bf16[128,128]{1,0:T(8,128)(2,1)S(1)}, bf16[128,128]{1,0:T(8,128)(2,1)S(1)}, u32[]{:S(2)}, u32[]{:S(2)}) collective-permute-start(bf16[128,128]{1,0:T(8,128)(2,1)S(1)} %get-tuple-element.26), channel_id=1, source_target_pairs={{0,2},{1,3},{2,0},{3,1},{4,6},{5,7},{6,4},{7,5},{8,10},{9,11},{10,... | collective-permute-start | bytes 98312 | tf_op jit(solution)/shard_map/ppermute | solution.py:176
  6.8 5.7 %collective-permute-start.2 = (bf16[128,128]{1,0:T(8,128)(2,1)S(1)}, bf16[128,128]{1,0:T(8,128)(2,1)S(1)}, u32[]{:S(2)}, u32[]{:S(2)}) collective-permute-start(bf16[128,128]{1,0:T(8,128)(2,1)S(1)} %get-tuple-element.27), channel_id=1, source_target_pairs={{0,3},{1,2},{2,1},{3,0},{4,7},{5,6},{6,5},{7,4},{8,11},{9,10},{10,... | collective-permute-start | bytes 98312 | tf_op jit(solution)/shard_map/ppermute | solution.py:176
  7.5 6.6 %collective-permute-start.5 = (bf16[1,144,128]{2,1,0:T(8,128)(2,1)S(1)}, bf16[1,144,128]{2,1,0:T(8,128)(2,1)S(1)}, u32[]{:S(2)}, u32[]{:S(2)}) collective-permute-start(bf16[1,144,128]{2,1,0:T(8,128)(2,1)S(1)} %pad_bitcast_fusion), channel_id=1, source_target_pairs={{0,8},{4,20},{8,0},{12,28},{16,24},{20,4},{24,16},{28,12},{1,9},{5... | collective-permute-start | bytes 110600 | tf_op jit(solution)/shard_map/ppermute | solution.py:184
  12.5 4.9 %collective-permute-start.3 = (bf16[1,384,128]{2,1,0:T(8,128)(2,1)S(1)}, bf16[1,384,128]{2,1,0:T(8,128)(2,1)S(1)}, u32[]{:S(2)}, u32[]{:S(2)}) collective-permute-start(bf16[1,384,128]{2,1,0:T(8,128)(2,1)S(1)} %maximum_bitcast_fusion.refs_1_), channel_id=1, source_target_pairs={{0,8},{4,20},{8,0},{12,28},{16,24},{20,4},{24,16},{28,12},{1,9},{5... | collective-permute-start | bytes 294920 | tf_op jit(solution)/shard_map/ppermute | solution.py:184
  14.1 5.0 %collective-permute-start.6 = (bf16[2,144,128]{2,1,0:T(8,128)(2,1)S(1)}, bf16[2,144,128]{2,1,0:T(8,128)(2,1)S(1)}, u32[]{:S(2)}, u32[]{:S(2)}) collective-permute-start(bf16[2,144,128]{2,1,0:T(8,128)(2,1)S(1)} %pad_maximum_fusion.2), channel_id=1, source_target_pairs={{0,16},{4,12},{8,24},{12,4},{16,0},{20,28},{24,8},{28,20},{1,17},{... | collective-permute-start | bytes 221192 | tf_op jit(solution)/shard_map/ppermute | solution.py:184
  17.5 5.7 %collective-permute-start.4 = (bf16[2,384,128]{2,1,0:T(8,128)(2,1)S(1)}, bf16[2,384,128]{2,1,0:T(8,128)(2,1)S(1)}, u32[]{:S(2)}, u32[]{:S(2)}) collective-permute-start(bf16[2,384,128]{2,1,0:T(8,128)(2,1)S(1)} %pad_maximum_fusion), channel_id=1, source_target_pairs={{0,16},{4,12},{8,24},{12,4},{16,0},{20,28},{24,8},{28,20},{1,17},{... | collective-permute-start | bytes 589832 | tf_op jit(solution)/shard_map/ppermute | solution.py:184
  19.1 1.9 %collective-permute-start.7 = (bf16[4,144,128]{2,1,0:T(8,128)(2,1)S(1)}, bf16[4,144,128]{2,1,0:T(8,128)(2,1)S(1)}, u32[]{:S(2)}, u32[]{:S(2)}) collective-permute-start(bf16[4,144,128]{2,1,0:T(8,128)(2,1)S(1)} %pad_maximum_fusion.1.refs_0_.refs_3_), channel_id=1, source_target_pairs={{0,4},{4,0},{8,12},{12,8},{16,20},{20,16},{24,28},{28,24},{1,5},{5... | collective-permute-start | bytes 442376 | tf_op jit(solution)/shard_map/ppermute | solution.py:184
  19.2 1.8 %collective-permute-start.8 = (bf16[1,384,128]{2,1,0:T(8,128)(2,1)S(1)}, bf16[1,384,128]{2,1,0:T(8,128)(2,1)S(1)}, u32[]{:S(2)}, u32[]{:S(2)}) collective-permute-start(bf16[1,384,128]{2,1,0:T(8,128)(2,1)S(1)} %maximum_bitcast_fusion.refs_1_), channel_id=1, source_target_pairs={{0,4},{4,0},{8,12},{12,8},{16,20},{20,16},{24,28},{28,24},{1,5},{5... | collective-permute-start | bytes 294920 | tf_op jit(solution)/shard_map/ppermute | solution.py:184
  19.7 2.3 %collective-permute-start.9 = (bf16[1,384,128]{2,1,0:T(8,128)(2,1)S(1)}, bf16[1,384,128]{2,1,0:T(8,128)(2,1)S(1)}, u32[]{:S(2)}, u32[]{:S(2)}) collective-permute-start(bf16[1,384,128]{2,1,0:T(8,128)(2,1)S(1)} %collective-permute-done.3.refs_5_), channel_id=1, source_target_pairs={{0,4},{4,0},{8,12},{12,8},{16,20},{20,16},{24,28},{28,24},{1,5},{5... | collective-permute-start | bytes 294920 | tf_op jit(solution)/shard_map/ppermute | solution.py:184
  23.2 1.4 %collective-permute-start.10 = (bf16[2,384,128]{2,1,0:T(8,128)(2,1)S(1)}, bf16[2,384,128]{2,1,0:T(8,128)(2,1)S(1)}, u32[]{:S(2)}, u32[]{:S(2)}) collective-permute-start(bf16[2,384,128]{2,1,0:T(8,128)(2,1)S(1)} %collective-permute-done.4.refs_4_), channel_id=1, source_target_pairs={{0,4},{4,0},{8,12},{12,8},{16,20},{20,16},{24,28},{28,24},{1,5},{5... | collective-permute-start | bytes 589832 | tf_op jit(solution)/shard_map/ppermute | solution.py:184

commit v12 on v10

--- a/solution.py
+++ b/solution.py
@@ -15,10 +15,9 @@
 MIB = 1024 * 1024
 
 
-def pack(copies, pieces, part, own_ref, rows_ref, *out_refs):
+def pack(copies, pieces, part, kv_heads, rows_ref, *out_refs):
     here = lax.axis_index("head")
-    rows = rows_ref.shape[0] // 2
-    kv_heads = rows // part
+    rows = part * kv_heads
     at = lax.broadcasted_iota(jnp.int32, (part, rows), 0)
     source = lax.broadcasted_iota(jnp.int32, (part, rows), 1)
     picks = [
@@ -33,8 +32,6 @@
             for head in range(1, kv_heads):
                 rows_out = jnp.where(kv_head == head, chosen[head], rows_out)
             out_ref[pl.ds(half * part, part), :] = rows_out
-    place = jnp.broadcast_to(own_ref[...].astype(jnp.float32), (MARK, rows_ref.shape[1]))
-    out_refs[0][pl.ds(2 * part, MARK), :] = place.astype(jnp.bfloat16)
 
 
 def scale_queries(scale, query_ref, out_ref):
@@ -53,7 +50,8 @@
     query_rows = query_ref.shape[1]
     group = query_rows // (pieces * part)
     here = lax.axis_index("head")
-    own = own_ref[0].astype(jnp.float32)
+    own = own_ref[pl.ds(2 * part, MARK), :].astype(jnp.float32)[:SUBLANES]
+    own = jnp.concatenate([own] * (query_rows // head_width), axis=1)
 
     blocks = []
     for data, slot, offsets, shifts, mark in items:
@@ -136,7 +134,7 @@
     return pl.pallas_call(
         functools.partial(attend, pieces, part, first, last, items),
         out_shape=shapes,
-        in_specs=[pl.BlockSpec(memory_space=pltpu.SMEM)] + [whole] * (1 + len(operands)),
+        in_specs=[whole] * (2 + len(operands)),
         out_specs=out_specs,
         compiler_params=pltpu.CompilerParams(vmem_limit_bytes=24 * MIB),
         cost_estimate=pl.CostEstimate(flops=cost, bytes_accessed=0, transcendentals=0),
@@ -161,21 +159,20 @@
         compiler_params=pltpu.CompilerParams(vmem_limit_bytes=8 * MIB),
     )(own_queries)
     own, *payloads = pl.pallas_call(
-        functools.partial(pack, pieces // kv_heads, pieces, part),
-        out_shape=[
-            jax.ShapeDtypeStruct((2 * part + (0 if shift else MARK), head_width), jnp.bfloat16)
-            for shift in range(pieces)
-        ],
-        in_specs=[whole, whole],
+        functools.partial(pack, pieces // kv_heads, pieces, part, kv_heads),
+        out_shape=[jax.ShapeDtypeStruct((2 * part, head_width), jnp.bfloat16)] * pieces,
+        in_specs=[whole],
         out_specs=[whole] * pieces,
         compiler_params=pltpu.CompilerParams(vmem_limit_bytes=4 * MIB),
-    )(block_ids.reshape(1, 1), jnp.concatenate([keys, values]).reshape(2 * part * kv_heads, head_width))
+    )(jnp.concatenate([keys, values]).reshape(2 * part * kv_heads, head_width))
+    mark = jnp.broadcast_to(block_ids.astype(jnp.bfloat16)[:, None], (MARK, head_width))
+    own = jnp.concatenate([own, mark])
     near = [
         lax.ppermute(rows, "head", [(i, (i + shift + 1) % pieces) for i in range(pieces)])
         for shift, rows in enumerate(payloads)
     ]
     rest = jnp.concatenate(near)
-    fold = functools.partial(attend_call, pieces, part, block_ids, scaled)
+    fold = functools.partial(attend_call, pieces, part, own, scaled)
     shifts = tuple(range(pieces))
     offsets = tuple(2 * part * i for i in range(pieces))
 
@@ -200,12 +197,22 @@
             False,
             1000000000,
         )
+        mine, rest = lax.optimization_barrier((mine, rest))
         mine_other, rest_other = swap(mine, 1), swap(rest, 1)
         state = fold(state, [mine_other, rest_other], small(0, range(4)) + [large(1, 0, 0)], False)
-        *rests, state = lax.optimization_barrier((*rests, state))
-        rests_other = [swap(rows, 1) for rows in rests]
-        state = fold(state, [mine] + rests, [large(i, 0, i) for i in range(1, 4)], False)
-        result = fold(state, [mine_other] + rests_other, [large(i, 0, i) for i in range(1, 4)], True)
+        along_x, along_y, across = rests
+        along_x, along_y, state = lax.optimization_barrier((along_x, along_y, state))
+        others = [swap(rows, 1) for rows in (along_x, along_y)]
+        state = fold(state, [mine, along_x, along_y], [large(i, 0, i) for i in (1, 2)], False)
+        across, state = lax.optimization_barrier((across, state))
+        other_across = swap(across, 1)
+        state = fold(
+            state,
+            [mine, mine_other, across] + others,
+            [large(2, 0, 3)] + [large(2 + i, 1, i) for i in (1, 2)],
+            False,
+        )
+        result = fold(state, [mine_other, other_across], [large(1, 0, 3)], True)
     else:
         block = jnp.concatenate([own[: 2 * part], rest, own[2 * part :]])
         far = lax.all_gather(block, "seq", axis=0, tiled=False)

time: 24.8 us -> 24.1 us (0.972)
  waiting for transfers between devices: 2.97 us -> 1.15 us
  starting transfers between devices: 14.7 us -> 15.4 us
  Pallas kernels: 5.08 us -> 5.44 us
    ppermute x11, waiting for transfers between devices: 2.97 us -> 1.15 us  [swap(): return lax.ppermute(rows, 'seq', [(i, i ^ flip) for i in range(blocks)])]
    ppermute x11, starting transfers between devices: 7.7 us -> 8.4 us  [swap(): return lax.ppermute(rows, 'seq', [(i, i ^ flip) for i in range(blocks)])]
    pallas_call x4 -> x5, Pallas kernels: 4.71 us -> 5.08 us  [attend_call(): pl.pallas_call(functools.partial(attend, pieces, part, first, last, items...]
  transfers between devices with their start and end apart: 14 -> 14, of which waited for: 5 -> 2; matrix products, arithmetic and copies ran while one was open for 1% -> 1% of each run, Pallas kernels for 12% -> 16%
where the time goes in v12:
time: 24.1 us; the launch traced here: 23.9 us
  starting transfers between devices  15.4 us (64%)
  Pallas kernels  5.44 us (23%)
  waiting for transfers between devices  1.15 us (5%)
  other arithmetic  0.98 us (4%)
  between operations  0.77 us (3%)
    ppermute x11, starting transfers between devices, swap(): return lax.ppermute(rows, 'seq', [(i, i ^ flip) for i in range(blocks)])  8.4 us
    ppermute x3, starting transfers between devices, shards(): lax.ppermute(rows, 'head', [(i, (i + shift + 1) % pieces) for i in range(...  7.01 us
    pallas_call x5, Pallas kernels, attend_call(): pl.pallas_call(functools.partial(attend, pieces, part, first, last, items...  5.08 us
    ppermute x11, waiting for transfers between devices, swap(): return lax.ppermute(rows, 'seq', [(i, i ^ flip) for i in range(blocks)])  1.15 us
    concatenate x1, other arithmetic, shards(): jnp.concatenate([keys, values]).reshape(2 * part * kv_heads, head_width)  0.95 us
  transfers between devices with their start and end apart: 14, of which 2 were waited for; matrix products, arithmetic and copies ran while one was open for 1% of the time, Pallas kernels for 16%

profile of v12, /device:TPU:0, one launch (start us, length us, event | category | flops | bytes accessed | tf_op | source)
XLA Modules:
  0.0 23.9 jit_solution(13404015327722836182)
XLA Ops:
  0.0 0.0 copy-start
  0.0 1.0 %pad_maximum_fusion.1 = bf16[128,2,128]{2,1,0:T(2,128)(2,1)S(1)} fusion(bf16[64,2,128]{2,1,0:T(2,128)(2,1)} %param.6, bf16[64,2,128]{2,1,0:T(2,128)(2,1)} %param.5), kind=kLoop, calls=%fused_computation.2 | loop fusion | flops 32768 | bytes 131072 | tf_op jit(solution)/shard_map/concatenate | solution.py:167
  1.0 0.2 shard_map.46
  1.1 3.1 %collective-permute-start = (bf16[128,128]{1,0:T(8,128)(2,1)S(1)}, bf16[128,128]{1,0:T(8,128)(2,1)S(1)}, u32[]{:S(2)}, u32[]{:S(2)}) collective-permute-start(bf16[128,128]{1,0:T(8,128)(2,1)S(1)} %get-tuple-element.33), channel_id=1, source_target_pairs={{0,1},{1,2},{2,3},{3,0},{4,5},{5,6},{6,7},{7,4},{8,9},{9,10},{10,1... | collective-permute-start | bytes 98312 | tf_op jit(solution)/shard_map/ppermute | solution.py:171
  4.2 2.6 %collective-permute-start.1 = (bf16[128,128]{1,0:T(8,128)(2,1)S(1)}, bf16[128,128]{1,0:T(8,128)(2,1)S(1)}, u32[]{:S(2)}, u32[]{:S(2)}) collective-permute-start(bf16[128,128]{1,0:T(8,128)(2,1)S(1)} %get-tuple-element.34), channel_id=1, source_target_pairs={{0,2},{1,3},{2,0},{3,1},{4,6},{5,7},{6,4},{7,5},{8,10},{9,11},{10,... | collective-permute-start | bytes 98312 | tf_op jit(solution)/shard_map/ppermute | solution.py:171
  6.8 1.3 %collective-permute-start.2 = (bf16[128,128]{1,0:T(8,128)(2,1)S(1)}, bf16[128,128]{1,0:T(8,128)(2,1)S(1)}, u32[]{:S(2)}, u32[]{:S(2)}) collective-permute-start(bf16[128,128]{1,0:T(8,128)(2,1)S(1)} %get-tuple-element.35), channel_id=1, source_target_pairs={{0,3},{1,0},{2,1},{3,2},{4,7},{5,4},{6,5},{7,6},{8,11},{9,8},{10,9... | collective-permute-start | bytes 98312 | tf_op jit(solution)/shard_map/ppermute | solution.py:171
  8.8 1.6 %collective-permute-start.6 = (bf16[144,128]{1,0:T(8,128)(2,1)S(1)}, bf16[144,128]{1,0:T(8,128)(2,1)S(1)}, u32[]{:S(2)}, u32[]{:S(2)}) collective-permute-start(bf16[144,128]{1,0:T(8,128)(2,1)S(1)} %get-tuple-element.60.own_ref), channel_id=1, source_target_pairs={{0,8},{4,12},{8,0},{12,4},{16,24},{20,28},{24,16},{28,20},{1,9},{5... | collective-permute-start | bytes 110600 | tf_op jit(solution)/shard_map/ppermute | solution.py:180
  10.4 1.5 %collective-permute-start.7 = (bf16[144,128]{1,0:T(8,128)(2,1)S(1)}, bf16[144,128]{1,0:T(8,128)(2,1)S(1)}, u32[]{:S(2)}, u32[]{:S(2)}) collective-permute-start(bf16[144,128]{1,0:T(8,128)(2,1)S(1)} %get-tuple-element.60.own_ref), channel_id=1, source_target_pairs={{0,16},{4,20},{8,24},{12,28},{16,0},{20,4},{24,8},{28,12},{1,17},{... | collective-permute-start | bytes 110600 | tf_op jit(solution)/shard_map/ppermute | solution.py:180
  11.9 0.0 collective-permute-done
  11.9 0.5 %collective-permute-start.8 = (bf16[144,128]{1,0:T(8,128)(2,1)S(1)}, bf16[144,128]{1,0:T(8,128)(2,1)S(1)}, u32[]{:S(2)}, u32[]{:S(2)}) collective-permute-start(bf16[144,128]{1,0:T(8,128)(2,1)S(1)} %get-tuple-element.60.own_ref), channel_id=1, source_target_pairs={{0,24},{4,28},{8,16},{12,20},{16,8},{20,12},{24,0},{28,4},{1,25},{... | collective-permute-start | bytes 110600 | tf_op jit(solution)/shard_map/ppermute | solution.py:180
  12.4 0.0 collective-permute-done.1
  12.4 0.0 collective-permute-done.2
  12.4 1.6 %collective-permute-start.4 = (bf16[1,384,128]{2,1,0:T(8,128)(2,1)S(1)}, bf16[1,384,128]{2,1,0:T(8,128)(2,1)S(1)}, u32[]{:S(2)}, u32[]{:S(2)}) collective-permute-start(bf16[1,384,128]{2,1,0:T(8,128)(2,1)S(1)} %maximum_bitcast_fusion.refs_1_), channel_id=1, source_target_pairs={{0,8},{4,12},{8,0},{12,4},{16,24},{20,28},{24,16},{28,20},{1,9},{5... | collective-permute-start | bytes 294920 | tf_op jit(solution)/shard_map/ppermute | solution.py:180
  14.0 1.5 %collective-permute-start.5 = (bf16[1,384,128]{2,1,0:T(8,128)(2,1)S(1)}, bf16[1,384,128]{2,1,0:T(8,128)(2,1)S(1)}, u32[]{:S(2)}, u32[]{:S(2)}) collective-permute-start(bf16[1,384,128]{2,1,0:T(8,128)(2,1)S(1)} %maximum_bitcast_fusion.refs_1_), channel_id=1, source_target_pairs={{0,16},{4,20},{8,24},{12,28},{16,0},{20,4},{24,8},{28,12},{1,17},{... | collective-permute-start | bytes 294920 | tf_op jit(solution)/shard_map/ppermute | solution.py:180
  15.5 0.0 collective-permute-done.6
  15.5 0.5 %collective-permute-start.3 = (bf16[1,384,128]{2,1,0:T(8,128)(2,1)S(1)}, bf16[1,384,128]{2,1,0:T(8,128)(2,1)S(1)}, u32[]{:S(2)}, u32[]{:S(2)}) collective-permute-start(bf16[1,384,128]{2,1,0:T(8,128)(2,1)S(1)} %maximum_bitcast_fusion.refs_1_), channel_id=1, source_target_pairs={{0,24},{4,28},{8,16},{12,20},{16,8},{20,12},{24,0},{28,4},{1,25},{... | collective-permute-start | bytes 294920 | tf_op jit(solution)/shard_map/ppermute | solution.py:180
  16.0 0.0 collective-permute-done.7
  16.0 1.0 %collective-permute-done.8 = bf16[144,128]{1,0:T(8,128)(2,1)S(1)} collective-permute-done((bf16[144,128]{1,0:T(8,128)(2,1)S(1)}, bf16[144,128]{1,0:T(8,128)(2,1)S(1)}, u32[]{:S(2)}, u32[]{:S(2)}) %collective-permute-start.8) | collective-permute-done | bytes 36896 | tf_op jit(solution)/shard_map/ppermute | solution.py:180
  17.0 0.1 collective-permute-start.9
  17.1 0.5 %collective-permute-start.10 = (bf16[1,384,128]{2,1,0:T(8,128)(2,1)S(1)}, bf16[1,384,128]{2,1,0:T(8,128)(2,1)S(1)}, u32[]{:S(2)}, u32[]{:S(2)}) collective-permute-start(bf16[1,384,128]{2,1,0:T(8,128)(2,1)S(1)} %maximum_bitcast_fusion.refs_1_), channel_id=1, source_target_pairs={{0,4},{4,0},{8,12},{12,8},{16,20},{20,16},{24,28},{28,24},{1,5},{5... | collective-permute-start | bytes 294920 | tf_op jit(solution)/shard_map/ppermute | solution.py:180
  17.6 0.0 copy-done
  17.6 0.1 constant_dynamic-slice_fusion
  17.7 0.2 shard_map.47.query_ref
  17.9 0.9 %shard_map.48 = (f32[1,1024]{1,0:T(1,128)S(1)}, f32[1,1024]{1,0:T(1,128)S(1)}, f32[128,1024]{1,0:T(8,128)S(1)}) custom-call(bf16[144,128]{1,0:T(8,128)(2,1)S(1)} %get-tuple-element.60.own_ref, bf16[256,1024]{1,0:T(8,128)(2,1)S(1)} %shard_map.47.query_ref, bf16[4,144,128]{2,1,0:T(8,128)(2,1)S(1)} %pad_maximum_fusion.refs_0_.refs_3_, ...), custom_call_target="tpu_custom_call" | custom-call | flops 1000000000 | tf_op jit(solution)/shard_map/pallas_call | solution.py:134
  18.8 0.0 collective-permute-done.10.refs_4_
  18.8 0.0 collective-permute-done.9.refs_3_.refs_4_
  18.8 0.9 %shard_map.49 = (f32[1,1024]{1,0:T(1,128)S(1)}, f32[1,1024]{1,0:T(1,128)S(1)}, f32[128,1024]{1,0:T(8,128)S(1)}) custom-call(bf16[144,128]{1,0:T(8,128)(2,1)S(1)} %get-tuple-element.60.own_ref, bf16[256,1024]{1,0:T(8,128)(2,1)S(1)} %shard_map.47.query_ref, f32[1,1024]{1,0:T(1,128)S(1)} %get-tuple-element.36.refs_0_, f32[1,1024]{1,0:T(1,128)S(1)} %get-tuple-element.37.refs_1_, ...), custom_call_target="tpu_custom_call" | custom-call | tf_op jit(solution)/shard_map/pallas_call | solution.py:134
  19.8 0.0 collective-permute-done.4.refs_4_
  19.8 0.0 collective-permute-done.5.refs_5_
  19.8 0.1 collective-permute-start.11
  19.9 0.4 %collective-permute-start.12 = (bf16[1,384,128]{2,1,0:T(8,128)(2,1)S(1)}, bf16[1,384,128]{2,1,0:T(8,128)(2,1)S(1)}, u32[]{:S(2)}, u32[]{:S(2)}) collective-permute-start(bf16[1,384,128]{2,1,0:T(8,128)(2,1)S(1)} %collective-permute-done.5.refs_5_), channel_id=1, source_target_pairs={{0,4},{4,0},{8,12},{12,8},{16,20},{20,16},{24,28},{28,24},{1,5},{5... | collective-permute-start | bytes 294920 | tf_op jit(solution)/shard_map/ppermute | solution.py:180
  20.4 0.8 %shard_map.50 = (f32[1,1024]{1,0:T(1,128)S(1)}, f32[1,1024]{1,0:T(1,128)S(1)}, f32[128,1024]{1,0:T(8,128)S(1)}) custom-call(bf16[144,128]{1,0:T(8,128)(2,1)S(1)} %get-tuple-element.60.own_ref, bf16[256,1024]{1,0:T(8,128)(2,1)S(1)} %shard_map.47.query_ref, f32[1,1024]{1,0:T(1,128)S(1)} %get-tuple-element.44.refs_0_, f32[1,1024]{1,0:T(1,128)S(1)} %get-tuple-element.45.refs_1_, ...), custom_call_target="tpu_custom_call" | custom-call | tf_op jit(solution)/shard_map/pallas_call | solution.py:134
  21.2 0.0 collective-permute-done.3.refs_5_
  21.2 0.1 collective-permute-start.13
  21.3 0.0 collective-permute-done.11.refs_6_
  21.3 0.0 collective-permute-done.12.refs_7_
  21.3 1.1 %shard_map.51 = (f32[1,1024]{1,0:T(1,128)S(1)}, f32[1,1024]{1,0:T(1,128)S(1)}, f32[128,1024]{1,0:T(8,128)S(1)}) custom-call(bf16[144,128]{1,0:T(8,128)(2,1)S(1)} %get-tuple-element.60.own_ref, bf16[256,1024]{1,0:T(8,128)(2,1)S(1)} %shard_map.47.query_ref, f32[1,1024]{1,0:T(1,128)S(1)} %get-tuple-element.52.refs_0_, f32[1,1024]{1,0:T(1,128)S(1)} %get-tuple-element.53.refs_1_, ...), custom_call_target="tpu_custom_call" | custom-call | tf_op jit(solution)/shard_map/pallas_call | solution.py:134
  22.4 0.1 collective-permute-done.13.refs_4_
  22.6 1.4 %shard_map.52 = bf16[1024,128]{1,0:T(8,128)(2,1)} custom-call(bf16[144,128]{1,0:T(8,128)(2,1)S(1)} %get-tuple-element.60.own_ref, bf16[256,1024]{1,0:T(8,128)(2,1)S(1)} %shard_map.47.query_ref, f32[1,1024]{1,0:T(1,128)S(1)} %get-tuple-element.56.refs_0_, f32[1,1024]{1,0:T(1,128)S(1)} %get-tuple-element.57.refs_1_, ...), custom_call_target="tpu_custom_call" | custom-call | tf_op jit(solution)/shard_map/pallas_call | solution.py:134
  (3 shorter events, 0.0 us)
Async XLA Ops:
  0.0 17.6 %copy-start = (bf16[256,16,128]{2,1,0:T(8,128)(2,1)S(1)}, bf16[256,16,128]{2,1,0:T(8,128)(2,1)}, u32[]{:S(2)}) copy-start(bf16[256,16,128]{2,1,0:T(8,128)(2,1)} %param.4) | copy-start | bytes 3145732
  1.1 10.8 %collective-permute-start = (bf16[128,128]{1,0:T(8,128)(2,1)S(1)}, bf16[128,128]{1,0:T(8,128)(2,1)S(1)}, u32[]{:S(2)}, u32[]{:S(2)}) collective-permute-start(bf16[128,128]{1,0:T(8,128)(2,1)S(1)} %get-tuple-element.33), channel_id=1, source_target_pairs={{0,1},{1,2},{2,3},{3,0},{4,5},{5,6},{6,7},{7,4},{8,9},{9,10},{10,1... | collective-permute-start | bytes 98312 | tf_op jit(solution)/shard_map/ppermute | solution.py:171
  4.2 8.2 %collective-permute-start.1 = (bf16[128,128]{1,0:T(8,128)(2,1)S(1)}, bf16[128,128]{1,0:T(8,128)(2,1)S(1)}, u32[]{:S(2)}, u32[]{:S(2)}) collective-permute-start(bf16[128,128]{1,0:T(8,128)(2,1)S(1)} %get-tuple-element.34), channel_id=1, source_target_pairs={{0,2},{1,3},{2,0},{3,1},{4,6},{5,7},{6,4},{7,5},{8,10},{9,11},{10,... | collective-permute-start | bytes 98312 | tf_op jit(solution)/shard_map/ppermute | solution.py:171
  6.8 5.6 %collective-permute-start.2 = (bf16[128,128]{1,0:T(8,128)(2,1)S(1)}, bf16[128,128]{1,0:T(8,128)(2,1)S(1)}, u32[]{:S(2)}, u32[]{:S(2)}) collective-permute-start(bf16[128,128]{1,0:T(8,128)(2,1)S(1)} %get-tuple-element.35), channel_id=1, source_target_pairs={{0,3},{1,0},{2,1},{3,2},{4,7},{5,4},{6,5},{7,6},{8,11},{9,8},{10,9... | collective-permute-start | bytes 98312 | tf_op jit(solution)/shard_map/ppermute | solution.py:171
  8.8 6.7 %collective-permute-start.6 = (bf16[144,128]{1,0:T(8,128)(2,1)S(1)}, bf16[144,128]{1,0:T(8,128)(2,1)S(1)}, u32[]{:S(2)}, u32[]{:S(2)}) collective-permute-start(bf16[144,128]{1,0:T(8,128)(2,1)S(1)} %get-tuple-element.60.own_ref), channel_id=1, source_target_pairs={{0,8},{4,12},{8,0},{12,4},{16,24},{20,28},{24,16},{28,20},{1,9},{5... | collective-permute-start | bytes 110600 | tf_op jit(solution)/shard_map/ppermute | solution.py:180
  10.4 5.6 %collective-permute-start.7 = (bf16[144,128]{1,0:T(8,128)(2,1)S(1)}, bf16[144,128]{1,0:T(8,128)(2,1)S(1)}, u32[]{:S(2)}, u32[]{:S(2)}) collective-permute-start(bf16[144,128]{1,0:T(8,128)(2,1)S(1)} %get-tuple-element.60.own_ref), channel_id=1, source_target_pairs={{0,16},{4,20},{8,24},{12,28},{16,0},{20,4},{24,8},{28,12},{1,17},{... | collective-permute-start | bytes 110600 | tf_op jit(solution)/shard_map/ppermute | solution.py:180
  11.9 5.0 %collective-permute-start.8 = (bf16[144,128]{1,0:T(8,128)(2,1)S(1)}, bf16[144,128]{1,0:T(8,128)(2,1)S(1)}, u32[]{:S(2)}, u32[]{:S(2)}) collective-permute-start(bf16[144,128]{1,0:T(8,128)(2,1)S(1)} %get-tuple-element.60.own_ref), channel_id=1, source_target_pairs={{0,24},{4,28},{8,16},{12,20},{16,8},{20,12},{24,0},{28,4},{1,25},{... | collective-permute-start | bytes 110600 | tf_op jit(solution)/shard_map/ppermute | solution.py:180
  12.4 7.4 %collective-permute-start.4 = (bf16[1,384,128]{2,1,0:T(8,128)(2,1)S(1)}, bf16[1,384,128]{2,1,0:T(8,128)(2,1)S(1)}, u32[]{:S(2)}, u32[]{:S(2)}) collective-permute-start(bf16[1,384,128]{2,1,0:T(8,128)(2,1)S(1)} %maximum_bitcast_fusion.refs_1_), channel_id=1, source_target_pairs={{0,8},{4,12},{8,0},{12,4},{16,24},{20,28},{24,16},{28,20},{1,9},{5... | collective-permute-start | bytes 294920 | tf_op jit(solution)/shard_map/ppermute | solution.py:180
  14.0 5.8 %collective-permute-start.5 = (bf16[1,384,128]{2,1,0:T(8,128)(2,1)S(1)}, bf16[1,384,128]{2,1,0:T(8,128)(2,1)S(1)}, u32[]{:S(2)}, u32[]{:S(2)}) collective-permute-start(bf16[1,384,128]{2,1,0:T(8,128)(2,1)S(1)} %maximum_bitcast_fusion.refs_1_), channel_id=1, source_target_pairs={{0,16},{4,20},{8,24},{12,28},{16,0},{20,4},{24,8},{28,12},{1,17},{... | collective-permute-start | bytes 294920 | tf_op jit(solution)/shard_map/ppermute | solution.py:180
  15.5 5.7 %collective-permute-start.3 = (bf16[1,384,128]{2,1,0:T(8,128)(2,1)S(1)}, bf16[1,384,128]{2,1,0:T(8,128)(2,1)S(1)}, u32[]{:S(2)}, u32[]{:S(2)}) collective-permute-start(bf16[1,384,128]{2,1,0:T(8,128)(2,1)S(1)} %maximum_bitcast_fusion.refs_1_), channel_id=1, source_target_pairs={{0,24},{4,28},{8,16},{12,20},{16,8},{20,12},{24,0},{28,4},{1,25},{... | collective-permute-start | bytes 294920 | tf_op jit(solution)/shard_map/ppermute | solution.py:180
  17.0 1.8 %collective-permute-start.9 = (bf16[4,144,128]{2,1,0:T(8,128)(2,1)S(1)}, bf16[4,144,128]{2,1,0:T(8,128)(2,1)S(1)}, u32[]{:S(2)}, u32[]{:S(2)}) collective-permute-start(bf16[4,144,128]{2,1,0:T(8,128)(2,1)S(1)} %pad_maximum_fusion.refs_0_.refs_3_), channel_id=1, source_target_pairs={{0,4},{4,0},{8,12},{12,8},{16,20},{20,16},{24,28},{28,24},{1,5},{5... | collective-permute-start | bytes 442376 | tf_op jit(solution)/shard_map/ppermute | solution.py:180
  17.1 1.7 %collective-permute-start.10 = (bf16[1,384,128]{2,1,0:T(8,128)(2,1)S(1)}, bf16[1,384,128]{2,1,0:T(8,128)(2,1)S(1)}, u32[]{:S(2)}, u32[]{:S(2)}) collective-permute-start(bf16[1,384,128]{2,1,0:T(8,128)(2,1)S(1)} %maximum_bitcast_fusion.refs_1_), channel_id=1, source_target_pairs={{0,4},{4,0},{8,12},{12,8},{16,20},{20,16},{24,28},{28,24},{1,5},{5... | collective-permute-start | bytes 294920 | tf_op jit(solution)/shard_map/ppermute | solution.py:180
  19.8 1.6 %collective-permute-start.11 = (bf16[1,384,128]{2,1,0:T(8,128)(2,1)S(1)}, bf16[1,384,128]{2,1,0:T(8,128)(2,1)S(1)}, u32[]{:S(2)}, u32[]{:S(2)}) collective-permute-start(bf16[1,384,128]{2,1,0:T(8,128)(2,1)S(1)} %collective-permute-done.4.refs_4_), channel_id=1, source_target_pairs={{0,4},{4,0},{8,12},{12,8},{16,20},{20,16},{24,28},{28,24},{1,5},{5... | collective-permute-start | bytes 294920 | tf_op jit(solution)/shard_map/ppermute | solution.py:180
  19.9 1.4 %collective-permute-start.12 = (bf16[1,384,128]{2,1,0:T(8,128)(2,1)S(1)}, bf16[1,384,128]{2,1,0:T(8,128)(2,1)S(1)}, u32[]{:S(2)}, u32[]{:S(2)}) collective-permute-start(bf16[1,384,128]{2,1,0:T(8,128)(2,1)S(1)} %collective-permute-done.5.refs_5_), channel_id=1, source_target_pairs={{0,4},{4,0},{8,12},{12,8},{16,20},{20,16},{24,28},{28,24},{1,5},{5... | collective-permute-start | bytes 294920 | tf_op jit(solution)/shard_map/ppermute | solution.py:180
  21.2 1.4 %collective-permute-start.13 = (bf16[1,384,128]{2,1,0:T(8,128)(2,1)S(1)}, bf16[1,384,128]{2,1,0:T(8,128)(2,1)S(1)}, u32[]{:S(2)}, u32[]{:S(2)}) collective-permute-start(bf16[1,384,128]{2,1,0:T(8,128)(2,1)S(1)} %collective-permute-done.3.refs_5_), channel_id=1, source_target_pairs={{0,4},{4,0},{8,12},{12,8},{16,20},{20,16},{24,28},{28,24},{1,5},{5... | collective-permute-start | bytes 294920 | tf_op jit(solution)/shard_map/ppermute | solution.py:180

commit v13 on v12

--- a/solution.py
+++ b/solution.py
@@ -10,6 +10,7 @@
 
 MARK = 16
 SUBLANES = 8
+FINAL = 256
 LOW = -1e30
 HIGH = 1e30
 MIB = 1024 * 1024
@@ -45,7 +46,7 @@
 def attend(pieces, part, first, last, items, own_ref, query_ref, *refs):
     refs = list(refs)
     state = None if first else [refs.pop(0) for _ in range(3)]
-    outs = [refs.pop() for _ in range(1 if last else 3)][::-1]
+    outs = [refs.pop() for _ in range(3)][::-1]
     head_width = query_ref.shape[0] // 2
     query_rows = query_ref.shape[1]
     group = query_rows // (pieces * part)
@@ -109,7 +110,16 @@
         total = total + state[1][...] * keep
         accum = accum + state[2][...] * keep
     if last:
-        outs[0][...] = (accum * (1.0 / total)).astype(outs[0].dtype).T
+        out_hbm, out_ref, sems = outs
+        inverse = 1.0 / total
+        copies = []
+        for i in range(query_rows // FINAL):
+            span = slice(i * FINAL, (i + 1) * FINAL)
+            out_ref[span, :] = (accum[:, span] * inverse[:, span]).astype(out_ref.dtype).T
+            copies.append(pltpu.make_async_copy(out_ref.at[span], out_hbm.at[span], sems.at[i]))
+            copies[-1].start()
+        for copy in copies:
+            copy.wait()
     else:
         outs[0][...] = high
         outs[1][...] = total
@@ -123,8 +133,13 @@
     operands = ([] if first else list(state)) + list(datas)
     if last:
         shapes = jax.ShapeDtypeStruct((query_rows, head_width), jnp.bfloat16)
-        out_specs = whole
+        out_specs = pl.BlockSpec(memory_space=pl.ANY)
+        scratch = [
+            pltpu.VMEM((query_rows, head_width), jnp.bfloat16),
+            pltpu.SemaphoreType.DMA((query_rows // FINAL,)),
+        ]
     else:
+        scratch = []
         shapes = [
             jax.ShapeDtypeStruct((1, query_rows), jnp.float32),
             jax.ShapeDtypeStruct((1, query_rows), jnp.float32),
@@ -136,6 +151,7 @@
         out_shape=shapes,
         in_specs=[whole] * (2 + len(operands)),
         out_specs=out_specs,
+        scratch_shapes=scratch,
         compiler_params=pltpu.CompilerParams(vmem_limit_bytes=24 * MIB),
         cost_estimate=pl.CostEstimate(flops=cost, bytes_accessed=0, transcendentals=0),
     )(own, query, *operands)

time: 24.1 us -> 24 us (level)
  no operation moved by 1% of the time
where the time goes in v13:
time: 24 us; the launch traced here: 23.9 us
  starting transfers between devices  15.4 us (64%)
  Pallas kernels  5.41 us (23%)
  waiting for transfers between devices  1.15 us (5%)
  other arithmetic  0.98 us (4%)
  between operations  0.77 us (3%)
    ppermute x11, starting transfers between devices, swap(): return lax.ppermute(rows, 'seq', [(i, i ^ flip) for i in range(blocks)])  8.4 us
    ppermute x3, starting transfers between devices, shards(): lax.ppermute(rows, 'head', [(i, (i + shift + 1) % pieces) for i in range(...  7.01 us
    pallas_call x5, Pallas kernels, attend_call(): pl.pallas_call(functools.partial(attend, pieces, part, first, last, items...  5.05 us
    ppermute x11, waiting for transfers between devices, swap(): return lax.ppermute(rows, 'seq', [(i, i ^ flip) for i in range(blocks)])  1.15 us
    concatenate x1, other arithmetic, shards(): jnp.concatenate([keys, values]).reshape(2 * part * kv_heads, head_width)  0.95 us
  transfers between devices with their start and end apart: 14, of which 2 were waited for; matrix products, arithmetic and copies ran while one was open for 1% of the time, Pallas kernels for 16%

profile of v13, /device:TPU:0, one launch (start us, length us, event | category | flops | bytes accessed | tf_op | source)
XLA Modules:
  0.0 23.9 jit_solution(3379980381953142145)
XLA Ops:
  0.0 0.0 copy-start
  0.0 1.0 %pad_maximum_fusion.1 = bf16[128,2,128]{2,1,0:T(2,128)(2,1)S(1)} fusion(bf16[64,2,128]{2,1,0:T(2,128)(2,1)} %param.6, bf16[64,2,128]{2,1,0:T(2,128)(2,1)} %param.5), kind=kLoop, calls=%fused_computation.2 | loop fusion | flops 32768 | bytes 131072 | tf_op jit(solution)/shard_map/concatenate | solution.py:183
  1.0 0.2 shard_map.46
  1.1 3.1 %collective-permute-start = (bf16[128,128]{1,0:T(8,128)(2,1)S(1)}, bf16[128,128]{1,0:T(8,128)(2,1)S(1)}, u32[]{:S(2)}, u32[]{:S(2)}) collective-permute-start(bf16[128,128]{1,0:T(8,128)(2,1)S(1)} %get-tuple-element.33), channel_id=1, source_target_pairs={{0,1},{1,2},{2,3},{3,0},{4,5},{5,6},{6,7},{7,4},{8,9},{9,10},{10,1... | collective-permute-start | bytes 98312 | tf_op jit(solution)/shard_map/ppermute | solution.py:187
  4.2 2.6 %collective-permute-start.1 = (bf16[128,128]{1,0:T(8,128)(2,1)S(1)}, bf16[128,128]{1,0:T(8,128)(2,1)S(1)}, u32[]{:S(2)}, u32[]{:S(2)}) collective-permute-start(bf16[128,128]{1,0:T(8,128)(2,1)S(1)} %get-tuple-element.34), channel_id=1, source_target_pairs={{0,2},{1,3},{2,0},{3,1},{4,6},{5,7},{6,4},{7,5},{8,10},{9,11},{10,... | collective-permute-start | bytes 98312 | tf_op jit(solution)/shard_map/ppermute | solution.py:187
  6.8 1.3 %collective-permute-start.2 = (bf16[128,128]{1,0:T(8,128)(2,1)S(1)}, bf16[128,128]{1,0:T(8,128)(2,1)S(1)}, u32[]{:S(2)}, u32[]{:S(2)}) collective-permute-start(bf16[128,128]{1,0:T(8,128)(2,1)S(1)} %get-tuple-element.35), channel_id=1, source_target_pairs={{0,3},{1,0},{2,1},{3,2},{4,7},{5,4},{6,5},{7,6},{8,11},{9,8},{10,9... | collective-permute-start | bytes 98312 | tf_op jit(solution)/shard_map/ppermute | solution.py:187
  8.8 1.6 %collective-permute-start.6 = (bf16[144,128]{1,0:T(8,128)(2,1)S(1)}, bf16[144,128]{1,0:T(8,128)(2,1)S(1)}, u32[]{:S(2)}, u32[]{:S(2)}) collective-permute-start(bf16[144,128]{1,0:T(8,128)(2,1)S(1)} %get-tuple-element.60.own_ref), channel_id=1, source_target_pairs={{0,8},{4,12},{8,0},{12,4},{16,24},{20,28},{24,16},{28,20},{1,9},{5... | collective-permute-start | bytes 110600 | tf_op jit(solution)/shard_map/ppermute | solution.py:196
  10.4 1.5 %collective-permute-start.7 = (bf16[144,128]{1,0:T(8,128)(2,1)S(1)}, bf16[144,128]{1,0:T(8,128)(2,1)S(1)}, u32[]{:S(2)}, u32[]{:S(2)}) collective-permute-start(bf16[144,128]{1,0:T(8,128)(2,1)S(1)} %get-tuple-element.60.own_ref), channel_id=1, source_target_pairs={{0,16},{4,20},{8,24},{12,28},{16,0},{20,4},{24,8},{28,12},{1,17},{... | collective-permute-start | bytes 110600 | tf_op jit(solution)/shard_map/ppermute | solution.py:196
  11.9 0.0 collective-permute-done
  11.9 0.5 %collective-permute-start.8 = (bf16[144,128]{1,0:T(8,128)(2,1)S(1)}, bf16[144,128]{1,0:T(8,128)(2,1)S(1)}, u32[]{:S(2)}, u32[]{:S(2)}) collective-permute-start(bf16[144,128]{1,0:T(8,128)(2,1)S(1)} %get-tuple-element.60.own_ref), channel_id=1, source_target_pairs={{0,24},{4,28},{8,16},{12,20},{16,8},{20,12},{24,0},{28,4},{1,25},{... | collective-permute-start | bytes 110600 | tf_op jit(solution)/shard_map/ppermute | solution.py:196
  12.4 0.0 collective-permute-done.1
  12.4 0.0 collective-permute-done.2
  12.4 1.6 %collective-permute-start.4 = (bf16[1,384,128]{2,1,0:T(8,128)(2,1)S(1)}, bf16[1,384,128]{2,1,0:T(8,128)(2,1)S(1)}, u32[]{:S(2)}, u32[]{:S(2)}) collective-permute-start(bf16[1,384,128]{2,1,0:T(8,128)(2,1)S(1)} %maximum_bitcast_fusion.refs_1_), channel_id=1, source_target_pairs={{0,8},{4,12},{8,0},{12,4},{16,24},{20,28},{24,16},{28,20},{1,9},{5... | collective-permute-start | bytes 294920 | tf_op jit(solution)/shard_map/ppermute | solution.py:196
  14.0 1.5 %collective-permute-start.5 = (bf16[1,384,128]{2,1,0:T(8,128)(2,1)S(1)}, bf16[1,384,128]{2,1,0:T(8,128)(2,1)S(1)}, u32[]{:S(2)}, u32[]{:S(2)}) collective-permute-start(bf16[1,384,128]{2,1,0:T(8,128)(2,1)S(1)} %maximum_bitcast_fusion.refs_1_), channel_id=1, source_target_pairs={{0,16},{4,20},{8,24},{12,28},{16,0},{20,4},{24,8},{28,12},{1,17},{... | collective-permute-start | bytes 294920 | tf_op jit(solution)/shard_map/ppermute | solution.py:196
  15.5 0.0 collective-permute-done.6
  15.5 0.5 %collective-permute-start.3 = (bf16[1,384,128]{2,1,0:T(8,128)(2,1)S(1)}, bf16[1,384,128]{2,1,0:T(8,128)(2,1)S(1)}, u32[]{:S(2)}, u32[]{:S(2)}) collective-permute-start(bf16[1,384,128]{2,1,0:T(8,128)(2,1)S(1)} %maximum_bitcast_fusion.refs_1_), channel_id=1, source_target_pairs={{0,24},{4,28},{8,16},{12,20},{16,8},{20,12},{24,0},{28,4},{1,25},{... | collective-permute-start | bytes 294920 | tf_op jit(solution)/shard_map/ppermute | solution.py:196
  16.0 0.0 collective-permute-done.7
  16.0 1.0 %collective-permute-done.8 = bf16[144,128]{1,0:T(8,128)(2,1)S(1)} collective-permute-done((bf16[144,128]{1,0:T(8,128)(2,1)S(1)}, bf16[144,128]{1,0:T(8,128)(2,1)S(1)}, u32[]{:S(2)}, u32[]{:S(2)}) %collective-permute-start.8) | collective-permute-done | bytes 36896 | tf_op jit(solution)/shard_map/ppermute | solution.py:196
  17.0 0.1 collective-permute-start.9
  17.1 0.5 %collective-permute-start.10 = (bf16[1,384,128]{2,1,0:T(8,128)(2,1)S(1)}, bf16[1,384,128]{2,1,0:T(8,128)(2,1)S(1)}, u32[]{:S(2)}, u32[]{:S(2)}) collective-permute-start(bf16[1,384,128]{2,1,0:T(8,128)(2,1)S(1)} %maximum_bitcast_fusion.refs_1_), channel_id=1, source_target_pairs={{0,4},{4,0},{8,12},{12,8},{16,20},{20,16},{24,28},{28,24},{1,5},{5... | collective-permute-start | bytes 294920 | tf_op jit(solution)/shard_map/ppermute | solution.py:196
  17.6 0.0 copy-done
  17.6 0.1 constant_dynamic-slice_fusion
  17.7 0.2 shard_map.47.query_ref
  17.9 0.9 %shard_map.48 = (f32[1,1024]{1,0:T(1,128)S(1)}, f32[1,1024]{1,0:T(1,128)S(1)}, f32[128,1024]{1,0:T(8,128)S(1)}) custom-call(bf16[144,128]{1,0:T(8,128)(2,1)S(1)} %get-tuple-element.60.own_ref, bf16[256,1024]{1,0:T(8,128)(2,1)S(1)} %shard_map.47.query_ref, bf16[4,144,128]{2,1,0:T(8,128)(2,1)S(1)} %pad_maximum_fusion.refs_0_.refs_3_, ...), custom_call_target="tpu_custom_call" | custom-call | flops 1000000000 | tf_op jit(solution)/shard_map/pallas_call | solution.py:149
  18.8 0.0 collective-permute-done.10.refs_4_
  18.8 0.0 collective-permute-done.9.refs_3_.refs_4_
  18.8 0.9 %shard_map.49 = (f32[1,1024]{1,0:T(1,128)S(1)}, f32[1,1024]{1,0:T(1,128)S(1)}, f32[128,1024]{1,0:T(8,128)S(1)}) custom-call(bf16[144,128]{1,0:T(8,128)(2,1)S(1)} %get-tuple-element.60.own_ref, bf16[256,1024]{1,0:T(8,128)(2,1)S(1)} %shard_map.47.query_ref, f32[1,1024]{1,0:T(1,128)S(1)} %get-tuple-element.36.refs_0_, f32[1,1024]{1,0:T(1,128)S(1)} %get-tuple-element.37.refs_1_, ...), custom_call_target="tpu_custom_call" | custom-call | tf_op jit(solution)/shard_map/pallas_call | solution.py:149
  19.8 0.0 collective-permute-done.4.refs_4_
  19.8 0.0 collective-permute-done.5.refs_5_
  19.8 0.1 collective-permute-start.11
  19.9 0.4 %collective-permute-start.12 = (bf16[1,384,128]{2,1,0:T(8,128)(2,1)S(1)}, bf16[1,384,128]{2,1,0:T(8,128)(2,1)S(1)}, u32[]{:S(2)}, u32[]{:S(2)}) collective-permute-start(bf16[1,384,128]{2,1,0:T(8,128)(2,1)S(1)} %collective-permute-done.5.refs_5_), channel_id=1, source_target_pairs={{0,4},{4,0},{8,12},{12,8},{16,20},{20,16},{24,28},{28,24},{1,5},{5... | collective-permute-start | bytes 294920 | tf_op jit(solution)/shard_map/ppermute | solution.py:196
  20.4 0.8 %shard_map.50 = (f32[1,1024]{1,0:T(1,128)S(1)}, f32[1,1024]{1,0:T(1,128)S(1)}, f32[128,1024]{1,0:T(8,128)S(1)}) custom-call(bf16[144,128]{1,0:T(8,128)(2,1)S(1)} %get-tuple-element.60.own_ref, bf16[256,1024]{1,0:T(8,128)(2,1)S(1)} %shard_map.47.query_ref, f32[1,1024]{1,0:T(1,128)S(1)} %get-tuple-element.44.refs_0_, f32[1,1024]{1,0:T(1,128)S(1)} %get-tuple-element.45.refs_1_, ...), custom_call_target="tpu_custom_call" | custom-call | tf_op jit(solution)/shard_map/pallas_call | solution.py:149
  21.2 0.0 collective-permute-done.3.refs_5_
  21.2 0.1 collective-permute-start.13
  21.3 0.0 collective-permute-done.11.refs_6_
  21.3 0.0 collective-permute-done.12.refs_7_
  21.3 1.1 %shard_map.51 = (f32[1,1024]{1,0:T(1,128)S(1)}, f32[1,1024]{1,0:T(1,128)S(1)}, f32[128,1024]{1,0:T(8,128)S(1)}) custom-call(bf16[144,128]{1,0:T(8,128)(2,1)S(1)} %get-tuple-element.60.own_ref, bf16[256,1024]{1,0:T(8,128)(2,1)S(1)} %shard_map.47.query_ref, f32[1,1024]{1,0:T(1,128)S(1)} %get-tuple-element.52.refs_0_, f32[1,1024]{1,0:T(1,128)S(1)} %get-tuple-element.53.refs_1_, ...), custom_call_target="tpu_custom_call" | custom-call | tf_op jit(solution)/shard_map/pallas_call | solution.py:149
  22.4 0.1 collective-permute-done.13.refs_4_
  22.6 1.3 %shard_map.52 = bf16[1024,128]{1,0:T(8,128)(2,1)} custom-call(bf16[144,128]{1,0:T(8,128)(2,1)S(1)} %get-tuple-element.60.own_ref, bf16[256,1024]{1,0:T(8,128)(2,1)S(1)} %shard_map.47.query_ref, f32[1,1024]{1,0:T(1,128)S(1)} %get-tuple-element.56.refs_0_, f32[1,1024]{1,0:T(1,128)S(1)} %get-tuple-element.57.refs_1_, ...), custom_call_target="tpu_custom_call" | custom-call | tf_op jit(solution)/shard_map/pallas_call | solution.py:149
  (3 shorter events, 0.0 us)
Async XLA Ops:
  0.0 17.6 %copy-start = (bf16[256,16,128]{2,1,0:T(8,128)(2,1)S(1)}, bf16[256,16,128]{2,1,0:T(8,128)(2,1)}, u32[]{:S(2)}) copy-start(bf16[256,16,128]{2,1,0:T(8,128)(2,1)} %param.4) | copy-start | bytes 3145732
  1.1 10.8 %collective-permute-start = (bf16[128,128]{1,0:T(8,128)(2,1)S(1)}, bf16[128,128]{1,0:T(8,128)(2,1)S(1)}, u32[]{:S(2)}, u32[]{:S(2)}) collective-permute-start(bf16[128,128]{1,0:T(8,128)(2,1)S(1)} %get-tuple-element.33), channel_id=1, source_target_pairs={{0,1},{1,2},{2,3},{3,0},{4,5},{5,6},{6,7},{7,4},{8,9},{9,10},{10,1... | collective-permute-start | bytes 98312 | tf_op jit(solution)/shard_map/ppermute | solution.py:187
  4.2 8.2 %collective-permute-start.1 = (bf16[128,128]{1,0:T(8,128)(2,1)S(1)}, bf16[128,128]{1,0:T(8,128)(2,1)S(1)}, u32[]{:S(2)}, u32[]{:S(2)}) collective-permute-start(bf16[128,128]{1,0:T(8,128)(2,1)S(1)} %get-tuple-element.34), channel_id=1, source_target_pairs={{0,2},{1,3},{2,0},{3,1},{4,6},{5,7},{6,4},{7,5},{8,10},{9,11},{10,... | collective-permute-start | bytes 98312 | tf_op jit(solution)/shard_map/ppermute | solution.py:187
  6.8 5.6 %collective-permute-start.2 = (bf16[128,128]{1,0:T(8,128)(2,1)S(1)}, bf16[128,128]{1,0:T(8,128)(2,1)S(1)}, u32[]{:S(2)}, u32[]{:S(2)}) collective-permute-start(bf16[128,128]{1,0:T(8,128)(2,1)S(1)} %get-tuple-element.35), channel_id=1, source_target_pairs={{0,3},{1,0},{2,1},{3,2},{4,7},{5,4},{6,5},{7,6},{8,11},{9,8},{10,9... | collective-permute-start | bytes 98312 | tf_op jit(solution)/shard_map/ppermute | solution.py:187
  8.8 6.7 %collective-permute-start.6 = (bf16[144,128]{1,0:T(8,128)(2,1)S(1)}, bf16[144,128]{1,0:T(8,128)(2,1)S(1)}, u32[]{:S(2)}, u32[]{:S(2)}) collective-permute-start(bf16[144,128]{1,0:T(8,128)(2,1)S(1)} %get-tuple-element.60.own_ref), channel_id=1, source_target_pairs={{0,8},{4,12},{8,0},{12,4},{16,24},{20,28},{24,16},{28,20},{1,9},{5... | collective-permute-start | bytes 110600 | tf_op jit(solution)/shard_map/ppermute | solution.py:196
  10.4 5.6 %collective-permute-start.7 = (bf16[144,128]{1,0:T(8,128)(2,1)S(1)}, bf16[144,128]{1,0:T(8,128)(2,1)S(1)}, u32[]{:S(2)}, u32[]{:S(2)}) collective-permute-start(bf16[144,128]{1,0:T(8,128)(2,1)S(1)} %get-tuple-element.60.own_ref), channel_id=1, source_target_pairs={{0,16},{4,20},{8,24},{12,28},{16,0},{20,4},{24,8},{28,12},{1,17},{... | collective-permute-start | bytes 110600 | tf_op jit(solution)/shard_map/ppermute | solution.py:196
  11.9 5.0 %collective-permute-start.8 = (bf16[144,128]{1,0:T(8,128)(2,1)S(1)}, bf16[144,128]{1,0:T(8,128)(2,1)S(1)}, u32[]{:S(2)}, u32[]{:S(2)}) collective-permute-start(bf16[144,128]{1,0:T(8,128)(2,1)S(1)} %get-tuple-element.60.own_ref), channel_id=1, source_target_pairs={{0,24},{4,28},{8,16},{12,20},{16,8},{20,12},{24,0},{28,4},{1,25},{... | collective-permute-start | bytes 110600 | tf_op jit(solution)/shard_map/ppermute | solution.py:196
  12.4 7.4 %collective-permute-start.4 = (bf16[1,384,128]{2,1,0:T(8,128)(2,1)S(1)}, bf16[1,384,128]{2,1,0:T(8,128)(2,1)S(1)}, u32[]{:S(2)}, u32[]{:S(2)}) collective-permute-start(bf16[1,384,128]{2,1,0:T(8,128)(2,1)S(1)} %maximum_bitcast_fusion.refs_1_), channel_id=1, source_target_pairs={{0,8},{4,12},{8,0},{12,4},{16,24},{20,28},{24,16},{28,20},{1,9},{5... | collective-permute-start | bytes 294920 | tf_op jit(solution)/shard_map/ppermute | solution.py:196
  14.0 5.8 %collective-permute-start.5 = (bf16[1,384,128]{2,1,0:T(8,128)(2,1)S(1)}, bf16[1,384,128]{2,1,0:T(8,128)(2,1)S(1)}, u32[]{:S(2)}, u32[]{:S(2)}) collective-permute-start(bf16[1,384,128]{2,1,0:T(8,128)(2,1)S(1)} %maximum_bitcast_fusion.refs_1_), channel_id=1, source_target_pairs={{0,16},{4,20},{8,24},{12,28},{16,0},{20,4},{24,8},{28,12},{1,17},{... | collective-permute-start | bytes 294920 | tf_op jit(solution)/shard_map/ppermute | solution.py:196
  15.5 5.7 %collective-permute-start.3 = (bf16[1,384,128]{2,1,0:T(8,128)(2,1)S(1)}, bf16[1,384,128]{2,1,0:T(8,128)(2,1)S(1)}, u32[]{:S(2)}, u32[]{:S(2)}) collective-permute-start(bf16[1,384,128]{2,1,0:T(8,128)(2,1)S(1)} %maximum_bitcast_fusion.refs_1_), channel_id=1, source_target_pairs={{0,24},{4,28},{8,16},{12,20},{16,8},{20,12},{24,0},{28,4},{1,25},{... | collective-permute-start | bytes 294920 | tf_op jit(solution)/shard_map/ppermute | solution.py:196
  17.0 1.8 %collective-permute-start.9 = (bf16[4,144,128]{2,1,0:T(8,128)(2,1)S(1)}, bf16[4,144,128]{2,1,0:T(8,128)(2,1)S(1)}, u32[]{:S(2)}, u32[]{:S(2)}) collective-permute-start(bf16[4,144,128]{2,1,0:T(8,128)(2,1)S(1)} %pad_maximum_fusion.refs_0_.refs_3_), channel_id=1, source_target_pairs={{0,4},{4,0},{8,12},{12,8},{16,20},{20,16},{24,28},{28,24},{1,5},{5... | collective-permute-start | bytes 442376 | tf_op jit(solution)/shard_map/ppermute | solution.py:196
  17.1 1.7 %collective-permute-start.10 = (bf16[1,384,128]{2,1,0:T(8,128)(2,1)S(1)}, bf16[1,384,128]{2,1,0:T(8,128)(2,1)S(1)}, u32[]{:S(2)}, u32[]{:S(2)}) collective-permute-start(bf16[1,384,128]{2,1,0:T(8,128)(2,1)S(1)} %maximum_bitcast_fusion.refs_1_), channel_id=1, source_target_pairs={{0,4},{4,0},{8,12},{12,8},{16,20},{20,16},{24,28},{28,24},{1,5},{5... | collective-permute-start | bytes 294920 | tf_op jit(solution)/shard_map/ppermute | solution.py:196
  19.8 1.6 %collective-permute-start.11 = (bf16[1,384,128]{2,1,0:T(8,128)(2,1)S(1)}, bf16[1,384,128]{2,1,0:T(8,128)(2,1)S(1)}, u32[]{:S(2)}, u32[]{:S(2)}) collective-permute-start(bf16[1,384,128]{2,1,0:T(8,128)(2,1)S(1)} %collective-permute-done.4.refs_4_), channel_id=1, source_target_pairs={{0,4},{4,0},{8,12},{12,8},{16,20},{20,16},{24,28},{28,24},{1,5},{5... | collective-permute-start | bytes 294920 | tf_op jit(solution)/shard_map/ppermute | solution.py:196
  19.9 1.4 %collective-permute-start.12 = (bf16[1,384,128]{2,1,0:T(8,128)(2,1)S(1)}, bf16[1,384,128]{2,1,0:T(8,128)(2,1)S(1)}, u32[]{:S(2)}, u32[]{:S(2)}) collective-permute-start(bf16[1,384,128]{2,1,0:T(8,128)(2,1)S(1)} %collective-permute-done.5.refs_5_), channel_id=1, source_target_pairs={{0,4},{4,0},{8,12},{12,8},{16,20},{20,16},{24,28},{28,24},{1,5},{5... | collective-permute-start | bytes 294920 | tf_op jit(solution)/shard_map/ppermute | solution.py:196
  21.2 1.4 %collective-permute-start.13 = (bf16[1,384,128]{2,1,0:T(8,128)(2,1)S(1)}, bf16[1,384,128]{2,1,0:T(8,128)(2,1)S(1)}, u32[]{:S(2)}, u32[]{:S(2)}) collective-permute-start(bf16[1,384,128]{2,1,0:T(8,128)(2,1)S(1)} %collective-permute-done.3.refs_5_), channel_id=1, source_target_pairs={{0,4},{4,0},{8,12},{12,8},{16,20},{20,16},{24,28},{28,24},{1,5},{5... | collective-permute-start | bytes 294920 | tf_op jit(solution)/shard_map/ppermute | solution.py:196

commit v14 on v13

--- a/solution.py
+++ b/solution.py
@@ -197,38 +197,54 @@
 
     if blocks == 8:
         rest = rest[None]
-        mine = jnp.stack([own] + [swap(own, flip) for flip in (2, 4, 6)])
-        rests = [swap(rest, flip) for flip in (2, 4, 6)]
+        near_x, near_y, near_far = [swap(own, flip) for flip in (2, 4, 6)]
+        mine = jnp.stack([own, near_x, near_y])
+        along_x, along_y, across = [swap(rest, flip) for flip in (2, 4, 6)]
 
         def small(data, slots):
             return [(data, slot, (0,), None, (data, slot, 2 * part)) for slot in slots]
 
-        def large(data, mark, slot):
-            return (data, 0, offsets[:-1], None, (mark, slot, 2 * part))
+        def large(data, mark, slot, at=0):
+            return (data, 0, tuple(at + offset for offset in offsets[:-1]), None, (mark, slot, 2 * part))
 
         state = fold(
             None,
             [mine, rest],
-            [(0, 0, (0,), shifts[:1], None), (1, 0, offsets[:-1], shifts[1:], None)] + small(0, range(1, 4)),
+            [(0, 0, (0,), shifts[:1], None), (1, 0, offsets[:-1], shifts[1:], None)] + small(0, (1, 2)),
             False,
             1000000000,
         )
-        mine, rest = lax.optimization_barrier((mine, rest))
-        mine_other, rest_other = swap(mine, 1), swap(rest, 1)
-        state = fold(state, [mine_other, rest_other], small(0, range(4)) + [large(1, 0, 0)], False)
-        along_x, along_y, across = rests
+        early_rows = mine.shape[0] * mine.shape[1]
+        both_other = swap(jnp.concatenate([mine.reshape(1, early_rows, head_width), rest], axis=1), 1)
+        size = own.shape[0]
+        state = fold(
+            state,
+            [both_other, near_far[None]],
+            [(0, 0, (size * i,), None, (0, 0, size * i + 2 * part)) for i in range(3)]
+            + [(0, 0, tuple(early_rows + offset for offset in offsets[:-1]), None, (0, 0, 2 * part))]
+            + small(1, (0,)),
+            False,
+            0000000,
+        )
         along_x, along_y, state = lax.optimization_barrier((along_x, along_y, state))
         others = [swap(rows, 1) for rows in (along_x, along_y)]
         state = fold(state, [mine, along_x, along_y], [large(i, 0, i) for i in (1, 2)], False)
         across, state = lax.optimization_barrier((across, state))
+        across = jnp.concatenate([near_far[None], across], axis=1)
+        across = lax.optimization_barrier((across, *(others if isinstance(others, list) else [others])))[0]
         other_across = swap(across, 1)
         state = fold(
             state,
-            [mine, mine_other, across] + others,
-            [large(2, 0, 3)] + [large(2 + i, 1, i) for i in (1, 2)],
+            [across, both_other] + others,
+            [large(0, 0, 0, size)] + [(1 + i, 0, offsets[:-1], None, (1, 0, size * i + 2 * part)) for i in (1, 2)],
             False,
         )
-        result = fold(state, [mine_other, other_across], [large(1, 0, 3)], True)
+        result = fold(
+            state,
+            [other_across],
+            [(0, 0, (0,) + tuple(own.shape[0] + offset for offset in offsets[:-1]), None, (0, 0, 2 * part))],
+            True,
+        )
     else:
         block = jnp.concatenate([own[: 2 * part], rest, own[2 * part :]])
         far = lax.all_gather(block, "seq", axis=0, tiled=False)

time: 24 us -> 24 us (level)
  starting transfers between devices: 15.4 us -> 14.8 us
  waiting for transfers between devices: 1.15 us -> 1.64 us
    ppermute x11 -> x10, starting transfers between devices: 8.4 us -> 7.83 us  [swap(): return lax.ppermute(rows, 'seq', [(i, i ^ flip) for i in range(blocks)])]
    ppermute x11 -> x10, waiting for transfers between devices: 1.15 us -> 1.63 us  [swap(): return lax.ppermute(rows, 'seq', [(i, i ^ flip) for i in range(blocks)])]
  transfers between devices with their start and end apart: 14 -> 13, of which waited for: 2 -> 4; matrix products, arithmetic and copies ran while one was open for 1% -> 1% of each run, Pallas kernels for 16% -> 16%
where the time goes in v14:
time: 24 us; the launch traced here: 23.9 us
  starting transfers between devices  14.8 us (62%)
  Pallas kernels  5.43 us (23%)
  waiting for transfers between devices  1.64 us (7%)
  other arithmetic  1 us (4%)
  between operations  0.8 us (3%)
    ppermute x10, starting transfers between devices, swap(): return lax.ppermute(rows, 'seq', [(i, i ^ flip) for i in range(blocks)])  7.83 us
    ppermute x3, starting transfers between devices, shards(): lax.ppermute(rows, 'head', [(i, (i + shift + 1) % pieces) for i in range(...  7.01 us
    pallas_call x5, Pallas kernels, attend_call(): pl.pallas_call(functools.partial(attend, pieces, part, first, last, items...  5.07 us
    ppermute x10, waiting for transfers between devices, swap(): return lax.ppermute(rows, 'seq', [(i, i ^ flip) for i in range(blocks)])  1.63 us
    concatenate x1, other arithmetic, shards(): jnp.concatenate([keys, values]).reshape(2 * part * kv_heads, head_width)  0.95 us
  transfers between devices with their start and end apart: 13, of which 4 were waited for; matrix products, arithmetic and copies ran while one was open for 1% of the time, Pallas kernels for 16%

profile of v14, /device:TPU:0, one launch (start us, length us, event | category | flops | bytes accessed | tf_op | source)
XLA Modules:
  0.0 23.9 jit_solution(16000247631173527680)
XLA Ops:
  0.0 0.0 copy-start
  0.0 1.0 %pad_maximum_fusion.3 = bf16[128,2,128]{2,1,0:T(2,128)(2,1)S(1)} fusion(bf16[64,2,128]{2,1,0:T(2,128)(2,1)} %param.6, bf16[64,2,128]{2,1,0:T(2,128)(2,1)} %param.5), kind=kLoop, calls=%fused_computation.4 | loop fusion | flops 32768 | bytes 131072 | tf_op jit(solution)/shard_map/concatenate | solution.py:183
  1.0 0.2 shard_map.46
  1.1 3.1 %collective-permute-start = (bf16[128,128]{1,0:T(8,128)(2,1)S(1)}, bf16[128,128]{1,0:T(8,128)(2,1)S(1)}, u32[]{:S(2)}, u32[]{:S(2)}) collective-permute-start(bf16[128,128]{1,0:T(8,128)(2,1)S(1)} %get-tuple-element.32), channel_id=1, source_target_pairs={{0,1},{1,2},{2,3},{3,0},{4,5},{5,6},{6,7},{7,4},{8,9},{9,10},{10,1... | collective-permute-start | bytes 98312 | tf_op jit(solution)/shard_map/ppermute | solution.py:187
  4.2 2.6 %collective-permute-start.1 = (bf16[128,128]{1,0:T(8,128)(2,1)S(1)}, bf16[128,128]{1,0:T(8,128)(2,1)S(1)}, u32[]{:S(2)}, u32[]{:S(2)}) collective-permute-start(bf16[128,128]{1,0:T(8,128)(2,1)S(1)} %get-tuple-element.33), channel_id=1, source_target_pairs={{0,2},{1,3},{2,0},{3,1},{4,6},{5,7},{6,4},{7,5},{8,10},{9,11},{10,... | collective-permute-start | bytes 98312 | tf_op jit(solution)/shard_map/ppermute | solution.py:187
  6.8 1.3 %collective-permute-start.2 = (bf16[128,128]{1,0:T(8,128)(2,1)S(1)}, bf16[128,128]{1,0:T(8,128)(2,1)S(1)}, u32[]{:S(2)}, u32[]{:S(2)}) collective-permute-start(bf16[128,128]{1,0:T(8,128)(2,1)S(1)} %get-tuple-element.34), channel_id=1, source_target_pairs={{0,3},{1,0},{2,1},{3,2},{4,7},{5,4},{6,5},{7,6},{8,11},{9,8},{10,9... | collective-permute-start | bytes 98312 | tf_op jit(solution)/shard_map/ppermute | solution.py:187
  8.8 2.5 %collective-permute-start.9 = (bf16[144,128]{1,0:T(8,128)(2,1)S(1)}, bf16[144,128]{1,0:T(8,128)(2,1)S(1)}, u32[]{:S(2)}, u32[]{:S(2)}) collective-permute-start(bf16[144,128]{1,0:T(8,128)(2,1)S(1)} %get-tuple-element.58.own_ref), channel_id=1, source_target_pairs={{0,24},{4,28},{8,16},{12,20},{16,8},{20,12},{24,0},{28,4},{1,25},{... | collective-permute-start | bytes 110600 | tf_op jit(solution)/shard_map/ppermute | solution.py:196
  11.3 0.5 %collective-permute-start.7 = (bf16[144,128]{1,0:T(8,128)(2,1)S(1)}, bf16[144,128]{1,0:T(8,128)(2,1)S(1)}, u32[]{:S(2)}, u32[]{:S(2)}) collective-permute-start(bf16[144,128]{1,0:T(8,128)(2,1)S(1)} %get-tuple-element.58.own_ref), channel_id=1, source_target_pairs={{0,16},{4,20},{8,24},{12,28},{16,0},{20,4},{24,8},{28,12},{1,17},{... | collective-permute-start | bytes 110600 | tf_op jit(solution)/shard_map/ppermute | solution.py:196
  11.8 0.0 collective-permute-done
  11.8 0.5 %collective-permute-start.6 = (bf16[144,128]{1,0:T(8,128)(2,1)S(1)}, bf16[144,128]{1,0:T(8,128)(2,1)S(1)}, u32[]{:S(2)}, u32[]{:S(2)}) collective-permute-start(bf16[144,128]{1,0:T(8,128)(2,1)S(1)} %get-tuple-element.58.own_ref), channel_id=1, source_target_pairs={{0,8},{4,12},{8,0},{12,4},{16,24},{20,28},{24,16},{28,20},{1,9},{5... | collective-permute-start | bytes 110600 | tf_op jit(solution)/shard_map/ppermute | solution.py:196
  12.4 0.0 collective-permute-done.1
  12.4 0.0 collective-permute-done.2
  12.4 1.6 %collective-permute-start.5 = (bf16[1,384,128]{2,1,0:T(8,128)(2,1)S(1)}, bf16[1,384,128]{2,1,0:T(8,128)(2,1)S(1)}, u32[]{:S(2)}, u32[]{:S(2)}) collective-permute-start(bf16[1,384,128]{2,1,0:T(8,128)(2,1)S(1)} %maximum_bitcast_fusion.refs_1_), channel_id=1, source_target_pairs={{0,16},{4,20},{8,24},{12,28},{16,0},{20,4},{24,8},{28,12},{1,17},{... | collective-permute-start | bytes 294920 | tf_op jit(solution)/shard_map/ppermute | solution.py:196
  14.0 1.5 %collective-permute-start.4 = (bf16[1,384,128]{2,1,0:T(8,128)(2,1)S(1)}, bf16[1,384,128]{2,1,0:T(8,128)(2,1)S(1)}, u32[]{:S(2)}, u32[]{:S(2)}) collective-permute-start(bf16[1,384,128]{2,1,0:T(8,128)(2,1)S(1)} %maximum_bitcast_fusion.refs_1_), channel_id=1, source_target_pairs={{0,8},{4,12},{8,0},{12,4},{16,24},{20,28},{24,16},{28,20},{1,9},{5... | collective-permute-start | bytes 294920 | tf_op jit(solution)/shard_map/ppermute | solution.py:196
  15.5 0.0 collective-permute-done.7
  15.5 0.5 %collective-permute-start.3 = (bf16[1,384,128]{2,1,0:T(8,128)(2,1)S(1)}, bf16[1,384,128]{2,1,0:T(8,128)(2,1)S(1)}, u32[]{:S(2)}, u32[]{:S(2)}) collective-permute-start(bf16[1,384,128]{2,1,0:T(8,128)(2,1)S(1)} %maximum_bitcast_fusion.refs_1_), channel_id=1, source_target_pairs={{0,24},{4,28},{8,16},{12,20},{16,8},{20,12},{24,0},{28,4},{1,25},{... | collective-permute-start | bytes 294920 | tf_op jit(solution)/shard_map/ppermute | solution.py:196
  16.0 0.2 collective-permute-done.6
  16.2 0.1 collective-permute-start.8
  16.3 0.0 copy-done
  16.3 0.1 constant_dynamic-slice_fusion
  16.5 0.2 shard_map.47.query_ref
  16.7 0.8 %shard_map.48 = (f32[1,1024]{1,0:T(1,128)S(1)}, f32[1,1024]{1,0:T(1,128)S(1)}, f32[128,1024]{1,0:T(8,128)S(1)}) custom-call(bf16[144,128]{1,0:T(8,128)(2,1)S(1)} %get-tuple-element.58.own_ref, bf16[256,1024]{1,0:T(8,128)(2,1)S(1)} %shard_map.47.query_ref, bf16[3,144,128]{2,1,0:T(8,128)(2,1)S(1)} %pad_maximum_fusion.2.refs_0_.refs_3_, ...), custom_call_target="tpu_custom_call" | custom-call | flops 1000000000 | tf_op jit(solution)/shard_map/pallas_call | solution.py:149
  17.5 0.0 collective-permute-done.9
  17.5 0.3 %collective-permute-done.8.refs_3_.refs_4_ = bf16[1,816,128]{2,1,0:T(8,128)(2,1)S(1)} collective-permute-done((bf16[1,816,128]{2,1,0:T(8,128)(2,1)S(1)}, bf16[1,816,128]{2,1,0:T(8,128)(2,1)S(1)}, u32[]{:S(2)}, u32[]{:S(2)}) %collective-permute-start.8) | collective-permute-done | bytes 208928 | tf_op jit(solution)/shard_map/ppermute | solution.py:196
  17.8 0.9 %shard_map.49 = (f32[1,1024]{1,0:T(1,128)S(1)}, f32[1,1024]{1,0:T(1,128)S(1)}, f32[128,1024]{1,0:T(8,128)S(1)}) custom-call(bf16[144,128]{1,0:T(8,128)(2,1)S(1)} %get-tuple-element.58.own_ref, bf16[256,1024]{1,0:T(8,128)(2,1)S(1)} %shard_map.47.query_ref, f32[1,1024]{1,0:T(1,128)S(1)} %get-tuple-element.35.refs_0_, f32[1,1024]{1,0:T(1,128)S(1)} %get-tuple-element.36.refs_1_, ...), custom_call_target="tpu_custom_call" | custom-call | tf_op jit(solution)/shard_map/pallas_call | solution.py:149
  18.7 0.0 collective-permute-done.5.refs_5_
  18.7 0.0 collective-permute-done.4.refs_4_
  18.7 0.3 %collective-permute-start.10 = (bf16[1,384,128]{2,1,0:T(8,128)(2,1)S(1)}, bf16[1,384,128]{2,1,0:T(8,128)(2,1)S(1)}, u32[]{:S(2)}, u32[]{:S(2)}) collective-permute-start(bf16[1,384,128]{2,1,0:T(8,128)(2,1)S(1)} %collective-permute-done.4.refs_4_), channel_id=1, source_target_pairs={{0,4},{4,0},{8,12},{12,8},{16,20},{20,16},{24,28},{28,24},{1,5},{5... | collective-permute-start | bytes 294920 | tf_op jit(solution)/shard_map/ppermute | solution.py:196
  19.0 0.3 %collective-permute-start.11 = (bf16[1,384,128]{2,1,0:T(8,128)(2,1)S(1)}, bf16[1,384,128]{2,1,0:T(8,128)(2,1)S(1)}, u32[]{:S(2)}, u32[]{:S(2)}) collective-permute-start(bf16[1,384,128]{2,1,0:T(8,128)(2,1)S(1)} %collective-permute-done.5.refs_5_), channel_id=1, source_target_pairs={{0,4},{4,0},{8,12},{12,8},{16,20},{20,16},{24,28},{28,24},{1,5},{5... | collective-permute-start | bytes 294920 | tf_op jit(solution)/shard_map/ppermute | solution.py:196
  19.3 0.8 %shard_map.50 = (f32[1,1024]{1,0:T(1,128)S(1)}, f32[1,1024]{1,0:T(1,128)S(1)}, f32[128,1024]{1,0:T(8,128)S(1)}) custom-call(bf16[144,128]{1,0:T(8,128)(2,1)S(1)} %get-tuple-element.58.own_ref, bf16[256,1024]{1,0:T(8,128)(2,1)S(1)} %shard_map.47.query_ref, f32[1,1024]{1,0:T(1,128)S(1)} %get-tuple-element.41.refs_0_, f32[1,1024]{1,0:T(1,128)S(1)} %get-tuple-element.42.refs_1_, ...), custom_call_target="tpu_custom_call" | custom-call | tf_op jit(solution)/shard_map/pallas_call | solution.py:149
  20.1 0.9 %collective-permute-done.3 = bf16[1,384,128]{2,1,0:T(8,128)(2,1)S(1)} collective-permute-done((bf16[1,384,128]{2,1,0:T(8,128)(2,1)S(1)}, bf16[1,384,128]{2,1,0:T(8,128)(2,1)S(1)}, u32[]{:S(2)}, u32[]{:S(2)}) %collective-permute-start.3) | collective-permute-done | bytes 98336 | tf_op jit(solution)/shard_map/ppermute | solution.py:196
  21.0 0.0 collective-permute-done.10.refs_5_
  21.0 0.0 collective-permute-done.11.refs_6_
  21.0 0.1 collective-permute-start.12
  21.1 1.1 %shard_map.51 = (f32[1,1024]{1,0:T(1,128)S(1)}, f32[1,1024]{1,0:T(1,128)S(1)}, f32[128,1024]{1,0:T(8,128)S(1)}) custom-call(bf16[144,128]{1,0:T(8,128)(2,1)S(1)} %get-tuple-element.58.own_ref, bf16[256,1024]{1,0:T(8,128)(2,1)S(1)} %shard_map.47.query_ref, f32[1,1024]{1,0:T(1,128)S(1)} %get-tuple-element.49.refs_0_, f32[1,1024]{1,0:T(1,128)S(1)} %get-tuple-element.50.refs_1_, ...), custom_call_target="tpu_custom_call" | custom-call | tf_op jit(solution)/shard_map/pallas_call | solution.py:149
  22.2 0.3 %collective-permute-done.12.refs_3_ = bf16[1,528,128]{2,1,0:T(8,128)(2,1)S(1)} collective-permute-done((bf16[1,528,128]{2,1,0:T(8,128)(2,1)S(1)}, bf16[1,528,128]{2,1,0:T(8,128)(2,1)S(1)}, u32[]{:S(2)}, u32[]{:S(2)}) %collective-permute-start.12) | collective-permute-done | bytes 135200 | tf_op jit(solution)/shard_map/ppermute | solution.py:196
  22.5 1.4 %shard_map.52 = bf16[1024,128]{1,0:T(8,128)(2,1)} custom-call(bf16[144,128]{1,0:T(8,128)(2,1)S(1)} %get-tuple-element.58.own_ref, bf16[256,1024]{1,0:T(8,128)(2,1)S(1)} %shard_map.47.query_ref, f32[1,1024]{1,0:T(1,128)S(1)} %get-tuple-element.54.refs_0_, f32[1,1024]{1,0:T(1,128)S(1)} %get-tuple-element.55.refs_1_, ...), custom_call_target="tpu_custom_call" | custom-call | tf_op jit(solution)/shard_map/pallas_call | solution.py:149
  (5 shorter events, 0.1 us)
Async XLA Ops:
  0.0 16.3 %copy-start = (bf16[256,16,128]{2,1,0:T(8,128)(2,1)S(1)}, bf16[256,16,128]{2,1,0:T(8,128)(2,1)}, u32[]{:S(2)}) copy-start(bf16[256,16,128]{2,1,0:T(8,128)(2,1)} %param.4) | copy-start | bytes 3145732
  1.1 10.7 %collective-permute-start = (bf16[128,128]{1,0:T(8,128)(2,1)S(1)}, bf16[128,128]{1,0:T(8,128)(2,1)S(1)}, u32[]{:S(2)}, u32[]{:S(2)}) collective-permute-start(bf16[128,128]{1,0:T(8,128)(2,1)S(1)} %get-tuple-element.32), channel_id=1, source_target_pairs={{0,1},{1,2},{2,3},{3,0},{4,5},{5,6},{6,7},{7,4},{8,9},{9,10},{10,1... | collective-permute-start | bytes 98312 | tf_op jit(solution)/shard_map/ppermute | solution.py:187
  4.2 8.2 %collective-permute-start.1 = (bf16[128,128]{1,0:T(8,128)(2,1)S(1)}, bf16[128,128]{1,0:T(8,128)(2,1)S(1)}, u32[]{:S(2)}, u32[]{:S(2)}) collective-permute-start(bf16[128,128]{1,0:T(8,128)(2,1)S(1)} %get-tuple-element.33), channel_id=1, source_target_pairs={{0,2},{1,3},{2,0},{3,1},{4,6},{5,7},{6,4},{7,5},{8,10},{9,11},{10,... | collective-permute-start | bytes 98312 | tf_op jit(solution)/shard_map/ppermute | solution.py:187
  6.8 5.6 %collective-permute-start.2 = (bf16[128,128]{1,0:T(8,128)(2,1)S(1)}, bf16[128,128]{1,0:T(8,128)(2,1)S(1)}, u32[]{:S(2)}, u32[]{:S(2)}) collective-permute-start(bf16[128,128]{1,0:T(8,128)(2,1)S(1)} %get-tuple-element.34), channel_id=1, source_target_pairs={{0,3},{1,0},{2,1},{3,2},{4,7},{5,4},{6,5},{7,6},{8,11},{9,8},{10,9... | collective-permute-start | bytes 98312 | tf_op jit(solution)/shard_map/ppermute | solution.py:187
  8.8 8.7 %collective-permute-start.9 = (bf16[144,128]{1,0:T(8,128)(2,1)S(1)}, bf16[144,128]{1,0:T(8,128)(2,1)S(1)}, u32[]{:S(2)}, u32[]{:S(2)}) collective-permute-start(bf16[144,128]{1,0:T(8,128)(2,1)S(1)} %get-tuple-element.58.own_ref), channel_id=1, source_target_pairs={{0,24},{4,28},{8,16},{12,20},{16,8},{20,12},{24,0},{28,4},{1,25},{... | collective-permute-start | bytes 110600 | tf_op jit(solution)/shard_map/ppermute | solution.py:196
  11.3 4.1 %collective-permute-start.7 = (bf16[144,128]{1,0:T(8,128)(2,1)S(1)}, bf16[144,128]{1,0:T(8,128)(2,1)S(1)}, u32[]{:S(2)}, u32[]{:S(2)}) collective-permute-start(bf16[144,128]{1,0:T(8,128)(2,1)S(1)} %get-tuple-element.58.own_ref), channel_id=1, source_target_pairs={{0,16},{4,20},{8,24},{12,28},{16,0},{20,4},{24,8},{28,12},{1,17},{... | collective-permute-start | bytes 110600 | tf_op jit(solution)/shard_map/ppermute | solution.py:196
  11.8 4.3 %collective-permute-start.6 = (bf16[144,128]{1,0:T(8,128)(2,1)S(1)}, bf16[144,128]{1,0:T(8,128)(2,1)S(1)}, u32[]{:S(2)}, u32[]{:S(2)}) collective-permute-start(bf16[144,128]{1,0:T(8,128)(2,1)S(1)} %get-tuple-element.58.own_ref), channel_id=1, source_target_pairs={{0,8},{4,12},{8,0},{12,4},{16,24},{20,28},{24,16},{28,20},{1,9},{5... | collective-permute-start | bytes 110600 | tf_op jit(solution)/shard_map/ppermute | solution.py:196
  12.4 6.3 %collective-permute-start.5 = (bf16[1,384,128]{2,1,0:T(8,128)(2,1)S(1)}, bf16[1,384,128]{2,1,0:T(8,128)(2,1)S(1)}, u32[]{:S(2)}, u32[]{:S(2)}) collective-permute-start(bf16[1,384,128]{2,1,0:T(8,128)(2,1)S(1)} %maximum_bitcast_fusion.refs_1_), channel_id=1, source_target_pairs={{0,16},{4,20},{8,24},{12,28},{16,0},{20,4},{24,8},{28,12},{1,17},{... | collective-permute-start | bytes 294920 | tf_op jit(solution)/shard_map/ppermute | solution.py:196
  14.0 4.7 %collective-permute-start.4 = (bf16[1,384,128]{2,1,0:T(8,128)(2,1)S(1)}, bf16[1,384,128]{2,1,0:T(8,128)(2,1)S(1)}, u32[]{:S(2)}, u32[]{:S(2)}) collective-permute-start(bf16[1,384,128]{2,1,0:T(8,128)(2,1)S(1)} %maximum_bitcast_fusion.refs_1_), channel_id=1, source_target_pairs={{0,8},{4,12},{8,0},{12,4},{16,24},{20,28},{24,16},{28,20},{1,9},{5... | collective-permute-start | bytes 294920 | tf_op jit(solution)/shard_map/ppermute | solution.py:196
  15.5 5.5 %collective-permute-start.3 = (bf16[1,384,128]{2,1,0:T(8,128)(2,1)S(1)}, bf16[1,384,128]{2,1,0:T(8,128)(2,1)S(1)}, u32[]{:S(2)}, u32[]{:S(2)}) collective-permute-start(bf16[1,384,128]{2,1,0:T(8,128)(2,1)S(1)} %maximum_bitcast_fusion.refs_1_), channel_id=1, source_target_pairs={{0,24},{4,28},{8,16},{12,20},{16,8},{20,12},{24,0},{28,4},{1,25},{... | collective-permute-start | bytes 294920 | tf_op jit(solution)/shard_map/ppermute | solution.py:196
  16.2 1.5 %collective-permute-start.8 = (bf16[1,816,128]{2,1,0:T(8,128)(2,1)S(1)}, bf16[1,816,128]{2,1,0:T(8,128)(2,1)S(1)}, u32[]{:S(2)}, u32[]{:S(2)}) collective-permute-start(bf16[1,816,128]{2,1,0:T(8,128)(2,1)S(1)} %pad_maximum_fusion), channel_id=1, source_target_pairs={{0,4},{4,0},{8,12},{12,8},{16,20},{20,16},{24,28},{28,24},{1,5},{5... | collective-permute-start | bytes 626696 | tf_op jit(solution)/shard_map/ppermute | solution.py:196
  18.7 2.3 %collective-permute-start.10 = (bf16[1,384,128]{2,1,0:T(8,128)(2,1)S(1)}, bf16[1,384,128]{2,1,0:T(8,128)(2,1)S(1)}, u32[]{:S(2)}, u32[]{:S(2)}) collective-permute-start(bf16[1,384,128]{2,1,0:T(8,128)(2,1)S(1)} %collective-permute-done.4.refs_4_), channel_id=1, source_target_pairs={{0,4},{4,0},{8,12},{12,8},{16,20},{20,16},{24,28},{28,24},{1,5},{5... | collective-permute-start | bytes 294920 | tf_op jit(solution)/shard_map/ppermute | solution.py:196
  19.0 2.0 %collective-permute-start.11 = (bf16[1,384,128]{2,1,0:T(8,128)(2,1)S(1)}, bf16[1,384,128]{2,1,0:T(8,128)(2,1)S(1)}, u32[]{:S(2)}, u32[]{:S(2)}) collective-permute-start(bf16[1,384,128]{2,1,0:T(8,128)(2,1)S(1)} %collective-permute-done.5.refs_5_), channel_id=1, source_target_pairs={{0,4},{4,0},{8,12},{12,8},{16,20},{20,16},{24,28},{28,24},{1,5},{5... | collective-permute-start | bytes 294920 | tf_op jit(solution)/shard_map/ppermute | solution.py:196
  21.0 1.4 %collective-permute-start.12 = (bf16[1,528,128]{2,1,0:T(8,128)(2,1)S(1)}, bf16[1,528,128]{2,1,0:T(8,128)(2,1)S(1)}, u32[]{:S(2)}, u32[]{:S(2)}) collective-permute-start(bf16[1,528,128]{2,1,0:T(8,128)(2,1)S(1)} %pad_maximum_fusion.1.refs_3_), channel_id=1, source_target_pairs={{0,4},{4,0},{8,12},{12,8},{16,20},{20,16},{24,28},{28,24},{1,5},{5... | collective-permute-start | bytes 405512 | tf_op jit(solution)/shard_map/ppermute | solution.py:196

commit v15 on v14

--- a/solution.py
+++ b/solution.py
@@ -11,6 +11,7 @@
 MARK = 16
 SUBLANES = 8
 FINAL = 256
+OVERLAP = 1000000000
 LOW = -1e30
 HIGH = 1e30
 MIB = 1024 * 1024
@@ -197,9 +198,14 @@
 
     if blocks == 8:
         rest = rest[None]
-        near_x, near_y, near_far = [swap(own, flip) for flip in (2, 4, 6)]
-        mine = jnp.stack([own, near_x, near_y])
-        along_x, along_y, across = [swap(rest, flip) for flip in (2, 4, 6)]
+
+        def hop(rows, even, odd):
+            return lax.ppermute(rows, "seq", [(i, i ^ (odd if i & 1 else even)) for i in range(blocks)])
+
+        near_one, near_two, near_far = hop(own, 2, 4), hop(own, 4, 2), swap(own, 6)
+        mine = jnp.stack([own, near_one, near_two])
+        along_one, along_two = hop(rest, 2, 4), hop(rest, 4, 2)
+        across = hop(along_one, 4, 2)
 
         def small(data, slots):
             return [(data, slot, (0,), None, (data, slot, 2 * part)) for slot in slots]
@@ -212,7 +218,7 @@
             [mine, rest],
             [(0, 0, (0,), shifts[:1], None), (1, 0, offsets[:-1], shifts[1:], None)] + small(0, (1, 2)),
             False,
-            1000000000,
+            OVERLAP,
         )
         early_rows = mine.shape[0] * mine.shape[1]
         both_other = swap(jnp.concatenate([mine.reshape(1, early_rows, head_width), rest], axis=1), 1)
@@ -224,14 +230,14 @@
             + [(0, 0, tuple(early_rows + offset for offset in offsets[:-1]), None, (0, 0, 2 * part))]
             + small(1, (0,)),
             False,
-            0000000,
-        )
-        along_x, along_y, state = lax.optimization_barrier((along_x, along_y, state))
-        others = [swap(rows, 1) for rows in (along_x, along_y)]
-        state = fold(state, [mine, along_x, along_y], [large(i, 0, i) for i in (1, 2)], False)
+            0,
+        )
+        along_one, along_two, state = lax.optimization_barrier((along_one, along_two, state))
+        others = [swap(rows, 1) for rows in (along_one, along_two)]
+        state = fold(state, [mine, along_one, along_two], [large(i, 0, i) for i in (1, 2)], False, OVERLAP)
         across, state = lax.optimization_barrier((across, state))
         across = jnp.concatenate([near_far[None], across], axis=1)
-        across = lax.optimization_barrier((across, *(others if isinstance(others, list) else [others])))[0]
+        across, *others = lax.optimization_barrier((across, *others))
         other_across = swap(across, 1)
         state = fold(
             state,

time: 24 us -> 24.9 us (1.037)
  starting transfers between devices: 14.8 us -> 16.2 us
  waiting for transfers between devices: 1.64 us -> 1.23 us
    ppermute x0 -> x5, starting transfers between devices: none -> 7.67 us  [hop(): lax.ppermute(rows, 'seq', [(i, i ^ (odd if i & 1 else even)) for i in ran...]
    ppermute x10 -> x5, starting transfers between devices: 7.83 us -> 1.47 us  [swap(): return lax.ppermute(rows, 'seq', [(i, i ^ flip) for i in range(blocks)])]
    ppermute x10 -> x5, waiting for transfers between devices: 1.63 us -> 0.09 us  [swap(): return lax.ppermute(rows, 'seq', [(i, i ^ flip) for i in range(blocks)])]
    ppermute x0 -> x5, waiting for transfers between devices: none -> 1.12 us  [hop(): lax.ppermute(rows, 'seq', [(i, i ^ (odd if i & 1 else even)) for i in ran...]
  transfers between devices with their start and end apart: 13 -> 13, of which waited for: 4 -> 2; matrix products, arithmetic and copies ran while one was open for 1% -> 1% of each run, Pallas kernels for 16% -> 15%
where the time goes in v15:
time: 24.9 us; the launch traced here: 24.8 us
  starting transfers between devices  16.2 us (65%)
  Pallas kernels  5.43 us (22%)
  waiting for transfers between devices  1.23 us (5%)
  other arithmetic  1 us (4%)
  between operations  0.82 us (3%)
    ppermute x5, starting transfers between devices, hop(): lax.ppermute(rows, 'seq', [(i, i ^ (odd if i & 1 else even)) for i in ran...  7.67 us
    ppermute x3, starting transfers between devices, shards(): lax.ppermute(rows, 'head', [(i, (i + shift + 1) % pieces) for i in range(...  7.01 us
    pallas_call x5, Pallas kernels, attend_call(): pl.pallas_call(functools.partial(attend, pieces, part, first, last, items...  5.07 us
    ppermute x5, starting transfers between devices, swap(): return lax.ppermute(rows, 'seq', [(i, i ^ flip) for i in range(blocks)])  1.47 us
    ppermute x5, waiting for transfers between devices, hop(): lax.ppermute(rows, 'seq', [(i, i ^ (odd if i & 1 else even)) for i in ran...  1.12 us
    concatenate x1, other arithmetic, shards(): jnp.concatenate([keys, values]).reshape(2 * part * kv_heads, head_width)  0.95 us
  transfers between devices with their start and end apart: 13, of which 2 were waited for; matrix products, arithmetic and copies ran while one was open for 1% of the time, Pallas kernels for 15%

profile of v15, /device:TPU:0, one launch (start us, length us, event | category | flops | bytes accessed | tf_op | source)
XLA Modules:
  0.0 24.8 jit_solution(9595375231884328395)
XLA Ops:
  0.0 0.0 copy-start
  0.0 1.0 %pad_maximum_fusion.3 = bf16[128,2,128]{2,1,0:T(2,128)(2,1)S(1)} fusion(bf16[64,2,128]{2,1,0:T(2,128)(2,1)} %param.6, bf16[64,2,128]{2,1,0:T(2,128)(2,1)} %param.5), kind=kLoop, calls=%fused_computation.4 | loop fusion | flops 32768 | bytes 131072 | tf_op jit(solution)/shard_map/concatenate | solution.py:184
  1.0 0.2 shard_map.46
  1.1 3.1 %collective-permute-start = (bf16[128,128]{1,0:T(8,128)(2,1)S(1)}, bf16[128,128]{1,0:T(8,128)(2,1)S(1)}, u32[]{:S(2)}, u32[]{:S(2)}) collective-permute-start(bf16[128,128]{1,0:T(8,128)(2,1)S(1)} %get-tuple-element.34), channel_id=1, source_target_pairs={{0,1},{1,2},{2,3},{3,0},{4,5},{5,6},{6,7},{7,4},{8,9},{9,10},{10,1... | collective-permute-start | bytes 98312 | tf_op jit(solution)/shard_map/ppermute | solution.py:188
  4.2 2.6 %collective-permute-start.1 = (bf16[128,128]{1,0:T(8,128)(2,1)S(1)}, bf16[128,128]{1,0:T(8,128)(2,1)S(1)}, u32[]{:S(2)}, u32[]{:S(2)}) collective-permute-start(bf16[128,128]{1,0:T(8,128)(2,1)S(1)} %get-tuple-element.35), channel_id=1, source_target_pairs={{0,2},{1,3},{2,0},{3,1},{4,6},{5,7},{6,4},{7,5},{8,10},{9,11},{10,... | collective-permute-start | bytes 98312 | tf_op jit(solution)/shard_map/ppermute | solution.py:188
  6.8 1.3 %collective-permute-start.2 = (bf16[128,128]{1,0:T(8,128)(2,1)S(1)}, bf16[128,128]{1,0:T(8,128)(2,1)S(1)}, u32[]{:S(2)}, u32[]{:S(2)}) collective-permute-start(bf16[128,128]{1,0:T(8,128)(2,1)S(1)} %get-tuple-element.36), channel_id=1, source_target_pairs={{0,3},{1,0},{2,1},{3,2},{4,7},{5,4},{6,5},{7,6},{8,11},{9,8},{10,9... | collective-permute-start | bytes 98312 | tf_op jit(solution)/shard_map/ppermute | solution.py:188
  8.8 1.6 %collective-permute-start.6 = (bf16[144,128]{1,0:T(8,128)(2,1)S(1)}, bf16[144,128]{1,0:T(8,128)(2,1)S(1)}, u32[]{:S(2)}, u32[]{:S(2)}) collective-permute-start(bf16[144,128]{1,0:T(8,128)(2,1)S(1)} %get-tuple-element.62.own_ref), channel_id=1, source_target_pairs={{0,8},{4,20},{8,0},{12,28},{16,24},{20,4},{24,16},{28,12},{1,9},{5... | collective-permute-start | bytes 110600 | tf_op jit(solution)/shard_map/ppermute | solution.py:203
  10.4 1.5 %collective-permute-start.7 = (bf16[144,128]{1,0:T(8,128)(2,1)S(1)}, bf16[144,128]{1,0:T(8,128)(2,1)S(1)}, u32[]{:S(2)}, u32[]{:S(2)}) collective-permute-start(bf16[144,128]{1,0:T(8,128)(2,1)S(1)} %get-tuple-element.62.own_ref), channel_id=1, source_target_pairs={{0,16},{4,12},{8,24},{12,4},{16,0},{20,28},{24,8},{28,20},{1,17},{... | collective-permute-start | bytes 110600 | tf_op jit(solution)/shard_map/ppermute | solution.py:203
  11.9 0.0 collective-permute-done
  11.9 0.5 %collective-permute-start.9 = (bf16[144,128]{1,0:T(8,128)(2,1)S(1)}, bf16[144,128]{1,0:T(8,128)(2,1)S(1)}, u32[]{:S(2)}, u32[]{:S(2)}) collective-permute-start(bf16[144,128]{1,0:T(8,128)(2,1)S(1)} %get-tuple-element.62.own_ref), channel_id=1, source_target_pairs={{0,24},{4,28},{8,16},{12,20},{16,8},{20,12},{24,0},{28,4},{1,25},{... | collective-permute-start | bytes 110600 | tf_op jit(solution)/shard_map/ppermute | solution.py:197
  12.4 0.0 collective-permute-done.1
  12.4 0.0 collective-permute-done.2
  12.4 1.6 %collective-permute-start.3 = (bf16[1,384,128]{2,1,0:T(8,128)(2,1)S(1)}, bf16[1,384,128]{2,1,0:T(8,128)(2,1)S(1)}, u32[]{:S(2)}, u32[]{:S(2)}) collective-permute-start(bf16[1,384,128]{2,1,0:T(8,128)(2,1)S(1)} %maximum_bitcast_fusion.refs_1_), channel_id=1, source_target_pairs={{0,8},{4,20},{8,0},{12,28},{16,24},{20,4},{24,16},{28,12},{1,9},{5... | collective-permute-start | bytes 294920 | tf_op jit(solution)/shard_map/ppermute | solution.py:203
  14.0 1.5 %collective-permute-start.5 = (bf16[1,384,128]{2,1,0:T(8,128)(2,1)S(1)}, bf16[1,384,128]{2,1,0:T(8,128)(2,1)S(1)}, u32[]{:S(2)}, u32[]{:S(2)}) collective-permute-start(bf16[1,384,128]{2,1,0:T(8,128)(2,1)S(1)} %maximum_bitcast_fusion.refs_1_), channel_id=1, source_target_pairs={{0,16},{4,12},{8,24},{12,4},{16,0},{20,28},{24,8},{28,20},{1,17},{... | collective-permute-start | bytes 294920 | tf_op jit(solution)/shard_map/ppermute | solution.py:203
  15.5 0.0 collective-permute-done.6
  15.5 0.0 collective-permute-done.7
  15.5 0.1 collective-permute-start.8
  15.6 0.0 copy-done
  15.6 0.1 constant_dynamic-slice_fusion
  15.8 0.2 shard_map.47.query_ref
  16.0 1.1 %collective-permute-done.3.refs_4_ = bf16[1,384,128]{2,1,0:T(8,128)(2,1)S(1)} collective-permute-done((bf16[1,384,128]{2,1,0:T(8,128)(2,1)S(1)}, bf16[1,384,128]{2,1,0:T(8,128)(2,1)S(1)}, u32[]{:S(2)}, u32[]{:S(2)}) %collective-permute-start.3) | collective-permute-done | bytes 98336 | tf_op jit(solution)/shard_map/ppermute | solution.py:203
  17.1 1.5 %collective-permute-start.4 = (bf16[1,384,128]{2,1,0:T(8,128)(2,1)S(1)}, bf16[1,384,128]{2,1,0:T(8,128)(2,1)S(1)}, u32[]{:S(2)}, u32[]{:S(2)}) collective-permute-start(bf16[1,384,128]{2,1,0:T(8,128)(2,1)S(1)} %collective-permute-done.3.refs_4_), channel_id=1, source_target_pairs={{0,16},{4,12},{8,24},{12,4},{16,0},{20,28},{24,8},{28,20},{1,17},{... | collective-permute-start | bytes 294920 | tf_op jit(solution)/shard_map/ppermute | solution.py:203
  18.6 0.8 %shard_map.48 = (f32[1,1024]{1,0:T(1,128)S(1)}, f32[1,1024]{1,0:T(1,128)S(1)}, f32[128,1024]{1,0:T(8,128)S(1)}) custom-call(bf16[144,128]{1,0:T(8,128)(2,1)S(1)} %get-tuple-element.62.own_ref, bf16[256,1024]{1,0:T(8,128)(2,1)S(1)} %shard_map.47.query_ref, bf16[3,144,128]{2,1,0:T(8,128)(2,1)S(1)} %pad_maximum_fusion.2.refs_0_.refs_3_, ...), custom_call_target="tpu_custom_call" | custom-call | flops 1000000000 | tf_op jit(solution)/shard_map/pallas_call | solution.py:150
  19.4 0.0 collective-permute-done.9
  19.4 0.0 collective-permute-done.8.refs_3_.refs_4_
  19.4 0.9 %shard_map.49 = (f32[1,1024]{1,0:T(1,128)S(1)}, f32[1,1024]{1,0:T(1,128)S(1)}, f32[128,1024]{1,0:T(8,128)S(1)}) custom-call(bf16[144,128]{1,0:T(8,128)(2,1)S(1)} %get-tuple-element.62.own_ref, bf16[256,1024]{1,0:T(8,128)(2,1)S(1)} %shard_map.47.query_ref, f32[1,1024]{1,0:T(1,128)S(1)} %get-tuple-element.37.refs_0_, f32[1,1024]{1,0:T(1,128)S(1)} %get-tuple-element.38.refs_1_, ...), custom_call_target="tpu_custom_call" | custom-call | tf_op jit(solution)/shard_map/pallas_call | solution.py:150
  20.4 0.0 collective-permute-done.5.refs_5_
  20.4 0.1 collective-permute-start.10
  20.5 0.5 %collective-permute-start.11 = (bf16[1,384,128]{2,1,0:T(8,128)(2,1)S(1)}, bf16[1,384,128]{2,1,0:T(8,128)(2,1)S(1)}, u32[]{:S(2)}, u32[]{:S(2)}) collective-permute-start(bf16[1,384,128]{2,1,0:T(8,128)(2,1)S(1)} %collective-permute-done.5.refs_5_), channel_id=1, source_target_pairs={{0,4},{4,0},{8,12},{12,8},{16,20},{20,16},{24,28},{28,24},{1,5},{5... | collective-permute-start | bytes 294920 | tf_op jit(solution)/shard_map/ppermute | solution.py:197
  21.0 0.8 %shard_map.50 = (f32[1,1024]{1,0:T(1,128)S(1)}, f32[1,1024]{1,0:T(1,128)S(1)}, f32[128,1024]{1,0:T(8,128)S(1)}) custom-call(bf16[144,128]{1,0:T(8,128)(2,1)S(1)} %get-tuple-element.62.own_ref, bf16[256,1024]{1,0:T(8,128)(2,1)S(1)} %shard_map.47.query_ref, f32[1,1024]{1,0:T(1,128)S(1)} %get-tuple-element.43.refs_0_, f32[1,1024]{1,0:T(1,128)S(1)} %get-tuple-element.44.refs_1_, ...), custom_call_target="tpu_custom_call" | custom-call | flops 1000000000 | tf_op jit(solution)/shard_map/pallas_call | solution.py:150
  21.8 0.0 collective-permute-done.4
  21.8 0.0 collective-permute-done.10.refs_5_
  21.8 0.1 collective-permute-done.11.refs_6_
  21.9 0.4 %collective-permute-start.12 = (bf16[1,528,128]{2,1,0:T(8,128)(2,1)S(1)}, bf16[1,528,128]{2,1,0:T(8,128)(2,1)S(1)}, u32[]{:S(2)}, u32[]{:S(2)}) collective-permute-start(bf16[1,528,128]{2,1,0:T(8,128)(2,1)S(1)} %pad_maximum_fusion.1.refs_3_), channel_id=1, source_target_pairs={{0,4},{4,0},{8,12},{12,8},{16,20},{20,16},{24,28},{28,24},{1,5},{5... | collective-permute-start | bytes 405512 | tf_op jit(solution)/shard_map/ppermute | solution.py:197
  22.3 1.1 %shard_map.51 = (f32[1,1024]{1,0:T(1,128)S(1)}, f32[1,1024]{1,0:T(1,128)S(1)}, f32[128,1024]{1,0:T(8,128)S(1)}) custom-call(bf16[144,128]{1,0:T(8,128)(2,1)S(1)} %get-tuple-element.62.own_ref, bf16[256,1024]{1,0:T(8,128)(2,1)S(1)} %shard_map.47.query_ref, f32[1,1024]{1,0:T(1,128)S(1)} %get-tuple-element.51.refs_0_, f32[1,1024]{1,0:T(1,128)S(1)} %get-tuple-element.52.refs_1_, ...), custom_call_target="tpu_custom_call" | custom-call | tf_op jit(solution)/shard_map/pallas_call | solution.py:150
  23.4 0.0 collective-permute-done.12.refs_3_
  23.4 1.4 %shard_map.52 = bf16[1024,128]{1,0:T(8,128)(2,1)} custom-call(bf16[144,128]{1,0:T(8,128)(2,1)S(1)} %get-tuple-element.62.own_ref, bf16[256,1024]{1,0:T(8,128)(2,1)S(1)} %shard_map.47.query_ref, f32[1,1024]{1,0:T(1,128)S(1)} %get-tuple-element.58.refs_0_, f32[1,1024]{1,0:T(1,128)S(1)} %get-tuple-element.59.refs_1_, ...), custom_call_target="tpu_custom_call" | custom-call | tf_op jit(solution)/shard_map/pallas_call | solution.py:150
  (5 shorter events, 0.1 us)
Async XLA Ops:
  0.0 15.6 %copy-start = (bf16[256,16,128]{2,1,0:T(8,128)(2,1)S(1)}, bf16[256,16,128]{2,1,0:T(8,128)(2,1)}, u32[]{:S(2)}) copy-start(bf16[256,16,128]{2,1,0:T(8,128)(2,1)} %param.4) | copy-start | bytes 3145732
  1.1 10.8 %collective-permute-start = (bf16[128,128]{1,0:T(8,128)(2,1)S(1)}, bf16[128,128]{1,0:T(8,128)(2,1)S(1)}, u32[]{:S(2)}, u32[]{:S(2)}) collective-permute-start(bf16[128,128]{1,0:T(8,128)(2,1)S(1)} %get-tuple-element.34), channel_id=1, source_target_pairs={{0,1},{1,2},{2,3},{3,0},{4,5},{5,6},{6,7},{7,4},{8,9},{9,10},{10,1... | collective-permute-start | bytes 98312 | tf_op jit(solution)/shard_map/ppermute | solution.py:188
  4.2 8.2 %collective-permute-start.1 = (bf16[128,128]{1,0:T(8,128)(2,1)S(1)}, bf16[128,128]{1,0:T(8,128)(2,1)S(1)}, u32[]{:S(2)}, u32[]{:S(2)}) collective-permute-start(bf16[128,128]{1,0:T(8,128)(2,1)S(1)} %get-tuple-element.35), channel_id=1, source_target_pairs={{0,2},{1,3},{2,0},{3,1},{4,6},{5,7},{6,4},{7,5},{8,10},{9,11},{10,... | collective-permute-start | bytes 98312 | tf_op jit(solution)/shard_map/ppermute | solution.py:188
  6.8 5.6 %collective-permute-start.2 = (bf16[128,128]{1,0:T(8,128)(2,1)S(1)}, bf16[128,128]{1,0:T(8,128)(2,1)S(1)}, u32[]{:S(2)}, u32[]{:S(2)}) collective-permute-start(bf16[128,128]{1,0:T(8,128)(2,1)S(1)} %get-tuple-element.36), channel_id=1, source_target_pairs={{0,3},{1,0},{2,1},{3,2},{4,7},{5,4},{6,5},{7,6},{8,11},{9,8},{10,9... | collective-permute-start | bytes 98312 | tf_op jit(solution)/shard_map/ppermute | solution.py:188
  8.8 6.7 %collective-permute-start.6 = (bf16[144,128]{1,0:T(8,128)(2,1)S(1)}, bf16[144,128]{1,0:T(8,128)(2,1)S(1)}, u32[]{:S(2)}, u32[]{:S(2)}) collective-permute-start(bf16[144,128]{1,0:T(8,128)(2,1)S(1)} %get-tuple-element.62.own_ref), channel_id=1, source_target_pairs={{0,8},{4,20},{8,0},{12,28},{16,24},{20,4},{24,16},{28,12},{1,9},{5... | collective-permute-start | bytes 110600 | tf_op jit(solution)/shard_map/ppermute | solution.py:203
  10.4 5.1 %collective-permute-start.7 = (bf16[144,128]{1,0:T(8,128)(2,1)S(1)}, bf16[144,128]{1,0:T(8,128)(2,1)S(1)}, u32[]{:S(2)}, u32[]{:S(2)}) collective-permute-start(bf16[144,128]{1,0:T(8,128)(2,1)S(1)} %get-tuple-element.62.own_ref), channel_id=1, source_target_pairs={{0,16},{4,12},{8,24},{12,4},{16,0},{20,28},{24,8},{28,20},{1,17},{... | collective-permute-start | bytes 110600 | tf_op jit(solution)/shard_map/ppermute | solution.py:203
  11.9 7.5 %collective-permute-start.9 = (bf16[144,128]{1,0:T(8,128)(2,1)S(1)}, bf16[144,128]{1,0:T(8,128)(2,1)S(1)}, u32[]{:S(2)}, u32[]{:S(2)}) collective-permute-start(bf16[144,128]{1,0:T(8,128)(2,1)S(1)} %get-tuple-element.62.own_ref), channel_id=1, source_target_pairs={{0,24},{4,28},{8,16},{12,20},{16,8},{20,12},{24,0},{28,4},{1,25},{... | collective-permute-start | bytes 110600 | tf_op jit(solution)/shard_map/ppermute | solution.py:197
  12.4 4.7 %collective-permute-start.3 = (bf16[1,384,128]{2,1,0:T(8,128)(2,1)S(1)}, bf16[1,384,128]{2,1,0:T(8,128)(2,1)S(1)}, u32[]{:S(2)}, u32[]{:S(2)}) collective-permute-start(bf16[1,384,128]{2,1,0:T(8,128)(2,1)S(1)} %maximum_bitcast_fusion.refs_1_), channel_id=1, source_target_pairs={{0,8},{4,20},{8,0},{12,28},{16,24},{20,4},{24,16},{28,12},{1,9},{5... | collective-permute-start | bytes 294920 | tf_op jit(solution)/shard_map/ppermute | solution.py:203
  14.0 6.4 %collective-permute-start.5 = (bf16[1,384,128]{2,1,0:T(8,128)(2,1)S(1)}, bf16[1,384,128]{2,1,0:T(8,128)(2,1)S(1)}, u32[]{:S(2)}, u32[]{:S(2)}) collective-permute-start(bf16[1,384,128]{2,1,0:T(8,128)(2,1)S(1)} %maximum_bitcast_fusion.refs_1_), channel_id=1, source_target_pairs={{0,16},{4,12},{8,24},{12,4},{16,0},{20,28},{24,8},{28,20},{1,17},{... | collective-permute-start | bytes 294920 | tf_op jit(solution)/shard_map/ppermute | solution.py:203
  15.5 3.9 %collective-permute-start.8 = (bf16[1,816,128]{2,1,0:T(8,128)(2,1)S(1)}, bf16[1,816,128]{2,1,0:T(8,128)(2,1)S(1)}, u32[]{:S(2)}, u32[]{:S(2)}) collective-permute-start(bf16[1,816,128]{2,1,0:T(8,128)(2,1)S(1)} %pad_maximum_fusion), channel_id=1, source_target_pairs={{0,4},{4,0},{8,12},{12,8},{16,20},{20,16},{24,28},{28,24},{1,5},{5... | collective-permute-start | bytes 626696 | tf_op jit(solution)/shard_map/ppermute | solution.py:197
  17.1 4.7 %collective-permute-start.4 = (bf16[1,384,128]{2,1,0:T(8,128)(2,1)S(1)}, bf16[1,384,128]{2,1,0:T(8,128)(2,1)S(1)}, u32[]{:S(2)}, u32[]{:S(2)}) collective-permute-start(bf16[1,384,128]{2,1,0:T(8,128)(2,1)S(1)} %collective-permute-done.3.refs_4_), channel_id=1, source_target_pairs={{0,16},{4,12},{8,24},{12,4},{16,0},{20,28},{24,8},{28,20},{1,17},{... | collective-permute-start | bytes 294920 | tf_op jit(solution)/shard_map/ppermute | solution.py:203
  20.4 1.4 %collective-permute-start.10 = (bf16[1,384,128]{2,1,0:T(8,128)(2,1)S(1)}, bf16[1,384,128]{2,1,0:T(8,128)(2,1)S(1)}, u32[]{:S(2)}, u32[]{:S(2)}) collective-permute-start(bf16[1,384,128]{2,1,0:T(8,128)(2,1)S(1)} %collective-permute-done.3.refs_4_), channel_id=1, source_target_pairs={{0,4},{4,0},{8,12},{12,8},{16,20},{20,16},{24,28},{28,24},{1,5},{5... | collective-permute-start | bytes 294920 | tf_op jit(solution)/shard_map/ppermute | solution.py:197
  20.5 1.4 %collective-permute-start.11 = (bf16[1,384,128]{2,1,0:T(8,128)(2,1)S(1)}, bf16[1,384,128]{2,1,0:T(8,128)(2,1)S(1)}, u32[]{:S(2)}, u32[]{:S(2)}) collective-permute-start(bf16[1,384,128]{2,1,0:T(8,128)(2,1)S(1)} %collective-permute-done.5.refs_5_), channel_id=1, source_target_pairs={{0,4},{4,0},{8,12},{12,8},{16,20},{20,16},{24,28},{28,24},{1,5},{5... | collective-permute-start | bytes 294920 | tf_op jit(solution)/shard_map/ppermute | solution.py:197
  21.9 1.4 %collective-permute-start.12 = (bf16[1,528,128]{2,1,0:T(8,128)(2,1)S(1)}, bf16[1,528,128]{2,1,0:T(8,128)(2,1)S(1)}, u32[]{:S(2)}, u32[]{:S(2)}) collective-permute-start(bf16[1,528,128]{2,1,0:T(8,128)(2,1)S(1)} %pad_maximum_fusion.1.refs_3_), channel_id=1, source_target_pairs={{0,4},{4,0},{8,12},{12,8},{16,20},{20,16},{24,28},{28,24},{1,5},{5... | collective-permute-start | bytes 405512 | tf_op jit(solution)/shard_map/ppermute | solution.py:197

commit v16 on v15

--- a/solution.py
+++ b/solution.py
@@ -198,14 +198,14 @@
 
     if blocks == 8:
         rest = rest[None]
-
-        def hop(rows, even, odd):
-            return lax.ppermute(rows, "seq", [(i, i ^ (odd if i & 1 else even)) for i in range(blocks)])
-
-        near_one, near_two, near_far = hop(own, 2, 4), hop(own, 4, 2), swap(own, 6)
+        ways = ((4, 2), (2, 6), (6, 4))
+
+        def hop(rows, way):
+            return lax.ppermute(rows, "seq", [(i, i ^ way[i & 1]) for i in range(blocks)])
+
+        near_one, near_two, near_last = [hop(own, way) for way in ways]
         mine = jnp.stack([own, near_one, near_two])
-        along_one, along_two = hop(rest, 2, 4), hop(rest, 4, 2)
-        across = hop(along_one, 4, 2)
+        along_one, along_two, along_last = [hop(rest, way) for way in ways]
 
         def small(data, slots):
             return [(data, slot, (0,), None, (data, slot, 2 * part)) for slot in slots]
@@ -225,29 +225,28 @@
         size = own.shape[0]
         state = fold(
             state,
-            [both_other, near_far[None]],
+            [both_other, near_last[None]],
             [(0, 0, (size * i,), None, (0, 0, size * i + 2 * part)) for i in range(3)]
             + [(0, 0, tuple(early_rows + offset for offset in offsets[:-1]), None, (0, 0, 2 * part))]
             + small(1, (0,)),
             False,
-            0,
         )
         along_one, along_two, state = lax.optimization_barrier((along_one, along_two, state))
         others = [swap(rows, 1) for rows in (along_one, along_two)]
-        state = fold(state, [mine, along_one, along_two], [large(i, 0, i) for i in (1, 2)], False, OVERLAP)
-        across, state = lax.optimization_barrier((across, state))
-        across = jnp.concatenate([near_far[None], across], axis=1)
-        across, *others = lax.optimization_barrier((across, *others))
-        other_across = swap(across, 1)
+        state = fold(state, [mine, along_one, along_two], [large(i, 0, i) for i in (1, 2)], False)
+        along_last, state = lax.optimization_barrier((along_last, state))
+        along_last = jnp.concatenate([near_last[None], along_last], axis=1)
+        along_last, *others = lax.optimization_barrier((along_last, *others))
+        other_last = swap(along_last, 1)
         state = fold(
             state,
-            [across, both_other] + others,
+            [along_last, both_other] + others,
             [large(0, 0, 0, size)] + [(1 + i, 0, offsets[:-1], None, (1, 0, size * i + 2 * part)) for i in (1, 2)],
             False,
         )
         result = fold(
             state,
-            [other_across],
+            [other_last],
             [(0, 0, (0,) + tuple(own.shape[0] + offset for offset in offsets[:-1]), None, (0, 0, 2 * part))],
             True,
         )

time: 24.9 us -> 24.2 us (0.972)
  starting transfers between devices: 16.2 us -> 14.7 us
  waiting for transfers between devices: 1.23 us -> 1.97 us
    ppermute x5 -> x4, starting transfers between devices: 1.47 us -> 0.72 us  [swap(): return lax.ppermute(rows, 'seq', [(i, i ^ flip) for i in range(blocks)])]
    ppermute x5 -> x6, starting transfers between devices: 7.67 us -> 6.94 us  [hop(): lax.ppermute(rows, 'seq', [(i, i ^ way[i & 1]) for i in range(blocks)])]
    ppermute x5 -> x4, waiting for transfers between devices: 0.09 us -> 0.52 us  [swap(): return lax.ppermute(rows, 'seq', [(i, i ^ flip) for i in range(blocks)])]
    ppermute x5 -> x6, waiting for transfers between devices: 1.12 us -> 1.44 us  [hop(): lax.ppermute(rows, 'seq', [(i, i ^ way[i & 1]) for i in range(blocks)])]
  transfers between devices with their start and end apart: 13 -> 13, of which waited for: 2 -> 5; matrix products, arithmetic and copies ran while one was open for 1% -> 1% of each run, Pallas kernels for 15% -> 16%
where the time goes in v16:
time: 24.2 us; the launch traced here: 24 us
  starting transfers between devices  14.7 us (61%)
  Pallas kernels  5.44 us (22%)
  waiting for transfers between devices  1.97 us (8%)
  other arithmetic  1 us (4%)
  between operations  0.8 us (3%)
    ppermute x3, starting transfers between devices, shards(): lax.ppermute(rows, 'head', [(i, (i + shift + 1) % pieces) for i in range(...  7.01 us
    ppermute x6, starting transfers between devices, hop(): lax.ppermute(rows, 'seq', [(i, i ^ way[i & 1]) for i in range(blocks)])  6.94 us
    pallas_call x5, Pallas kernels, attend_call(): pl.pallas_call(functools.partial(attend, pieces, part, first, last, items...  5.08 us
    ppermute x6, waiting for transfers between devices, hop(): lax.ppermute(rows, 'seq', [(i, i ^ way[i & 1]) for i in range(blocks)])  1.44 us
    concatenate x1, other arithmetic, shards(): jnp.concatenate([keys, values]).reshape(2 * part * kv_heads, head_width)  0.95 us
    ppermute x4, starting transfers between devices, swap(): return lax.ppermute(rows, 'seq', [(i, i ^ flip) for i in range(blocks)])  0.72 us
    ppermute x4, waiting for transfers between devices, swap(): return lax.ppermute(rows, 'seq', [(i, i ^ flip) for i in range(blocks)])  0.52 us
  transfers between devices with their start and end apart: 13, of which 5 were waited for; matrix products, arithmetic and copies ran while one was open for 1% of the time, Pallas kernels for 16%

profile of v16, /device:TPU:0, one launch (start us, length us, event | category | flops | bytes accessed | tf_op | source)
XLA Modules:
  0.0 24.0 jit_solution(13515105011755950275)
XLA Ops:
  0.0 0.0 copy-start
  0.0 1.0 %pad_maximum_fusion.3 = bf16[128,2,128]{2,1,0:T(2,128)(2,1)S(1)} fusion(bf16[64,2,128]{2,1,0:T(2,128)(2,1)} %param.6, bf16[64,2,128]{2,1,0:T(2,128)(2,1)} %param.5), kind=kLoop, calls=%fused_computation.4 | loop fusion | flops 32768 | bytes 131072 | tf_op jit(solution)/shard_map/concatenate | solution.py:184
  1.0 0.2 shard_map.46
  1.1 3.1 %collective-permute-start = (bf16[128,128]{1,0:T(8,128)(2,1)S(1)}, bf16[128,128]{1,0:T(8,128)(2,1)S(1)}, u32[]{:S(2)}, u32[]{:S(2)}) collective-permute-start(bf16[128,128]{1,0:T(8,128)(2,1)S(1)} %get-tuple-element.34), channel_id=1, source_target_pairs={{0,1},{1,2},{2,3},{3,0},{4,5},{5,6},{6,7},{7,4},{8,9},{9,10},{10,1... | collective-permute-start | bytes 98312 | tf_op jit(solution)/shard_map/ppermute | solution.py:188
  4.2 2.6 %collective-permute-start.1 = (bf16[128,128]{1,0:T(8,128)(2,1)S(1)}, bf16[128,128]{1,0:T(8,128)(2,1)S(1)}, u32[]{:S(2)}, u32[]{:S(2)}) collective-permute-start(bf16[128,128]{1,0:T(8,128)(2,1)S(1)} %get-tuple-element.35), channel_id=1, source_target_pairs={{0,2},{1,3},{2,0},{3,1},{4,6},{5,7},{6,4},{7,5},{8,10},{9,11},{10,... | collective-permute-start | bytes 98312 | tf_op jit(solution)/shard_map/ppermute | solution.py:188
  6.8 1.3 %collective-permute-start.2 = (bf16[128,128]{1,0:T(8,128)(2,1)S(1)}, bf16[128,128]{1,0:T(8,128)(2,1)S(1)}, u32[]{:S(2)}, u32[]{:S(2)}) collective-permute-start(bf16[128,128]{1,0:T(8,128)(2,1)S(1)} %get-tuple-element.36), channel_id=1, source_target_pairs={{0,3},{1,0},{2,1},{3,2},{4,7},{5,4},{6,5},{7,6},{8,11},{9,8},{10,9... | collective-permute-start | bytes 98312 | tf_op jit(solution)/shard_map/ppermute | solution.py:188
  8.8 2.5 %collective-permute-start.9 = (bf16[144,128]{1,0:T(8,128)(2,1)S(1)}, bf16[144,128]{1,0:T(8,128)(2,1)S(1)}, u32[]{:S(2)}, u32[]{:S(2)}) collective-permute-start(bf16[144,128]{1,0:T(8,128)(2,1)S(1)} %get-tuple-element.62.own_ref), channel_id=1, source_target_pairs={{0,24},{4,20},{8,16},{12,28},{16,8},{20,4},{24,0},{28,12},{1,25},{... | collective-permute-start | bytes 110600 | tf_op jit(solution)/shard_map/ppermute | solution.py:204
  11.3 0.5 %collective-permute-start.7 = (bf16[144,128]{1,0:T(8,128)(2,1)S(1)}, bf16[144,128]{1,0:T(8,128)(2,1)S(1)}, u32[]{:S(2)}, u32[]{:S(2)}) collective-permute-start(bf16[144,128]{1,0:T(8,128)(2,1)S(1)} %get-tuple-element.62.own_ref), channel_id=1, source_target_pairs={{0,8},{4,28},{8,0},{12,20},{16,24},{20,12},{24,16},{28,4},{1,9},{5... | collective-permute-start | bytes 110600 | tf_op jit(solution)/shard_map/ppermute | solution.py:204
  11.9 0.0 collective-permute-done
  11.9 0.5 %collective-permute-start.6 = (bf16[144,128]{1,0:T(8,128)(2,1)S(1)}, bf16[144,128]{1,0:T(8,128)(2,1)S(1)}, u32[]{:S(2)}, u32[]{:S(2)}) collective-permute-start(bf16[144,128]{1,0:T(8,128)(2,1)S(1)} %get-tuple-element.62.own_ref), channel_id=1, source_target_pairs={{0,16},{4,12},{8,24},{12,4},{16,0},{20,28},{24,8},{28,20},{1,17},{... | collective-permute-start | bytes 110600 | tf_op jit(solution)/shard_map/ppermute | solution.py:204
  12.4 0.0 collective-permute-done.1
  12.4 0.0 collective-permute-done.2
  12.4 1.6 %collective-permute-start.5 = (bf16[1,384,128]{2,1,0:T(8,128)(2,1)S(1)}, bf16[1,384,128]{2,1,0:T(8,128)(2,1)S(1)}, u32[]{:S(2)}, u32[]{:S(2)}) collective-permute-start(bf16[1,384,128]{2,1,0:T(8,128)(2,1)S(1)} %maximum_bitcast_fusion.refs_1_), channel_id=1, source_target_pairs={{0,8},{4,28},{8,0},{12,20},{16,24},{20,12},{24,16},{28,4},{1,9},{5... | collective-permute-start | bytes 294920 | tf_op jit(solution)/shard_map/ppermute | solution.py:204
  14.0 1.5 %collective-permute-start.4 = (bf16[1,384,128]{2,1,0:T(8,128)(2,1)S(1)}, bf16[1,384,128]{2,1,0:T(8,128)(2,1)S(1)}, u32[]{:S(2)}, u32[]{:S(2)}) collective-permute-start(bf16[1,384,128]{2,1,0:T(8,128)(2,1)S(1)} %maximum_bitcast_fusion.refs_1_), channel_id=1, source_target_pairs={{0,16},{4,12},{8,24},{12,4},{16,0},{20,28},{24,8},{28,20},{1,17},{... | collective-permute-start | bytes 294920 | tf_op jit(solution)/shard_map/ppermute | solution.py:204
  15.5 0.2 collective-permute-done.7
  15.6 0.3 %collective-permute-start.3 = (bf16[1,384,128]{2,1,0:T(8,128)(2,1)S(1)}, bf16[1,384,128]{2,1,0:T(8,128)(2,1)S(1)}, u32[]{:S(2)}, u32[]{:S(2)}) collective-permute-start(bf16[1,384,128]{2,1,0:T(8,128)(2,1)S(1)} %maximum_bitcast_fusion.refs_1_), channel_id=1, source_target_pairs={{0,24},{4,20},{8,16},{12,28},{16,8},{20,4},{24,0},{28,12},{1,25},{... | collective-permute-start | bytes 294920 | tf_op jit(solution)/shard_map/ppermute | solution.py:204
  16.0 0.3 %collective-permute-done.6 = bf16[144,128]{1,0:T(8,128)(2,1)S(1)} collective-permute-done((bf16[144,128]{1,0:T(8,128)(2,1)S(1)}, bf16[144,128]{1,0:T(8,128)(2,1)S(1)}, u32[]{:S(2)}, u32[]{:S(2)}) %collective-permute-start.6) | collective-permute-done | bytes 36896 | tf_op jit(solution)/shard_map/ppermute | solution.py:204
  16.3 0.1 collective-permute-start.8
  16.4 0.0 copy-done
  16.4 0.1 constant_dynamic-slice_fusion
  16.6 0.2 shard_map.47.query_ref
  16.8 0.8 %shard_map.48 = (f32[1,1024]{1,0:T(1,128)S(1)}, f32[1,1024]{1,0:T(1,128)S(1)}, f32[128,1024]{1,0:T(8,128)S(1)}) custom-call(bf16[144,128]{1,0:T(8,128)(2,1)S(1)} %get-tuple-element.62.own_ref, bf16[256,1024]{1,0:T(8,128)(2,1)S(1)} %shard_map.47.query_ref, bf16[3,144,128]{2,1,0:T(8,128)(2,1)S(1)} %pad_maximum_fusion.2.refs_0_.refs_3_, ...), custom_call_target="tpu_custom_call" | custom-call | flops 1000000000 | tf_op jit(solution)/shard_map/pallas_call | solution.py:150
  17.6 0.0 collective-permute-done.9
  17.6 0.3 %collective-permute-done.8.refs_3_.refs_4_ = bf16[1,816,128]{2,1,0:T(8,128)(2,1)S(1)} collective-permute-done((bf16[1,816,128]{2,1,0:T(8,128)(2,1)S(1)}, bf16[1,816,128]{2,1,0:T(8,128)(2,1)S(1)}, u32[]{:S(2)}, u32[]{:S(2)}) %collective-permute-start.8) | collective-permute-done | bytes 208928 | tf_op jit(solution)/shard_map/ppermute | solution.py:197
  17.8 0.9 %shard_map.49 = (f32[1,1024]{1,0:T(1,128)S(1)}, f32[1,1024]{1,0:T(1,128)S(1)}, f32[128,1024]{1,0:T(8,128)S(1)}) custom-call(bf16[144,128]{1,0:T(8,128)(2,1)S(1)} %get-tuple-element.62.own_ref, bf16[256,1024]{1,0:T(8,128)(2,1)S(1)} %shard_map.47.query_ref, f32[1,1024]{1,0:T(1,128)S(1)} %get-tuple-element.37.refs_0_, f32[1,1024]{1,0:T(1,128)S(1)} %get-tuple-element.38.refs_1_, ...), custom_call_target="tpu_custom_call" | custom-call | tf_op jit(solution)/shard_map/pallas_call | solution.py:150
  18.8 0.0 collective-permute-done.5.refs_5_
  18.8 0.0 collective-permute-done.4.refs_4_
  18.8 0.3 %collective-permute-start.10 = (bf16[1,384,128]{2,1,0:T(8,128)(2,1)S(1)}, bf16[1,384,128]{2,1,0:T(8,128)(2,1)S(1)}, u32[]{:S(2)}, u32[]{:S(2)}) collective-permute-start(bf16[1,384,128]{2,1,0:T(8,128)(2,1)S(1)} %collective-permute-done.4.refs_4_), channel_id=1, source_target_pairs={{0,4},{4,0},{8,12},{12,8},{16,20},{20,16},{24,28},{28,24},{1,5},{5... | collective-permute-start | bytes 294920 | tf_op jit(solution)/shard_map/ppermute | solution.py:197
  19.1 0.3 %collective-permute-start.11 = (bf16[1,384,128]{2,1,0:T(8,128)(2,1)S(1)}, bf16[1,384,128]{2,1,0:T(8,128)(2,1)S(1)}, u32[]{:S(2)}, u32[]{:S(2)}) collective-permute-start(bf16[1,384,128]{2,1,0:T(8,128)(2,1)S(1)} %collective-permute-done.5.refs_5_), channel_id=1, source_target_pairs={{0,4},{4,0},{8,12},{12,8},{16,20},{20,16},{24,28},{28,24},{1,5},{5... | collective-permute-start | bytes 294920 | tf_op jit(solution)/shard_map/ppermute | solution.py:197
  19.4 0.8 %shard_map.50 = (f32[1,1024]{1,0:T(1,128)S(1)}, f32[1,1024]{1,0:T(1,128)S(1)}, f32[128,1024]{1,0:T(8,128)S(1)}) custom-call(bf16[144,128]{1,0:T(8,128)(2,1)S(1)} %get-tuple-element.62.own_ref, bf16[256,1024]{1,0:T(8,128)(2,1)S(1)} %shard_map.47.query_ref, f32[1,1024]{1,0:T(1,128)S(1)} %get-tuple-element.43.refs_0_, f32[1,1024]{1,0:T(1,128)S(1)} %get-tuple-element.44.refs_1_, ...), custom_call_target="tpu_custom_call" | custom-call | tf_op jit(solution)/shard_map/pallas_call | solution.py:150
  20.2 1.0 %collective-permute-done.3 = bf16[1,384,128]{2,1,0:T(8,128)(2,1)S(1)} collective-permute-done((bf16[1,384,128]{2,1,0:T(8,128)(2,1)S(1)}, bf16[1,384,128]{2,1,0:T(8,128)(2,1)S(1)}, u32[]{:S(2)}, u32[]{:S(2)}) %collective-permute-start.3) | collective-permute-done | bytes 98336 | tf_op jit(solution)/shard_map/ppermute | solution.py:204
  21.2 0.0 collective-permute-done.10.refs_5_
  21.2 0.0 collective-permute-done.11.refs_6_
  21.2 0.1 collective-permute-start.12
  21.3 1.1 %shard_map.51 = (f32[1,1024]{1,0:T(1,128)S(1)}, f32[1,1024]{1,0:T(1,128)S(1)}, f32[128,1024]{1,0:T(8,128)S(1)}) custom-call(bf16[144,128]{1,0:T(8,128)(2,1)S(1)} %get-tuple-element.62.own_ref, bf16[256,1024]{1,0:T(8,128)(2,1)S(1)} %shard_map.47.query_ref, f32[1,1024]{1,0:T(1,128)S(1)} %get-tuple-element.51.refs_0_, f32[1,1024]{1,0:T(1,128)S(1)} %get-tuple-element.52.refs_1_, ...), custom_call_target="tpu_custom_call" | custom-call | tf_op jit(solution)/shard_map/pallas_call | solution.py:150
  22.4 0.3 %collective-permute-done.12.refs_3_ = bf16[1,528,128]{2,1,0:T(8,128)(2,1)S(1)} collective-permute-done((bf16[1,528,128]{2,1,0:T(8,128)(2,1)S(1)}, bf16[1,528,128]{2,1,0:T(8,128)(2,1)S(1)}, u32[]{:S(2)}, u32[]{:S(2)}) %collective-permute-start.12) | collective-permute-done | bytes 135200 | tf_op jit(solution)/shard_map/ppermute | solution.py:197
  22.6 1.4 %shard_map.52 = bf16[1024,128]{1,0:T(8,128)(2,1)} custom-call(bf16[144,128]{1,0:T(8,128)(2,1)S(1)} %get-tuple-element.62.own_ref, bf16[256,1024]{1,0:T(8,128)(2,1)S(1)} %shard_map.47.query_ref, f32[1,1024]{1,0:T(1,128)S(1)} %get-tuple-element.58.refs_0_, f32[1,1024]{1,0:T(1,128)S(1)} %get-tuple-element.59.refs_1_, ...), custom_call_target="tpu_custom_call" | custom-call | tf_op jit(solution)/shard_map/pallas_call | solution.py:150
  (5 shorter events, 0.1 us)
Async XLA Ops:
  0.0 16.4 %copy-start = (bf16[256,16,128]{2,1,0:T(8,128)(2,1)S(1)}, bf16[256,16,128]{2,1,0:T(8,128)(2,1)}, u32[]{:S(2)}) copy-start(bf16[256,16,128]{2,1,0:T(8,128)(2,1)} %param.4) | copy-start | bytes 3145732
  1.1 10.7 %collective-permute-start = (bf16[128,128]{1,0:T(8,128)(2,1)S(1)}, bf16[128,128]{1,0:T(8,128)(2,1)S(1)}, u32[]{:S(2)}, u32[]{:S(2)}) collective-permute-start(bf16[128,128]{1,0:T(8,128)(2,1)S(1)} %get-tuple-element.34), channel_id=1, source_target_pairs={{0,1},{1,2},{2,3},{3,0},{4,5},{5,6},{6,7},{7,4},{8,9},{9,10},{10,1... | collective-permute-start | bytes 98312 | tf_op jit(solution)/shard_map/ppermute | solution.py:188
  4.2 8.2 %collective-permute-start.1 = (bf16[128,128]{1,0:T(8,128)(2,1)S(1)}, bf16[128,128]{1,0:T(8,128)(2,1)S(1)}, u32[]{:S(2)}, u32[]{:S(2)}) collective-permute-start(bf16[128,128]{1,0:T(8,128)(2,1)S(1)} %get-tuple-element.35), channel_id=1, source_target_pairs={{0,2},{1,3},{2,0},{3,1},{4,6},{5,7},{6,4},{7,5},{8,10},{9,11},{10,... | collective-permute-start | bytes 98312 | tf_op jit(solution)/shard_map/ppermute | solution.py:188
  6.8 5.6 %collective-permute-start.2 = (bf16[128,128]{1,0:T(8,128)(2,1)S(1)}, bf16[128,128]{1,0:T(8,128)(2,1)S(1)}, u32[]{:S(2)}, u32[]{:S(2)}) collective-permute-start(bf16[128,128]{1,0:T(8,128)(2,1)S(1)} %get-tuple-element.36), channel_id=1, source_target_pairs={{0,3},{1,0},{2,1},{3,2},{4,7},{5,4},{6,5},{7,6},{8,11},{9,8},{10,9... | collective-permute-start | bytes 98312 | tf_op jit(solution)/shard_map/ppermute | solution.py:188
  8.8 8.8 %collective-permute-start.9 = (bf16[144,128]{1,0:T(8,128)(2,1)S(1)}, bf16[144,128]{1,0:T(8,128)(2,1)S(1)}, u32[]{:S(2)}, u32[]{:S(2)}) collective-permute-start(bf16[144,128]{1,0:T(8,128)(2,1)S(1)} %get-tuple-element.62.own_ref), channel_id=1, source_target_pairs={{0,24},{4,20},{8,16},{12,28},{16,8},{20,4},{24,0},{28,12},{1,25},{... | collective-permute-start | bytes 110600 | tf_op jit(solution)/shard_map/ppermute | solution.py:204
  11.3 4.3 %collective-permute-start.7 = (bf16[144,128]{1,0:T(8,128)(2,1)S(1)}, bf16[144,128]{1,0:T(8,128)(2,1)S(1)}, u32[]{:S(2)}, u32[]{:S(2)}) collective-permute-start(bf16[144,128]{1,0:T(8,128)(2,1)S(1)} %get-tuple-element.62.own_ref), channel_id=1, source_target_pairs={{0,8},{4,28},{8,0},{12,20},{16,24},{20,12},{24,16},{28,4},{1,9},{5... | collective-permute-start | bytes 110600 | tf_op jit(solution)/shard_map/ppermute | solution.py:204
  11.9 4.4 %collective-permute-start.6 = (bf16[144,128]{1,0:T(8,128)(2,1)S(1)}, bf16[144,128]{1,0:T(8,128)(2,1)S(1)}, u32[]{:S(2)}, u32[]{:S(2)}) collective-permute-start(bf16[144,128]{1,0:T(8,128)(2,1)S(1)} %get-tuple-element.62.own_ref), channel_id=1, source_target_pairs={{0,16},{4,12},{8,24},{12,4},{16,0},{20,28},{24,8},{28,20},{1,17},{... | collective-permute-start | bytes 110600 | tf_op jit(solution)/shard_map/ppermute | solution.py:204
  12.4 6.4 %collective-permute-start.5 = (bf16[1,384,128]{2,1,0:T(8,128)(2,1)S(1)}, bf16[1,384,128]{2,1,0:T(8,128)(2,1)S(1)}, u32[]{:S(2)}, u32[]{:S(2)}) collective-permute-start(bf16[1,384,128]{2,1,0:T(8,128)(2,1)S(1)} %maximum_bitcast_fusion.refs_1_), channel_id=1, source_target_pairs={{0,8},{4,28},{8,0},{12,20},{16,24},{20,12},{24,16},{28,4},{1,9},{5... | collective-permute-start | bytes 294920 | tf_op jit(solution)/shard_map/ppermute | solution.py:204
  14.0 4.8 %collective-permute-start.4 = (bf16[1,384,128]{2,1,0:T(8,128)(2,1)S(1)}, bf16[1,384,128]{2,1,0:T(8,128)(2,1)S(1)}, u32[]{:S(2)}, u32[]{:S(2)}) collective-permute-start(bf16[1,384,128]{2,1,0:T(8,128)(2,1)S(1)} %maximum_bitcast_fusion.refs_1_), channel_id=1, source_target_pairs={{0,16},{4,12},{8,24},{12,4},{16,0},{20,28},{24,8},{28,20},{1,17},{... | collective-permute-start | bytes 294920 | tf_op jit(solution)/shard_map/ppermute | solution.py:204
  15.6 5.5 %collective-permute-start.3 = (bf16[1,384,128]{2,1,0:T(8,128)(2,1)S(1)}, bf16[1,384,128]{2,1,0:T(8,128)(2,1)S(1)}, u32[]{:S(2)}, u32[]{:S(2)}) collective-permute-start(bf16[1,384,128]{2,1,0:T(8,128)(2,1)S(1)} %maximum_bitcast_fusion.refs_1_), channel_id=1, source_target_pairs={{0,24},{4,20},{8,16},{12,28},{16,8},{20,4},{24,0},{28,12},{1,25},{... | collective-permute-start | bytes 294920 | tf_op jit(solution)/shard_map/ppermute | solution.py:204
  16.3 1.5 %collective-permute-start.8 = (bf16[1,816,128]{2,1,0:T(8,128)(2,1)S(1)}, bf16[1,816,128]{2,1,0:T(8,128)(2,1)S(1)}, u32[]{:S(2)}, u32[]{:S(2)}) collective-permute-start(bf16[1,816,128]{2,1,0:T(8,128)(2,1)S(1)} %pad_maximum_fusion), channel_id=1, source_target_pairs={{0,4},{4,0},{8,12},{12,8},{16,20},{20,16},{24,28},{28,24},{1,5},{5... | collective-permute-start | bytes 626696 | tf_op jit(solution)/shard_map/ppermute | solution.py:197
  18.8 2.4 %collective-permute-start.10 = (bf16[1,384,128]{2,1,0:T(8,128)(2,1)S(1)}, bf16[1,384,128]{2,1,0:T(8,128)(2,1)S(1)}, u32[]{:S(2)}, u32[]{:S(2)}) collective-permute-start(bf16[1,384,128]{2,1,0:T(8,128)(2,1)S(1)} %collective-permute-done.4.refs_4_), channel_id=1, source_target_pairs={{0,4},{4,0},{8,12},{12,8},{16,20},{20,16},{24,28},{28,24},{1,5},{5... | collective-permute-start | bytes 294920 | tf_op jit(solution)/shard_map/ppermute | solution.py:197
  19.1 2.1 %collective-permute-start.11 = (bf16[1,384,128]{2,1,0:T(8,128)(2,1)S(1)}, bf16[1,384,128]{2,1,0:T(8,128)(2,1)S(1)}, u32[]{:S(2)}, u32[]{:S(2)}) collective-permute-start(bf16[1,384,128]{2,1,0:T(8,128)(2,1)S(1)} %collective-permute-done.5.refs_5_), channel_id=1, source_target_pairs={{0,4},{4,0},{8,12},{12,8},{16,20},{20,16},{24,28},{28,24},{1,5},{5... | collective-permute-start | bytes 294920 | tf_op jit(solution)/shard_map/ppermute | solution.py:197
  21.2 1.4 %collective-permute-start.12 = (bf16[1,528,128]{2,1,0:T(8,128)(2,1)S(1)}, bf16[1,528,128]{2,1,0:T(8,128)(2,1)S(1)}, u32[]{:S(2)}, u32[]{:S(2)}) collective-permute-start(bf16[1,528,128]{2,1,0:T(8,128)(2,1)S(1)} %pad_maximum_fusion.1.refs_3_), channel_id=1, source_target_pairs={{0,4},{4,0},{8,12},{12,8},{16,20},{20,16},{24,28},{28,24},{1,5},{5... | collective-permute-start | bytes 405512 | tf_op jit(solution)/shard_map/ppermute | solution.py:197

commit v17 on v16

--- a/solution.py
+++ b/solution.py
@@ -198,7 +198,7 @@
 
     if blocks == 8:
         rest = rest[None]
-        ways = ((4, 2), (2, 6), (6, 4))
+        ways = ((2, 4), (6, 2), (4, 6))
 
         def hop(rows, way):
             return lax.ppermute(rows, "seq", [(i, i ^ way[i & 1]) for i in range(blocks)])

time: 24.2 us -> 24 us (level)
  waiting for transfers between devices: 1.97 us -> 1.41 us
  starting transfers between devices: 14.7 us -> 15 us
    ppermute x6, waiting for transfers between devices: 1.44 us -> 1.06 us  [hop(): lax.ppermute(rows, 'seq', [(i, i ^ way[i & 1]) for i in range(blocks)])]
where the time goes in v17:
time: 24 us; the launch traced here: 23.9 us
  starting transfers between devices  15 us (62%)
  Pallas kernels  5.44 us (23%)
  waiting for transfers between devices  1.41 us (6%)
  other arithmetic  1 us (4%)
  between operations  0.79 us (3%)
    ppermute x6, starting transfers between devices, hop(): lax.ppermute(rows, 'seq', [(i, i ^ way[i & 1]) for i in range(blocks)])  7.1 us
    ppermute x3, starting transfers between devices, shards(): lax.ppermute(rows, 'head', [(i, (i + shift + 1) % pieces) for i in range(...  7.01 us
    pallas_call x5, Pallas kernels, attend_call(): pl.pallas_call(functools.partial(attend, pieces, part, first, last, items...  5.08 us
    ppermute x6, waiting for transfers between devices, hop(): lax.ppermute(rows, 'seq', [(i, i ^ way[i & 1]) for i in range(blocks)])  1.06 us
    concatenate x1, other arithmetic, shards(): jnp.concatenate([keys, values]).reshape(2 * part * kv_heads, head_width)  0.95 us
    ppermute x4, starting transfers between devices, swap(): return lax.ppermute(rows, 'seq', [(i, i ^ flip) for i in range(blocks)])  0.94 us
  transfers between devices with their start and end apart: 13, of which 5 were waited for; matrix products, arithmetic and copies ran while one was open for 1% of the time, Pallas kernels for 16%

profile of v17, /device:TPU:0, one launch (start us, length us, event | category | flops | bytes accessed | tf_op | source)
XLA Modules:
  0.0 23.9 jit_solution(11355772557685668449)
XLA Ops:
  0.0 0.0 copy-start
  0.0 1.0 %pad_maximum_fusion.3 = bf16[128,2,128]{2,1,0:T(2,128)(2,1)S(1)} fusion(bf16[64,2,128]{2,1,0:T(2,128)(2,1)} %param.6, bf16[64,2,128]{2,1,0:T(2,128)(2,1)} %param.5), kind=kLoop, calls=%fused_computation.4 | loop fusion | flops 32768 | bytes 131072 | tf_op jit(solution)/shard_map/concatenate | solution.py:184
  1.0 0.2 shard_map.46
  1.1 3.1 %collective-permute-start = (bf16[128,128]{1,0:T(8,128)(2,1)S(1)}, bf16[128,128]{1,0:T(8,128)(2,1)S(1)}, u32[]{:S(2)}, u32[]{:S(2)}) collective-permute-start(bf16[128,128]{1,0:T(8,128)(2,1)S(1)} %get-tuple-element.34), channel_id=1, source_target_pairs={{0,1},{1,2},{2,3},{3,0},{4,5},{5,6},{6,7},{7,4},{8,9},{9,10},{10,1... | collective-permute-start | bytes 98312 | tf_op jit(solution)/shard_map/ppermute | solution.py:188
  4.2 2.6 %collective-permute-start.1 = (bf16[128,128]{1,0:T(8,128)(2,1)S(1)}, bf16[128,128]{1,0:T(8,128)(2,1)S(1)}, u32[]{:S(2)}, u32[]{:S(2)}) collective-permute-start(bf16[128,128]{1,0:T(8,128)(2,1)S(1)} %get-tuple-element.35), channel_id=1, source_target_pairs={{0,2},{1,3},{2,0},{3,1},{4,6},{5,7},{6,4},{7,5},{8,10},{9,11},{10,... | collective-permute-start | bytes 98312 | tf_op jit(solution)/shard_map/ppermute | solution.py:188
  6.8 1.3 %collective-permute-start.2 = (bf16[128,128]{1,0:T(8,128)(2,1)S(1)}, bf16[128,128]{1,0:T(8,128)(2,1)S(1)}, u32[]{:S(2)}, u32[]{:S(2)}) collective-permute-start(bf16[128,128]{1,0:T(8,128)(2,1)S(1)} %get-tuple-element.36), channel_id=1, source_target_pairs={{0,3},{1,0},{2,1},{3,2},{4,7},{5,4},{6,5},{7,6},{8,11},{9,8},{10,9... | collective-permute-start | bytes 98312 | tf_op jit(solution)/shard_map/ppermute | solution.py:188
  8.8 1.6 %collective-permute-start.9 = (bf16[144,128]{1,0:T(8,128)(2,1)S(1)}, bf16[144,128]{1,0:T(8,128)(2,1)S(1)}, u32[]{:S(2)}, u32[]{:S(2)}) collective-permute-start(bf16[144,128]{1,0:T(8,128)(2,1)S(1)} %get-tuple-element.62.own_ref), channel_id=1, source_target_pairs={{0,16},{4,28},{8,24},{12,20},{16,0},{20,12},{24,8},{28,4},{1,17},{... | collective-permute-start | bytes 110600 | tf_op jit(solution)/shard_map/ppermute | solution.py:204
  10.4 1.4 %collective-permute-start.7 = (bf16[144,128]{1,0:T(8,128)(2,1)S(1)}, bf16[144,128]{1,0:T(8,128)(2,1)S(1)}, u32[]{:S(2)}, u32[]{:S(2)}) collective-permute-start(bf16[144,128]{1,0:T(8,128)(2,1)S(1)} %get-tuple-element.62.own_ref), channel_id=1, source_target_pairs={{0,24},{4,12},{8,16},{12,4},{16,8},{20,28},{24,0},{28,20},{1,25},{... | collective-permute-start | bytes 110600 | tf_op jit(solution)/shard_map/ppermute | solution.py:204
  11.8 0.0 collective-permute-done
  11.8 0.5 %collective-permute-start.6 = (bf16[144,128]{1,0:T(8,128)(2,1)S(1)}, bf16[144,128]{1,0:T(8,128)(2,1)S(1)}, u32[]{:S(2)}, u32[]{:S(2)}) collective-permute-start(bf16[144,128]{1,0:T(8,128)(2,1)S(1)} %get-tuple-element.62.own_ref), channel_id=1, source_target_pairs={{0,8},{4,20},{8,0},{12,28},{16,24},{20,4},{24,16},{28,12},{1,9},{5... | collective-permute-start | bytes 110600 | tf_op jit(solution)/shard_map/ppermute | solution.py:204
  12.4 0.0 collective-permute-done.1
  12.4 0.0 collective-permute-done.2
  12.4 2.5 %collective-permute-start.5 = (bf16[1,384,128]{2,1,0:T(8,128)(2,1)S(1)}, bf16[1,384,128]{2,1,0:T(8,128)(2,1)S(1)}, u32[]{:S(2)}, u32[]{:S(2)}) collective-permute-start(bf16[1,384,128]{2,1,0:T(8,128)(2,1)S(1)} %maximum_bitcast_fusion.refs_1_), channel_id=1, source_target_pairs={{0,24},{4,12},{8,16},{12,4},{16,8},{20,28},{24,0},{28,20},{1,25},{... | collective-permute-start | bytes 294920 | tf_op jit(solution)/shard_map/ppermute | solution.py:204
  14.9 0.5 %collective-permute-start.4 = (bf16[1,384,128]{2,1,0:T(8,128)(2,1)S(1)}, bf16[1,384,128]{2,1,0:T(8,128)(2,1)S(1)}, u32[]{:S(2)}, u32[]{:S(2)}) collective-permute-start(bf16[1,384,128]{2,1,0:T(8,128)(2,1)S(1)} %maximum_bitcast_fusion.refs_1_), channel_id=1, source_target_pairs={{0,8},{4,20},{8,0},{12,28},{16,24},{20,4},{24,16},{28,12},{1,9},{5... | collective-permute-start | bytes 294920 | tf_op jit(solution)/shard_map/ppermute | solution.py:204
  15.4 0.2 collective-permute-done.7
  15.6 0.5 %collective-permute-start.3 = (bf16[1,384,128]{2,1,0:T(8,128)(2,1)S(1)}, bf16[1,384,128]{2,1,0:T(8,128)(2,1)S(1)}, u32[]{:S(2)}, u32[]{:S(2)}) collective-permute-start(bf16[1,384,128]{2,1,0:T(8,128)(2,1)S(1)} %maximum_bitcast_fusion.refs_1_), channel_id=1, source_target_pairs={{0,16},{4,28},{8,24},{12,20},{16,0},{20,12},{24,8},{28,4},{1,17},{... | collective-permute-start | bytes 294920 | tf_op jit(solution)/shard_map/ppermute | solution.py:204
  16.1 0.0 collective-permute-done.6
  16.2 0.1 collective-permute-start.8
  16.2 0.0 copy-done
  16.2 0.1 constant_dynamic-slice_fusion
  16.4 0.2 shard_map.47.query_ref
  16.6 0.8 %shard_map.48 = (f32[1,1024]{1,0:T(1,128)S(1)}, f32[1,1024]{1,0:T(1,128)S(1)}, f32[128,1024]{1,0:T(8,128)S(1)}) custom-call(bf16[144,128]{1,0:T(8,128)(2,1)S(1)} %get-tuple-element.62.own_ref, bf16[256,1024]{1,0:T(8,128)(2,1)S(1)} %shard_map.47.query_ref, bf16[3,144,128]{2,1,0:T(8,128)(2,1)S(1)} %pad_maximum_fusion.2.refs_0_.refs_3_, ...), custom_call_target="tpu_custom_call" | custom-call | flops 1000000000 | tf_op jit(solution)/shard_map/pallas_call | solution.py:150
  17.4 0.0 collective-permute-done.9
  17.4 0.2 %collective-permute-done.8.refs_3_.refs_4_ = bf16[1,816,128]{2,1,0:T(8,128)(2,1)S(1)} collective-permute-done((bf16[1,816,128]{2,1,0:T(8,128)(2,1)S(1)}, bf16[1,816,128]{2,1,0:T(8,128)(2,1)S(1)}, u32[]{:S(2)}, u32[]{:S(2)}) %collective-permute-start.8) | collective-permute-done | bytes 208928 | tf_op jit(solution)/shard_map/ppermute | solution.py:197
  17.7 0.9 %shard_map.49 = (f32[1,1024]{1,0:T(1,128)S(1)}, f32[1,1024]{1,0:T(1,128)S(1)}, f32[128,1024]{1,0:T(8,128)S(1)}) custom-call(bf16[144,128]{1,0:T(8,128)(2,1)S(1)} %get-tuple-element.62.own_ref, bf16[256,1024]{1,0:T(8,128)(2,1)S(1)} %shard_map.47.query_ref, f32[1,1024]{1,0:T(1,128)S(1)} %get-tuple-element.37.refs_0_, f32[1,1024]{1,0:T(1,128)S(1)} %get-tuple-element.38.refs_1_, ...), custom_call_target="tpu_custom_call" | custom-call | tf_op jit(solution)/shard_map/pallas_call | solution.py:150
  18.6 0.2 collective-permute-done.5.refs_5_
  18.9 0.7 %collective-permute-done.4.refs_4_ = bf16[1,384,128]{2,1,0:T(8,128)(2,1)S(1)} collective-permute-done((bf16[1,384,128]{2,1,0:T(8,128)(2,1)S(1)}, bf16[1,384,128]{2,1,0:T(8,128)(2,1)S(1)}, u32[]{:S(2)}, u32[]{:S(2)}) %collective-permute-start.4) | collective-permute-done | bytes 98336 | tf_op jit(solution)/shard_map/ppermute | solution.py:204
  19.5 0.0 collective-permute-start.10
  19.5 0.5 %collective-permute-start.11 = (bf16[1,384,128]{2,1,0:T(8,128)(2,1)S(1)}, bf16[1,384,128]{2,1,0:T(8,128)(2,1)S(1)}, u32[]{:S(2)}, u32[]{:S(2)}) collective-permute-start(bf16[1,384,128]{2,1,0:T(8,128)(2,1)S(1)} %collective-permute-done.5.refs_5_), channel_id=1, source_target_pairs={{0,4},{4,0},{8,12},{12,8},{16,20},{20,16},{24,28},{28,24},{1,5},{5... | collective-permute-start | bytes 294920 | tf_op jit(solution)/shard_map/ppermute | solution.py:197
  20.0 0.8 %shard_map.50 = (f32[1,1024]{1,0:T(1,128)S(1)}, f32[1,1024]{1,0:T(1,128)S(1)}, f32[128,1024]{1,0:T(8,128)S(1)}) custom-call(bf16[144,128]{1,0:T(8,128)(2,1)S(1)} %get-tuple-element.62.own_ref, bf16[256,1024]{1,0:T(8,128)(2,1)S(1)} %shard_map.47.query_ref, f32[1,1024]{1,0:T(1,128)S(1)} %get-tuple-element.43.refs_0_, f32[1,1024]{1,0:T(1,128)S(1)} %get-tuple-element.44.refs_1_, ...), custom_call_target="tpu_custom_call" | custom-call | tf_op jit(solution)/shard_map/pallas_call | solution.py:150
  20.9 0.0 collective-permute-done.3
  20.9 0.0 collective-permute-done.10.refs_5_
  20.9 0.1 collective-permute-done.11.refs_6_
  21.0 0.4 %collective-permute-start.12 = (bf16[1,528,128]{2,1,0:T(8,128)(2,1)S(1)}, bf16[1,528,128]{2,1,0:T(8,128)(2,1)S(1)}, u32[]{:S(2)}, u32[]{:S(2)}) collective-permute-start(bf16[1,528,128]{2,1,0:T(8,128)(2,1)S(1)} %pad_maximum_fusion.1.refs_3_), channel_id=1, source_target_pairs={{0,4},{4,0},{8,12},{12,8},{16,20},{20,16},{24,28},{28,24},{1,5},{5... | collective-permute-start | bytes 405512 | tf_op jit(solution)/shard_map/ppermute | solution.py:197
  21.3 1.1 %shard_map.51 = (f32[1,1024]{1,0:T(1,128)S(1)}, f32[1,1024]{1,0:T(1,128)S(1)}, f32[128,1024]{1,0:T(8,128)S(1)}) custom-call(bf16[144,128]{1,0:T(8,128)(2,1)S(1)} %get-tuple-element.62.own_ref, bf16[256,1024]{1,0:T(8,128)(2,1)S(1)} %shard_map.47.query_ref, f32[1,1024]{1,0:T(1,128)S(1)} %get-tuple-element.51.refs_0_, f32[1,1024]{1,0:T(1,128)S(1)} %get-tuple-element.52.refs_1_, ...), custom_call_target="tpu_custom_call" | custom-call | tf_op jit(solution)/shard_map/pallas_call | solution.py:150
  22.4 0.0 collective-permute-done.12.refs_3_
  22.4 1.4 %shard_map.52 = bf16[1024,128]{1,0:T(8,128)(2,1)} custom-call(bf16[144,128]{1,0:T(8,128)(2,1)S(1)} %get-tuple-element.62.own_ref, bf16[256,1024]{1,0:T(8,128)(2,1)S(1)} %shard_map.47.query_ref, f32[1,1024]{1,0:T(1,128)S(1)} %get-tuple-element.58.refs_0_, f32[1,1024]{1,0:T(1,128)S(1)} %get-tuple-element.59.refs_1_, ...), custom_call_target="tpu_custom_call" | custom-call | tf_op jit(solution)/shard_map/pallas_call | solution.py:150
  (5 shorter events, 0.1 us)
Async XLA Ops:
  0.0 16.2 %copy-start = (bf16[256,16,128]{2,1,0:T(8,128)(2,1)S(1)}, bf16[256,16,128]{2,1,0:T(8,128)(2,1)}, u32[]{:S(2)}) copy-start(bf16[256,16,128]{2,1,0:T(8,128)(2,1)} %param.4) | copy-start | bytes 3145732
  1.1 10.7 %collective-permute-start = (bf16[128,128]{1,0:T(8,128)(2,1)S(1)}, bf16[128,128]{1,0:T(8,128)(2,1)S(1)}, u32[]{:S(2)}, u32[]{:S(2)}) collective-permute-start(bf16[128,128]{1,0:T(8,128)(2,1)S(1)} %get-tuple-element.34), channel_id=1, source_target_pairs={{0,1},{1,2},{2,3},{3,0},{4,5},{5,6},{6,7},{7,4},{8,9},{9,10},{10,1... | collective-permute-start | bytes 98312 | tf_op jit(solution)/shard_map/ppermute | solution.py:188
  4.2 8.2 %collective-permute-start.1 = (bf16[128,128]{1,0:T(8,128)(2,1)S(1)}, bf16[128,128]{1,0:T(8,128)(2,1)S(1)}, u32[]{:S(2)}, u32[]{:S(2)}) collective-permute-start(bf16[128,128]{1,0:T(8,128)(2,1)S(1)} %get-tuple-element.35), channel_id=1, source_target_pairs={{0,2},{1,3},{2,0},{3,1},{4,6},{5,7},{6,4},{7,5},{8,10},{9,11},{10,... | collective-permute-start | bytes 98312 | tf_op jit(solution)/shard_map/ppermute | solution.py:188
  6.8 5.6 %collective-permute-start.2 = (bf16[128,128]{1,0:T(8,128)(2,1)S(1)}, bf16[128,128]{1,0:T(8,128)(2,1)S(1)}, u32[]{:S(2)}, u32[]{:S(2)}) collective-permute-start(bf16[128,128]{1,0:T(8,128)(2,1)S(1)} %get-tuple-element.36), channel_id=1, source_target_pairs={{0,3},{1,0},{2,1},{3,2},{4,7},{5,4},{6,5},{7,6},{8,11},{9,8},{10,9... | collective-permute-start | bytes 98312 | tf_op jit(solution)/shard_map/ppermute | solution.py:188
  8.8 8.6 %collective-permute-start.9 = (bf16[144,128]{1,0:T(8,128)(2,1)S(1)}, bf16[144,128]{1,0:T(8,128)(2,1)S(1)}, u32[]{:S(2)}, u32[]{:S(2)}) collective-permute-start(bf16[144,128]{1,0:T(8,128)(2,1)S(1)} %get-tuple-element.62.own_ref), channel_id=1, source_target_pairs={{0,16},{4,28},{8,24},{12,20},{16,0},{20,12},{24,8},{28,4},{1,17},{... | collective-permute-start | bytes 110600 | tf_op jit(solution)/shard_map/ppermute | solution.py:204
  10.4 5.2 %collective-permute-start.7 = (bf16[144,128]{1,0:T(8,128)(2,1)S(1)}, bf16[144,128]{1,0:T(8,128)(2,1)S(1)}, u32[]{:S(2)}, u32[]{:S(2)}) collective-permute-start(bf16[144,128]{1,0:T(8,128)(2,1)S(1)} %get-tuple-element.62.own_ref), channel_id=1, source_target_pairs={{0,24},{4,12},{8,16},{12,4},{16,8},{20,28},{24,0},{28,20},{1,25},{... | collective-permute-start | bytes 110600 | tf_op jit(solution)/shard_map/ppermute | solution.py:204
  11.8 4.3 %collective-permute-start.6 = (bf16[144,128]{1,0:T(8,128)(2,1)S(1)}, bf16[144,128]{1,0:T(8,128)(2,1)S(1)}, u32[]{:S(2)}, u32[]{:S(2)}) collective-permute-start(bf16[144,128]{1,0:T(8,128)(2,1)S(1)} %get-tuple-element.62.own_ref), channel_id=1, source_target_pairs={{0,8},{4,20},{8,0},{12,28},{16,24},{20,4},{24,16},{28,12},{1,9},{5... | collective-permute-start | bytes 110600 | tf_op jit(solution)/shard_map/ppermute | solution.py:204
  12.4 6.5 %collective-permute-start.5 = (bf16[1,384,128]{2,1,0:T(8,128)(2,1)S(1)}, bf16[1,384,128]{2,1,0:T(8,128)(2,1)S(1)}, u32[]{:S(2)}, u32[]{:S(2)}) collective-permute-start(bf16[1,384,128]{2,1,0:T(8,128)(2,1)S(1)} %maximum_bitcast_fusion.refs_1_), channel_id=1, source_target_pairs={{0,24},{4,12},{8,16},{12,4},{16,8},{20,28},{24,0},{28,20},{1,25},{... | collective-permute-start | bytes 294920 | tf_op jit(solution)/shard_map/ppermute | solution.py:204
  14.9 4.6 %collective-permute-start.4 = (bf16[1,384,128]{2,1,0:T(8,128)(2,1)S(1)}, bf16[1,384,128]{2,1,0:T(8,128)(2,1)S(1)}, u32[]{:S(2)}, u32[]{:S(2)}) collective-permute-start(bf16[1,384,128]{2,1,0:T(8,128)(2,1)S(1)} %maximum_bitcast_fusion.refs_1_), channel_id=1, source_target_pairs={{0,8},{4,20},{8,0},{12,28},{16,24},{20,4},{24,16},{28,12},{1,9},{5... | collective-permute-start | bytes 294920 | tf_op jit(solution)/shard_map/ppermute | solution.py:204
  15.6 5.2 %collective-permute-start.3 = (bf16[1,384,128]{2,1,0:T(8,128)(2,1)S(1)}, bf16[1,384,128]{2,1,0:T(8,128)(2,1)S(1)}, u32[]{:S(2)}, u32[]{:S(2)}) collective-permute-start(bf16[1,384,128]{2,1,0:T(8,128)(2,1)S(1)} %maximum_bitcast_fusion.refs_1_), channel_id=1, source_target_pairs={{0,16},{4,28},{8,24},{12,20},{16,0},{20,12},{24,8},{28,4},{1,17},{... | collective-permute-start | bytes 294920 | tf_op jit(solution)/shard_map/ppermute | solution.py:204
  16.2 1.5 %collective-permute-start.8 = (bf16[1,816,128]{2,1,0:T(8,128)(2,1)S(1)}, bf16[1,816,128]{2,1,0:T(8,128)(2,1)S(1)}, u32[]{:S(2)}, u32[]{:S(2)}) collective-permute-start(bf16[1,816,128]{2,1,0:T(8,128)(2,1)S(1)} %pad_maximum_fusion), channel_id=1, source_target_pairs={{0,4},{4,0},{8,12},{12,8},{16,20},{20,16},{24,28},{28,24},{1,5},{5... | collective-permute-start | bytes 626696 | tf_op jit(solution)/shard_map/ppermute | solution.py:197
  19.5 1.4 %collective-permute-start.10 = (bf16[1,384,128]{2,1,0:T(8,128)(2,1)S(1)}, bf16[1,384,128]{2,1,0:T(8,128)(2,1)S(1)}, u32[]{:S(2)}, u32[]{:S(2)}) collective-permute-start(bf16[1,384,128]{2,1,0:T(8,128)(2,1)S(1)} %collective-permute-done.4.refs_4_), channel_id=1, source_target_pairs={{0,4},{4,0},{8,12},{12,8},{16,20},{20,16},{24,28},{28,24},{1,5},{5... | collective-permute-start | bytes 294920 | tf_op jit(solution)/shard_map/ppermute | solution.py:197
  19.5 1.5 %collective-permute-start.11 = (bf16[1,384,128]{2,1,0:T(8,128)(2,1)S(1)}, bf16[1,384,128]{2,1,0:T(8,128)(2,1)S(1)}, u32[]{:S(2)}, u32[]{:S(2)}) collective-permute-start(bf16[1,384,128]{2,1,0:T(8,128)(2,1)S(1)} %collective-permute-done.5.refs_5_), channel_id=1, source_target_pairs={{0,4},{4,0},{8,12},{12,8},{16,20},{20,16},{24,28},{28,24},{1,5},{5... | collective-permute-start | bytes 294920 | tf_op jit(solution)/shard_map/ppermute | solution.py:197
  21.0 1.4 %collective-permute-start.12 = (bf16[1,528,128]{2,1,0:T(8,128)(2,1)S(1)}, bf16[1,528,128]{2,1,0:T(8,128)(2,1)S(1)}, u32[]{:S(2)}, u32[]{:S(2)}) collective-permute-start(bf16[1,528,128]{2,1,0:T(8,128)(2,1)S(1)} %pad_maximum_fusion.1.refs_3_), channel_id=1, source_target_pairs={{0,4},{4,0},{8,12},{12,8},{16,20},{20,16},{24,28},{28,24},{1,5},{5... | collective-permute-start | bytes 405512 | tf_op jit(solution)/shard_map/ppermute | solution.py:197

commit v18 on v17

--- a/solution.py
+++ b/solution.py
@@ -198,7 +198,7 @@
 
     if blocks == 8:
         rest = rest[None]
-        ways = ((2, 4), (6, 2), (4, 6))
+        ways = ((2, 4), (6, 6), (4, 2))
 
         def hop(rows, way):
             return lax.ppermute(rows, "seq", [(i, i ^ way[i & 1]) for i in range(blocks)])
@@ -232,16 +232,16 @@
             False,
         )
         along_one, along_two, state = lax.optimization_barrier((along_one, along_two, state))
-        others = [swap(rows, 1) for rows in (along_one, along_two)]
+        others = swap(jnp.concatenate([along_one, along_two]), 1)
         state = fold(state, [mine, along_one, along_two], [large(i, 0, i) for i in (1, 2)], False)
         along_last, state = lax.optimization_barrier((along_last, state))
         along_last = jnp.concatenate([near_last[None], along_last], axis=1)
-        along_last, *others = lax.optimization_barrier((along_last, *others))
+        along_last, others = lax.optimization_barrier((along_last, others))
         other_last = swap(along_last, 1)
         state = fold(
             state,
-            [along_last, both_other] + others,
-            [large(0, 0, 0, size)] + [(1 + i, 0, offsets[:-1], None, (1, 0, size * i + 2 * part)) for i in (1, 2)],
+            [along_last, both_other, others],
+            [large(0, 0, 0, size)] + [(2, i - 1, offsets[:-1], None, (1, 0, size * i + 2 * part)) for i in (1, 2)],
             False,
         )
         result = fold(

time: 24 us -> 24.2 us (level)
  starting transfers between devices: 15 us -> 15.5 us
  waiting for transfers between devices: 1.41 us -> 1.06 us
    ppermute x6, starting transfers between devices: 7.1 us -> 8.19 us  [hop(): lax.ppermute(rows, 'seq', [(i, i ^ way[i & 1]) for i in range(blocks)])]
    ppermute x4 -> x3, starting transfers between devices: 0.94 us -> 0.33 us  [swap(): return lax.ppermute(rows, 'seq', [(i, i ^ flip) for i in range(blocks)])]
    ppermute x6, waiting for transfers between devices: 1.06 us -> 0.67 us  [hop(): lax.ppermute(rows, 'seq', [(i, i ^ way[i & 1]) for i in range(blocks)])]
  transfers between devices with their start and end apart: 13 -> 12, of which waited for: 5 -> 5; matrix products, arithmetic and copies ran while one was open for 1% -> 1% of each run, Pallas kernels for 16% -> 16%
where the time goes in v18:
time: 24.2 us; the launch traced here: 24 us
  starting transfers between devices  15.5 us (64%)
  Pallas kernels  5.44 us (22%)
  waiting for transfers between devices  1.06 us (4%)
  other arithmetic  1.02 us (4%)
  between operations  0.8 us (3%)
    ppermute x6, starting transfers between devices, hop(): lax.ppermute(rows, 'seq', [(i, i ^ way[i & 1]) for i in range(blocks)])  8.19 us
    ppermute x3, starting transfers between devices, shards(): lax.ppermute(rows, 'head', [(i, (i + shift + 1) % pieces) for i in range(...  7.01 us
    pallas_call x5, Pallas kernels, attend_call(): pl.pallas_call(functools.partial(attend, pieces, part, first, last, items...  5.08 us
    concatenate x1, other arithmetic, shards(): jnp.concatenate([keys, values]).reshape(2 * part * kv_heads, head_width)  0.95 us
    ppermute x6, waiting for transfers between devices, hop(): lax.ppermute(rows, 'seq', [(i, i ^ way[i & 1]) for i in range(blocks)])  0.67 us
  transfers between devices with their start and end apart: 12, of which 5 were waited for; matrix products, arithmetic and copies ran while one was open for 1% of the time, Pallas kernels for 16%

profile of v18, /device:TPU:0, one launch (start us, length us, event | category | flops | bytes accessed | tf_op | source)
XLA Modules:
  0.0 24.0 jit_solution(9281371561816795153)
XLA Ops:
  0.0 0.0 copy-start
  0.0 1.0 %pad_maximum_fusion.4 = bf16[128,2,128]{2,1,0:T(2,128)(2,1)S(1)} fusion(bf16[64,2,128]{2,1,0:T(2,128)(2,1)} %param.6, bf16[64,2,128]{2,1,0:T(2,128)(2,1)} %param.5), kind=kLoop, calls=%fused_computation.5 | loop fusion | flops 32768 | bytes 131072 | tf_op jit(solution)/shard_map/concatenate | solution.py:184
  1.0 0.2 shard_map.46
  1.1 3.1 %collective-permute-start = (bf16[128,128]{1,0:T(8,128)(2,1)S(1)}, bf16[128,128]{1,0:T(8,128)(2,1)S(1)}, u32[]{:S(2)}, u32[]{:S(2)}) collective-permute-start(bf16[128,128]{1,0:T(8,128)(2,1)S(1)} %get-tuple-element.33), channel_id=1, source_target_pairs={{0,1},{1,2},{2,3},{3,0},{4,5},{5,6},{6,7},{7,4},{8,9},{9,10},{10,1... | collective-permute-start | bytes 98312 | tf_op jit(solution)/shard_map/ppermute | solution.py:188
  4.2 2.6 %collective-permute-start.1 = (bf16[128,128]{1,0:T(8,128)(2,1)S(1)}, bf16[128,128]{1,0:T(8,128)(2,1)S(1)}, u32[]{:S(2)}, u32[]{:S(2)}) collective-permute-start(bf16[128,128]{1,0:T(8,128)(2,1)S(1)} %get-tuple-element.34), channel_id=1, source_target_pairs={{0,2},{1,3},{2,0},{3,1},{4,6},{5,7},{6,4},{7,5},{8,10},{9,11},{10,... | collective-permute-start | bytes 98312 | tf_op jit(solution)/shard_map/ppermute | solution.py:188
  6.8 1.3 %collective-permute-start.2 = (bf16[128,128]{1,0:T(8,128)(2,1)S(1)}, bf16[128,128]{1,0:T(8,128)(2,1)S(1)}, u32[]{:S(2)}, u32[]{:S(2)}) collective-permute-start(bf16[128,128]{1,0:T(8,128)(2,1)S(1)} %get-tuple-element.35), channel_id=1, source_target_pairs={{0,3},{1,0},{2,1},{3,2},{4,7},{5,4},{6,5},{7,6},{8,11},{9,8},{10,9... | collective-permute-start | bytes 98312 | tf_op jit(solution)/shard_map/ppermute | solution.py:188
  8.8 1.6 %collective-permute-start.9 = (bf16[144,128]{1,0:T(8,128)(2,1)S(1)}, bf16[144,128]{1,0:T(8,128)(2,1)S(1)}, u32[]{:S(2)}, u32[]{:S(2)}) collective-permute-start(bf16[144,128]{1,0:T(8,128)(2,1)S(1)} %get-tuple-element.60.own_ref), channel_id=1, source_target_pairs={{0,16},{4,12},{8,24},{12,4},{16,0},{20,28},{24,8},{28,20},{1,17},{... | collective-permute-start | bytes 110600 | tf_op jit(solution)/shard_map/ppermute | solution.py:204
  10.4 1.4 %collective-permute-start.7 = (bf16[144,128]{1,0:T(8,128)(2,1)S(1)}, bf16[144,128]{1,0:T(8,128)(2,1)S(1)}, u32[]{:S(2)}, u32[]{:S(2)}) collective-permute-start(bf16[144,128]{1,0:T(8,128)(2,1)S(1)} %get-tuple-element.60.own_ref), channel_id=1, source_target_pairs={{0,24},{4,28},{8,16},{12,20},{16,8},{20,12},{24,0},{28,4},{1,25},{... | collective-permute-start | bytes 110600 | tf_op jit(solution)/shard_map/ppermute | solution.py:204
  11.8 0.0 collective-permute-done
  11.8 0.5 %collective-permute-start.6 = (bf16[144,128]{1,0:T(8,128)(2,1)S(1)}, bf16[144,128]{1,0:T(8,128)(2,1)S(1)}, u32[]{:S(2)}, u32[]{:S(2)}) collective-permute-start(bf16[144,128]{1,0:T(8,128)(2,1)S(1)} %get-tuple-element.60.own_ref), channel_id=1, source_target_pairs={{0,8},{4,20},{8,0},{12,28},{16,24},{20,4},{24,16},{28,12},{1,9},{5... | collective-permute-start | bytes 110600 | tf_op jit(solution)/shard_map/ppermute | solution.py:204
  12.4 0.0 collective-permute-done.1
  12.4 0.0 collective-permute-done.2
  12.4 2.5 %collective-permute-start.5 = (bf16[1,384,128]{2,1,0:T(8,128)(2,1)S(1)}, bf16[1,384,128]{2,1,0:T(8,128)(2,1)S(1)}, u32[]{:S(2)}, u32[]{:S(2)}) collective-permute-start(bf16[1,384,128]{2,1,0:T(8,128)(2,1)S(1)} %maximum_bitcast_fusion.refs_1_), channel_id=1, source_target_pairs={{0,24},{4,28},{8,16},{12,20},{16,8},{20,12},{24,0},{28,4},{1,25},{... | collective-permute-start | bytes 294920 | tf_op jit(solution)/shard_map/ppermute | solution.py:204
  14.9 0.5 %collective-permute-start.4 = (bf16[1,384,128]{2,1,0:T(8,128)(2,1)S(1)}, bf16[1,384,128]{2,1,0:T(8,128)(2,1)S(1)}, u32[]{:S(2)}, u32[]{:S(2)}) collective-permute-start(bf16[1,384,128]{2,1,0:T(8,128)(2,1)S(1)} %maximum_bitcast_fusion.refs_1_), channel_id=1, source_target_pairs={{0,8},{4,20},{8,0},{12,28},{16,24},{20,4},{24,16},{28,12},{1,9},{5... | collective-permute-start | bytes 294920 | tf_op jit(solution)/shard_map/ppermute | solution.py:204
  15.4 0.1 collective-permute-done.7
  15.6 0.2 collective-permute-done.6
  15.8 0.1 collective-permute-start.8
  15.9 0.0 copy-done
  15.9 0.1 constant_dynamic-slice_fusion
  16.1 0.2 shard_map.47.query_ref
  16.3 1.6 %collective-permute-start.3 = (bf16[1,384,128]{2,1,0:T(8,128)(2,1)S(1)}, bf16[1,384,128]{2,1,0:T(8,128)(2,1)S(1)}, u32[]{:S(2)}, u32[]{:S(2)}) collective-permute-start(bf16[1,384,128]{2,1,0:T(8,128)(2,1)S(1)} %maximum_bitcast_fusion.refs_1_), channel_id=1, source_target_pairs={{0,16},{4,12},{8,24},{12,4},{16,0},{20,28},{24,8},{28,20},{1,17},{... | collective-permute-start | bytes 294920 | tf_op jit(solution)/shard_map/ppermute | solution.py:204
  17.9 0.8 %shard_map.48 = (f32[1,1024]{1,0:T(1,128)S(1)}, f32[1,1024]{1,0:T(1,128)S(1)}, f32[128,1024]{1,0:T(8,128)S(1)}) custom-call(bf16[144,128]{1,0:T(8,128)(2,1)S(1)} %get-tuple-element.60.own_ref, bf16[256,1024]{1,0:T(8,128)(2,1)S(1)} %shard_map.47.query_ref, bf16[3,144,128]{2,1,0:T(8,128)(2,1)S(1)} %pad_maximum_fusion.3.refs_0_.refs_3_, ...), custom_call_target="tpu_custom_call" | custom-call | flops 1000000000 | tf_op jit(solution)/shard_map/pallas_call | solution.py:150
  18.7 0.0 collective-permute-done.9
  18.7 0.0 collective-permute-done.8.refs_3_.refs_4_
  18.7 1.0 %shard_map.49 = (f32[1,1024]{1,0:T(1,128)S(1)}, f32[1,1024]{1,0:T(1,128)S(1)}, f32[128,1024]{1,0:T(8,128)S(1)}) custom-call(bf16[144,128]{1,0:T(8,128)(2,1)S(1)} %get-tuple-element.60.own_ref, bf16[256,1024]{1,0:T(8,128)(2,1)S(1)} %shard_map.47.query_ref, f32[1,1024]{1,0:T(1,128)S(1)} %get-tuple-element.36.refs_0_, f32[1,1024]{1,0:T(1,128)S(1)} %get-tuple-element.37.refs_1_, ...), custom_call_target="tpu_custom_call" | custom-call | tf_op jit(solution)/shard_map/pallas_call | solution.py:150
  19.7 0.0 collective-permute-done.5.refs_5_
  19.7 0.0 collective-permute-done.4.refs_4_
  19.7 0.1 collective-permute-start.10
  19.8 0.8 %shard_map.50 = (f32[1,1024]{1,0:T(1,128)S(1)}, f32[1,1024]{1,0:T(1,128)S(1)}, f32[128,1024]{1,0:T(8,128)S(1)}) custom-call(bf16[144,128]{1,0:T(8,128)(2,1)S(1)} %get-tuple-element.60.own_ref, bf16[256,1024]{1,0:T(8,128)(2,1)S(1)} %shard_map.47.query_ref, f32[1,1024]{1,0:T(1,128)S(1)} %get-tuple-element.42.refs_0_, f32[1,1024]{1,0:T(1,128)S(1)} %get-tuple-element.43.refs_1_, ...), custom_call_target="tpu_custom_call" | custom-call | tf_op jit(solution)/shard_map/pallas_call | solution.py:150
  20.7 0.3 %collective-permute-done.3 = bf16[1,384,128]{2,1,0:T(8,128)(2,1)S(1)} collective-permute-done((bf16[1,384,128]{2,1,0:T(8,128)(2,1)S(1)}, bf16[1,384,128]{2,1,0:T(8,128)(2,1)S(1)}, u32[]{:S(2)}, u32[]{:S(2)}) %collective-permute-start.3) | collective-permute-done | bytes 98336 | tf_op jit(solution)/shard_map/ppermute | solution.py:204
  21.0 0.2 %collective-permute-done.10.refs_5_ = bf16[2,384,128]{2,1,0:T(8,128)(2,1)S(1)} collective-permute-done((bf16[2,384,128]{2,1,0:T(8,128)(2,1)S(1)}, bf16[2,384,128]{2,1,0:T(8,128)(2,1)S(1)}, u32[]{:S(2)}, u32[]{:S(2)}) %collective-permute-start.10) | collective-permute-done | bytes 196640 | tf_op jit(solution)/shard_map/ppermute | solution.py:197
  21.2 0.1 collective-permute-start.11
  21.4 1.1 %shard_map.51 = (f32[1,1024]{1,0:T(1,128)S(1)}, f32[1,1024]{1,0:T(1,128)S(1)}, f32[128,1024]{1,0:T(8,128)S(1)}) custom-call(bf16[144,128]{1,0:T(8,128)(2,1)S(1)} %get-tuple-element.60.own_ref, bf16[256,1024]{1,0:T(8,128)(2,1)S(1)} %shard_map.47.query_ref, f32[1,1024]{1,0:T(1,128)S(1)} %get-tuple-element.50.refs_0_, f32[1,1024]{1,0:T(1,128)S(1)} %get-tuple-element.51.refs_1_, ...), custom_call_target="tpu_custom_call" | custom-call | tf_op jit(solution)/shard_map/pallas_call | solution.py:150
  22.5 0.1 collective-permute-done.11.refs_3_
  22.6 1.4 %shard_map.52 = bf16[1024,128]{1,0:T(8,128)(2,1)} custom-call(bf16[144,128]{1,0:T(8,128)(2,1)S(1)} %get-tuple-element.60.own_ref, bf16[256,1024]{1,0:T(8,128)(2,1)S(1)} %shard_map.47.query_ref, f32[1,1024]{1,0:T(1,128)S(1)} %get-tuple-element.56.refs_0_, f32[1,1024]{1,0:T(1,128)S(1)} %get-tuple-element.57.refs_1_, ...), custom_call_target="tpu_custom_call" | custom-call | tf_op jit(solution)/shard_map/pallas_call | solution.py:150
  (6 shorter events, 0.1 us)
Async XLA Ops:
  0.0 15.9 %copy-start = (bf16[256,16,128]{2,1,0:T(8,128)(2,1)S(1)}, bf16[256,16,128]{2,1,0:T(8,128)(2,1)}, u32[]{:S(2)}) copy-start(bf16[256,16,128]{2,1,0:T(8,128)(2,1)} %param.4) | copy-start | bytes 3145732
  1.1 10.7 %collective-permute-start = (bf16[128,128]{1,0:T(8,128)(2,1)S(1)}, bf16[128,128]{1,0:T(8,128)(2,1)S(1)}, u32[]{:S(2)}, u32[]{:S(2)}) collective-permute-start(bf16[128,128]{1,0:T(8,128)(2,1)S(1)} %get-tuple-element.33), channel_id=1, source_target_pairs={{0,1},{1,2},{2,3},{3,0},{4,5},{5,6},{6,7},{7,4},{8,9},{9,10},{10,1... | collective-permute-start | bytes 98312 | tf_op jit(solution)/shard_map/ppermute | solution.py:188
  4.2 8.2 %collective-permute-start.1 = (bf16[128,128]{1,0:T(8,128)(2,1)S(1)}, bf16[128,128]{1,0:T(8,128)(2,1)S(1)}, u32[]{:S(2)}, u32[]{:S(2)}) collective-permute-start(bf16[128,128]{1,0:T(8,128)(2,1)S(1)} %get-tuple-element.34), channel_id=1, source_target_pairs={{0,2},{1,3},{2,0},{3,1},{4,6},{5,7},{6,4},{7,5},{8,10},{9,11},{10,... | collective-permute-start | bytes 98312 | tf_op jit(solution)/shard_map/ppermute | solution.py:188
  6.8 5.6 %collective-permute-start.2 = (bf16[128,128]{1,0:T(8,128)(2,1)S(1)}, bf16[128,128]{1,0:T(8,128)(2,1)S(1)}, u32[]{:S(2)}, u32[]{:S(2)}) collective-permute-start(bf16[128,128]{1,0:T(8,128)(2,1)S(1)} %get-tuple-element.35), channel_id=1, source_target_pairs={{0,3},{1,0},{2,1},{3,2},{4,7},{5,4},{6,5},{7,6},{8,11},{9,8},{10,9... | collective-permute-start | bytes 98312 | tf_op jit(solution)/shard_map/ppermute | solution.py:188
  8.8 9.9 %collective-permute-start.9 = (bf16[144,128]{1,0:T(8,128)(2,1)S(1)}, bf16[144,128]{1,0:T(8,128)(2,1)S(1)}, u32[]{:S(2)}, u32[]{:S(2)}) collective-permute-start(bf16[144,128]{1,0:T(8,128)(2,1)S(1)} %get-tuple-element.60.own_ref), channel_id=1, source_target_pairs={{0,16},{4,12},{8,24},{12,4},{16,0},{20,28},{24,8},{28,20},{1,17},{... | collective-permute-start | bytes 110600 | tf_op jit(solution)/shard_map/ppermute | solution.py:204
  10.4 5.2 %collective-permute-start.7 = (bf16[144,128]{1,0:T(8,128)(2,1)S(1)}, bf16[144,128]{1,0:T(8,128)(2,1)S(1)}, u32[]{:S(2)}, u32[]{:S(2)}) collective-permute-start(bf16[144,128]{1,0:T(8,128)(2,1)S(1)} %get-tuple-element.60.own_ref), channel_id=1, source_target_pairs={{0,24},{4,28},{8,16},{12,20},{16,8},{20,12},{24,0},{28,4},{1,25},{... | collective-permute-start | bytes 110600 | tf_op jit(solution)/shard_map/ppermute | solution.py:204
  11.8 4.0 %collective-permute-start.6 = (bf16[144,128]{1,0:T(8,128)(2,1)S(1)}, bf16[144,128]{1,0:T(8,128)(2,1)S(1)}, u32[]{:S(2)}, u32[]{:S(2)}) collective-permute-start(bf16[144,128]{1,0:T(8,128)(2,1)S(1)} %get-tuple-element.60.own_ref), channel_id=1, source_target_pairs={{0,8},{4,20},{8,0},{12,28},{16,24},{20,4},{24,16},{28,12},{1,9},{5... | collective-permute-start | bytes 110600 | tf_op jit(solution)/shard_map/ppermute | solution.py:204
  12.4 7.3 %collective-permute-start.5 = (bf16[1,384,128]{2,1,0:T(8,128)(2,1)S(1)}, bf16[1,384,128]{2,1,0:T(8,128)(2,1)S(1)}, u32[]{:S(2)}, u32[]{:S(2)}) collective-permute-start(bf16[1,384,128]{2,1,0:T(8,128)(2,1)S(1)} %maximum_bitcast_fusion.refs_1_), channel_id=1, source_target_pairs={{0,24},{4,28},{8,16},{12,20},{16,8},{20,12},{24,0},{28,4},{1,25},{... | collective-permute-start | bytes 294920 | tf_op jit(solution)/shard_map/ppermute | solution.py:204
  14.9 4.8 %collective-permute-start.4 = (bf16[1,384,128]{2,1,0:T(8,128)(2,1)S(1)}, bf16[1,384,128]{2,1,0:T(8,128)(2,1)S(1)}, u32[]{:S(2)}, u32[]{:S(2)}) collective-permute-start(bf16[1,384,128]{2,1,0:T(8,128)(2,1)S(1)} %maximum_bitcast_fusion.refs_1_), channel_id=1, source_target_pairs={{0,8},{4,20},{8,0},{12,28},{16,24},{20,4},{24,16},{28,12},{1,9},{5... | collective-permute-start | bytes 294920 | tf_op jit(solution)/shard_map/ppermute | solution.py:204
  15.8 2.9 %collective-permute-start.8 = (bf16[1,816,128]{2,1,0:T(8,128)(2,1)S(1)}, bf16[1,816,128]{2,1,0:T(8,128)(2,1)S(1)}, u32[]{:S(2)}, u32[]{:S(2)}) collective-permute-start(bf16[1,816,128]{2,1,0:T(8,128)(2,1)S(1)} %pad_maximum_fusion), channel_id=1, source_target_pairs={{0,4},{4,0},{8,12},{12,8},{16,20},{20,16},{24,28},{28,24},{1,5},{5... | collective-permute-start | bytes 626696 | tf_op jit(solution)/shard_map/ppermute | solution.py:197
  16.3 4.7 %collective-permute-start.3 = (bf16[1,384,128]{2,1,0:T(8,128)(2,1)S(1)}, bf16[1,384,128]{2,1,0:T(8,128)(2,1)S(1)}, u32[]{:S(2)}, u32[]{:S(2)}) collective-permute-start(bf16[1,384,128]{2,1,0:T(8,128)(2,1)S(1)} %maximum_bitcast_fusion.refs_1_), channel_id=1, source_target_pairs={{0,16},{4,12},{8,24},{12,4},{16,0},{20,28},{24,8},{28,20},{1,17},{... | collective-permute-start | bytes 294920 | tf_op jit(solution)/shard_map/ppermute | solution.py:204
  19.7 1.5 %collective-permute-start.10 = (bf16[2,384,128]{2,1,0:T(8,128)(2,1)S(1)}, bf16[2,384,128]{2,1,0:T(8,128)(2,1)S(1)}, u32[]{:S(2)}, u32[]{:S(2)}) collective-permute-start(bf16[2,384,128]{2,1,0:T(8,128)(2,1)S(1)} %pad_maximum_fusion.1), channel_id=1, source_target_pairs={{0,4},{4,0},{8,12},{12,8},{16,20},{20,16},{24,28},{28,24},{1,5},{5... | collective-permute-start | bytes 589832 | tf_op jit(solution)/shard_map/ppermute | solution.py:197
  21.2 1.4 %collective-permute-start.11 = (bf16[1,528,128]{2,1,0:T(8,128)(2,1)S(1)}, bf16[1,528,128]{2,1,0:T(8,128)(2,1)S(1)}, u32[]{:S(2)}, u32[]{:S(2)}) collective-permute-start(bf16[1,528,128]{2,1,0:T(8,128)(2,1)S(1)} %pad_maximum_fusion.2.refs_3_), channel_id=1, source_target_pairs={{0,4},{4,0},{8,12},{12,8},{16,20},{20,16},{24,28},{28,24},{1,5},{5... | collective-permute-start | bytes 405512 | tf_op jit(solution)/shard_map/ppermute | solution.py:197

commit v19 on v18

--- a/solution.py
+++ b/solution.py
@@ -36,19 +36,16 @@
             out_ref[pl.ds(half * part, part), :] = rows_out
 
 
-def scale_queries(scale, query_ref, out_ref):
-    head_width = query_ref.shape[1]
-    scaled = query_ref[...].astype(jnp.float32) * (scale * math.log2(math.e))
-    coarse = scaled.astype(jnp.bfloat16)
-    out_ref[:head_width, :] = coarse.T
-    out_ref[head_width:, :] = (scaled - coarse.astype(jnp.float32)).astype(jnp.bfloat16).T
+def turn_queries(query_ref, out_ref):
+    out_ref[...] = query_ref[...].T
 
 
 def attend(pieces, part, first, last, items, own_ref, query_ref, *refs):
     refs = list(refs)
     state = None if first else [refs.pop(0) for _ in range(3)]
     outs = [refs.pop() for _ in range(3)][::-1]
-    head_width = query_ref.shape[0] // 2
+    head_width = query_ref.shape[0]
+    factor = head_width ** (-0.5) * math.log2(math.e)
     query_rows = query_ref.shape[1]
     group = query_rows // (pieces * part)
     here = lax.axis_index("head")
@@ -76,7 +73,6 @@
         )
 
     keys = side(0)
-    keys = jnp.concatenate([keys, keys], axis=1)
     values = side(1).T
     scores = jnp.dot(keys, query_ref[...], preferred_element_type=jnp.float32)
     cuts, tops, at = [], [], 0
@@ -101,13 +97,13 @@
     weights, sums = [], []
     for score, (_, _, _, seen) in zip(cuts, blocks):
         base = high if seen is None else jnp.where(seen[:1], high, HIGH)
-        expo = jnp.exp2(score - base)
+        expo = jnp.exp2((score - base) * factor)
         sums.append(jnp.sum(expo.reshape(-1, SUBLANES, query_rows), axis=0))
         weights.append(expo.astype(jnp.bfloat16))
     total = jnp.sum(functools.reduce(jnp.add, sums), axis=0, keepdims=True)
     accum = jnp.dot(values, jnp.concatenate(weights), preferred_element_type=jnp.float32)
     if not first:
-        keep = jnp.exp2(old_high - high)
+        keep = jnp.exp2((old_high - high) * factor)
         total = total + state[1][...] * keep
         accum = accum + state[2][...] * keep
     if last:
@@ -128,7 +124,7 @@
 
 
 def attend_call(pieces, part, own, query, state, datas, items, last, cost=0):
-    head_width, query_rows = query.shape[0] // 2, query.shape[1]
+    head_width, query_rows = query.shape
     whole = pl.BlockSpec(memory_space=pltpu.VMEM)
     first = state is None
     operands = ([] if first else list(state)) + list(datas)
@@ -168,9 +164,9 @@
     own_queries = lax.dynamic_slice_in_dim(queries, head_index * heads_out, heads_out, 1)
     own_queries = own_queries.reshape(rows_dev * heads_out, head_width)
     whole = pl.BlockSpec(memory_space=pltpu.VMEM)
-    scaled = pl.pallas_call(
-        functools.partial(scale_queries, head_width ** (-0.5)),
-        out_shape=jax.ShapeDtypeStruct((2 * head_width, rows_dev * heads_out), jnp.bfloat16),
+    turned = pl.pallas_call(
+        turn_queries,
+        out_shape=jax.ShapeDtypeStruct((head_width, rows_dev * heads_out), jnp.bfloat16),
         in_specs=[whole],
         out_specs=whole,
         compiler_params=pltpu.CompilerParams(vmem_limit_bytes=8 * MIB),
@@ -189,7 +185,7 @@
         for shift, rows in enumerate(payloads)
     ]
     rest = jnp.concatenate(near)
-    fold = functools.partial(attend_call, pieces, part, own, scaled)
+    fold = functools.partial(attend_call, pieces, part, own, turned)
     shifts = tuple(range(pieces))
     offsets = tuple(2 * part * i for i in range(pieces))
 

time: 24.2 us -> 24.2 us (level)
  transfers between devices with their start and end apart: 12 -> 12, of which waited for: 5 -> 6; matrix products, arithmetic and copies ran while one was open for 1% -> 1% of each run, Pallas kernels for 16% -> 16%
where the time goes in v19:
time: 24.2 us; the launch traced here: 24 us
  starting transfers between devices  15.5 us (64%)
  Pallas kernels  5.41 us (22%)
  waiting for transfers between devices  1.16 us (5%)
  other arithmetic  1.02 us (4%)
  between operations  0.79 us (3%)
    ppermute x6, starting transfers between devices, hop(): lax.ppermute(rows, 'seq', [(i, i ^ way[i & 1]) for i in range(blocks)])  8.19 us
    ppermute x3, starting transfers between devices, shards(): lax.ppermute(rows, 'head', [(i, (i + shift + 1) % pieces) for i in range(...  7.01 us
    pallas_call x5, Pallas kernels, attend_call(): pl.pallas_call(functools.partial(attend, pieces, part, first, last, items...  5.12 us
    concatenate x1, other arithmetic, shards(): jnp.concatenate([keys, values]).reshape(2 * part * kv_heads, head_width)  0.95 us
    ppermute x6, waiting for transfers between devices, hop(): lax.ppermute(rows, 'seq', [(i, i ^ way[i & 1]) for i in range(blocks)])  0.7 us
  transfers between devices with their start and end apart: 12, of which 6 were waited for; matrix products, arithmetic and copies ran while one was open for 1% of the time, Pallas kernels for 16%

profile of v19, /device:TPU:0, one launch (start us, length us, event | category | flops | bytes accessed | tf_op | source)
XLA Modules:
  0.0 24.0 jit_solution(4680008236744799168)
XLA Ops:
  0.0 0.0 copy-start
  0.0 1.0 %pad_maximum_fusion.4 = bf16[128,2,128]{2,1,0:T(2,128)(2,1)S(1)} fusion(bf16[64,2,128]{2,1,0:T(2,128)(2,1)} %param.6, bf16[64,2,128]{2,1,0:T(2,128)(2,1)} %param.5), kind=kLoop, calls=%fused_computation.5 | loop fusion | flops 32768 | bytes 131072 | tf_op jit(solution)/shard_map/concatenate | solution.py:180
  1.0 0.2 shard_map.46
  1.1 3.1 %collective-permute-start = (bf16[128,128]{1,0:T(8,128)(2,1)S(1)}, bf16[128,128]{1,0:T(8,128)(2,1)S(1)}, u32[]{:S(2)}, u32[]{:S(2)}) collective-permute-start(bf16[128,128]{1,0:T(8,128)(2,1)S(1)} %get-tuple-element.33), channel_id=1, source_target_pairs={{0,1},{1,2},{2,3},{3,0},{4,5},{5,6},{6,7},{7,4},{8,9},{9,10},{10,1... | collective-permute-start | bytes 98312 | tf_op jit(solution)/shard_map/ppermute | solution.py:184
  4.2 2.6 %collective-permute-start.1 = (bf16[128,128]{1,0:T(8,128)(2,1)S(1)}, bf16[128,128]{1,0:T(8,128)(2,1)S(1)}, u32[]{:S(2)}, u32[]{:S(2)}) collective-permute-start(bf16[128,128]{1,0:T(8,128)(2,1)S(1)} %get-tuple-element.34), channel_id=1, source_target_pairs={{0,2},{1,3},{2,0},{3,1},{4,6},{5,7},{6,4},{7,5},{8,10},{9,11},{10,... | collective-permute-start | bytes 98312 | tf_op jit(solution)/shard_map/ppermute | solution.py:184
  6.8 1.3 %collective-permute-start.2 = (bf16[128,128]{1,0:T(8,128)(2,1)S(1)}, bf16[128,128]{1,0:T(8,128)(2,1)S(1)}, u32[]{:S(2)}, u32[]{:S(2)}) collective-permute-start(bf16[128,128]{1,0:T(8,128)(2,1)S(1)} %get-tuple-element.35), channel_id=1, source_target_pairs={{0,3},{1,0},{2,1},{3,2},{4,7},{5,4},{6,5},{7,6},{8,11},{9,8},{10,9... | collective-permute-start | bytes 98312 | tf_op jit(solution)/shard_map/ppermute | solution.py:184
  8.8 1.6 %collective-permute-start.9 = (bf16[144,128]{1,0:T(8,128)(2,1)S(1)}, bf16[144,128]{1,0:T(8,128)(2,1)S(1)}, u32[]{:S(2)}, u32[]{:S(2)}) collective-permute-start(bf16[144,128]{1,0:T(8,128)(2,1)S(1)} %get-tuple-element.60.own_ref), channel_id=1, source_target_pairs={{0,16},{4,12},{8,24},{12,4},{16,0},{20,28},{24,8},{28,20},{1,17},{... | collective-permute-start | bytes 110600 | tf_op jit(solution)/shard_map/ppermute | solution.py:200
  10.4 1.4 %collective-permute-start.7 = (bf16[144,128]{1,0:T(8,128)(2,1)S(1)}, bf16[144,128]{1,0:T(8,128)(2,1)S(1)}, u32[]{:S(2)}, u32[]{:S(2)}) collective-permute-start(bf16[144,128]{1,0:T(8,128)(2,1)S(1)} %get-tuple-element.60.own_ref), channel_id=1, source_target_pairs={{0,24},{4,28},{8,16},{12,20},{16,8},{20,12},{24,0},{28,4},{1,25},{... | collective-permute-start | bytes 110600 | tf_op jit(solution)/shard_map/ppermute | solution.py:200
  11.8 0.0 collective-permute-done
  11.8 0.5 %collective-permute-start.6 = (bf16[144,128]{1,0:T(8,128)(2,1)S(1)}, bf16[144,128]{1,0:T(8,128)(2,1)S(1)}, u32[]{:S(2)}, u32[]{:S(2)}) collective-permute-start(bf16[144,128]{1,0:T(8,128)(2,1)S(1)} %get-tuple-element.60.own_ref), channel_id=1, source_target_pairs={{0,8},{4,20},{8,0},{12,28},{16,24},{20,4},{24,16},{28,12},{1,9},{5... | collective-permute-start | bytes 110600 | tf_op jit(solution)/shard_map/ppermute | solution.py:200
  12.4 0.0 collective-permute-done.1
  12.4 0.0 collective-permute-done.2
  12.4 2.5 %collective-permute-start.5 = (bf16[1,384,128]{2,1,0:T(8,128)(2,1)S(1)}, bf16[1,384,128]{2,1,0:T(8,128)(2,1)S(1)}, u32[]{:S(2)}, u32[]{:S(2)}) collective-permute-start(bf16[1,384,128]{2,1,0:T(8,128)(2,1)S(1)} %maximum_bitcast_fusion.refs_1_), channel_id=1, source_target_pairs={{0,24},{4,28},{8,16},{12,20},{16,8},{20,12},{24,0},{28,4},{1,25},{... | collective-permute-start | bytes 294920 | tf_op jit(solution)/shard_map/ppermute | solution.py:200
  14.9 0.5 %collective-permute-start.4 = (bf16[1,384,128]{2,1,0:T(8,128)(2,1)S(1)}, bf16[1,384,128]{2,1,0:T(8,128)(2,1)S(1)}, u32[]{:S(2)}, u32[]{:S(2)}) collective-permute-start(bf16[1,384,128]{2,1,0:T(8,128)(2,1)S(1)} %maximum_bitcast_fusion.refs_1_), channel_id=1, source_target_pairs={{0,8},{4,20},{8,0},{12,28},{16,24},{20,4},{24,16},{28,12},{1,9},{5... | collective-permute-start | bytes 294920 | tf_op jit(solution)/shard_map/ppermute | solution.py:200
  15.4 0.1 collective-permute-done.7
  15.6 0.2 collective-permute-done.6
  15.8 0.1 collective-permute-start.8
  15.9 0.0 copy-done
  15.9 0.1 constant_dynamic-slice_fusion
  16.1 0.1 shard_map.47.query_ref
  16.2 1.6 %collective-permute-start.3 = (bf16[1,384,128]{2,1,0:T(8,128)(2,1)S(1)}, bf16[1,384,128]{2,1,0:T(8,128)(2,1)S(1)}, u32[]{:S(2)}, u32[]{:S(2)}) collective-permute-start(bf16[1,384,128]{2,1,0:T(8,128)(2,1)S(1)} %maximum_bitcast_fusion.refs_1_), channel_id=1, source_target_pairs={{0,16},{4,12},{8,24},{12,4},{16,0},{20,28},{24,8},{28,20},{1,17},{... | collective-permute-start | bytes 294920 | tf_op jit(solution)/shard_map/ppermute | solution.py:200
  17.8 0.8 %shard_map.48 = (f32[1,1024]{1,0:T(1,128)S(1)}, f32[1,1024]{1,0:T(1,128)S(1)}, f32[128,1024]{1,0:T(8,128)S(1)}) custom-call(bf16[144,128]{1,0:T(8,128)(2,1)S(1)} %get-tuple-element.60.own_ref, bf16[128,1024]{1,0:T(8,128)(2,1)S(1)} %shard_map.47.query_ref, bf16[3,144,128]{2,1,0:T(8,128)(2,1)S(1)} %pad_maximum_fusion.3.refs_0_.refs_3_, ...), custom_call_target="tpu_custom_call" | custom-call | flops 1000000000 | tf_op jit(solution)/shard_map/pallas_call | solution.py:146
  18.6 0.0 collective-permute-done.9
  18.7 0.0 collective-permute-done.8.refs_3_.refs_4_
  18.7 0.9 %shard_map.49 = (f32[1,1024]{1,0:T(1,128)S(1)}, f32[1,1024]{1,0:T(1,128)S(1)}, f32[128,1024]{1,0:T(8,128)S(1)}) custom-call(bf16[144,128]{1,0:T(8,128)(2,1)S(1)} %get-tuple-element.60.own_ref, bf16[128,1024]{1,0:T(8,128)(2,1)S(1)} %shard_map.47.query_ref, f32[1,1024]{1,0:T(1,128)S(1)} %get-tuple-element.36.refs_0_, f32[1,1024]{1,0:T(1,128)S(1)} %get-tuple-element.37.refs_1_, ...), custom_call_target="tpu_custom_call" | custom-call | tf_op jit(solution)/shard_map/pallas_call | solution.py:146
  19.6 0.0 collective-permute-done.5.refs_5_
  19.6 0.1 collective-permute-done.4.refs_4_
  19.8 0.1 collective-permute-start.10
  19.8 0.8 %shard_map.50 = (f32[1,1024]{1,0:T(1,128)S(1)}, f32[1,1024]{1,0:T(1,128)S(1)}, f32[128,1024]{1,0:T(8,128)S(1)}) custom-call(bf16[144,128]{1,0:T(8,128)(2,1)S(1)} %get-tuple-element.60.own_ref, bf16[128,1024]{1,0:T(8,128)(2,1)S(1)} %shard_map.47.query_ref, f32[1,1024]{1,0:T(1,128)S(1)} %get-tuple-element.42.refs_0_, f32[1,1024]{1,0:T(1,128)S(1)} %get-tuple-element.43.refs_1_, ...), custom_call_target="tpu_custom_call" | custom-call | tf_op jit(solution)/shard_map/pallas_call | solution.py:146
  20.7 0.2 %collective-permute-done.3 = bf16[1,384,128]{2,1,0:T(8,128)(2,1)S(1)} collective-permute-done((bf16[1,384,128]{2,1,0:T(8,128)(2,1)S(1)}, bf16[1,384,128]{2,1,0:T(8,128)(2,1)S(1)}, u32[]{:S(2)}, u32[]{:S(2)}) %collective-permute-start.3) | collective-permute-done | bytes 98336 | tf_op jit(solution)/shard_map/ppermute | solution.py:200
  20.9 0.3 %collective-permute-done.10.refs_5_ = bf16[2,384,128]{2,1,0:T(8,128)(2,1)S(1)} collective-permute-done((bf16[2,384,128]{2,1,0:T(8,128)(2,1)S(1)}, bf16[2,384,128]{2,1,0:T(8,128)(2,1)S(1)}, u32[]{:S(2)}, u32[]{:S(2)}) %collective-permute-start.10) | collective-permute-done | bytes 196640 | tf_op jit(solution)/shard_map/ppermute | solution.py:193
  21.3 0.1 collective-permute-start.11
  21.4 1.1 %shard_map.51 = (f32[1,1024]{1,0:T(1,128)S(1)}, f32[1,1024]{1,0:T(1,128)S(1)}, f32[128,1024]{1,0:T(8,128)S(1)}) custom-call(bf16[144,128]{1,0:T(8,128)(2,1)S(1)} %get-tuple-element.60.own_ref, bf16[128,1024]{1,0:T(8,128)(2,1)S(1)} %shard_map.47.query_ref, f32[1,1024]{1,0:T(1,128)S(1)} %get-tuple-element.50.refs_0_, f32[1,1024]{1,0:T(1,128)S(1)} %get-tuple-element.51.refs_1_, ...), custom_call_target="tpu_custom_call" | custom-call | tf_op jit(solution)/shard_map/pallas_call | solution.py:146
  22.5 0.1 collective-permute-done.11.refs_3_
  22.6 1.4 %shard_map.52 = bf16[1024,128]{1,0:T(8,128)(2,1)} custom-call(bf16[144,128]{1,0:T(8,128)(2,1)S(1)} %get-tuple-element.60.own_ref, bf16[128,1024]{1,0:T(8,128)(2,1)S(1)} %shard_map.47.query_ref, f32[1,1024]{1,0:T(1,128)S(1)} %get-tuple-element.56.refs_0_, f32[1,1024]{1,0:T(1,128)S(1)} %get-tuple-element.57.refs_1_, ...), custom_call_target="tpu_custom_call" | custom-call | tf_op jit(solution)/shard_map/pallas_call | solution.py:146
  (6 shorter events, 0.1 us)
Async XLA Ops:
  0.0 15.9 %copy-start = (bf16[256,16,128]{2,1,0:T(8,128)(2,1)S(1)}, bf16[256,16,128]{2,1,0:T(8,128)(2,1)}, u32[]{:S(2)}) copy-start(bf16[256,16,128]{2,1,0:T(8,128)(2,1)} %param.4) | copy-start | bytes 3145732
  1.1 10.7 %collective-permute-start = (bf16[128,128]{1,0:T(8,128)(2,1)S(1)}, bf16[128,128]{1,0:T(8,128)(2,1)S(1)}, u32[]{:S(2)}, u32[]{:S(2)}) collective-permute-start(bf16[128,128]{1,0:T(8,128)(2,1)S(1)} %get-tuple-element.33), channel_id=1, source_target_pairs={{0,1},{1,2},{2,3},{3,0},{4,5},{5,6},{6,7},{7,4},{8,9},{9,10},{10,1... | collective-permute-start | bytes 98312 | tf_op jit(solution)/shard_map/ppermute | solution.py:184
  4.2 8.2 %collective-permute-start.1 = (bf16[128,128]{1,0:T(8,128)(2,1)S(1)}, bf16[128,128]{1,0:T(8,128)(2,1)S(1)}, u32[]{:S(2)}, u32[]{:S(2)}) collective-permute-start(bf16[128,128]{1,0:T(8,128)(2,1)S(1)} %get-tuple-element.34), channel_id=1, source_target_pairs={{0,2},{1,3},{2,0},{3,1},{4,6},{5,7},{6,4},{7,5},{8,10},{9,11},{10,... | collective-permute-start | bytes 98312 | tf_op jit(solution)/shard_map/ppermute | solution.py:184
  6.8 5.6 %collective-permute-start.2 = (bf16[128,128]{1,0:T(8,128)(2,1)S(1)}, bf16[128,128]{1,0:T(8,128)(2,1)S(1)}, u32[]{:S(2)}, u32[]{:S(2)}) collective-permute-start(bf16[128,128]{1,0:T(8,128)(2,1)S(1)} %get-tuple-element.35), channel_id=1, source_target_pairs={{0,3},{1,0},{2,1},{3,2},{4,7},{5,4},{6,5},{7,6},{8,11},{9,8},{10,9... | collective-permute-start | bytes 98312 | tf_op jit(solution)/shard_map/ppermute | solution.py:184
  8.8 9.8 %collective-permute-start.9 = (bf16[144,128]{1,0:T(8,128)(2,1)S(1)}, bf16[144,128]{1,0:T(8,128)(2,1)S(1)}, u32[]{:S(2)}, u32[]{:S(2)}) collective-permute-start(bf16[144,128]{1,0:T(8,128)(2,1)S(1)} %get-tuple-element.60.own_ref), channel_id=1, source_target_pairs={{0,16},{4,12},{8,24},{12,4},{16,0},{20,28},{24,8},{28,20},{1,17},{... | collective-permute-start | bytes 110600 | tf_op jit(solution)/shard_map/ppermute | solution.py:200
  10.4 5.2 %collective-permute-start.7 = (bf16[144,128]{1,0:T(8,128)(2,1)S(1)}, bf16[144,128]{1,0:T(8,128)(2,1)S(1)}, u32[]{:S(2)}, u32[]{:S(2)}) collective-permute-start(bf16[144,128]{1,0:T(8,128)(2,1)S(1)} %get-tuple-element.60.own_ref), channel_id=1, source_target_pairs={{0,24},{4,28},{8,16},{12,20},{16,8},{20,12},{24,0},{28,4},{1,25},{... | collective-permute-start | bytes 110600 | tf_op jit(solution)/shard_map/ppermute | solution.py:200
  11.8 4.0 %collective-permute-start.6 = (bf16[144,128]{1,0:T(8,128)(2,1)S(1)}, bf16[144,128]{1,0:T(8,128)(2,1)S(1)}, u32[]{:S(2)}, u32[]{:S(2)}) collective-permute-start(bf16[144,128]{1,0:T(8,128)(2,1)S(1)} %get-tuple-element.60.own_ref), channel_id=1, source_target_pairs={{0,8},{4,20},{8,0},{12,28},{16,24},{20,4},{24,16},{28,12},{1,9},{5... | collective-permute-start | bytes 110600 | tf_op jit(solution)/shard_map/ppermute | solution.py:200
  12.4 7.2 %collective-permute-start.5 = (bf16[1,384,128]{2,1,0:T(8,128)(2,1)S(1)}, bf16[1,384,128]{2,1,0:T(8,128)(2,1)S(1)}, u32[]{:S(2)}, u32[]{:S(2)}) collective-permute-start(bf16[1,384,128]{2,1,0:T(8,128)(2,1)S(1)} %maximum_bitcast_fusion.refs_1_), channel_id=1, source_target_pairs={{0,24},{4,28},{8,16},{12,20},{16,8},{20,12},{24,0},{28,4},{1,25},{... | collective-permute-start | bytes 294920 | tf_op jit(solution)/shard_map/ppermute | solution.py:200
  14.9 4.8 %collective-permute-start.4 = (bf16[1,384,128]{2,1,0:T(8,128)(2,1)S(1)}, bf16[1,384,128]{2,1,0:T(8,128)(2,1)S(1)}, u32[]{:S(2)}, u32[]{:S(2)}) collective-permute-start(bf16[1,384,128]{2,1,0:T(8,128)(2,1)S(1)} %maximum_bitcast_fusion.refs_1_), channel_id=1, source_target_pairs={{0,8},{4,20},{8,0},{12,28},{16,24},{20,4},{24,16},{28,12},{1,9},{5... | collective-permute-start | bytes 294920 | tf_op jit(solution)/shard_map/ppermute | solution.py:200
  15.8 2.8 %collective-permute-start.8 = (bf16[1,816,128]{2,1,0:T(8,128)(2,1)S(1)}, bf16[1,816,128]{2,1,0:T(8,128)(2,1)S(1)}, u32[]{:S(2)}, u32[]{:S(2)}) collective-permute-start(bf16[1,816,128]{2,1,0:T(8,128)(2,1)S(1)} %pad_maximum_fusion), channel_id=1, source_target_pairs={{0,4},{4,0},{8,12},{12,8},{16,20},{20,16},{24,28},{28,24},{1,5},{5... | collective-permute-start | bytes 626696 | tf_op jit(solution)/shard_map/ppermute | solution.py:193
  16.2 4.7 %collective-permute-start.3 = (bf16[1,384,128]{2,1,0:T(8,128)(2,1)S(1)}, bf16[1,384,128]{2,1,0:T(8,128)(2,1)S(1)}, u32[]{:S(2)}, u32[]{:S(2)}) collective-permute-start(bf16[1,384,128]{2,1,0:T(8,128)(2,1)S(1)} %maximum_bitcast_fusion.refs_1_), channel_id=1, source_target_pairs={{0,16},{4,12},{8,24},{12,4},{16,0},{20,28},{24,8},{28,20},{1,17},{... | collective-permute-start | bytes 294920 | tf_op jit(solution)/shard_map/ppermute | solution.py:200
  19.8 1.5 %collective-permute-start.10 = (bf16[2,384,128]{2,1,0:T(8,128)(2,1)S(1)}, bf16[2,384,128]{2,1,0:T(8,128)(2,1)S(1)}, u32[]{:S(2)}, u32[]{:S(2)}) collective-permute-start(bf16[2,384,128]{2,1,0:T(8,128)(2,1)S(1)} %pad_maximum_fusion.1), channel_id=1, source_target_pairs={{0,4},{4,0},{8,12},{12,8},{16,20},{20,16},{24,28},{28,24},{1,5},{5... | collective-permute-start | bytes 589832 | tf_op jit(solution)/shard_map/ppermute | solution.py:193
  21.3 1.4 %collective-permute-start.11 = (bf16[1,528,128]{2,1,0:T(8,128)(2,1)S(1)}, bf16[1,528,128]{2,1,0:T(8,128)(2,1)S(1)}, u32[]{:S(2)}, u32[]{:S(2)}) collective-permute-start(bf16[1,528,128]{2,1,0:T(8,128)(2,1)S(1)} %pad_maximum_fusion.2.refs_3_), channel_id=1, source_target_pairs={{0,4},{4,0},{8,12},{12,8},{16,20},{20,16},{24,28},{28,24},{1,5},{5... | collective-permute-start | bytes 405512 | tf_op jit(solution)/shard_map/ppermute | solution.py:193

commit v20 on v17

--- a/solution.py
+++ b/solution.py
@@ -11,7 +11,7 @@
 MARK = 16
 SUBLANES = 8
 FINAL = 256
-OVERLAP = 1000000000
+OVERLAP = 0
 LOW = -1e30
 HIGH = 1e30
 MIB = 1024 * 1024
@@ -198,14 +198,15 @@
 
     if blocks == 8:
         rest = rest[None]
-        ways = ((2, 4), (6, 2), (4, 6))
+        ways = ((2, 4), (6, 6), (4, 2))
 
         def hop(rows, way):
             return lax.ppermute(rows, "seq", [(i, i ^ way[i & 1]) for i in range(blocks)])
 
-        near_one, near_two, near_last = [hop(own, way) for way in ways]
+        near_one, near_two = [hop(own, way) for way in ways[:2]]
         mine = jnp.stack([own, near_one, near_two])
-        along_one, along_two, along_last = [hop(rest, way) for way in ways]
+        along_one, along_two = [hop(rest, way) for way in ways[:2]]
+        along_last = hop(jnp.concatenate([own[None], rest], axis=1), ways[2])
 
         def small(data, slots):
             return [(data, slot, (0,), None, (data, slot, 2 * part)) for slot in slots]
@@ -225,23 +226,21 @@
         size = own.shape[0]
         state = fold(
             state,
-            [both_other, near_last[None]],
+            [both_other],
             [(0, 0, (size * i,), None, (0, 0, size * i + 2 * part)) for i in range(3)]
-            + [(0, 0, tuple(early_rows + offset for offset in offsets[:-1]), None, (0, 0, 2 * part))]
-            + small(1, (0,)),
+            + [(0, 0, tuple(early_rows + offset for offset in offsets[:-1]), None, (0, 0, 2 * part))],
             False,
         )
         along_one, along_two, state = lax.optimization_barrier((along_one, along_two, state))
         others = [swap(rows, 1) for rows in (along_one, along_two)]
         state = fold(state, [mine, along_one, along_two], [large(i, 0, i) for i in (1, 2)], False)
         along_last, state = lax.optimization_barrier((along_last, state))
-        along_last = jnp.concatenate([near_last[None], along_last], axis=1)
         along_last, *others = lax.optimization_barrier((along_last, *others))
         other_last = swap(along_last, 1)
         state = fold(
             state,
             [along_last, both_other] + others,
-            [large(0, 0, 0, size)] + [(1 + i, 0, offsets[:-1], None, (1, 0, size * i + 2 * part)) for i in (1, 2)],
+            [(0, 0, (0,) + tuple(size + offset for offset in offsets[:-1]), None, (0, 0, 2 * part))] + [(1 + i, 0, offsets[:-1], None, (1, 0, size * i + 2 * part)) for i in (1, 2)],
             False,
         )
         result = fold(

time: 24 us -> 23.5 us (0.979)
  starting transfers between devices: 15 us -> 13.6 us
  waiting for transfers between devices: 1.41 us -> 2.36 us
    ppermute x6 -> x5, starting transfers between devices: 7.1 us -> 5.65 us  [hop(): lax.ppermute(rows, 'seq', [(i, i ^ way[i & 1]) for i in range(blocks)])]
    ppermute x6 -> x5, waiting for transfers between devices: 1.06 us -> 2.15 us  [hop(): lax.ppermute(rows, 'seq', [(i, i ^ way[i & 1]) for i in range(blocks)])]
  transfers between devices with their start and end apart: 13 -> 12, of which waited for: 5 -> 3; matrix products, arithmetic and copies ran while one was open for 1% -> 1% of each run, Pallas kernels for 16% -> 17%
where the time goes in v20:
time: 23.5 us; the launch traced here: 23.4 us
  starting transfers between devices  13.6 us (58%)
  Pallas kernels  5.47 us (23%)
  waiting for transfers between devices  2.36 us (10%)
  other arithmetic  1.01 us (4%)
  between operations  0.78 us (3%)
    ppermute x3, starting transfers between devices, shards(): lax.ppermute(rows, 'head', [(i, (i + shift + 1) % pieces) for i in range(...  7.01 us
    ppermute x5, starting transfers between devices, hop(): lax.ppermute(rows, 'seq', [(i, i ^ way[i & 1]) for i in range(blocks)])  5.65 us
    pallas_call x5, Pallas kernels, attend_call(): pl.pallas_call(functools.partial(attend, pieces, part, first, last, items...  5.11 us
    ppermute x5, waiting for transfers between devices, hop(): lax.ppermute(rows, 'seq', [(i, i ^ way[i & 1]) for i in range(blocks)])  2.15 us
    concatenate x1, other arithmetic, shards(): jnp.concatenate([keys, values]).reshape(2 * part * kv_heads, head_width)  0.95 us
    ppermute x4, starting transfers between devices, swap(): return lax.ppermute(rows, 'seq', [(i, i ^ flip) for i in range(blocks)])  0.94 us
  transfers between devices with their start and end apart: 12, of which 3 were waited for; matrix products, arithmetic and copies ran while one was open for 1% of the time, Pallas kernels for 17%

profile of v20, /device:TPU:0, one launch (start us, length us, event | category | flops | bytes accessed | tf_op | source)
XLA Modules:
  0.0 23.4 jit_solution(14480831042024935694)
XLA Ops:
  0.0 0.0 copy-start
  0.0 1.0 %pad_maximum_fusion.3 = bf16[128,2,128]{2,1,0:T(2,128)(2,1)S(1)} fusion(bf16[64,2,128]{2,1,0:T(2,128)(2,1)} %param.6, bf16[64,2,128]{2,1,0:T(2,128)(2,1)} %param.5), kind=kLoop, calls=%fused_computation.4 | loop fusion | flops 32768 | bytes 131072 | tf_op jit(solution)/shard_map/concatenate | solution.py:184
  1.0 0.2 shard_map.46
  1.1 3.1 %collective-permute-start = (bf16[128,128]{1,0:T(8,128)(2,1)S(1)}, bf16[128,128]{1,0:T(8,128)(2,1)S(1)}, u32[]{:S(2)}, u32[]{:S(2)}) collective-permute-start(bf16[128,128]{1,0:T(8,128)(2,1)S(1)} %get-tuple-element.34), channel_id=1, source_target_pairs={{0,1},{1,2},{2,3},{3,0},{4,5},{5,6},{6,7},{7,4},{8,9},{9,10},{10,1... | collective-permute-start | bytes 98312 | tf_op jit(solution)/shard_map/ppermute | solution.py:188
  4.2 2.6 %collective-permute-start.1 = (bf16[128,128]{1,0:T(8,128)(2,1)S(1)}, bf16[128,128]{1,0:T(8,128)(2,1)S(1)}, u32[]{:S(2)}, u32[]{:S(2)}) collective-permute-start(bf16[128,128]{1,0:T(8,128)(2,1)S(1)} %get-tuple-element.35), channel_id=1, source_target_pairs={{0,2},{1,3},{2,0},{3,1},{4,6},{5,7},{6,4},{7,5},{8,10},{9,11},{10,... | collective-permute-start | bytes 98312 | tf_op jit(solution)/shard_map/ppermute | solution.py:188
  6.8 1.3 %collective-permute-start.2 = (bf16[128,128]{1,0:T(8,128)(2,1)S(1)}, bf16[128,128]{1,0:T(8,128)(2,1)S(1)}, u32[]{:S(2)}, u32[]{:S(2)}) collective-permute-start(bf16[128,128]{1,0:T(8,128)(2,1)S(1)} %get-tuple-element.36), channel_id=1, source_target_pairs={{0,3},{1,0},{2,1},{3,2},{4,7},{5,4},{6,5},{7,6},{8,11},{9,8},{10,9... | collective-permute-start | bytes 98312 | tf_op jit(solution)/shard_map/ppermute | solution.py:188
  8.8 2.5 %collective-permute-start.7 = (bf16[144,128]{1,0:T(8,128)(2,1)S(1)}, bf16[144,128]{1,0:T(8,128)(2,1)S(1)}, u32[]{:S(2)}, u32[]{:S(2)}) collective-permute-start(bf16[144,128]{1,0:T(8,128)(2,1)S(1)} %get-tuple-element.62.own_ref), channel_id=1, source_target_pairs={{0,24},{4,28},{8,16},{12,20},{16,8},{20,12},{24,0},{28,4},{1,25},{... | collective-permute-start | bytes 110600 | tf_op jit(solution)/shard_map/ppermute | solution.py:204
  11.3 0.5 %collective-permute-start.6 = (bf16[144,128]{1,0:T(8,128)(2,1)S(1)}, bf16[144,128]{1,0:T(8,128)(2,1)S(1)}, u32[]{:S(2)}, u32[]{:S(2)}) collective-permute-start(bf16[144,128]{1,0:T(8,128)(2,1)S(1)} %get-tuple-element.62.own_ref), channel_id=1, source_target_pairs={{0,8},{4,20},{8,0},{12,28},{16,24},{20,4},{24,16},{28,12},{1,9},{5... | collective-permute-start | bytes 110600 | tf_op jit(solution)/shard_map/ppermute | solution.py:204
  11.9 0.0 collective-permute-done
  11.9 0.0 collective-permute-done.1
  11.9 0.0 collective-permute-done.2
  11.9 1.5 %collective-permute-start.5 = (bf16[1,384,128]{2,1,0:T(8,128)(2,1)S(1)}, bf16[1,384,128]{2,1,0:T(8,128)(2,1)S(1)}, u32[]{:S(2)}, u32[]{:S(2)}) collective-permute-start(bf16[1,384,128]{2,1,0:T(8,128)(2,1)S(1)} %maximum_bitcast_fusion.refs_1_), channel_id=1, source_target_pairs={{0,24},{4,28},{8,16},{12,20},{16,8},{20,12},{24,0},{28,4},{1,25},{... | collective-permute-start | bytes 294920 | tf_op jit(solution)/shard_map/ppermute | solution.py:204
  13.4 0.5 %collective-permute-start.4 = (bf16[1,384,128]{2,1,0:T(8,128)(2,1)S(1)}, bf16[1,384,128]{2,1,0:T(8,128)(2,1)S(1)}, u32[]{:S(2)}, u32[]{:S(2)}) collective-permute-start(bf16[1,384,128]{2,1,0:T(8,128)(2,1)S(1)} %maximum_bitcast_fusion.refs_1_), channel_id=1, source_target_pairs={{0,8},{4,20},{8,0},{12,28},{16,24},{20,4},{24,16},{28,12},{1,9},{5... | collective-permute-start | bytes 294920 | tf_op jit(solution)/shard_map/ppermute | solution.py:204
  13.9 0.0 collective-permute-done.7
  13.9 1.4 %collective-permute-done.6 = bf16[144,128]{1,0:T(8,128)(2,1)S(1)} collective-permute-done((bf16[144,128]{1,0:T(8,128)(2,1)S(1)}, bf16[144,128]{1,0:T(8,128)(2,1)S(1)}, u32[]{:S(2)}, u32[]{:S(2)}) %collective-permute-start.6) | collective-permute-done | bytes 36896 | tf_op jit(solution)/shard_map/ppermute | solution.py:204
  15.4 0.1 collective-permute-start.8
  15.5 0.6 %collective-permute-start.3 = (bf16[1,528,128]{2,1,0:T(8,128)(2,1)S(1)}, bf16[1,528,128]{2,1,0:T(8,128)(2,1)S(1)}, u32[]{:S(2)}, u32[]{:S(2)}) collective-permute-start(bf16[1,528,128]{2,1,0:T(8,128)(2,1)S(1)} %pad_maximum_fusion.1), channel_id=1, source_target_pairs={{0,16},{4,12},{8,24},{12,4},{16,0},{20,28},{24,8},{28,20},{1,17},{... | collective-permute-start | bytes 405512 | tf_op jit(solution)/shard_map/ppermute | solution.py:204
  16.1 0.0 copy-done
  16.1 0.1 constant_dynamic-slice_fusion
  16.2 0.2 shard_map.47.query_ref
  16.4 0.8 %shard_map.48 = (f32[1,1024]{1,0:T(1,128)S(1)}, f32[1,1024]{1,0:T(1,128)S(1)}, f32[128,1024]{1,0:T(8,128)S(1)}) custom-call(bf16[144,128]{1,0:T(8,128)(2,1)S(1)} %get-tuple-element.62.own_ref, bf16[256,1024]{1,0:T(8,128)(2,1)S(1)} %shard_map.47.query_ref, bf16[3,144,128]{2,1,0:T(8,128)(2,1)S(1)} %pad_maximum_fusion.2.refs_0_.refs_3_, ...), custom_call_target="tpu_custom_call" | custom-call | tf_op jit(solution)/shard_map/pallas_call | solution.py:150
  17.3 0.0 collective-permute-done.8.refs_3_.refs_4_
  17.3 0.9 %shard_map.49 = (f32[1,1024]{1,0:T(1,128)S(1)}, f32[1,1024]{1,0:T(1,128)S(1)}, f32[128,1024]{1,0:T(8,128)S(1)}) custom-call(bf16[144,128]{1,0:T(8,128)(2,1)S(1)} %get-tuple-element.62.own_ref, bf16[256,1024]{1,0:T(8,128)(2,1)S(1)} %shard_map.47.query_ref, f32[1,1024]{1,0:T(1,128)S(1)} %get-tuple-element.37.refs_0_, f32[1,1024]{1,0:T(1,128)S(1)} %get-tuple-element.38.refs_1_, ...), custom_call_target="tpu_custom_call" | custom-call | tf_op jit(solution)/shard_map/pallas_call | solution.py:150
  18.2 0.0 collective-permute-done.5.refs_5_
  18.2 0.0 collective-permute-done.4.refs_4_
  18.2 0.8 %collective-permute-start.9 = (bf16[1,384,128]{2,1,0:T(8,128)(2,1)S(1)}, bf16[1,384,128]{2,1,0:T(8,128)(2,1)S(1)}, u32[]{:S(2)}, u32[]{:S(2)}) collective-permute-start(bf16[1,384,128]{2,1,0:T(8,128)(2,1)S(1)} %collective-permute-done.4.refs_4_), channel_id=1, source_target_pairs={{0,4},{4,0},{8,12},{12,8},{16,20},{20,16},{24,28},{28,24},{1,5},{5... | collective-permute-start | bytes 294920 | tf_op jit(solution)/shard_map/ppermute | solution.py:197
  19.0 0.1 collective-permute-start.10
  19.1 0.8 %shard_map.50 = (f32[1,1024]{1,0:T(1,128)S(1)}, f32[1,1024]{1,0:T(1,128)S(1)}, f32[128,1024]{1,0:T(8,128)S(1)}) custom-call(bf16[144,128]{1,0:T(8,128)(2,1)S(1)} %get-tuple-element.62.own_ref, bf16[256,1024]{1,0:T(8,128)(2,1)S(1)} %shard_map.47.query_ref, f32[1,1024]{1,0:T(1,128)S(1)} %get-tuple-element.43.refs_0_, f32[1,1024]{1,0:T(1,128)S(1)} %get-tuple-element.44.refs_1_, ...), custom_call_target="tpu_custom_call" | custom-call | tf_op jit(solution)/shard_map/pallas_call | solution.py:150
  19.9 0.7 %collective-permute-done.3.refs_3_ = bf16[1,528,128]{2,1,0:T(8,128)(2,1)S(1)} collective-permute-done((bf16[1,528,128]{2,1,0:T(8,128)(2,1)S(1)}, bf16[1,528,128]{2,1,0:T(8,128)(2,1)S(1)}, u32[]{:S(2)}, u32[]{:S(2)}) %collective-permute-start.3) | collective-permute-done | bytes 135200 | tf_op jit(solution)/shard_map/ppermute | solution.py:204
  20.6 0.0 collective-permute-done.9.refs_5_
  20.6 0.0 collective-permute-done.10.refs_6_
  20.6 0.0 collective-permute-start.11
  20.6 1.1 %shard_map.51 = (f32[1,1024]{1,0:T(1,128)S(1)}, f32[1,1024]{1,0:T(1,128)S(1)}, f32[128,1024]{1,0:T(8,128)S(1)}) custom-call(bf16[144,128]{1,0:T(8,128)(2,1)S(1)} %get-tuple-element.62.own_ref, bf16[256,1024]{1,0:T(8,128)(2,1)S(1)} %shard_map.47.query_ref, f32[1,1024]{1,0:T(1,128)S(1)} %get-tuple-element.51.refs_0_, f32[1,1024]{1,0:T(1,128)S(1)} %get-tuple-element.52.refs_1_, ...), custom_call_target="tpu_custom_call" | custom-call | tf_op jit(solution)/shard_map/pallas_call | solution.py:150
  21.8 0.2 collective-permute-done.11.refs_3_
  22.0 1.4 %shard_map.52 = bf16[1024,128]{1,0:T(8,128)(2,1)} custom-call(bf16[144,128]{1,0:T(8,128)(2,1)S(1)} %get-tuple-element.62.own_ref, bf16[256,1024]{1,0:T(8,128)(2,1)S(1)} %shard_map.47.query_ref, f32[1,1024]{1,0:T(1,128)S(1)} %get-tuple-element.58.refs_0_, f32[1,1024]{1,0:T(1,128)S(1)} %get-tuple-element.59.refs_1_, ...), custom_call_target="tpu_custom_call" | custom-call | tf_op jit(solution)/shard_map/pallas_call | solution.py:150
  (5 shorter events, 0.1 us)
Async XLA Ops:
  0.0 16.1 %copy-start = (bf16[256,16,128]{2,1,0:T(8,128)(2,1)S(1)}, bf16[256,16,128]{2,1,0:T(8,128)(2,1)}, u32[]{:S(2)}) copy-start(bf16[256,16,128]{2,1,0:T(8,128)(2,1)} %param.4) | copy-start | bytes 3145732
  1.1 10.7 %collective-permute-start = (bf16[128,128]{1,0:T(8,128)(2,1)S(1)}, bf16[128,128]{1,0:T(8,128)(2,1)S(1)}, u32[]{:S(2)}, u32[]{:S(2)}) collective-permute-start(bf16[128,128]{1,0:T(8,128)(2,1)S(1)} %get-tuple-element.34), channel_id=1, source_target_pairs={{0,1},{1,2},{2,3},{3,0},{4,5},{5,6},{6,7},{7,4},{8,9},{9,10},{10,1... | collective-permute-start | bytes 98312 | tf_op jit(solution)/shard_map/ppermute | solution.py:188
  4.2 7.7 %collective-permute-start.1 = (bf16[128,128]{1,0:T(8,128)(2,1)S(1)}, bf16[128,128]{1,0:T(8,128)(2,1)S(1)}, u32[]{:S(2)}, u32[]{:S(2)}) collective-permute-start(bf16[128,128]{1,0:T(8,128)(2,1)S(1)} %get-tuple-element.35), channel_id=1, source_target_pairs={{0,2},{1,3},{2,0},{3,1},{4,6},{5,7},{6,4},{7,5},{8,10},{9,11},{10,... | collective-permute-start | bytes 98312 | tf_op jit(solution)/shard_map/ppermute | solution.py:188
  6.8 5.1 %collective-permute-start.2 = (bf16[128,128]{1,0:T(8,128)(2,1)S(1)}, bf16[128,128]{1,0:T(8,128)(2,1)S(1)}, u32[]{:S(2)}, u32[]{:S(2)}) collective-permute-start(bf16[128,128]{1,0:T(8,128)(2,1)S(1)} %get-tuple-element.36), channel_id=1, source_target_pairs={{0,3},{1,0},{2,1},{3,2},{4,7},{5,4},{6,5},{7,6},{8,11},{9,8},{10,9... | collective-permute-start | bytes 98312 | tf_op jit(solution)/shard_map/ppermute | solution.py:188
  8.8 5.1 %collective-permute-start.7 = (bf16[144,128]{1,0:T(8,128)(2,1)S(1)}, bf16[144,128]{1,0:T(8,128)(2,1)S(1)}, u32[]{:S(2)}, u32[]{:S(2)}) collective-permute-start(bf16[144,128]{1,0:T(8,128)(2,1)S(1)} %get-tuple-element.62.own_ref), channel_id=1, source_target_pairs={{0,24},{4,28},{8,16},{12,20},{16,8},{20,12},{24,0},{28,4},{1,25},{... | collective-permute-start | bytes 110600 | tf_op jit(solution)/shard_map/ppermute | solution.py:204
  11.3 4.0 %collective-permute-start.6 = (bf16[144,128]{1,0:T(8,128)(2,1)S(1)}, bf16[144,128]{1,0:T(8,128)(2,1)S(1)}, u32[]{:S(2)}, u32[]{:S(2)}) collective-permute-start(bf16[144,128]{1,0:T(8,128)(2,1)S(1)} %get-tuple-element.62.own_ref), channel_id=1, source_target_pairs={{0,8},{4,20},{8,0},{12,28},{16,24},{20,4},{24,16},{28,12},{1,9},{5... | collective-permute-start | bytes 110600 | tf_op jit(solution)/shard_map/ppermute | solution.py:204
  11.9 6.3 %collective-permute-start.5 = (bf16[1,384,128]{2,1,0:T(8,128)(2,1)S(1)}, bf16[1,384,128]{2,1,0:T(8,128)(2,1)S(1)}, u32[]{:S(2)}, u32[]{:S(2)}) collective-permute-start(bf16[1,384,128]{2,1,0:T(8,128)(2,1)S(1)} %maximum_bitcast_fusion.refs_1_), channel_id=1, source_target_pairs={{0,24},{4,28},{8,16},{12,20},{16,8},{20,12},{24,0},{28,4},{1,25},{... | collective-permute-start | bytes 294920 | tf_op jit(solution)/shard_map/ppermute | solution.py:204
  13.4 4.8 %collective-permute-start.4 = (bf16[1,384,128]{2,1,0:T(8,128)(2,1)S(1)}, bf16[1,384,128]{2,1,0:T(8,128)(2,1)S(1)}, u32[]{:S(2)}, u32[]{:S(2)}) collective-permute-start(bf16[1,384,128]{2,1,0:T(8,128)(2,1)S(1)} %maximum_bitcast_fusion.refs_1_), channel_id=1, source_target_pairs={{0,8},{4,20},{8,0},{12,28},{16,24},{20,4},{24,16},{28,12},{1,9},{5... | collective-permute-start | bytes 294920 | tf_op jit(solution)/shard_map/ppermute | solution.py:204
  15.4 1.8 %collective-permute-start.8 = (bf16[1,816,128]{2,1,0:T(8,128)(2,1)S(1)}, bf16[1,816,128]{2,1,0:T(8,128)(2,1)S(1)}, u32[]{:S(2)}, u32[]{:S(2)}) collective-permute-start(bf16[1,816,128]{2,1,0:T(8,128)(2,1)S(1)} %pad_maximum_fusion), channel_id=1, source_target_pairs={{0,4},{4,0},{8,12},{12,8},{16,20},{20,16},{24,28},{28,24},{1,5},{5... | collective-permute-start | bytes 626696 | tf_op jit(solution)/shard_map/ppermute | solution.py:197
  15.5 5.1 %collective-permute-start.3 = (bf16[1,528,128]{2,1,0:T(8,128)(2,1)S(1)}, bf16[1,528,128]{2,1,0:T(8,128)(2,1)S(1)}, u32[]{:S(2)}, u32[]{:S(2)}) collective-permute-start(bf16[1,528,128]{2,1,0:T(8,128)(2,1)S(1)} %pad_maximum_fusion.1), channel_id=1, source_target_pairs={{0,16},{4,12},{8,24},{12,4},{16,0},{20,28},{24,8},{28,20},{1,17},{... | collective-permute-start | bytes 405512 | tf_op jit(solution)/shard_map/ppermute | solution.py:204
  18.2 2.4 %collective-permute-start.9 = (bf16[1,384,128]{2,1,0:T(8,128)(2,1)S(1)}, bf16[1,384,128]{2,1,0:T(8,128)(2,1)S(1)}, u32[]{:S(2)}, u32[]{:S(2)}) collective-permute-start(bf16[1,384,128]{2,1,0:T(8,128)(2,1)S(1)} %collective-permute-done.4.refs_4_), channel_id=1, source_target_pairs={{0,4},{4,0},{8,12},{12,8},{16,20},{20,16},{24,28},{28,24},{1,5},{5... | collective-permute-start | bytes 294920 | tf_op jit(solution)/shard_map/ppermute | solution.py:197
  19.0 1.6 %collective-permute-start.10 = (bf16[1,384,128]{2,1,0:T(8,128)(2,1)S(1)}, bf16[1,384,128]{2,1,0:T(8,128)(2,1)S(1)}, u32[]{:S(2)}, u32[]{:S(2)}) collective-permute-start(bf16[1,384,128]{2,1,0:T(8,128)(2,1)S(1)} %collective-permute-done.5.refs_5_), channel_id=1, source_target_pairs={{0,4},{4,0},{8,12},{12,8},{16,20},{20,16},{24,28},{28,24},{1,5},{5... | collective-permute-start | bytes 294920 | tf_op jit(solution)/shard_map/ppermute | solution.py:197
  20.6 1.4 %collective-permute-start.11 = (bf16[1,528,128]{2,1,0:T(8,128)(2,1)S(1)}, bf16[1,528,128]{2,1,0:T(8,128)(2,1)S(1)}, u32[]{:S(2)}, u32[]{:S(2)}) collective-permute-start(bf16[1,528,128]{2,1,0:T(8,128)(2,1)S(1)} %collective-permute-done.3.refs_3_), channel_id=1, source_target_pairs={{0,4},{4,0},{8,12},{12,8},{16,20},{20,16},{24,28},{28,24},{1,5},{5... | collective-permute-start | bytes 405512 | tf_op jit(solution)/shard_map/ppermute | solution.py:197

commit v21 on v20

--- a/solution.py
+++ b/solution.py
@@ -198,7 +198,7 @@
 
     if blocks == 8:
         rest = rest[None]
-        ways = ((2, 4), (6, 6), (4, 2))
+        ways = ((4, 2), (2, 4), (6, 6))
 
         def hop(rows, way):
             return lax.ppermute(rows, "seq", [(i, i ^ way[i & 1]) for i in range(blocks)])

time: 23.5 us -> 24.5 us (1.043)
  starting transfers between devices: 13.6 us -> 14.2 us
  waiting for transfers between devices: 2.36 us -> 2.73 us
    ppermute x5, starting transfers between devices: 5.65 us -> 6.55 us  [hop(): lax.ppermute(rows, 'seq', [(i, i ^ way[i & 1]) for i in range(blocks)])]
    ppermute x5, waiting for transfers between devices: 2.15 us -> 2.52 us  [hop(): lax.ppermute(rows, 'seq', [(i, i ^ way[i & 1]) for i in range(blocks)])]
    ppermute x4, starting transfers between devices: 0.94 us -> 0.65 us  [swap(): return lax.ppermute(rows, 'seq', [(i, i ^ flip) for i in range(blocks)])]
  transfers between devices with their start and end apart: 12 -> 12, of which waited for: 3 -> 3; matrix products, arithmetic and copies ran while one was open for 1% -> 1% of each run, Pallas kernels for 17% -> 16%
where the time goes in v21:
time: 24.5 us; the launch traced here: 24.3 us
  starting transfers between devices  14.2 us (58%)
  Pallas kernels  5.47 us (22%)
  waiting for transfers between devices  2.73 us (11%)
  other arithmetic  1.01 us (4%)
  between operations  0.78 us (3%)
    ppermute x3, starting transfers between devices, shards(): lax.ppermute(rows, 'head', [(i, (i + shift + 1) % pieces) for i in range(...  7.01 us
    ppermute x5, starting transfers between devices, hop(): lax.ppermute(rows, 'seq', [(i, i ^ way[i & 1]) for i in range(blocks)])  6.55 us
    pallas_call x5, Pallas kernels, attend_call(): pl.pallas_call(functools.partial(attend, pieces, part, first, last, items...  5.11 us
    ppermute x5, waiting for transfers between devices, hop(): lax.ppermute(rows, 'seq', [(i, i ^ way[i & 1]) for i in range(blocks)])  2.52 us
    concatenate x1, other arithmetic, shards(): jnp.concatenate([keys, values]).reshape(2 * part * kv_heads, head_width)  0.95 us
    ppermute x4, starting transfers between devices, swap(): return lax.ppermute(rows, 'seq', [(i, i ^ flip) for i in range(blocks)])  0.65 us
  transfers between devices with their start and end apart: 12, of which 3 were waited for; matrix products, arithmetic and copies ran while one was open for 1% of the time, Pallas kernels for 16%

profile of v21, /device:TPU:0, one launch (start us, length us, event | category | flops | bytes accessed | tf_op | source)
XLA Modules:
  0.0 24.3 jit_solution(15942200751730215436)
XLA Ops:
  0.0 0.0 copy-start
  0.0 1.0 %pad_maximum_fusion.3 = bf16[128,2,128]{2,1,0:T(2,128)(2,1)S(1)} fusion(bf16[64,2,128]{2,1,0:T(2,128)(2,1)} %param.6, bf16[64,2,128]{2,1,0:T(2,128)(2,1)} %param.5), kind=kLoop, calls=%fused_computation.4 | loop fusion | flops 32768 | bytes 131072 | tf_op jit(solution)/shard_map/concatenate | solution.py:184
  1.0 0.2 shard_map.46
  1.1 3.1 %collective-permute-start = (bf16[128,128]{1,0:T(8,128)(2,1)S(1)}, bf16[128,128]{1,0:T(8,128)(2,1)S(1)}, u32[]{:S(2)}, u32[]{:S(2)}) collective-permute-start(bf16[128,128]{1,0:T(8,128)(2,1)S(1)} %get-tuple-element.34), channel_id=1, source_target_pairs={{0,1},{1,2},{2,3},{3,0},{4,5},{5,6},{6,7},{7,4},{8,9},{9,10},{10,1... | collective-permute-start | bytes 98312 | tf_op jit(solution)/shard_map/ppermute | solution.py:188
  4.2 2.6 %collective-permute-start.1 = (bf16[128,128]{1,0:T(8,128)(2,1)S(1)}, bf16[128,128]{1,0:T(8,128)(2,1)S(1)}, u32[]{:S(2)}, u32[]{:S(2)}) collective-permute-start(bf16[128,128]{1,0:T(8,128)(2,1)S(1)} %get-tuple-element.35), channel_id=1, source_target_pairs={{0,2},{1,3},{2,0},{3,1},{4,6},{5,7},{6,4},{7,5},{8,10},{9,11},{10,... | collective-permute-start | bytes 98312 | tf_op jit(solution)/shard_map/ppermute | solution.py:188
  6.8 1.3 %collective-permute-start.2 = (bf16[128,128]{1,0:T(8,128)(2,1)S(1)}, bf16[128,128]{1,0:T(8,128)(2,1)S(1)}, u32[]{:S(2)}, u32[]{:S(2)}) collective-permute-start(bf16[128,128]{1,0:T(8,128)(2,1)S(1)} %get-tuple-element.36), channel_id=1, source_target_pairs={{0,3},{1,0},{2,1},{3,2},{4,7},{5,4},{6,5},{7,6},{8,11},{9,8},{10,9... | collective-permute-start | bytes 98312 | tf_op jit(solution)/shard_map/ppermute | solution.py:188
  8.8 1.6 %collective-permute-start.7 = (bf16[144,128]{1,0:T(8,128)(2,1)S(1)}, bf16[144,128]{1,0:T(8,128)(2,1)S(1)}, u32[]{:S(2)}, u32[]{:S(2)}) collective-permute-start(bf16[144,128]{1,0:T(8,128)(2,1)S(1)} %get-tuple-element.62.own_ref), channel_id=1, source_target_pairs={{0,8},{4,20},{8,0},{12,28},{16,24},{20,4},{24,16},{28,12},{1,9},{5... | collective-permute-start | bytes 110600 | tf_op jit(solution)/shard_map/ppermute | solution.py:204
  10.4 1.5 %collective-permute-start.6 = (bf16[144,128]{1,0:T(8,128)(2,1)S(1)}, bf16[144,128]{1,0:T(8,128)(2,1)S(1)}, u32[]{:S(2)}, u32[]{:S(2)}) collective-permute-start(bf16[144,128]{1,0:T(8,128)(2,1)S(1)} %get-tuple-element.62.own_ref), channel_id=1, source_target_pairs={{0,16},{4,12},{8,24},{12,4},{16,0},{20,28},{24,8},{28,20},{1,17},{... | collective-permute-start | bytes 110600 | tf_op jit(solution)/shard_map/ppermute | solution.py:204
  11.9 0.0 collective-permute-done
  11.9 0.0 collective-permute-done.1
  11.9 0.0 collective-permute-done.2
  11.9 0.6 %collective-permute-start.5 = (bf16[1,384,128]{2,1,0:T(8,128)(2,1)S(1)}, bf16[1,384,128]{2,1,0:T(8,128)(2,1)S(1)}, u32[]{:S(2)}, u32[]{:S(2)}) collective-permute-start(bf16[1,384,128]{2,1,0:T(8,128)(2,1)S(1)} %maximum_bitcast_fusion.refs_1_), channel_id=1, source_target_pairs={{0,8},{4,20},{8,0},{12,28},{16,24},{20,4},{24,16},{28,12},{1,9},{5... | collective-permute-start | bytes 294920 | tf_op jit(solution)/shard_map/ppermute | solution.py:204
  12.5 1.3 %collective-permute-start.4 = (bf16[1,384,128]{2,1,0:T(8,128)(2,1)S(1)}, bf16[1,384,128]{2,1,0:T(8,128)(2,1)S(1)}, u32[]{:S(2)}, u32[]{:S(2)}) collective-permute-start(bf16[1,384,128]{2,1,0:T(8,128)(2,1)S(1)} %maximum_bitcast_fusion.refs_1_), channel_id=1, source_target_pairs={{0,16},{4,12},{8,24},{12,4},{16,0},{20,28},{24,8},{28,20},{1,17},{... | collective-permute-start | bytes 294920 | tf_op jit(solution)/shard_map/ppermute | solution.py:204
  13.8 0.0 collective-permute-done.7
  13.8 0.7 %collective-permute-done.6 = bf16[144,128]{1,0:T(8,128)(2,1)S(1)} collective-permute-done((bf16[144,128]{1,0:T(8,128)(2,1)S(1)}, bf16[144,128]{1,0:T(8,128)(2,1)S(1)}, u32[]{:S(2)}, u32[]{:S(2)}) %collective-permute-start.6) | collective-permute-done | bytes 36896 | tf_op jit(solution)/shard_map/ppermute | solution.py:204
  14.5 0.1 collective-permute-start.8
  14.6 1.6 %collective-permute-start.3 = (bf16[1,528,128]{2,1,0:T(8,128)(2,1)S(1)}, bf16[1,528,128]{2,1,0:T(8,128)(2,1)S(1)}, u32[]{:S(2)}, u32[]{:S(2)}) collective-permute-start(bf16[1,528,128]{2,1,0:T(8,128)(2,1)S(1)} %pad_maximum_fusion.1), channel_id=1, source_target_pairs={{0,24},{4,28},{8,16},{12,20},{16,8},{20,12},{24,0},{28,4},{1,25},{... | collective-permute-start | bytes 405512 | tf_op jit(solution)/shard_map/ppermute | solution.py:204
  16.2 0.0 copy-done
  16.2 0.1 constant_dynamic-slice_fusion
  16.4 0.2 shard_map.47.query_ref
  16.6 0.8 %shard_map.48 = (f32[1,1024]{1,0:T(1,128)S(1)}, f32[1,1024]{1,0:T(1,128)S(1)}, f32[128,1024]{1,0:T(8,128)S(1)}) custom-call(bf16[144,128]{1,0:T(8,128)(2,1)S(1)} %get-tuple-element.62.own_ref, bf16[256,1024]{1,0:T(8,128)(2,1)S(1)} %shard_map.47.query_ref, bf16[3,144,128]{2,1,0:T(8,128)(2,1)S(1)} %pad_maximum_fusion.2.refs_0_.refs_3_, ...), custom_call_target="tpu_custom_call" | custom-call | tf_op jit(solution)/shard_map/pallas_call | solution.py:150
  17.4 0.0 collective-permute-done.8.refs_3_.refs_4_
  17.4 0.9 %shard_map.49 = (f32[1,1024]{1,0:T(1,128)S(1)}, f32[1,1024]{1,0:T(1,128)S(1)}, f32[128,1024]{1,0:T(8,128)S(1)}) custom-call(bf16[144,128]{1,0:T(8,128)(2,1)S(1)} %get-tuple-element.62.own_ref, bf16[256,1024]{1,0:T(8,128)(2,1)S(1)} %shard_map.47.query_ref, f32[1,1024]{1,0:T(1,128)S(1)} %get-tuple-element.37.refs_0_, f32[1,1024]{1,0:T(1,128)S(1)} %get-tuple-element.38.refs_1_, ...), custom_call_target="tpu_custom_call" | custom-call | tf_op jit(solution)/shard_map/pallas_call | solution.py:150
  18.3 0.0 collective-permute-done.5.refs_5_
  18.3 0.0 collective-permute-done.4.refs_4_
  18.3 0.3 %collective-permute-start.9 = (bf16[1,384,128]{2,1,0:T(8,128)(2,1)S(1)}, bf16[1,384,128]{2,1,0:T(8,128)(2,1)S(1)}, u32[]{:S(2)}, u32[]{:S(2)}) collective-permute-start(bf16[1,384,128]{2,1,0:T(8,128)(2,1)S(1)} %collective-permute-done.4.refs_4_), channel_id=1, source_target_pairs={{0,4},{4,0},{8,12},{12,8},{16,20},{20,16},{24,28},{28,24},{1,5},{5... | collective-permute-start | bytes 294920 | tf_op jit(solution)/shard_map/ppermute | solution.py:197
  18.6 0.3 %collective-permute-start.10 = (bf16[1,384,128]{2,1,0:T(8,128)(2,1)S(1)}, bf16[1,384,128]{2,1,0:T(8,128)(2,1)S(1)}, u32[]{:S(2)}, u32[]{:S(2)}) collective-permute-start(bf16[1,384,128]{2,1,0:T(8,128)(2,1)S(1)} %collective-permute-done.5.refs_5_), channel_id=1, source_target_pairs={{0,4},{4,0},{8,12},{12,8},{16,20},{20,16},{24,28},{28,24},{1,5},{5... | collective-permute-start | bytes 294920 | tf_op jit(solution)/shard_map/ppermute | solution.py:197
  18.9 0.8 %shard_map.50 = (f32[1,1024]{1,0:T(1,128)S(1)}, f32[1,1024]{1,0:T(1,128)S(1)}, f32[128,1024]{1,0:T(8,128)S(1)}) custom-call(bf16[144,128]{1,0:T(8,128)(2,1)S(1)} %get-tuple-element.62.own_ref, bf16[256,1024]{1,0:T(8,128)(2,1)S(1)} %shard_map.47.query_ref, f32[1,1024]{1,0:T(1,128)S(1)} %get-tuple-element.43.refs_0_, f32[1,1024]{1,0:T(1,128)S(1)} %get-tuple-element.44.refs_1_, ...), custom_call_target="tpu_custom_call" | custom-call | tf_op jit(solution)/shard_map/pallas_call | solution.py:150
  19.7 1.8 %collective-permute-done.3.refs_3_ = bf16[1,528,128]{2,1,0:T(8,128)(2,1)S(1)} collective-permute-done((bf16[1,528,128]{2,1,0:T(8,128)(2,1)S(1)}, bf16[1,528,128]{2,1,0:T(8,128)(2,1)S(1)}, u32[]{:S(2)}, u32[]{:S(2)}) %collective-permute-start.3) | collective-permute-done | bytes 135200 | tf_op jit(solution)/shard_map/ppermute | solution.py:204
  21.6 0.0 collective-permute-done.9.refs_5_
  21.6 0.0 collective-permute-done.10.refs_6_
  21.6 0.0 collective-permute-start.11
  21.6 1.1 %shard_map.51 = (f32[1,1024]{1,0:T(1,128)S(1)}, f32[1,1024]{1,0:T(1,128)S(1)}, f32[128,1024]{1,0:T(8,128)S(1)}) custom-call(bf16[144,128]{1,0:T(8,128)(2,1)S(1)} %get-tuple-element.62.own_ref, bf16[256,1024]{1,0:T(8,128)(2,1)S(1)} %shard_map.47.query_ref, f32[1,1024]{1,0:T(1,128)S(1)} %get-tuple-element.51.refs_0_, f32[1,1024]{1,0:T(1,128)S(1)} %get-tuple-element.52.refs_1_, ...), custom_call_target="tpu_custom_call" | custom-call | tf_op jit(solution)/shard_map/pallas_call | solution.py:150
  22.7 0.2 collective-permute-done.11.refs_3_
  22.9 1.4 %shard_map.52 = bf16[1024,128]{1,0:T(8,128)(2,1)} custom-call(bf16[144,128]{1,0:T(8,128)(2,1)S(1)} %get-tuple-element.62.own_ref, bf16[256,1024]{1,0:T(8,128)(2,1)S(1)} %shard_map.47.query_ref, f32[1,1024]{1,0:T(1,128)S(1)} %get-tuple-element.58.refs_0_, f32[1,1024]{1,0:T(1,128)S(1)} %get-tuple-element.59.refs_1_, ...), custom_call_target="tpu_custom_call" | custom-call | tf_op jit(solution)/shard_map/pallas_call | solution.py:150
  (5 shorter events, 0.1 us)
Async XLA Ops:
  0.0 16.2 %copy-start = (bf16[256,16,128]{2,1,0:T(8,128)(2,1)S(1)}, bf16[256,16,128]{2,1,0:T(8,128)(2,1)}, u32[]{:S(2)}) copy-start(bf16[256,16,128]{2,1,0:T(8,128)(2,1)} %param.4) | copy-start | bytes 3145732
  1.1 10.8 %collective-permute-start = (bf16[128,128]{1,0:T(8,128)(2,1)S(1)}, bf16[128,128]{1,0:T(8,128)(2,1)S(1)}, u32[]{:S(2)}, u32[]{:S(2)}) collective-permute-start(bf16[128,128]{1,0:T(8,128)(2,1)S(1)} %get-tuple-element.34), channel_id=1, source_target_pairs={{0,1},{1,2},{2,3},{3,0},{4,5},{5,6},{6,7},{7,4},{8,9},{9,10},{10,1... | collective-permute-start | bytes 98312 | tf_op jit(solution)/shard_map/ppermute | solution.py:188
  4.2 7.7 %collective-permute-start.1 = (bf16[128,128]{1,0:T(8,128)(2,1)S(1)}, bf16[128,128]{1,0:T(8,128)(2,1)S(1)}, u32[]{:S(2)}, u32[]{:S(2)}) collective-permute-start(bf16[128,128]{1,0:T(8,128)(2,1)S(1)} %get-tuple-element.35), channel_id=1, source_target_pairs={{0,2},{1,3},{2,0},{3,1},{4,6},{5,7},{6,4},{7,5},{8,10},{9,11},{10,... | collective-permute-start | bytes 98312 | tf_op jit(solution)/shard_map/ppermute | solution.py:188
  6.8 5.1 %collective-permute-start.2 = (bf16[128,128]{1,0:T(8,128)(2,1)S(1)}, bf16[128,128]{1,0:T(8,128)(2,1)S(1)}, u32[]{:S(2)}, u32[]{:S(2)}) collective-permute-start(bf16[128,128]{1,0:T(8,128)(2,1)S(1)} %get-tuple-element.36), channel_id=1, source_target_pairs={{0,3},{1,0},{2,1},{3,2},{4,7},{5,4},{6,5},{7,6},{8,11},{9,8},{10,9... | collective-permute-start | bytes 98312 | tf_op jit(solution)/shard_map/ppermute | solution.py:188
  8.8 5.0 %collective-permute-start.7 = (bf16[144,128]{1,0:T(8,128)(2,1)S(1)}, bf16[144,128]{1,0:T(8,128)(2,1)S(1)}, u32[]{:S(2)}, u32[]{:S(2)}) collective-permute-start(bf16[144,128]{1,0:T(8,128)(2,1)S(1)} %get-tuple-element.62.own_ref), channel_id=1, source_target_pairs={{0,8},{4,20},{8,0},{12,28},{16,24},{20,4},{24,16},{28,12},{1,9},{5... | collective-permute-start | bytes 110600 | tf_op jit(solution)/shard_map/ppermute | solution.py:204
  10.4 4.1 %collective-permute-start.6 = (bf16[144,128]{1,0:T(8,128)(2,1)S(1)}, bf16[144,128]{1,0:T(8,128)(2,1)S(1)}, u32[]{:S(2)}, u32[]{:S(2)}) collective-permute-start(bf16[144,128]{1,0:T(8,128)(2,1)S(1)} %get-tuple-element.62.own_ref), channel_id=1, source_target_pairs={{0,16},{4,12},{8,24},{12,4},{16,0},{20,28},{24,8},{28,20},{1,17},{... | collective-permute-start | bytes 110600 | tf_op jit(solution)/shard_map/ppermute | solution.py:204
  11.9 6.4 %collective-permute-start.5 = (bf16[1,384,128]{2,1,0:T(8,128)(2,1)S(1)}, bf16[1,384,128]{2,1,0:T(8,128)(2,1)S(1)}, u32[]{:S(2)}, u32[]{:S(2)}) collective-permute-start(bf16[1,384,128]{2,1,0:T(8,128)(2,1)S(1)} %maximum_bitcast_fusion.refs_1_), channel_id=1, source_target_pairs={{0,8},{4,20},{8,0},{12,28},{16,24},{20,4},{24,16},{28,12},{1,9},{5... | collective-permute-start | bytes 294920 | tf_op jit(solution)/shard_map/ppermute | solution.py:204
  12.5 5.8 %collective-permute-start.4 = (bf16[1,384,128]{2,1,0:T(8,128)(2,1)S(1)}, bf16[1,384,128]{2,1,0:T(8,128)(2,1)S(1)}, u32[]{:S(2)}, u32[]{:S(2)}) collective-permute-start(bf16[1,384,128]{2,1,0:T(8,128)(2,1)S(1)} %maximum_bitcast_fusion.refs_1_), channel_id=1, source_target_pairs={{0,16},{4,12},{8,24},{12,4},{16,0},{20,28},{24,8},{28,20},{1,17},{... | collective-permute-start | bytes 294920 | tf_op jit(solution)/shard_map/ppermute | solution.py:204
  14.5 2.9 %collective-permute-start.8 = (bf16[1,816,128]{2,1,0:T(8,128)(2,1)S(1)}, bf16[1,816,128]{2,1,0:T(8,128)(2,1)S(1)}, u32[]{:S(2)}, u32[]{:S(2)}) collective-permute-start(bf16[1,816,128]{2,1,0:T(8,128)(2,1)S(1)} %pad_maximum_fusion), channel_id=1, source_target_pairs={{0,4},{4,0},{8,12},{12,8},{16,20},{20,16},{24,28},{28,24},{1,5},{5... | collective-permute-start | bytes 626696 | tf_op jit(solution)/shard_map/ppermute | solution.py:197
  14.6 6.9 %collective-permute-start.3 = (bf16[1,528,128]{2,1,0:T(8,128)(2,1)S(1)}, bf16[1,528,128]{2,1,0:T(8,128)(2,1)S(1)}, u32[]{:S(2)}, u32[]{:S(2)}) collective-permute-start(bf16[1,528,128]{2,1,0:T(8,128)(2,1)S(1)} %pad_maximum_fusion.1), channel_id=1, source_target_pairs={{0,24},{4,28},{8,16},{12,20},{16,8},{20,12},{24,0},{28,4},{1,25},{... | collective-permute-start | bytes 405512 | tf_op jit(solution)/shard_map/ppermute | solution.py:204
  18.3 3.2 %collective-permute-start.9 = (bf16[1,384,128]{2,1,0:T(8,128)(2,1)S(1)}, bf16[1,384,128]{2,1,0:T(8,128)(2,1)S(1)}, u32[]{:S(2)}, u32[]{:S(2)}) collective-permute-start(bf16[1,384,128]{2,1,0:T(8,128)(2,1)S(1)} %collective-permute-done.4.refs_4_), channel_id=1, source_target_pairs={{0,4},{4,0},{8,12},{12,8},{16,20},{20,16},{24,28},{28,24},{1,5},{5... | collective-permute-start | bytes 294920 | tf_op jit(solution)/shard_map/ppermute | solution.py:197
  18.6 3.0 %collective-permute-start.10 = (bf16[1,384,128]{2,1,0:T(8,128)(2,1)S(1)}, bf16[1,384,128]{2,1,0:T(8,128)(2,1)S(1)}, u32[]{:S(2)}, u32[]{:S(2)}) collective-permute-start(bf16[1,384,128]{2,1,0:T(8,128)(2,1)S(1)} %collective-permute-done.5.refs_5_), channel_id=1, source_target_pairs={{0,4},{4,0},{8,12},{12,8},{16,20},{20,16},{24,28},{28,24},{1,5},{5... | collective-permute-start | bytes 294920 | tf_op jit(solution)/shard_map/ppermute | solution.py:197
  21.6 1.4 %collective-permute-start.11 = (bf16[1,528,128]{2,1,0:T(8,128)(2,1)S(1)}, bf16[1,528,128]{2,1,0:T(8,128)(2,1)S(1)}, u32[]{:S(2)}, u32[]{:S(2)}) collective-permute-start(bf16[1,528,128]{2,1,0:T(8,128)(2,1)S(1)} %collective-permute-done.3.refs_3_), channel_id=1, source_target_pairs={{0,4},{4,0},{8,12},{12,8},{16,20},{20,16},{24,28},{28,24},{1,5},{5... | collective-permute-start | bytes 405512 | tf_op jit(solution)/shard_map/ppermute | solution.py:197

commit v22 on v21

--- a/solution.py
+++ b/solution.py
@@ -198,7 +198,7 @@
 
     if blocks == 8:
         rest = rest[None]
-        ways = ((4, 2), (2, 4), (6, 6))
+        ways = ((2, 6), (6, 2), (4, 4))
 
         def hop(rows, way):
             return lax.ppermute(rows, "seq", [(i, i ^ way[i & 1]) for i in range(blocks)])

time: 24.5 us -> 24.9 us (1.016)
  waiting for transfers between devices: 2.73 us -> 4.33 us
  starting transfers between devices: 14.2 us -> 13 us
    ppermute x5, waiting for transfers between devices: 2.52 us -> 4.11 us  [hop(): lax.ppermute(rows, 'seq', [(i, i ^ way[i & 1]) for i in range(blocks)])]
    ppermute x5, starting transfers between devices: 6.55 us -> 5.33 us  [hop(): lax.ppermute(rows, 'seq', [(i, i ^ way[i & 1]) for i in range(blocks)])]
  transfers between devices with their start and end apart: 12 -> 12, of which waited for: 3 -> 4; matrix products, arithmetic and copies ran while one was open for 1% -> 1% of each run, Pallas kernels for 16% -> 16%
where the time goes in v22:
time: 24.9 us; the launch traced here: 24.7 us
  starting transfers between devices  13 us (52%)
  Pallas kernels  5.47 us (22%)
  waiting for transfers between devices  4.33 us (17%)
  other arithmetic  1.01 us (4%)
  between operations  0.78 us (3%)
    ppermute x3, starting transfers between devices, shards(): lax.ppermute(rows, 'head', [(i, (i + shift + 1) % pieces) for i in range(...  7.01 us
    ppermute x5, starting transfers between devices, hop(): lax.ppermute(rows, 'seq', [(i, i ^ way[i & 1]) for i in range(blocks)])  5.33 us
    pallas_call x5, Pallas kernels, attend_call(): pl.pallas_call(functools.partial(attend, pieces, part, first, last, items...  5.11 us
    ppermute x5, waiting for transfers between devices, hop(): lax.ppermute(rows, 'seq', [(i, i ^ way[i & 1]) for i in range(blocks)])  4.11 us
    concatenate x1, other arithmetic, shards(): jnp.concatenate([keys, values]).reshape(2 * part * kv_heads, head_width)  0.95 us
    ppermute x4, starting transfers between devices, swap(): return lax.ppermute(rows, 'seq', [(i, i ^ flip) for i in range(blocks)])  0.65 us
  transfers between devices with their start and end apart: 12, of which 4 were waited for; matrix products, arithmetic and copies ran while one was open for 1% of the time, Pallas kernels for 16%

profile of v22, /device:TPU:0, one launch (start us, length us, event | category | flops | bytes accessed | tf_op | source)
XLA Modules:
  0.0 24.7 jit_solution(17729524118106743437)
XLA Ops:
  0.0 0.0 copy-start
  0.0 1.0 %pad_maximum_fusion.3 = bf16[128,2,128]{2,1,0:T(2,128)(2,1)S(1)} fusion(bf16[64,2,128]{2,1,0:T(2,128)(2,1)} %param.6, bf16[64,2,128]{2,1,0:T(2,128)(2,1)} %param.5), kind=kLoop, calls=%fused_computation.4 | loop fusion | flops 32768 | bytes 131072 | tf_op jit(solution)/shard_map/concatenate | solution.py:184
  1.0 0.2 shard_map.46
  1.1 3.1 %collective-permute-start = (bf16[128,128]{1,0:T(8,128)(2,1)S(1)}, bf16[128,128]{1,0:T(8,128)(2,1)S(1)}, u32[]{:S(2)}, u32[]{:S(2)}) collective-permute-start(bf16[128,128]{1,0:T(8,128)(2,1)S(1)} %get-tuple-element.34), channel_id=1, source_target_pairs={{0,1},{1,2},{2,3},{3,0},{4,5},{5,6},{6,7},{7,4},{8,9},{9,10},{10,1... | collective-permute-start | bytes 98312 | tf_op jit(solution)/shard_map/ppermute | solution.py:188
  4.2 2.6 %collective-permute-start.1 = (bf16[128,128]{1,0:T(8,128)(2,1)S(1)}, bf16[128,128]{1,0:T(8,128)(2,1)S(1)}, u32[]{:S(2)}, u32[]{:S(2)}) collective-permute-start(bf16[128,128]{1,0:T(8,128)(2,1)S(1)} %get-tuple-element.35), channel_id=1, source_target_pairs={{0,2},{1,3},{2,0},{3,1},{4,6},{5,7},{6,4},{7,5},{8,10},{9,11},{10,... | collective-permute-start | bytes 98312 | tf_op jit(solution)/shard_map/ppermute | solution.py:188
  6.8 1.3 %collective-permute-start.2 = (bf16[128,128]{1,0:T(8,128)(2,1)S(1)}, bf16[128,128]{1,0:T(8,128)(2,1)S(1)}, u32[]{:S(2)}, u32[]{:S(2)}) collective-permute-start(bf16[128,128]{1,0:T(8,128)(2,1)S(1)} %get-tuple-element.36), channel_id=1, source_target_pairs={{0,3},{1,0},{2,1},{3,2},{4,7},{5,4},{6,5},{7,6},{8,11},{9,8},{10,9... | collective-permute-start | bytes 98312 | tf_op jit(solution)/shard_map/ppermute | solution.py:188
  8.8 2.5 %collective-permute-start.7 = (bf16[144,128]{1,0:T(8,128)(2,1)S(1)}, bf16[144,128]{1,0:T(8,128)(2,1)S(1)}, u32[]{:S(2)}, u32[]{:S(2)}) collective-permute-start(bf16[144,128]{1,0:T(8,128)(2,1)S(1)} %get-tuple-element.62.own_ref), channel_id=1, source_target_pairs={{0,24},{4,12},{8,16},{12,4},{16,8},{20,28},{24,0},{28,20},{1,25},{... | collective-permute-start | bytes 110600 | tf_op jit(solution)/shard_map/ppermute | solution.py:204
  11.3 0.5 %collective-permute-start.6 = (bf16[144,128]{1,0:T(8,128)(2,1)S(1)}, bf16[144,128]{1,0:T(8,128)(2,1)S(1)}, u32[]{:S(2)}, u32[]{:S(2)}) collective-permute-start(bf16[144,128]{1,0:T(8,128)(2,1)S(1)} %get-tuple-element.62.own_ref), channel_id=1, source_target_pairs={{0,8},{4,28},{8,0},{12,20},{16,24},{20,12},{24,16},{28,4},{1,9},{5... | collective-permute-start | bytes 110600 | tf_op jit(solution)/shard_map/ppermute | solution.py:204
  11.9 0.0 collective-permute-done
  11.9 0.0 collective-permute-done.1
  11.9 0.0 collective-permute-done.2
  11.9 1.5 %collective-permute-start.5 = (bf16[1,384,128]{2,1,0:T(8,128)(2,1)S(1)}, bf16[1,384,128]{2,1,0:T(8,128)(2,1)S(1)}, u32[]{:S(2)}, u32[]{:S(2)}) collective-permute-start(bf16[1,384,128]{2,1,0:T(8,128)(2,1)S(1)} %maximum_bitcast_fusion.refs_1_), channel_id=1, source_target_pairs={{0,24},{4,12},{8,16},{12,4},{16,8},{20,28},{24,0},{28,20},{1,25},{... | collective-permute-start | bytes 294920 | tf_op jit(solution)/shard_map/ppermute | solution.py:204
  13.4 0.5 %collective-permute-start.4 = (bf16[1,384,128]{2,1,0:T(8,128)(2,1)S(1)}, bf16[1,384,128]{2,1,0:T(8,128)(2,1)S(1)}, u32[]{:S(2)}, u32[]{:S(2)}) collective-permute-start(bf16[1,384,128]{2,1,0:T(8,128)(2,1)S(1)} %maximum_bitcast_fusion.refs_1_), channel_id=1, source_target_pairs={{0,8},{4,28},{8,0},{12,20},{16,24},{20,12},{24,16},{28,4},{1,9},{5... | collective-permute-start | bytes 294920 | tf_op jit(solution)/shard_map/ppermute | solution.py:204
  13.9 0.2 collective-permute-done.7
  14.1 1.6 %collective-permute-done.6 = bf16[144,128]{1,0:T(8,128)(2,1)S(1)} collective-permute-done((bf16[144,128]{1,0:T(8,128)(2,1)S(1)}, bf16[144,128]{1,0:T(8,128)(2,1)S(1)}, u32[]{:S(2)}, u32[]{:S(2)}) %collective-permute-start.6) | collective-permute-done | bytes 36896 | tf_op jit(solution)/shard_map/ppermute | solution.py:204
  15.8 0.1 collective-permute-start.8
  15.9 0.2 %collective-permute-start.3 = (bf16[1,528,128]{2,1,0:T(8,128)(2,1)S(1)}, bf16[1,528,128]{2,1,0:T(8,128)(2,1)S(1)}, u32[]{:S(2)}, u32[]{:S(2)}) collective-permute-start(bf16[1,528,128]{2,1,0:T(8,128)(2,1)S(1)} %pad_maximum_fusion.1), channel_id=1, source_target_pairs={{0,16},{4,20},{8,24},{12,28},{16,0},{20,4},{24,8},{28,12},{1,17},{... | collective-permute-start | bytes 405512 | tf_op jit(solution)/shard_map/ppermute | solution.py:204
  16.1 0.0 copy-done
  16.1 0.1 constant_dynamic-slice_fusion
  16.3 0.2 shard_map.47.query_ref
  16.5 0.8 %shard_map.48 = (f32[1,1024]{1,0:T(1,128)S(1)}, f32[1,1024]{1,0:T(1,128)S(1)}, f32[128,1024]{1,0:T(8,128)S(1)}) custom-call(bf16[144,128]{1,0:T(8,128)(2,1)S(1)} %get-tuple-element.62.own_ref, bf16[256,1024]{1,0:T(8,128)(2,1)S(1)} %shard_map.47.query_ref, bf16[3,144,128]{2,1,0:T(8,128)(2,1)S(1)} %pad_maximum_fusion.2.refs_0_.refs_3_, ...), custom_call_target="tpu_custom_call" | custom-call | tf_op jit(solution)/shard_map/pallas_call | solution.py:150
  17.3 0.0 collective-permute-done.8.refs_3_.refs_4_
  17.3 0.9 %shard_map.49 = (f32[1,1024]{1,0:T(1,128)S(1)}, f32[1,1024]{1,0:T(1,128)S(1)}, f32[128,1024]{1,0:T(8,128)S(1)}) custom-call(bf16[144,128]{1,0:T(8,128)(2,1)S(1)} %get-tuple-element.62.own_ref, bf16[256,1024]{1,0:T(8,128)(2,1)S(1)} %shard_map.47.query_ref, f32[1,1024]{1,0:T(1,128)S(1)} %get-tuple-element.37.refs_0_, f32[1,1024]{1,0:T(1,128)S(1)} %get-tuple-element.38.refs_1_, ...), custom_call_target="tpu_custom_call" | custom-call | tf_op jit(solution)/shard_map/pallas_call | solution.py:150
  18.2 0.0 collective-permute-done.5.refs_5_
  18.2 0.0 collective-permute-done.4.refs_4_
  18.2 0.4 %collective-permute-start.9 = (bf16[1,384,128]{2,1,0:T(8,128)(2,1)S(1)}, bf16[1,384,128]{2,1,0:T(8,128)(2,1)S(1)}, u32[]{:S(2)}, u32[]{:S(2)}) collective-permute-start(bf16[1,384,128]{2,1,0:T(8,128)(2,1)S(1)} %collective-permute-done.4.refs_4_), channel_id=1, source_target_pairs={{0,4},{4,0},{8,12},{12,8},{16,20},{20,16},{24,28},{28,24},{1,5},{5... | collective-permute-start | bytes 294920 | tf_op jit(solution)/shard_map/ppermute | solution.py:197
  18.6 0.2 collective-permute-start.10
  18.8 0.8 %shard_map.50 = (f32[1,1024]{1,0:T(1,128)S(1)}, f32[1,1024]{1,0:T(1,128)S(1)}, f32[128,1024]{1,0:T(8,128)S(1)}) custom-call(bf16[144,128]{1,0:T(8,128)(2,1)S(1)} %get-tuple-element.62.own_ref, bf16[256,1024]{1,0:T(8,128)(2,1)S(1)} %shard_map.47.query_ref, f32[1,1024]{1,0:T(1,128)S(1)} %get-tuple-element.43.refs_0_, f32[1,1024]{1,0:T(1,128)S(1)} %get-tuple-element.44.refs_1_, ...), custom_call_target="tpu_custom_call" | custom-call | tf_op jit(solution)/shard_map/pallas_call | solution.py:150
  19.6 2.3 %collective-permute-done.3.refs_3_ = bf16[1,528,128]{2,1,0:T(8,128)(2,1)S(1)} collective-permute-done((bf16[1,528,128]{2,1,0:T(8,128)(2,1)S(1)}, bf16[1,528,128]{2,1,0:T(8,128)(2,1)S(1)}, u32[]{:S(2)}, u32[]{:S(2)}) %collective-permute-start.3) | collective-permute-done | bytes 135200 | tf_op jit(solution)/shard_map/ppermute | solution.py:204
  21.9 0.0 collective-permute-done.9.refs_5_
  21.9 0.0 collective-permute-done.10.refs_6_
  21.9 0.0 collective-permute-start.11
  22.0 1.1 %shard_map.51 = (f32[1,1024]{1,0:T(1,128)S(1)}, f32[1,1024]{1,0:T(1,128)S(1)}, f32[128,1024]{1,0:T(8,128)S(1)}) custom-call(bf16[144,128]{1,0:T(8,128)(2,1)S(1)} %get-tuple-element.62.own_ref, bf16[256,1024]{1,0:T(8,128)(2,1)S(1)} %shard_map.47.query_ref, f32[1,1024]{1,0:T(1,128)S(1)} %get-tuple-element.51.refs_0_, f32[1,1024]{1,0:T(1,128)S(1)} %get-tuple-element.52.refs_1_, ...), custom_call_target="tpu_custom_call" | custom-call | tf_op jit(solution)/shard_map/pallas_call | solution.py:150
  23.1 0.2 collective-permute-done.11.refs_3_
  23.3 1.4 %shard_map.52 = bf16[1024,128]{1,0:T(8,128)(2,1)} custom-call(bf16[144,128]{1,0:T(8,128)(2,1)S(1)} %get-tuple-element.62.own_ref, bf16[256,1024]{1,0:T(8,128)(2,1)S(1)} %shard_map.47.query_ref, f32[1,1024]{1,0:T(1,128)S(1)} %get-tuple-element.58.refs_0_, f32[1,1024]{1,0:T(1,128)S(1)} %get-tuple-element.59.refs_1_, ...), custom_call_target="tpu_custom_call" | custom-call | tf_op jit(solution)/shard_map/pallas_call | solution.py:150
  (5 shorter events, 0.1 us)
Async XLA Ops:
  0.0 16.1 %copy-start = (bf16[256,16,128]{2,1,0:T(8,128)(2,1)S(1)}, bf16[256,16,128]{2,1,0:T(8,128)(2,1)}, u32[]{:S(2)}) copy-start(bf16[256,16,128]{2,1,0:T(8,128)(2,1)} %param.4) | copy-start | bytes 3145732
  1.1 10.7 %collective-permute-start = (bf16[128,128]{1,0:T(8,128)(2,1)S(1)}, bf16[128,128]{1,0:T(8,128)(2,1)S(1)}, u32[]{:S(2)}, u32[]{:S(2)}) collective-permute-start(bf16[128,128]{1,0:T(8,128)(2,1)S(1)} %get-tuple-element.34), channel_id=1, source_target_pairs={{0,1},{1,2},{2,3},{3,0},{4,5},{5,6},{6,7},{7,4},{8,9},{9,10},{10,1... | collective-permute-start | bytes 98312 | tf_op jit(solution)/shard_map/ppermute | solution.py:188
  4.2 7.7 %collective-permute-start.1 = (bf16[128,128]{1,0:T(8,128)(2,1)S(1)}, bf16[128,128]{1,0:T(8,128)(2,1)S(1)}, u32[]{:S(2)}, u32[]{:S(2)}) collective-permute-start(bf16[128,128]{1,0:T(8,128)(2,1)S(1)} %get-tuple-element.35), channel_id=1, source_target_pairs={{0,2},{1,3},{2,0},{3,1},{4,6},{5,7},{6,4},{7,5},{8,10},{9,11},{10,... | collective-permute-start | bytes 98312 | tf_op jit(solution)/shard_map/ppermute | solution.py:188
  6.8 5.1 %collective-permute-start.2 = (bf16[128,128]{1,0:T(8,128)(2,1)S(1)}, bf16[128,128]{1,0:T(8,128)(2,1)S(1)}, u32[]{:S(2)}, u32[]{:S(2)}) collective-permute-start(bf16[128,128]{1,0:T(8,128)(2,1)S(1)} %get-tuple-element.36), channel_id=1, source_target_pairs={{0,3},{1,0},{2,1},{3,2},{4,7},{5,4},{6,5},{7,6},{8,11},{9,8},{10,9... | collective-permute-start | bytes 98312 | tf_op jit(solution)/shard_map/ppermute | solution.py:188
  8.8 5.3 %collective-permute-start.7 = (bf16[144,128]{1,0:T(8,128)(2,1)S(1)}, bf16[144,128]{1,0:T(8,128)(2,1)S(1)}, u32[]{:S(2)}, u32[]{:S(2)}) collective-permute-start(bf16[144,128]{1,0:T(8,128)(2,1)S(1)} %get-tuple-element.62.own_ref), channel_id=1, source_target_pairs={{0,24},{4,12},{8,16},{12,4},{16,8},{20,28},{24,0},{28,20},{1,25},{... | collective-permute-start | bytes 110600 | tf_op jit(solution)/shard_map/ppermute | solution.py:204
  11.3 4.4 %collective-permute-start.6 = (bf16[144,128]{1,0:T(8,128)(2,1)S(1)}, bf16[144,128]{1,0:T(8,128)(2,1)S(1)}, u32[]{:S(2)}, u32[]{:S(2)}) collective-permute-start(bf16[144,128]{1,0:T(8,128)(2,1)S(1)} %get-tuple-element.62.own_ref), channel_id=1, source_target_pairs={{0,8},{4,28},{8,0},{12,20},{16,24},{20,12},{24,16},{28,4},{1,9},{5... | collective-permute-start | bytes 110600 | tf_op jit(solution)/shard_map/ppermute | solution.py:204
  11.9 6.3 %collective-permute-start.5 = (bf16[1,384,128]{2,1,0:T(8,128)(2,1)S(1)}, bf16[1,384,128]{2,1,0:T(8,128)(2,1)S(1)}, u32[]{:S(2)}, u32[]{:S(2)}) collective-permute-start(bf16[1,384,128]{2,1,0:T(8,128)(2,1)S(1)} %maximum_bitcast_fusion.refs_1_), channel_id=1, source_target_pairs={{0,24},{4,12},{8,16},{12,4},{16,8},{20,28},{24,0},{28,20},{1,25},{... | collective-permute-start | bytes 294920 | tf_op jit(solution)/shard_map/ppermute | solution.py:204
  13.4 4.8 %collective-permute-start.4 = (bf16[1,384,128]{2,1,0:T(8,128)(2,1)S(1)}, bf16[1,384,128]{2,1,0:T(8,128)(2,1)S(1)}, u32[]{:S(2)}, u32[]{:S(2)}) collective-permute-start(bf16[1,384,128]{2,1,0:T(8,128)(2,1)S(1)} %maximum_bitcast_fusion.refs_1_), channel_id=1, source_target_pairs={{0,8},{4,28},{8,0},{12,20},{16,24},{20,12},{24,16},{28,4},{1,9},{5... | collective-permute-start | bytes 294920 | tf_op jit(solution)/shard_map/ppermute | solution.py:204
  15.8 1.5 %collective-permute-start.8 = (bf16[1,816,128]{2,1,0:T(8,128)(2,1)S(1)}, bf16[1,816,128]{2,1,0:T(8,128)(2,1)S(1)}, u32[]{:S(2)}, u32[]{:S(2)}) collective-permute-start(bf16[1,816,128]{2,1,0:T(8,128)(2,1)S(1)} %pad_maximum_fusion), channel_id=1, source_target_pairs={{0,4},{4,0},{8,12},{12,8},{16,20},{20,16},{24,28},{28,24},{1,5},{5... | collective-permute-start | bytes 626696 | tf_op jit(solution)/shard_map/ppermute | solution.py:197
  15.9 6.0 %collective-permute-start.3 = (bf16[1,528,128]{2,1,0:T(8,128)(2,1)S(1)}, bf16[1,528,128]{2,1,0:T(8,128)(2,1)S(1)}, u32[]{:S(2)}, u32[]{:S(2)}) collective-permute-start(bf16[1,528,128]{2,1,0:T(8,128)(2,1)S(1)} %pad_maximum_fusion.1), channel_id=1, source_target_pairs={{0,16},{4,20},{8,24},{12,28},{16,0},{20,4},{24,8},{28,12},{1,17},{... | collective-permute-start | bytes 405512 | tf_op jit(solution)/shard_map/ppermute | solution.py:204
  18.2 3.7 %collective-permute-start.9 = (bf16[1,384,128]{2,1,0:T(8,128)(2,1)S(1)}, bf16[1,384,128]{2,1,0:T(8,128)(2,1)S(1)}, u32[]{:S(2)}, u32[]{:S(2)}) collective-permute-start(bf16[1,384,128]{2,1,0:T(8,128)(2,1)S(1)} %collective-permute-done.4.refs_4_), channel_id=1, source_target_pairs={{0,4},{4,0},{8,12},{12,8},{16,20},{20,16},{24,28},{28,24},{1,5},{5... | collective-permute-start | bytes 294920 | tf_op jit(solution)/shard_map/ppermute | solution.py:197
  18.6 3.3 %collective-permute-start.10 = (bf16[1,384,128]{2,1,0:T(8,128)(2,1)S(1)}, bf16[1,384,128]{2,1,0:T(8,128)(2,1)S(1)}, u32[]{:S(2)}, u32[]{:S(2)}) collective-permute-start(bf16[1,384,128]{2,1,0:T(8,128)(2,1)S(1)} %collective-permute-done.5.refs_5_), channel_id=1, source_target_pairs={{0,4},{4,0},{8,12},{12,8},{16,20},{20,16},{24,28},{28,24},{1,5},{5... | collective-permute-start | bytes 294920 | tf_op jit(solution)/shard_map/ppermute | solution.py:197
  21.9 1.4 %collective-permute-start.11 = (bf16[1,528,128]{2,1,0:T(8,128)(2,1)S(1)}, bf16[1,528,128]{2,1,0:T(8,128)(2,1)S(1)}, u32[]{:S(2)}, u32[]{:S(2)}) collective-permute-start(bf16[1,528,128]{2,1,0:T(8,128)(2,1)S(1)} %collective-permute-done.3.refs_3_), channel_id=1, source_target_pairs={{0,4},{4,0},{8,12},{12,8},{16,20},{20,16},{24,28},{28,24},{1,5},{5... | collective-permute-start | bytes 405512 | tf_op jit(solution)/shard_map/ppermute | solution.py:197

commit v23 on v22

--- a/solution.py
+++ b/solution.py
@@ -198,7 +198,7 @@
 
     if blocks == 8:
         rest = rest[None]
-        ways = ((2, 6), (6, 2), (4, 4))
+        ways = ((4, 2), (6, 6), (2, 4))
 
         def hop(rows, way):
             return lax.ppermute(rows, "seq", [(i, i ^ way[i & 1]) for i in range(blocks)])

time: 24.9 us -> 23.8 us (0.956)
  waiting for transfers between devices: 4.33 us -> 1.55 us
  starting transfers between devices: 13 us -> 14.6 us
    ppermute x5, waiting for transfers between devices: 4.11 us -> 1.44 us  [hop(): lax.ppermute(rows, 'seq', [(i, i ^ way[i & 1]) for i in range(blocks)])]
    ppermute x5, starting transfers between devices: 5.33 us -> 6.64 us  [hop(): lax.ppermute(rows, 'seq', [(i, i ^ way[i & 1]) for i in range(blocks)])]
    ppermute x4, starting transfers between devices: 0.65 us -> 1 us  [swap(): return lax.ppermute(rows, 'seq', [(i, i ^ flip) for i in range(blocks)])]
  transfers between devices with their start and end apart: 12 -> 12, of which waited for: 4 -> 2; matrix products, arithmetic and copies ran while one was open for 1% -> 1% of each run, Pallas kernels for 16% -> 16%
where the time goes in v23:
time: 23.8 us; the launch traced here: 23.6 us
  starting transfers between devices  14.6 us (61%)
  Pallas kernels  5.46 us (23%)
  waiting for transfers between devices  1.55 us (7%)
  other arithmetic  1.01 us (4%)
  between operations  0.79 us (3%)
    ppermute x3, starting transfers between devices, shards(): lax.ppermute(rows, 'head', [(i, (i + shift + 1) % pieces) for i in range(...  7.01 us
    ppermute x5, starting transfers between devices, hop(): lax.ppermute(rows, 'seq', [(i, i ^ way[i & 1]) for i in range(blocks)])  6.64 us
    pallas_call x5, Pallas kernels, attend_call(): pl.pallas_call(functools.partial(attend, pieces, part, first, last, items...  5.1 us
    ppermute x5, waiting for transfers between devices, hop(): lax.ppermute(rows, 'seq', [(i, i ^ way[i & 1]) for i in range(blocks)])  1.44 us
    ppermute x4, starting transfers between devices, swap(): return lax.ppermute(rows, 'seq', [(i, i ^ flip) for i in range(blocks)])  1 us
    concatenate x1, other arithmetic, shards(): jnp.concatenate([keys, values]).reshape(2 * part * kv_heads, head_width)  0.95 us
  transfers between devices with their start and end apart: 12, of which 2 were waited for; matrix products, arithmetic and copies ran while one was open for 1% of the time, Pallas kernels for 16%

profile of v23, /device:TPU:0, one launch (start us, length us, event | category | flops | bytes accessed | tf_op | source)
XLA Modules:
  0.0 23.6 jit_solution(1678657825267317125)
XLA Ops:
  0.0 0.0 copy-start
  0.0 1.0 %pad_maximum_fusion.3 = bf16[128,2,128]{2,1,0:T(2,128)(2,1)S(1)} fusion(bf16[64,2,128]{2,1,0:T(2,128)(2,1)} %param.6, bf16[64,2,128]{2,1,0:T(2,128)(2,1)} %param.5), kind=kLoop, calls=%fused_computation.4 | loop fusion | flops 32768 | bytes 131072 | tf_op jit(solution)/shard_map/concatenate | solution.py:184
  1.0 0.2 shard_map.46
  1.1 3.1 %collective-permute-start = (bf16[128,128]{1,0:T(8,128)(2,1)S(1)}, bf16[128,128]{1,0:T(8,128)(2,1)S(1)}, u32[]{:S(2)}, u32[]{:S(2)}) collective-permute-start(bf16[128,128]{1,0:T(8,128)(2,1)S(1)} %get-tuple-element.34), channel_id=1, source_target_pairs={{0,1},{1,2},{2,3},{3,0},{4,5},{5,6},{6,7},{7,4},{8,9},{9,10},{10,1... | collective-permute-start | bytes 98312 | tf_op jit(solution)/shard_map/ppermute | solution.py:188
  4.2 2.6 %collective-permute-start.1 = (bf16[128,128]{1,0:T(8,128)(2,1)S(1)}, bf16[128,128]{1,0:T(8,128)(2,1)S(1)}, u32[]{:S(2)}, u32[]{:S(2)}) collective-permute-start(bf16[128,128]{1,0:T(8,128)(2,1)S(1)} %get-tuple-element.35), channel_id=1, source_target_pairs={{0,2},{1,3},{2,0},{3,1},{4,6},{5,7},{6,4},{7,5},{8,10},{9,11},{10,... | collective-permute-start | bytes 98312 | tf_op jit(solution)/shard_map/ppermute | solution.py:188
  6.8 1.3 %collective-permute-start.2 = (bf16[128,128]{1,0:T(8,128)(2,1)S(1)}, bf16[128,128]{1,0:T(8,128)(2,1)S(1)}, u32[]{:S(2)}, u32[]{:S(2)}) collective-permute-start(bf16[128,128]{1,0:T(8,128)(2,1)S(1)} %get-tuple-element.36), channel_id=1, source_target_pairs={{0,3},{1,0},{2,1},{3,2},{4,7},{5,4},{6,5},{7,6},{8,11},{9,8},{10,9... | collective-permute-start | bytes 98312 | tf_op jit(solution)/shard_map/ppermute | solution.py:188
  8.8 2.5 %collective-permute-start.7 = (bf16[144,128]{1,0:T(8,128)(2,1)S(1)}, bf16[144,128]{1,0:T(8,128)(2,1)S(1)}, u32[]{:S(2)}, u32[]{:S(2)}) collective-permute-start(bf16[144,128]{1,0:T(8,128)(2,1)S(1)} %get-tuple-element.62.own_ref), channel_id=1, source_target_pairs={{0,24},{4,28},{8,16},{12,20},{16,8},{20,12},{24,0},{28,4},{1,25},{... | collective-permute-start | bytes 110600 | tf_op jit(solution)/shard_map/ppermute | solution.py:204
  11.3 0.5 %collective-permute-start.6 = (bf16[144,128]{1,0:T(8,128)(2,1)S(1)}, bf16[144,128]{1,0:T(8,128)(2,1)S(1)}, u32[]{:S(2)}, u32[]{:S(2)}) collective-permute-start(bf16[144,128]{1,0:T(8,128)(2,1)S(1)} %get-tuple-element.62.own_ref), channel_id=1, source_target_pairs={{0,16},{4,12},{8,24},{12,4},{16,0},{20,28},{24,8},{28,20},{1,17},{... | collective-permute-start | bytes 110600 | tf_op jit(solution)/shard_map/ppermute | solution.py:204
  11.8 0.0 collective-permute-done
  11.8 0.0 collective-permute-done.1
  11.8 0.0 collective-permute-done.2
  11.9 1.6 %collective-permute-start.5 = (bf16[1,384,128]{2,1,0:T(8,128)(2,1)S(1)}, bf16[1,384,128]{2,1,0:T(8,128)(2,1)S(1)}, u32[]{:S(2)}, u32[]{:S(2)}) collective-permute-start(bf16[1,384,128]{2,1,0:T(8,128)(2,1)S(1)} %maximum_bitcast_fusion.refs_1_), channel_id=1, source_target_pairs={{0,24},{4,28},{8,16},{12,20},{16,8},{20,12},{24,0},{28,4},{1,25},{... | collective-permute-start | bytes 294920 | tf_op jit(solution)/shard_map/ppermute | solution.py:204
  13.4 0.5 %collective-permute-start.4 = (bf16[1,384,128]{2,1,0:T(8,128)(2,1)S(1)}, bf16[1,384,128]{2,1,0:T(8,128)(2,1)S(1)}, u32[]{:S(2)}, u32[]{:S(2)}) collective-permute-start(bf16[1,384,128]{2,1,0:T(8,128)(2,1)S(1)} %maximum_bitcast_fusion.refs_1_), channel_id=1, source_target_pairs={{0,16},{4,12},{8,24},{12,4},{16,0},{20,28},{24,8},{28,20},{1,17},{... | collective-permute-start | bytes 294920 | tf_op jit(solution)/shard_map/ppermute | solution.py:204
  13.9 0.0 collective-permute-done.7
  13.9 1.4 %collective-permute-done.6 = bf16[144,128]{1,0:T(8,128)(2,1)S(1)} collective-permute-done((bf16[144,128]{1,0:T(8,128)(2,1)S(1)}, bf16[144,128]{1,0:T(8,128)(2,1)S(1)}, u32[]{:S(2)}, u32[]{:S(2)}) %collective-permute-start.6) | collective-permute-done | bytes 36896 | tf_op jit(solution)/shard_map/ppermute | solution.py:204
  15.4 0.1 collective-permute-start.8
  15.5 1.6 %collective-permute-start.3 = (bf16[1,528,128]{2,1,0:T(8,128)(2,1)S(1)}, bf16[1,528,128]{2,1,0:T(8,128)(2,1)S(1)}, u32[]{:S(2)}, u32[]{:S(2)}) collective-permute-start(bf16[1,528,128]{2,1,0:T(8,128)(2,1)S(1)} %pad_maximum_fusion.1), channel_id=1, source_target_pairs={{0,8},{4,20},{8,0},{12,28},{16,24},{20,4},{24,16},{28,12},{1,9},{5... | collective-permute-start | bytes 405512 | tf_op jit(solution)/shard_map/ppermute | solution.py:204
  17.0 0.0 copy-done
  17.0 0.1 constant_dynamic-slice_fusion
  17.2 0.2 shard_map.47.query_ref
  17.4 0.8 %shard_map.48 = (f32[1,1024]{1,0:T(1,128)S(1)}, f32[1,1024]{1,0:T(1,128)S(1)}, f32[128,1024]{1,0:T(8,128)S(1)}) custom-call(bf16[144,128]{1,0:T(8,128)(2,1)S(1)} %get-tuple-element.62.own_ref, bf16[256,1024]{1,0:T(8,128)(2,1)S(1)} %shard_map.47.query_ref, bf16[3,144,128]{2,1,0:T(8,128)(2,1)S(1)} %pad_maximum_fusion.2.refs_0_.refs_3_, ...), custom_call_target="tpu_custom_call" | custom-call | tf_op jit(solution)/shard_map/pallas_call | solution.py:150
  18.2 0.0 collective-permute-done.8.refs_3_.refs_4_
  18.2 0.9 %shard_map.49 = (f32[1,1024]{1,0:T(1,128)S(1)}, f32[1,1024]{1,0:T(1,128)S(1)}, f32[128,1024]{1,0:T(8,128)S(1)}) custom-call(bf16[144,128]{1,0:T(8,128)(2,1)S(1)} %get-tuple-element.62.own_ref, bf16[256,1024]{1,0:T(8,128)(2,1)S(1)} %shard_map.47.query_ref, f32[1,1024]{1,0:T(1,128)S(1)} %get-tuple-element.37.refs_0_, f32[1,1024]{1,0:T(1,128)S(1)} %get-tuple-element.38.refs_1_, ...), custom_call_target="tpu_custom_call" | custom-call | tf_op jit(solution)/shard_map/pallas_call | solution.py:150
  19.1 0.0 collective-permute-done.5.refs_5_
  19.1 0.0 collective-permute-done.4.refs_4_
  19.1 0.1 collective-permute-start.9
  19.2 0.5 %collective-permute-start.10 = (bf16[1,384,128]{2,1,0:T(8,128)(2,1)S(1)}, bf16[1,384,128]{2,1,0:T(8,128)(2,1)S(1)}, u32[]{:S(2)}, u32[]{:S(2)}) collective-permute-start(bf16[1,384,128]{2,1,0:T(8,128)(2,1)S(1)} %collective-permute-done.5.refs_5_), channel_id=1, source_target_pairs={{0,4},{4,0},{8,12},{12,8},{16,20},{20,16},{24,28},{28,24},{1,5},{5... | collective-permute-start | bytes 294920 | tf_op jit(solution)/shard_map/ppermute | solution.py:197
  19.7 0.8 %shard_map.50 = (f32[1,1024]{1,0:T(1,128)S(1)}, f32[1,1024]{1,0:T(1,128)S(1)}, f32[128,1024]{1,0:T(8,128)S(1)}) custom-call(bf16[144,128]{1,0:T(8,128)(2,1)S(1)} %get-tuple-element.62.own_ref, bf16[256,1024]{1,0:T(8,128)(2,1)S(1)} %shard_map.47.query_ref, f32[1,1024]{1,0:T(1,128)S(1)} %get-tuple-element.43.refs_0_, f32[1,1024]{1,0:T(1,128)S(1)} %get-tuple-element.44.refs_1_, ...), custom_call_target="tpu_custom_call" | custom-call | tf_op jit(solution)/shard_map/pallas_call | solution.py:150
  20.5 0.0 collective-permute-done.3.refs_3_
  20.6 0.0 collective-permute-done.9.refs_5_
  20.6 0.1 collective-permute-done.10.refs_6_
  20.7 0.4 %collective-permute-start.11 = (bf16[1,528,128]{2,1,0:T(8,128)(2,1)S(1)}, bf16[1,528,128]{2,1,0:T(8,128)(2,1)S(1)}, u32[]{:S(2)}, u32[]{:S(2)}) collective-permute-start(bf16[1,528,128]{2,1,0:T(8,128)(2,1)S(1)} %collective-permute-done.3.refs_3_), channel_id=1, source_target_pairs={{0,4},{4,0},{8,12},{12,8},{16,20},{20,16},{24,28},{28,24},{1,5},{5... | collective-permute-start | bytes 405512 | tf_op jit(solution)/shard_map/ppermute | solution.py:197
  21.0 1.1 %shard_map.51 = (f32[1,1024]{1,0:T(1,128)S(1)}, f32[1,1024]{1,0:T(1,128)S(1)}, f32[128,1024]{1,0:T(8,128)S(1)}) custom-call(bf16[144,128]{1,0:T(8,128)(2,1)S(1)} %get-tuple-element.62.own_ref, bf16[256,1024]{1,0:T(8,128)(2,1)S(1)} %shard_map.47.query_ref, f32[1,1024]{1,0:T(1,128)S(1)} %get-tuple-element.51.refs_0_, f32[1,1024]{1,0:T(1,128)S(1)} %get-tuple-element.52.refs_1_, ...), custom_call_target="tpu_custom_call" | custom-call | tf_op jit(solution)/shard_map/pallas_call | solution.py:150
  22.2 0.0 collective-permute-done.11.refs_3_
  22.2 1.4 %shard_map.52 = bf16[1024,128]{1,0:T(8,128)(2,1)} custom-call(bf16[144,128]{1,0:T(8,128)(2,1)S(1)} %get-tuple-element.62.own_ref, bf16[256,1024]{1,0:T(8,128)(2,1)S(1)} %shard_map.47.query_ref, f32[1,1024]{1,0:T(1,128)S(1)} %get-tuple-element.58.refs_0_, f32[1,1024]{1,0:T(1,128)S(1)} %get-tuple-element.59.refs_1_, ...), custom_call_target="tpu_custom_call" | custom-call | tf_op jit(solution)/shard_map/pallas_call | solution.py:150
  (5 shorter events, 0.1 us)
Async XLA Ops:
  0.0 17.0 %copy-start = (bf16[256,16,128]{2,1,0:T(8,128)(2,1)S(1)}, bf16[256,16,128]{2,1,0:T(8,128)(2,1)}, u32[]{:S(2)}) copy-start(bf16[256,16,128]{2,1,0:T(8,128)(2,1)} %param.4) | copy-start | bytes 3145732
  1.1 10.7 %collective-permute-start = (bf16[128,128]{1,0:T(8,128)(2,1)S(1)}, bf16[128,128]{1,0:T(8,128)(2,1)S(1)}, u32[]{:S(2)}, u32[]{:S(2)}) collective-permute-start(bf16[128,128]{1,0:T(8,128)(2,1)S(1)} %get-tuple-element.34), channel_id=1, source_target_pairs={{0,1},{1,2},{2,3},{3,0},{4,5},{5,6},{6,7},{7,4},{8,9},{9,10},{10,1... | collective-permute-start | bytes 98312 | tf_op jit(solution)/shard_map/ppermute | solution.py:188
  4.2 7.6 %collective-permute-start.1 = (bf16[128,128]{1,0:T(8,128)(2,1)S(1)}, bf16[128,128]{1,0:T(8,128)(2,1)S(1)}, u32[]{:S(2)}, u32[]{:S(2)}) collective-permute-start(bf16[128,128]{1,0:T(8,128)(2,1)S(1)} %get-tuple-element.35), channel_id=1, source_target_pairs={{0,2},{1,3},{2,0},{3,1},{4,6},{5,7},{6,4},{7,5},{8,10},{9,11},{10,... | collective-permute-start | bytes 98312 | tf_op jit(solution)/shard_map/ppermute | solution.py:188
  6.8 5.1 %collective-permute-start.2 = (bf16[128,128]{1,0:T(8,128)(2,1)S(1)}, bf16[128,128]{1,0:T(8,128)(2,1)S(1)}, u32[]{:S(2)}, u32[]{:S(2)}) collective-permute-start(bf16[128,128]{1,0:T(8,128)(2,1)S(1)} %get-tuple-element.36), channel_id=1, source_target_pairs={{0,3},{1,0},{2,1},{3,2},{4,7},{5,4},{6,5},{7,6},{8,11},{9,8},{10,9... | collective-permute-start | bytes 98312 | tf_op jit(solution)/shard_map/ppermute | solution.py:188
  8.8 5.1 %collective-permute-start.7 = (bf16[144,128]{1,0:T(8,128)(2,1)S(1)}, bf16[144,128]{1,0:T(8,128)(2,1)S(1)}, u32[]{:S(2)}, u32[]{:S(2)}) collective-permute-start(bf16[144,128]{1,0:T(8,128)(2,1)S(1)} %get-tuple-element.62.own_ref), channel_id=1, source_target_pairs={{0,24},{4,28},{8,16},{12,20},{16,8},{20,12},{24,0},{28,4},{1,25},{... | collective-permute-start | bytes 110600 | tf_op jit(solution)/shard_map/ppermute | solution.py:204
  11.3 4.0 %collective-permute-start.6 = (bf16[144,128]{1,0:T(8,128)(2,1)S(1)}, bf16[144,128]{1,0:T(8,128)(2,1)S(1)}, u32[]{:S(2)}, u32[]{:S(2)}) collective-permute-start(bf16[144,128]{1,0:T(8,128)(2,1)S(1)} %get-tuple-element.62.own_ref), channel_id=1, source_target_pairs={{0,16},{4,12},{8,24},{12,4},{16,0},{20,28},{24,8},{28,20},{1,17},{... | collective-permute-start | bytes 110600 | tf_op jit(solution)/shard_map/ppermute | solution.py:204
  11.9 7.2 %collective-permute-start.5 = (bf16[1,384,128]{2,1,0:T(8,128)(2,1)S(1)}, bf16[1,384,128]{2,1,0:T(8,128)(2,1)S(1)}, u32[]{:S(2)}, u32[]{:S(2)}) collective-permute-start(bf16[1,384,128]{2,1,0:T(8,128)(2,1)S(1)} %maximum_bitcast_fusion.refs_1_), channel_id=1, source_target_pairs={{0,24},{4,28},{8,16},{12,20},{16,8},{20,12},{24,0},{28,4},{1,25},{... | collective-permute-start | bytes 294920 | tf_op jit(solution)/shard_map/ppermute | solution.py:204
  13.4 5.7 %collective-permute-start.4 = (bf16[1,384,128]{2,1,0:T(8,128)(2,1)S(1)}, bf16[1,384,128]{2,1,0:T(8,128)(2,1)S(1)}, u32[]{:S(2)}, u32[]{:S(2)}) collective-permute-start(bf16[1,384,128]{2,1,0:T(8,128)(2,1)S(1)} %maximum_bitcast_fusion.refs_1_), channel_id=1, source_target_pairs={{0,16},{4,12},{8,24},{12,4},{16,0},{20,28},{24,8},{28,20},{1,17},{... | collective-permute-start | bytes 294920 | tf_op jit(solution)/shard_map/ppermute | solution.py:204
  15.4 2.8 %collective-permute-start.8 = (bf16[1,816,128]{2,1,0:T(8,128)(2,1)S(1)}, bf16[1,816,128]{2,1,0:T(8,128)(2,1)S(1)}, u32[]{:S(2)}, u32[]{:S(2)}) collective-permute-start(bf16[1,816,128]{2,1,0:T(8,128)(2,1)S(1)} %pad_maximum_fusion), channel_id=1, source_target_pairs={{0,4},{4,0},{8,12},{12,8},{16,20},{20,16},{24,28},{28,24},{1,5},{5... | collective-permute-start | bytes 626696 | tf_op jit(solution)/shard_map/ppermute | solution.py:197
  15.5 5.1 %collective-permute-start.3 = (bf16[1,528,128]{2,1,0:T(8,128)(2,1)S(1)}, bf16[1,528,128]{2,1,0:T(8,128)(2,1)S(1)}, u32[]{:S(2)}, u32[]{:S(2)}) collective-permute-start(bf16[1,528,128]{2,1,0:T(8,128)(2,1)S(1)} %pad_maximum_fusion.1), channel_id=1, source_target_pairs={{0,8},{4,20},{8,0},{12,28},{16,24},{20,4},{24,16},{28,12},{1,9},{5... | collective-permute-start | bytes 405512 | tf_op jit(solution)/shard_map/ppermute | solution.py:204
  19.1 1.4 %collective-permute-start.9 = (bf16[1,384,128]{2,1,0:T(8,128)(2,1)S(1)}, bf16[1,384,128]{2,1,0:T(8,128)(2,1)S(1)}, u32[]{:S(2)}, u32[]{:S(2)}) collective-permute-start(bf16[1,384,128]{2,1,0:T(8,128)(2,1)S(1)} %collective-permute-done.4.refs_4_), channel_id=1, source_target_pairs={{0,4},{4,0},{8,12},{12,8},{16,20},{20,16},{24,28},{28,24},{1,5},{5... | collective-permute-start | bytes 294920 | tf_op jit(solution)/shard_map/ppermute | solution.py:197
  19.2 1.4 %collective-permute-start.10 = (bf16[1,384,128]{2,1,0:T(8,128)(2,1)S(1)}, bf16[1,384,128]{2,1,0:T(8,128)(2,1)S(1)}, u32[]{:S(2)}, u32[]{:S(2)}) collective-permute-start(bf16[1,384,128]{2,1,0:T(8,128)(2,1)S(1)} %collective-permute-done.5.refs_5_), channel_id=1, source_target_pairs={{0,4},{4,0},{8,12},{12,8},{16,20},{20,16},{24,28},{28,24},{1,5},{5... | collective-permute-start | bytes 294920 | tf_op jit(solution)/shard_map/ppermute | solution.py:197
  20.7 1.5 %collective-permute-start.11 = (bf16[1,528,128]{2,1,0:T(8,128)(2,1)S(1)}, bf16[1,528,128]{2,1,0:T(8,128)(2,1)S(1)}, u32[]{:S(2)}, u32[]{:S(2)}) collective-permute-start(bf16[1,528,128]{2,1,0:T(8,128)(2,1)S(1)} %collective-permute-done.3.refs_3_), channel_id=1, source_target_pairs={{0,4},{4,0},{8,12},{12,8},{16,20},{20,16},{24,28},{28,24},{1,5},{5... | collective-permute-start | bytes 405512 | tf_op jit(solution)/shard_map/ppermute | solution.py:197

commit v24 on v20

--- a/solution.py
+++ b/solution.py
@@ -10,7 +10,7 @@
 
 MARK = 16
 SUBLANES = 8
-FINAL = 256
+FINAL = 512
 OVERLAP = 0
 LOW = -1e30
 HIGH = 1e30

time: 23.5 us -> 23.5 us (level)
  no operation moved by 1% of the time
where the time goes in v24:
time: 23.5 us; the launch traced here: 23.4 us
  starting transfers between devices  13.6 us (58%)
  Pallas kernels  5.47 us (23%)
  waiting for transfers between devices  2.36 us (10%)
  other arithmetic  1.01 us (4%)
  between operations  0.78 us (3%)
    ppermute x3, starting transfers between devices, shards(): lax.ppermute(rows, 'head', [(i, (i + shift + 1) % pieces) for i in range(...  7.01 us
    ppermute x5, starting transfers between devices, hop(): lax.ppermute(rows, 'seq', [(i, i ^ way[i & 1]) for i in range(blocks)])  5.65 us
    pallas_call x5, Pallas kernels, attend_call(): pl.pallas_call(functools.partial(attend, pieces, part, first, last, items...  5.11 us
    ppermute x5, waiting for transfers between devices, hop(): lax.ppermute(rows, 'seq', [(i, i ^ way[i & 1]) for i in range(blocks)])  2.15 us
    concatenate x1, other arithmetic, shards(): jnp.concatenate([keys, values]).reshape(2 * part * kv_heads, head_width)  0.95 us
    ppermute x4, starting transfers between devices, swap(): return lax.ppermute(rows, 'seq', [(i, i ^ flip) for i in range(blocks)])  0.94 us
  transfers between devices with their start and end apart: 12, of which 3 were waited for; matrix products, arithmetic and copies ran while one was open for 1% of the time, Pallas kernels for 17%

profile of v24, /device:TPU:0, one launch (start us, length us, event | category | flops | bytes accessed | tf_op | source)
XLA Modules:
  0.0 23.4 jit_solution(13256048816553703726)
XLA Ops:
  0.0 0.0 copy-start
  0.0 1.0 %pad_maximum_fusion.3 = bf16[128,2,128]{2,1,0:T(2,128)(2,1)S(1)} fusion(bf16[64,2,128]{2,1,0:T(2,128)(2,1)} %param.6, bf16[64,2,128]{2,1,0:T(2,128)(2,1)} %param.5), kind=kLoop, calls=%fused_computation.4 | loop fusion | flops 32768 | bytes 131072 | tf_op jit(solution)/shard_map/concatenate | solution.py:184
  1.0 0.2 shard_map.46
  1.1 3.1 %collective-permute-start = (bf16[128,128]{1,0:T(8,128)(2,1)S(1)}, bf16[128,128]{1,0:T(8,128)(2,1)S(1)}, u32[]{:S(2)}, u32[]{:S(2)}) collective-permute-start(bf16[128,128]{1,0:T(8,128)(2,1)S(1)} %get-tuple-element.34), channel_id=1, source_target_pairs={{0,1},{1,2},{2,3},{3,0},{4,5},{5,6},{6,7},{7,4},{8,9},{9,10},{10,1... | collective-permute-start | bytes 98312 | tf_op jit(solution)/shard_map/ppermute | solution.py:188
  4.2 2.6 %collective-permute-start.1 = (bf16[128,128]{1,0:T(8,128)(2,1)S(1)}, bf16[128,128]{1,0:T(8,128)(2,1)S(1)}, u32[]{:S(2)}, u32[]{:S(2)}) collective-permute-start(bf16[128,128]{1,0:T(8,128)(2,1)S(1)} %get-tuple-element.35), channel_id=1, source_target_pairs={{0,2},{1,3},{2,0},{3,1},{4,6},{5,7},{6,4},{7,5},{8,10},{9,11},{10,... | collective-permute-start | bytes 98312 | tf_op jit(solution)/shard_map/ppermute | solution.py:188
  6.8 1.3 %collective-permute-start.2 = (bf16[128,128]{1,0:T(8,128)(2,1)S(1)}, bf16[128,128]{1,0:T(8,128)(2,1)S(1)}, u32[]{:S(2)}, u32[]{:S(2)}) collective-permute-start(bf16[128,128]{1,0:T(8,128)(2,1)S(1)} %get-tuple-element.36), channel_id=1, source_target_pairs={{0,3},{1,0},{2,1},{3,2},{4,7},{5,4},{6,5},{7,6},{8,11},{9,8},{10,9... | collective-permute-start | bytes 98312 | tf_op jit(solution)/shard_map/ppermute | solution.py:188
  8.8 2.5 %collective-permute-start.7 = (bf16[144,128]{1,0:T(8,128)(2,1)S(1)}, bf16[144,128]{1,0:T(8,128)(2,1)S(1)}, u32[]{:S(2)}, u32[]{:S(2)}) collective-permute-start(bf16[144,128]{1,0:T(8,128)(2,1)S(1)} %get-tuple-element.62.own_ref), channel_id=1, source_target_pairs={{0,24},{4,28},{8,16},{12,20},{16,8},{20,12},{24,0},{28,4},{1,25},{... | collective-permute-start | bytes 110600 | tf_op jit(solution)/shard_map/ppermute | solution.py:204
  11.3 0.5 %collective-permute-start.6 = (bf16[144,128]{1,0:T(8,128)(2,1)S(1)}, bf16[144,128]{1,0:T(8,128)(2,1)S(1)}, u32[]{:S(2)}, u32[]{:S(2)}) collective-permute-start(bf16[144,128]{1,0:T(8,128)(2,1)S(1)} %get-tuple-element.62.own_ref), channel_id=1, source_target_pairs={{0,8},{4,20},{8,0},{12,28},{16,24},{20,4},{24,16},{28,12},{1,9},{5... | collective-permute-start | bytes 110600 | tf_op jit(solution)/shard_map/ppermute | solution.py:204
  11.9 0.0 collective-permute-done
  11.9 0.0 collective-permute-done.1
  11.9 0.0 collective-permute-done.2
  11.9 1.5 %collective-permute-start.5 = (bf16[1,384,128]{2,1,0:T(8,128)(2,1)S(1)}, bf16[1,384,128]{2,1,0:T(8,128)(2,1)S(1)}, u32[]{:S(2)}, u32[]{:S(2)}) collective-permute-start(bf16[1,384,128]{2,1,0:T(8,128)(2,1)S(1)} %maximum_bitcast_fusion.refs_1_), channel_id=1, source_target_pairs={{0,24},{4,28},{8,16},{12,20},{16,8},{20,12},{24,0},{28,4},{1,25},{... | collective-permute-start | bytes 294920 | tf_op jit(solution)/shard_map/ppermute | solution.py:204
  13.4 0.5 %collective-permute-start.4 = (bf16[1,384,128]{2,1,0:T(8,128)(2,1)S(1)}, bf16[1,384,128]{2,1,0:T(8,128)(2,1)S(1)}, u32[]{:S(2)}, u32[]{:S(2)}) collective-permute-start(bf16[1,384,128]{2,1,0:T(8,128)(2,1)S(1)} %maximum_bitcast_fusion.refs_1_), channel_id=1, source_target_pairs={{0,8},{4,20},{8,0},{12,28},{16,24},{20,4},{24,16},{28,12},{1,9},{5... | collective-permute-start | bytes 294920 | tf_op jit(solution)/shard_map/ppermute | solution.py:204
  13.9 0.0 collective-permute-done.7
  13.9 1.4 %collective-permute-done.6 = bf16[144,128]{1,0:T(8,128)(2,1)S(1)} collective-permute-done((bf16[144,128]{1,0:T(8,128)(2,1)S(1)}, bf16[144,128]{1,0:T(8,128)(2,1)S(1)}, u32[]{:S(2)}, u32[]{:S(2)}) %collective-permute-start.6) | collective-permute-done | bytes 36896 | tf_op jit(solution)/shard_map/ppermute | solution.py:204
  15.4 0.1 collective-permute-start.8
  15.5 0.6 %collective-permute-start.3 = (bf16[1,528,128]{2,1,0:T(8,128)(2,1)S(1)}, bf16[1,528,128]{2,1,0:T(8,128)(2,1)S(1)}, u32[]{:S(2)}, u32[]{:S(2)}) collective-permute-start(bf16[1,528,128]{2,1,0:T(8,128)(2,1)S(1)} %pad_maximum_fusion.1), channel_id=1, source_target_pairs={{0,16},{4,12},{8,24},{12,4},{16,0},{20,28},{24,8},{28,20},{1,17},{... | collective-permute-start | bytes 405512 | tf_op jit(solution)/shard_map/ppermute | solution.py:204
  16.1 0.0 copy-done
  16.1 0.1 constant_dynamic-slice_fusion
  16.2 0.2 shard_map.47.query_ref
  16.4 0.8 %shard_map.48 = (f32[1,1024]{1,0:T(1,128)S(1)}, f32[1,1024]{1,0:T(1,128)S(1)}, f32[128,1024]{1,0:T(8,128)S(1)}) custom-call(bf16[144,128]{1,0:T(8,128)(2,1)S(1)} %get-tuple-element.62.own_ref, bf16[256,1024]{1,0:T(8,128)(2,1)S(1)} %shard_map.47.query_ref, bf16[3,144,128]{2,1,0:T(8,128)(2,1)S(1)} %pad_maximum_fusion.2.refs_0_.refs_3_, ...), custom_call_target="tpu_custom_call" | custom-call | tf_op jit(solution)/shard_map/pallas_call | solution.py:150
  17.3 0.0 collective-permute-done.8.refs_3_.refs_4_
  17.3 0.9 %shard_map.49 = (f32[1,1024]{1,0:T(1,128)S(1)}, f32[1,1024]{1,0:T(1,128)S(1)}, f32[128,1024]{1,0:T(8,128)S(1)}) custom-call(bf16[144,128]{1,0:T(8,128)(2,1)S(1)} %get-tuple-element.62.own_ref, bf16[256,1024]{1,0:T(8,128)(2,1)S(1)} %shard_map.47.query_ref, f32[1,1024]{1,0:T(1,128)S(1)} %get-tuple-element.37.refs_0_, f32[1,1024]{1,0:T(1,128)S(1)} %get-tuple-element.38.refs_1_, ...), custom_call_target="tpu_custom_call" | custom-call | tf_op jit(solution)/shard_map/pallas_call | solution.py:150
  18.2 0.0 collective-permute-done.5.refs_5_
  18.2 0.0 collective-permute-done.4.refs_4_
  18.2 0.8 %collective-permute-start.9 = (bf16[1,384,128]{2,1,0:T(8,128)(2,1)S(1)}, bf16[1,384,128]{2,1,0:T(8,128)(2,1)S(1)}, u32[]{:S(2)}, u32[]{:S(2)}) collective-permute-start(bf16[1,384,128]{2,1,0:T(8,128)(2,1)S(1)} %collective-permute-done.4.refs_4_), channel_id=1, source_target_pairs={{0,4},{4,0},{8,12},{12,8},{16,20},{20,16},{24,28},{28,24},{1,5},{5... | collective-permute-start | bytes 294920 | tf_op jit(solution)/shard_map/ppermute | solution.py:197
  19.0 0.1 collective-permute-start.10
  19.1 0.8 %shard_map.50 = (f32[1,1024]{1,0:T(1,128)S(1)}, f32[1,1024]{1,0:T(1,128)S(1)}, f32[128,1024]{1,0:T(8,128)S(1)}) custom-call(bf16[144,128]{1,0:T(8,128)(2,1)S(1)} %get-tuple-element.62.own_ref, bf16[256,1024]{1,0:T(8,128)(2,1)S(1)} %shard_map.47.query_ref, f32[1,1024]{1,0:T(1,128)S(1)} %get-tuple-element.43.refs_0_, f32[1,1024]{1,0:T(1,128)S(1)} %get-tuple-element.44.refs_1_, ...), custom_call_target="tpu_custom_call" | custom-call | tf_op jit(solution)/shard_map/pallas_call | solution.py:150
  19.9 0.7 %collective-permute-done.3.refs_3_ = bf16[1,528,128]{2,1,0:T(8,128)(2,1)S(1)} collective-permute-done((bf16[1,528,128]{2,1,0:T(8,128)(2,1)S(1)}, bf16[1,528,128]{2,1,0:T(8,128)(2,1)S(1)}, u32[]{:S(2)}, u32[]{:S(2)}) %collective-permute-start.3) | collective-permute-done | bytes 135200 | tf_op jit(solution)/shard_map/ppermute | solution.py:204
  20.6 0.0 collective-permute-done.9.refs_5_
  20.6 0.0 collective-permute-done.10.refs_6_
  20.6 0.0 collective-permute-start.11
  20.6 1.1 %shard_map.51 = (f32[1,1024]{1,0:T(1,128)S(1)}, f32[1,1024]{1,0:T(1,128)S(1)}, f32[128,1024]{1,0:T(8,128)S(1)}) custom-call(bf16[144,128]{1,0:T(8,128)(2,1)S(1)} %get-tuple-element.62.own_ref, bf16[256,1024]{1,0:T(8,128)(2,1)S(1)} %shard_map.47.query_ref, f32[1,1024]{1,0:T(1,128)S(1)} %get-tuple-element.51.refs_0_, f32[1,1024]{1,0:T(1,128)S(1)} %get-tuple-element.52.refs_1_, ...), custom_call_target="tpu_custom_call" | custom-call | tf_op jit(solution)/shard_map/pallas_call | solution.py:150
  21.8 0.2 collective-permute-done.11.refs_3_
  22.0 1.4 %shard_map.52 = bf16[1024,128]{1,0:T(8,128)(2,1)} custom-call(bf16[144,128]{1,0:T(8,128)(2,1)S(1)} %get-tuple-element.62.own_ref, bf16[256,1024]{1,0:T(8,128)(2,1)S(1)} %shard_map.47.query_ref, f32[1,1024]{1,0:T(1,128)S(1)} %get-tuple-element.58.refs_0_, f32[1,1024]{1,0:T(1,128)S(1)} %get-tuple-element.59.refs_1_, ...), custom_call_target="tpu_custom_call" | custom-call | tf_op jit(solution)/shard_map/pallas_call | solution.py:150
  (5 shorter events, 0.1 us)
Async XLA Ops:
  0.0 16.1 %copy-start = (bf16[256,16,128]{2,1,0:T(8,128)(2,1)S(1)}, bf16[256,16,128]{2,1,0:T(8,128)(2,1)}, u32[]{:S(2)}) copy-start(bf16[256,16,128]{2,1,0:T(8,128)(2,1)} %param.4) | copy-start | bytes 3145732
  1.1 10.7 %collective-permute-start = (bf16[128,128]{1,0:T(8,128)(2,1)S(1)}, bf16[128,128]{1,0:T(8,128)(2,1)S(1)}, u32[]{:S(2)}, u32[]{:S(2)}) collective-permute-start(bf16[128,128]{1,0:T(8,128)(2,1)S(1)} %get-tuple-element.34), channel_id=1, source_target_pairs={{0,1},{1,2},{2,3},{3,0},{4,5},{5,6},{6,7},{7,4},{8,9},{9,10},{10,1... | collective-permute-start | bytes 98312 | tf_op jit(solution)/shard_map/ppermute | solution.py:188
  4.2 7.7 %collective-permute-start.1 = (bf16[128,128]{1,0:T(8,128)(2,1)S(1)}, bf16[128,128]{1,0:T(8,128)(2,1)S(1)}, u32[]{:S(2)}, u32[]{:S(2)}) collective-permute-start(bf16[128,128]{1,0:T(8,128)(2,1)S(1)} %get-tuple-element.35), channel_id=1, source_target_pairs={{0,2},{1,3},{2,0},{3,1},{4,6},{5,7},{6,4},{7,5},{8,10},{9,11},{10,... | collective-permute-start | bytes 98312 | tf_op jit(solution)/shard_map/ppermute | solution.py:188
  6.8 5.1 %collective-permute-start.2 = (bf16[128,128]{1,0:T(8,128)(2,1)S(1)}, bf16[128,128]{1,0:T(8,128)(2,1)S(1)}, u32[]{:S(2)}, u32[]{:S(2)}) collective-permute-start(bf16[128,128]{1,0:T(8,128)(2,1)S(1)} %get-tuple-element.36), channel_id=1, source_target_pairs={{0,3},{1,0},{2,1},{3,2},{4,7},{5,4},{6,5},{7,6},{8,11},{9,8},{10,9... | collective-permute-start | bytes 98312 | tf_op jit(solution)/shard_map/ppermute | solution.py:188
  8.8 5.1 %collective-permute-start.7 = (bf16[144,128]{1,0:T(8,128)(2,1)S(1)}, bf16[144,128]{1,0:T(8,128)(2,1)S(1)}, u32[]{:S(2)}, u32[]{:S(2)}) collective-permute-start(bf16[144,128]{1,0:T(8,128)(2,1)S(1)} %get-tuple-element.62.own_ref), channel_id=1, source_target_pairs={{0,24},{4,28},{8,16},{12,20},{16,8},{20,12},{24,0},{28,4},{1,25},{... | collective-permute-start | bytes 110600 | tf_op jit(solution)/shard_map/ppermute | solution.py:204
  11.3 4.0 %collective-permute-start.6 = (bf16[144,128]{1,0:T(8,128)(2,1)S(1)}, bf16[144,128]{1,0:T(8,128)(2,1)S(1)}, u32[]{:S(2)}, u32[]{:S(2)}) collective-permute-start(bf16[144,128]{1,0:T(8,128)(2,1)S(1)} %get-tuple-element.62.own_ref), channel_id=1, source_target_pairs={{0,8},{4,20},{8,0},{12,28},{16,24},{20,4},{24,16},{28,12},{1,9},{5... | collective-permute-start | bytes 110600 | tf_op jit(solution)/shard_map/ppermute | solution.py:204
  11.9 6.3 %collective-permute-start.5 = (bf16[1,384,128]{2,1,0:T(8,128)(2,1)S(1)}, bf16[1,384,128]{2,1,0:T(8,128)(2,1)S(1)}, u32[]{:S(2)}, u32[]{:S(2)}) collective-permute-start(bf16[1,384,128]{2,1,0:T(8,128)(2,1)S(1)} %maximum_bitcast_fusion.refs_1_), channel_id=1, source_target_pairs={{0,24},{4,28},{8,16},{12,20},{16,8},{20,12},{24,0},{28,4},{1,25},{... | collective-permute-start | bytes 294920 | tf_op jit(solution)/shard_map/ppermute | solution.py:204
  13.4 4.8 %collective-permute-start.4 = (bf16[1,384,128]{2,1,0:T(8,128)(2,1)S(1)}, bf16[1,384,128]{2,1,0:T(8,128)(2,1)S(1)}, u32[]{:S(2)}, u32[]{:S(2)}) collective-permute-start(bf16[1,384,128]{2,1,0:T(8,128)(2,1)S(1)} %maximum_bitcast_fusion.refs_1_), channel_id=1, source_target_pairs={{0,8},{4,20},{8,0},{12,28},{16,24},{20,4},{24,16},{28,12},{1,9},{5... | collective-permute-start | bytes 294920 | tf_op jit(solution)/shard_map/ppermute | solution.py:204
  15.4 1.8 %collective-permute-start.8 = (bf16[1,816,128]{2,1,0:T(8,128)(2,1)S(1)}, bf16[1,816,128]{2,1,0:T(8,128)(2,1)S(1)}, u32[]{:S(2)}, u32[]{:S(2)}) collective-permute-start(bf16[1,816,128]{2,1,0:T(8,128)(2,1)S(1)} %pad_maximum_fusion), channel_id=1, source_target_pairs={{0,4},{4,0},{8,12},{12,8},{16,20},{20,16},{24,28},{28,24},{1,5},{5... | collective-permute-start | bytes 626696 | tf_op jit(solution)/shard_map/ppermute | solution.py:197
  15.5 5.1 %collective-permute-start.3 = (bf16[1,528,128]{2,1,0:T(8,128)(2,1)S(1)}, bf16[1,528,128]{2,1,0:T(8,128)(2,1)S(1)}, u32[]{:S(2)}, u32[]{:S(2)}) collective-permute-start(bf16[1,528,128]{2,1,0:T(8,128)(2,1)S(1)} %pad_maximum_fusion.1), channel_id=1, source_target_pairs={{0,16},{4,12},{8,24},{12,4},{16,0},{20,28},{24,8},{28,20},{1,17},{... | collective-permute-start | bytes 405512 | tf_op jit(solution)/shard_map/ppermute | solution.py:204
  18.2 2.4 %collective-permute-start.9 = (bf16[1,384,128]{2,1,0:T(8,128)(2,1)S(1)}, bf16[1,384,128]{2,1,0:T(8,128)(2,1)S(1)}, u32[]{:S(2)}, u32[]{:S(2)}) collective-permute-start(bf16[1,384,128]{2,1,0:T(8,128)(2,1)S(1)} %collective-permute-done.4.refs_4_), channel_id=1, source_target_pairs={{0,4},{4,0},{8,12},{12,8},{16,20},{20,16},{24,28},{28,24},{1,5},{5... | collective-permute-start | bytes 294920 | tf_op jit(solution)/shard_map/ppermute | solution.py:197
  19.0 1.6 %collective-permute-start.10 = (bf16[1,384,128]{2,1,0:T(8,128)(2,1)S(1)}, bf16[1,384,128]{2,1,0:T(8,128)(2,1)S(1)}, u32[]{:S(2)}, u32[]{:S(2)}) collective-permute-start(bf16[1,384,128]{2,1,0:T(8,128)(2,1)S(1)} %collective-permute-done.5.refs_5_), channel_id=1, source_target_pairs={{0,4},{4,0},{8,12},{12,8},{16,20},{20,16},{24,28},{28,24},{1,5},{5... | collective-permute-start | bytes 294920 | tf_op jit(solution)/shard_map/ppermute | solution.py:197
  20.6 1.4 %collective-permute-start.11 = (bf16[1,528,128]{2,1,0:T(8,128)(2,1)S(1)}, bf16[1,528,128]{2,1,0:T(8,128)(2,1)S(1)}, u32[]{:S(2)}, u32[]{:S(2)}) collective-permute-start(bf16[1,528,128]{2,1,0:T(8,128)(2,1)S(1)} %collective-permute-done.3.refs_3_), channel_id=1, source_target_pairs={{0,4},{4,0},{8,12},{12,8},{16,20},{20,16},{24,28},{28,24},{1,5},{5... | collective-permute-start | bytes 405512 | tf_op jit(solution)/shard_map/ppermute | solution.py:197
